TPU v7x, 128 devices: a whole 4x4x4 slice. The times are simulated.
128 devices in a mesh: blk: 32 (over z, y, x_lo), val: 4 (over x_hi, core).
Axes of the slice: x: 4 (x_hi: 2, x_lo: 2; x = x_hi * 2 + x_lo), y: 4, z: 4, core: 2. Of those that a mesh axis runs over, the one named last changes fastest.
Arguments:
- data_rows: bfloat16 [8192, 4096], P('blk', 'val')
- noise_rows: bfloat16 [8192, 4096], P('blk', 'val')
Outputs:
- targets: bfloat16 [8192, 4096], P('blk', 'val')
All inputs are finite; a program needn't handle non-finite values.
Results may differ from a plain program's by a relative error of at most 0.0048.
Values may be sent and summed in bfloat16 or wider, within the bound.
No kernel may reach another device: no remote copies, remote signals or barrier semaphores. Data moves between devices by JAX's collectives and lax.ppermute only.
A program may use at most 128 MiB of HBM per device.

v0:
```python
import math

import jax
import jax.numpy as jnp
from jax import lax
from jax.sharding import PartitionSpec as P

ITERS = 2


def per_device(data_rows, noise_rows):
    width = data_rows.shape[1] * lax.axis_size("val")
    count = noise_rows.shape[0] * lax.axis_size("blk")
    eps = 0.64 / math.sqrt(width)
    data_f = data_rows.astype(jnp.float32)
    own_sq = jnp.sum(data_f * data_f, axis=1)
    every_noise = lax.all_gather(noise_rows, "blk", axis=0, tiled=True)
    piece_f = every_noise.astype(jnp.float32)
    piece_sq = jnp.sum(piece_f * piece_f, axis=1)
    cross = lax.dot_general(
        data_rows, every_noise, (((1,), (1,)), ((), ())), preferred_element_type=jnp.float32
    )
    partial_value = own_sq[:, None] + piece_sq[None, :] - 2.0 * cross
    cost = lax.psum(partial_value, "val") / width
    log_count = math.log(count)
    col_pot = jnp.zeros((count,), jnp.float32)
    for step in range(ITERS):
        row_pot = -eps * log_count - eps * jax.nn.logsumexp((col_pot[None, :] - cost) / eps, axis=1)
        scores = (row_pot[:, None] - cost) / eps
        col_max = jnp.max(scores, axis=0)
        col_total = jnp.sum(jnp.exp(scores - col_max[None, :]), axis=0)
        overall = lax.pmax(col_max.astype(jnp.bfloat16), "blk").astype(col_max.dtype)
        col_total = lax.psum(col_total * jnp.exp(col_max - overall), "blk")
        col_max = overall
        col_pot = -eps * log_count - eps * (col_max + jnp.log(col_total))
    weights = jax.nn.softmax((col_pot[None, :] - cost) / eps, axis=1).astype(jnp.bfloat16)
    targets = jnp.dot(weights, every_noise, preferred_element_type=jnp.float32)
    return targets.astype(jnp.bfloat16)


def solution(mesh):
    placed = (P("blk", "val"), P("blk", "val"))
    return jax.shard_map(
        per_device, mesh=mesh, in_specs=placed, out_specs=P("blk", "val"), check_vma=False
    )
```

profile of v0, /device:TPU:0, one launch (start us, length us, event | category | flops | bytes accessed | tf_op | source)
XLA Modules:
  0.0 1233.3 jit_solution(12989386052282008973)
XLA Ops:
  6.5 0.0 all-gather.2.cloned.1.call-start
  6.5 0.7 all-gather.2.cloned.1.call-update
  7.3 0.0 all-reduce.2.cloned.1.call-start
  7.3 1.2 multiply_reduce_fusion.1
  8.5 0.0 copy-start.1
  8.5 366.7 %all-gather.2.cloned.1.call-done = bf16[8192,1024]{1,0:T(8,128)(2,1)} async-done(((bf16[256,1024]{1,0:T(8,128)(2,1)}), bf16[8192,1024]{1,0:T(8,128)(2,1)}) %all-gather.2.cloned.1.call-update) | async-done | bytes 16777232 | tf_op jit(solution)/shard_map/all_gather | solution.py:17
  375.2 7.2 multiply_reduce_fusion
  382.4 0.0 copy-done.1
  382.4 19.1 %fusion = f32[256,8192]{1,0:T(8,128)} fusion(bf16[256,1024]{1,0:T(8,128)(2,1)S(1)} %copy-done.1, bf16[8192,1024]{1,0:T(8,128)(2,1)} %all-gather.2.cloned.1.call-done, f32[8192]{0:T(1024)S(1)} %multiply_reduce_fusion, f32[256]{0:T(256)S(1)} %multiply_reduce_fusion.1), kind=kOutput, calls=%fused_computation.2 | convolution fusion | flops 4301258752 | bytes 25723904 | tf_op jit(solution)/shard_map/dot_general | solution.py:20
  401.6 0.0 all-reduce.2.cloned.1.call-update
  401.6 158.0 %all-reduce.2.cloned.1.call-done = f32[256,8192]{1,0:T(8,128)} async-done(((f32[256,8192]{1,0:T(8,128)}), f32[256,8192]{1,0:T(8,128)}) %all-reduce.2.cloned.1.call-update) | async-done | bytes 8388624 | tf_op jit(solution)/shard_map/psum | solution.py:24
  559.6 0.0 copy-start
  559.6 4.7 fusion.1
  564.3 1.0 copy-done
  565.4 2.2 exponential_reduce_fusion.3
  567.6 1.2 fusion.2
  568.8 157.9 %pmax.14 = bf16[8192]{0:T(1024)(128)(2,1)S(1)} all-reduce(bf16[8192]{0:T(1024)(128)(2,1)S(1)} %convert_element_type.26), channel_id=1, replica_groups=mesh['blk'=32,'val'=4] {'blk'}, use_global_device_ids=true, to_apply=%region_6.0 | all-reduce | flops 8192 | bytes 32768 | tf_op jit(solution)/shard_map/pmax | solution.py:32
  726.7 4.5 exponential_reduce_fusion.2
  731.3 152.9 %psum.22 = f32[8192]{0:T(1024)S(1)} all-reduce(f32[8192]{0:T(1024)S(1)} %fusion.10), channel_id=1, replica_groups=mesh['blk'=32,'val'=4] {'blk'}, use_global_device_ids=true, to_apply=%region_8.0 | all-reduce | flops 8192 | bytes 65536 | tf_op jit(solution)/shard_map/psum | solution.py:33
  884.2 0.0 slice-start
  884.2 4.8 fusion.3
  889.1 0.0 slice-start.1
  889.1 4.7 exponential_reduce_fusion.1
  893.8 0.0 slice-done
  893.8 0.0 slice-done.1
  893.9 1.2 fusion.4
  895.1 152.8 %pmax.15 = bf16[8192]{0:T(1024)(128)(2,1)S(1)} all-reduce(bf16[8192]{0:T(1024)(128)(2,1)S(1)} %convert_element_type.28), channel_id=1, replica_groups=mesh['blk'=32,'val'=4] {'blk'}, use_global_device_ids=true, to_apply=%region_12.0 | all-reduce | flops 8192 | bytes 32768 | tf_op jit(solution)/shard_map/pmax | solution.py:32
  1047.9 4.5 exponential_reduce_fusion
  1052.5 152.7 %psum.23 = f32[8192]{0:T(1024)S(1)} all-reduce(f32[8192]{0:T(1024)S(1)} %fusion.14), channel_id=1, replica_groups=mesh['blk'=32,'val'=4] {'blk'}, use_global_device_ids=true, to_apply=%region_14.0 | all-reduce | flops 8192 | bytes 65536 | tf_op jit(solution)/shard_map/psum | solution.py:33
  1205.2 0.0 slice-start.2
  1205.2 4.8 fusion.5
  1210.1 0.0 slice-start.3
  1210.1 4.7 fusion.6
  1214.8 0.0 slice-done.2
  1214.8 0.0 slice-done.3
  1214.8 11.6 fusion.8
  (12 shorter events, 0.1 us)
Async XLA Ops:
  6.5 368.7 %all-gather.2.cloned.1.call-start = ((), (), s32[]{:S(2)}) async-start(), calls=%async_computation | async-start | bytes 17301504 | tf_op jit(solution)/shard_map/all_gather | solution.py:17
  7.3 552.4 %all-reduce.2.cloned.1.call-start = ((), (), s32[]{:S(2)}) async-start(), calls=%async_computation.1 | async-start | bytes 16777216 | tf_op jit(solution)/shard_map/psum | solution.py:24
  8.5 373.9 %copy-start.1 = (bf16[256,1024]{1,0:T(8,128)(2,1)S(1)}, bf16[256,1024]{1,0:T(8,128)(2,1)}, u32[]{:S(2)}) copy-start(bf16[256,1024]{1,0:T(8,128)(2,1)} %param.2) | copy-start | bytes 1572868
  559.6 5.8 copy-start
  884.2 9.6 slice-start
  889.1 4.8 slice-start.1
  1205.2 9.6 slice-start.2
  1210.1 4.8 slice-start.3
Sparse Core Ops, SparseCore 0:
  9.0 366.2 all-gather.1
  401.7 157.8 all-reduce.1
where the time goes:
time: 1230 us
  blocking collectives  616 us (50%)
  waiting for transfers between devices  525 us (43%)
  other arithmetic  46 us (4%)
  matrix products  30.7 us (2%)
  between operations  13.6 us (1%)
    all_gather x1, waiting for transfers between devices, per_device(): every_noise = lax.all_gather(noise_rows, 'blk', axis=0, tiled=True)  367 us
    pmax x2, blocking collectives, per_device(): lax.pmax(col_max.astype(jnp.bfloat16), 'blk').astype(col_max.dtype)  311 us
    psum x2, blocking collectives, per_device(): col_total = lax.psum(col_total * jnp.exp(col_max - overall), 'blk')  306 us
    psum x1, waiting for transfers between devices, per_device(): cost = lax.psum(partial_value, 'val') / width  158 us
  transfers between devices with their start and end apart: 2, of which 2 were waited for; matrix products, arithmetic and copies ran while one was open for 0% of the time, Pallas kernels for 0%

commit v1 on v0

v1 whole, which is shorter than its diff:
```python
import functools
import itertools
import math

import jax
import jax.numpy as jnp
from jax import lax
from jax.experimental import pallas as pl
from jax.experimental.pallas import tpu as pltpu
from jax.sharding import Mesh, PartitionSpec as P

AXES = ("z", "y", "l", "h", "c")
SIZES = (4, 4, 2, 2, 2)


def index_of(*place):
    index = 0
    for n, a in zip(SIZES, place):
        index = index * n + a % n
    return index


def move(value, dest):
    places = itertools.product(*(range(n) for n in SIZES))
    pairs = [(index_of(*place), index_of(*dest(*place))) for place in places]
    return lax.ppermute(value, AXES, pairs)


def from_y(value, k):
    return move(value, lambda z, y, l, h, c: (z, y - k, l, h, c))


def from_z(value, k):
    return move(value, lambda z, y, l, h, c: (z - k, y, l, h, c))


def flip(value, names):
    return move(
        value,
        lambda *place: [1 - a if name in names else a for name, a in zip(AXES, place)],
    )


def cross(a, b):
    return lax.dot_general(a, b, (((1,), (1,)), ((), ())), preferred_element_type=jnp.float32)


def dot(a, b):
    return jnp.dot(a, b, preferred_element_type=jnp.float32)


def exact_terms(total):
    terms = []
    for _ in range(3):
        terms.append(total.astype(jnp.bfloat16))
        total = total - terms[-1].astype(jnp.float32)
    return terms


def flat(blocks):
    return blocks.reshape(-1, blocks.shape[-1])


def half_squares(rows):
    sums = 0.0
    for at in range(0, rows.shape[1], 128):
        wide = rows[:, at : at + 128].astype(jnp.float32)
        sums = sums + wide * wide
    ones = jnp.full((16, 128), 0.5, jnp.bfloat16)
    return sum(cross(ones, term) for term in exact_terms(sums))[:1]


def call(kernel, outs, flops, *args, anywhere=0, spaces=None, scratch=()):
    moved = sum(a.size * a.dtype.itemsize for a in (*args, *outs))
    inner = len(args) - 1 - anywhere
    return pl.pallas_call(
        kernel,
        out_shape=outs,
        in_specs=[pl.BlockSpec(memory_space=pltpu.SMEM)]
        + [pl.BlockSpec(memory_space=pltpu.VMEM)] * inner
        + [pl.BlockSpec(memory_space=pl.ANY)] * anywhere,
        out_specs=[pl.BlockSpec(memory_space=spaces or pltpu.VMEM)] * len(outs),
        scratch_shapes=scratch,
        compiler_params=pltpu.CompilerParams(vmem_limit_bytes=20 * 2**20),
        cost_estimate=pl.CostEstimate(flops=flops, bytes_accessed=moved, transcendentals=0),
    )(*args)


def started(sems, *pairs):
    copies = [pltpu.make_async_copy(a, b, sems.at[n]) for n, (a, b) in enumerate(pairs)]
    for copy in copies:
        copy.start()
    return copies


def terms_in_rows(vec):
    row = lax.broadcasted_iota(jnp.int32, (16, vec.shape[1]), 0)
    terms = jnp.zeros(row.shape, jnp.float32)
    for n, term in enumerate(exact_terms(vec)):
        terms = jnp.where(row == n, term.astype(jnp.float32), terms)
    return terms.astype(jnp.bfloat16)


def to_rows(terms):
    ones = jnp.ones((terms.shape[0], 128), jnp.bfloat16)
    return lax.dot_general(
        terms, ones, (((0,), (0,)), ((), ())), preferred_element_type=jnp.float32
    )


def lane_sums(values):
    ones = jnp.ones((16, 128), jnp.bfloat16)
    return sum(cross(ones, term) for term in exact_terms(values))[:1]


def first_lanes(values):
    lane = lax.broadcasted_iota(jnp.int32, (16, 128), 1)
    pick = jnp.where(lane == 0, 1.0, 0.0).astype(jnp.bfloat16)
    return sum(cross(pick, term) for term in exact_terms(values))[:1]


def log_sum_exp(values):
    top = functools.reduce(jnp.maximum, values)
    return top + jnp.log(sum(jnp.exp(v - top) for v in values))


def stack_kernel(at, *refs):
    *blocks, out, sems = refs
    copies = started(sems, *((block, out.at[n]) for n, block in enumerate(blocks)))
    for copy in copies:
        copy.wait()


def halves_kernel(at, next_, last, low, high, sems):
    for copy in started(sems, (next_.at[:2], low), (last.at[2:], high)):
        copy.wait()


def near_place(at, k, r):
    return lax.rem(at[0] + k - 2 * at[4] + 4, 4), lax.rem(at[1] + r, 4)


def far_place(at, k, r):
    return lax.rem(at[0] + r - 2 * at[4] + 4, 4), lax.rem(at[1] + k, 4)


def first_kernel(at, *refs):
    data, noises, (out, x, held, sems) = refs[:4], refs[4:10], refs[10:]
    rows = data[0].shape[0]
    own, other = (pl.ds(pl.multiple_of(r * rows, rows), rows) for r in (at[2], 1 - at[2]))
    places = x.at[0, own], x.at[0, other], x.at[1, own], x.at[1, other]
    copies = started(
        sems, *zip(data, places), *((noise, held.at[n]) for n, noise in enumerate(noises))
    )
    for copy in copies[:4]:
        copy.wait()
    x_sq = 0.0
    for side in range(2):
        for span in range(0, x.shape[2], 128):
            wide = x[side, :, span : span + 128].astype(jnp.float32)
            x_sq = x_sq + wide * wide
    x_sq = jnp.broadcast_to(0.5 * jnp.sum(x_sq, axis=1, keepdims=True), x_sq.shape)
    for n, k in enumerate((0, 1, 3)):
        copies[4 + n].wait()
        for r in (0, 2):
            noise = flat(held[n, r : r + 2])
            value = cross(x[0], noise) - half_squares(noise)
            out[near_place(at, k, r)] = value[:, :128] - x_sq
            out[near_place(at, k, r + 1)] = value[:, 128:] - x_sq
    for r in range(4):
        out[near_place(at, 2, r)] = -x_sq
    for n, k in enumerate((0, 1, 3)):
        copies[7 + n].wait()
        for r in (0, 2):
            noise = flat(held[3 + n, r : r + 2])
            value = cross(x[1], noise) - half_squares(noise)
            out[far_place(at, k, r)] += value[:, :128]
            out[far_place(at, k, r + 1)] += value[:, 128:]


def second_kernel(half, at, x, acc, n_a, n_b, f_a, f_b, out, held, sems):
    copies = started(sems, *((p, held.at[n]) for n, p in enumerate((n_a, n_b, f_a, f_b))))
    for block in range(2):
        for j in range(4):
            out[block, j] = acc[2 * half + block, j]
    for copy in copies:
        copy.wait()
    block, _ = near_place(at, 2, 0)

    @pl.when((block >= 2) == bool(half))
    def _():
        for n, r in ((0, 0), (1, 2)):
            noise = flat(held[n])
            value = cross(x[0], noise) - half_squares(noise)
            out[block - 2 * half, near_place(at, 2, r)[1]] += value[:, :128]
            out[block - 2 * half, near_place(at, 2, r + 1)[1]] += value[:, 128:]

    for block in range(2):
        r = lax.rem(2 * at[4] + 2 * half + block - at[0] + 4, 4)
        j = far_place(at, 2, 0)[1]
        noise = held[2 + r // 2, lax.rem(r, 2)]
        out[block, j] += cross(x[1], noise) - half_squares(noise)


def weights_of(at, weights, place, own_rows):
    rows = weights.shape[2] // 2
    to_l = at[2] if own_rows else 1 - at[2]
    here = pl.ds(pl.multiple_of(to_l * rows, rows), rows)
    parts = []
    for k, rs in ((0, range(4)), (1, range(4)), (3, range(4)), (2, (0, 1)), (2, (2, 3))):
        blocks = [place(at, k, r) for r in rs]
        parts.append(
            jnp.concatenate([weights[block[0], block[1], here] for block in blocks], axis=1)
        )
    total = 0.0
    for value in parts:
        total = total + cross(jnp.ones((16, value.shape[1]), jnp.bfloat16), value)
    return parts, total[:1]


STEP = 256


def product(parts, noise, first):
    span = slice(first, first + STEP)
    return sum(dot(w, flat(p[:, :, span])) for w, p in zip(parts, noise))


def target_1_kernel(at, weights, p0, p1, p3, p2_a, p2_b, low, high):
    parts, total = weights_of(at, weights, far_place, True)
    mid = low.shape[0] - 16
    for first in range(0, p0.shape[-1], STEP):
        value = product(parts, (p0, p1, p3, p2_a, p2_b), first)
        low[:mid, first : first + STEP] = value[:mid].astype(low.dtype)
        high[:mid, first : first + STEP] = value[mid:].astype(high.dtype)
    for n, out in enumerate((low, high)):
        out[mid:, :] = jnp.zeros((16, out.shape[1]), out.dtype)
        out[mid:, :mid] = terms_in_rows(total[:, n * mid : n * mid + mid])


def target_2_kernel(place, own_rows, at, weights, p0, p1, p3, p2_a, p2_b, out, row_total):
    parts, total = weights_of(at, weights, place, own_rows)
    for first in range(0, p0.shape[-1], STEP):
        out[:, first : first + STEP] = product(parts, (p0, p1, p3, p2_a, p2_b), first)
    row_total[...] = jnp.broadcast_to(total, row_total.shape)


def add_kernel(part, at, values, row_total, came, out):
    mid = came.shape[0] - 16
    here = slice(part * mid, part * mid + mid)
    there = slice(mid - part * mid, 2 * mid - part * mid)
    out[here] = (values[here] + came[:mid].astype(jnp.float32)).astype(out.dtype)
    out[there] = values[there].astype(out.dtype)
    terms = came[mid:, :mid].astype(jnp.float32)
    total = [row_total[:1, :mid], row_total[:1, mid:]]
    total[part] = total[part] + terms[0:1] + terms[1:2] + terms[2:3]
    out[2 * mid :, :] = jnp.zeros((16, out.shape[1]), out.dtype)
    out[2 * mid :, : 2 * mid] = terms_in_rows(jnp.concatenate(total, axis=1))


def last_kernel(at, own, own_total, a, b, out):
    rows = own.shape[0]
    terms = [terms_in_rows(own_total[:1])] + [m[rows:, :rows] for m in (a, b)]
    total = to_rows(jnp.concatenate(terms, axis=0))
    for column in range(0, own.shape[1], 128):
        span = slice(column, column + 128)
        value = own[:, span]
        for m in (a, b):
            value = value + m[:rows, span].astype(jnp.float32)
        out[:, span] = (value / total).astype(out.dtype)


TILE = 64


def rows_1_kernel(scale, at, keep, got, score, sent, tops, sums):
    blocks = keep.shape[0]

    @pl.loop(0, keep.shape[1] // TILE)
    def _(t):
        here = pl.ds(pl.multiple_of(t * TILE, TILE), TILE)
        top = None
        for b in range(blocks):
            value = (keep[b, here] + got[b, here]) * scale
            score[b, here] = value
            top = value if top is None else jnp.maximum(top, value)
        top = jnp.broadcast_to(jnp.max(top, axis=1, keepdims=True), top.shape)
        tops[here] = top
        sums[here] = sum(jnp.exp(score[b, here] - top) for b in range(blocks))

    log_row = first_lanes(tops[...]) + jnp.log(lane_sums(sums[...]))
    for n in range(sent.shape[0]):
        sent[n] = log_row


def columns_1_kernel(log_count, at, came, score, row_pot, sent):
    pot = -log_count - log_sum_exp([came[n] for n in range(came.shape[0])])
    row_pot[...] = to_rows(terms_in_rows(pot))
    logs = []
    for b in range(score.shape[0]):
        value = score[b] + row_pot[...]
        top = jnp.max(value, axis=0, keepdims=True)
        total = jnp.sum(jnp.exp(value - top), axis=0, keepdims=True)
        logs.append(top + jnp.log(total))
    logs = jnp.concatenate(logs)
    for n in range(sent.shape[0]):
        sent[n] = logs


def rows_2_kernel(at, came, score, row_pot, plan, sent, sums):
    pot = -log_sum_exp([came[n] for n in range(came.shape[0])])

    @pl.loop(0, score.shape[1] // TILE)
    def _(t):
        here = pl.ds(pl.multiple_of(t * TILE, TILE), TILE)
        total = 0.0
        for b in range(score.shape[0]):
            value = score[b, here] + row_pot[here] + pot[b : b + 1]
            value = jnp.exp(jnp.minimum(value, 0.0))
            plan[b, here] = value
            total = total + value
        sums[here] = total

    row_sum = lane_sums(sums[...])
    for n in range(sent.shape[0]):
        sent[n] = row_sum


def columns_2_kernel(least, at, came, plan, row_scale, sent):
    total = sum(came[n] for n in range(came.shape[0]))
    row_scale[...] = to_rows(terms_in_rows(1.0 / jnp.maximum(total, least)))
    sums = []
    for b in range(plan.shape[0]):
        sums.append(jnp.sum(plan[b] * row_scale[...], axis=0, keepdims=True))
    sums = jnp.concatenate(sums)
    for n in range(sent.shape[0]):
        sent[n] = sums


def weights_kernel(least, at, came, plan, other, row_scale, weights):
    c = at[4]
    mine = sum(came[2 * n + c] for n in range(came.shape[0] // 2))
    theirs = sum(came[2 * n + 1 - c] for n in range(came.shape[0] // 2))
    for half, (values, total) in enumerate(((plan, mine), (other, theirs))):
        scale = 1.0 / jnp.maximum(total, least)
        for b in range(values.shape[0]):
            value = values[b] * row_scale[...] * scale[b : b + 1]
            weights[values.shape[0] * half + b] = value.astype(weights.dtype)


def per_device(data_rows, noise_rows):
    z, y, l, h, c = (lax.axis_index(name) for name in AXES)
    rows, part = data_rows.shape
    width = part * 4
    count = rows * 32
    eps = 0.64 / math.sqrt(width)
    log_count = math.log(count)
    piece = rows // 4

    def float32(*shape):
        return jax.ShapeDtypeStruct(shape, jnp.float32)

    def bfloat16(*shape):
        return jax.ShapeDtypeStruct(shape, jnp.bfloat16)

    at = jnp.stack([z, y, l, h, c])

    def quarter(to_l, to_h):
        return lax.dynamic_slice_in_dim(noise_rows, (2 * to_h + to_l) * piece, piece)

    wave = lax.optimization_barrier
    near_other, far_own, far_other = wave(
        (
            flip(quarter(1 - l, h), "l"),
            flip(quarter(l, 1 - h), "h"),
            flip(quarter(1 - l, 1 - h), "lh"),
        )
    )
    near = jnp.concatenate([quarter(l, h), near_other])
    far = jnp.concatenate([far_own, far_other])

    data_l = flip(data_rows, "l")
    near_1, near_3, far_1, far_3, data_rows = wave(
        (from_y(near, 1), from_y(near, 3), from_z(far, 1), from_z(far, 3), data_rows)
    )
    data_lh = flip(data_rows, "lh")
    near_2, far_2, data_l, data_rows = wave(
        (from_y(near_1, 1), from_z(far_1, 1), data_l, data_rows)
    )
    sems = pltpu.SemaphoreType.DMA((4,))

    def stacked(*blocks):
        out = [bfloat16(4, *blocks[0].shape)]
        return call(
            stack_kernel, out, 0, at, *blocks, anywhere=4, spaces=pl.ANY, scratch=[sems]
        )[0]

    def halves(next_, last):
        out = [bfloat16(2, *next_.shape[1:])] * 2
        return call(
            halves_kernel, out, 0, at, next_, last, anywhere=2, spaces=pl.ANY, scratch=[sems]
        )

    near, far = stacked(near, near_1, near_2, near_3), stacked(far, far_1, far_2, far_3)
    near_next, near_last = from_z(near, 1), from_z(near, 3)
    far_next, far_last = from_y(far, 1), from_y(far, 3)
    data_h = flip(data_rows, "h")
    near_next, near_last, far_next, far_last, data_lh, data_h = wave(
        (near_next, near_last, far_next, far_last, data_lh, data_h)
    )
    nears, fars = (near, near_next, near_last), (far, far_next, far_last)
    low, high = halves(near_next, near_last)
    near_two = from_z(low, 1), from_z(high, 3)
    low, high = halves(far_next, far_last)
    far_two = from_y(low, 1), from_y(high, 3)

    one = 2 * 2 * rows * part * 2 * 2 * piece
    noise_shape = 4, 2 * piece, part
    scores, x_all = call(
        first_kernel,
        [float32(4, 4, 2 * rows, 2 * piece), bfloat16(2, 2 * rows, part)],
        12 * one,
        *(at, data_rows, data_l, data_h, data_lh, *nears, *fars),
        anywhere=10,
        scratch=[pltpu.VMEM((6, *noise_shape), jnp.bfloat16), pltpu.SemaphoreType.DMA((10,))],
    )
    give, keep = (
        call(
            functools.partial(second_kernel, half),
            [float32(2, 4, 2 * rows, 2 * piece)],
            2 * one,
            *(at, x_all, scores, *near_two, *far_two),
            anywhere=4,
            scratch=[pltpu.VMEM((4, 2, *noise_shape[1:]), jnp.bfloat16), sems],
        )[0]
        for half in (1, 0)
    )

    blocks = (8, 2 * rows, 2 * piece)
    tall = 2 * rows, 2 * piece
    least = 0.5 / count
    row_axes, col_axes = ("l", "h", "c"), ("z", "y")
    row_sent, col_sent = float32(8, 1, 2 * rows), float32(16, 8, 2 * piece)

    def exchange(sent, axes):
        return lax.all_to_all(sent, axes, 0, 0, tiled=True)

    keep, give = keep.reshape(blocks), give.reshape(blocks)
    kernel = functools.partial(rows_1_kernel, 2.0 / (width * eps))
    score, sent = call(
        kernel, [float32(*blocks), row_sent], 0, at, keep, flip(give, "c"), scratch=[pltpu.VMEM(tall, jnp.float32)] * 2
    )
    kernel = functools.partial(columns_1_kernel, log_count)
    row_pot, sent = call(
        kernel, [float32(*tall), col_sent], 0, at, exchange(sent, row_axes), score
    )
    plan, sent = call(
        rows_2_kernel,
        [float32(*blocks), row_sent],
        0,
        *(at, exchange(sent, col_axes), score, row_pot),
        scratch=[pltpu.VMEM(tall, jnp.float32)],
    )
    plan_other = flip(plan, "c")
    kernel = functools.partial(columns_2_kernel, least)
    col_sent = float32(32, 8, 2 * piece)
    row_scale, sent = call(
        kernel, [float32(*tall), col_sent], 0, at, exchange(sent, row_axes), plan
    )
    kernel = functools.partial(weights_kernel, least)
    (weights,) = call(
        kernel,
        [bfloat16(16, *blocks[1:])],
        0,
        *(at, exchange(sent, ("z", "y", "c")), plan, plan_other, row_scale),
    )
    weights = weights.reshape(4, 4, *blocks[1:])

    near_noise, far_noise = (*nears, *near_two), (*fars, *far_two)
    low, high = call(
        target_1_kernel, [bfloat16(rows // 2 + 16, part)] * 2, 8 * one, at, weights, *far_noise
    )
    low, high = flip(low, "l"), flip(high, "lh")

    def target(place, own_rows):
        kernel = functools.partial(target_2_kernel, place, own_rows)
        noise = near_noise if place is near_place else far_noise
        return call(kernel, [float32(rows, part), float32(8, rows)], 8 * one, at, weights, *noise)

    def message(half, came, values, row_total):
        kernel = functools.partial(add_kernel, half)
        return call(kernel, [bfloat16(rows + 16, part)], 0, at, values, row_total, came)[0]

    to_lh = flip(message(0, low, *target(far_place, False)), "lh")
    to_l = flip(message(1, high, *target(near_place, False)), "l")
    own, own_total = target(near_place, True)
    return call(last_kernel, [bfloat16(rows, part)], 0, at, own, own_total, to_l, to_lh)[0]


def solution(mesh):
    fine = Mesh(mesh.devices.reshape(SIZES), AXES)
    spec = P(("z", "y", "l"), ("h", "c"))
    return jax.shard_map(
        per_device, mesh=fine, in_specs=(spec, spec), out_specs=spec, check_vma=False
    )
```

time: 1230 us -> 159 us (0.13)
  blocking collectives: 616 us -> 39 us
  waiting for transfers between devices: 525 us -> 51 us
  other arithmetic: 46 us -> 0.02 us
  starting transfers between devices: 0.04 us -> 35 us
  Pallas kernels: 0 us -> 32.3 us
  matrix products: 30.7 us -> 0 us
  between operations: 13.6 us -> 0.23 us
    all_gather x1 -> x0, waiting for transfers between devices: 367 us -> none  [per_device(): every_noise = lax.all_gather(noise_rows, 'blk', axis=0, tiled=True)]
    pmax x2 -> x0, blocking collectives: 311 us -> none  [per_device(): lax.pmax(col_max.astype(jnp.bfloat16), 'blk').astype(col_max.dtype)]
    psum x2 -> x0, blocking collectives: 306 us -> none  [per_device(): col_total = lax.psum(col_total * jnp.exp(col_max - overall), 'blk')]
    psum x1 -> x0, waiting for transfers between devices: 158 us -> none  [per_device(): cost = lax.psum(partial_value, 'val') / width]
    ppermute x0 -> x26, waiting for transfers between devices: none -> 51 us  [move(): return lax.ppermute(value, AXES, pairs)]
    all_to_all x0 -> x4, blocking collectives: none -> 39 us  [exchange(): return lax.all_to_all(sent, axes, 0, 0, tiled=True)]
    ppermute x0 -> x26, starting transfers between devices: none -> 35 us  [move(): return lax.ppermute(value, AXES, pairs)]
    pallas_call x0 -> x19, Pallas kernels: none -> 32.3 us  [call(): pl.pallas_call(kernel, out_shape=outs, in_specs=[pl.BlockSpec(memory_spac...]
  transfers between devices with their start and end apart: 2 -> 26, of which waited for: 2 -> 16; matrix products, arithmetic and copies ran while one was open for 0% -> 0% of each run, Pallas kernels for 0% -> 12%
where the time goes in v1:
time: 159 us
  waiting for transfers between devices  51 us (32%)
  blocking collectives  39 us (25%)
  starting transfers between devices  35 us (22%)
  Pallas kernels  32.3 us (20%)
    ppermute x26, waiting for transfers between devices, move(): return lax.ppermute(value, AXES, pairs)  51 us
    all_to_all x4, blocking collectives, exchange(): return lax.all_to_all(sent, axes, 0, 0, tiled=True)  39 us
    ppermute x26, starting transfers between devices, move(): return lax.ppermute(value, AXES, pairs)  35 us
    pallas_call x19, Pallas kernels, call(): pl.pallas_call(kernel, out_shape=outs, in_specs=[pl.BlockSpec(memory_spac...  32.3 us
  transfers between devices with their start and end apart: 26, of which 16 were waited for; matrix products, arithmetic and copies ran while one was open for 0% of the time, Pallas kernels for 12%

profile of v1, /device:TPU:0, one launch (start us, length us, event | category | flops | bytes accessed | tf_op | source)
XLA Modules:
  0.0 158.9 jit_solution(8031229316927527950)
XLA Ops:
  0.0 1.2 constant_dynamic-slice_fusion.3
  1.2 1.7 %collective-permute-start = (bf16[64,1024]{1,0:T(8,128)(2,1)S(1)}, bf16[64,1024]{1,0:T(8,128)(2,1)S(1)}, u32[]{:S(2)}, u32[]{:S(2)}) collective-permute-start(bf16[64,1024]{1,0:T(8,128)(2,1)S(1)} %get-tuple-element.86), channel_id=1, source_target_pairs={{0,4},{1,5},{2,6},{3,7},{4,0},{5,1},{6,2},{7,3},{8,12},{9,13},{10,... | collective-permute-start | bytes 393224 | tf_op jit(solution)/shard_map/ppermute | solution.py:26
  2.8 2.1 %collective-permute-start.2 = (bf16[64,1024]{1,0:T(8,128)(2,1)S(1)}, bf16[64,1024]{1,0:T(8,128)(2,1)S(1)}, u32[]{:S(2)}, u32[]{:S(2)}) collective-permute-start(bf16[64,1024]{1,0:T(8,128)(2,1)S(1)} %get-tuple-element.87), channel_id=1, source_target_pairs={{0,6},{1,7},{2,4},{3,5},{4,2},{5,3},{6,0},{7,1},{8,14},{9,15},{10,... | collective-permute-start | bytes 393224 | tf_op jit(solution)/shard_map/ppermute | solution.py:26
  4.9 0.6 collective-permute-start.1
  5.6 0.8 collective-permute-done
  6.3 5.5 %collective-permute-done.2 = bf16[64,1024]{1,0:T(8,128)(2,1)S(1)} collective-permute-done((bf16[64,1024]{1,0:T(8,128)(2,1)S(1)}, bf16[64,1024]{1,0:T(8,128)(2,1)S(1)}, u32[]{:S(2)}, u32[]{:S(2)}) %collective-permute-start.2) | collective-permute-done | bytes 131104 | tf_op jit(solution)/shard_map/ppermute | solution.py:26
  11.9 2.0 %collective-permute-start.6 = (bf16[128,1024]{1,0:T(8,128)(2,1)S(1)}, bf16[128,1024]{1,0:T(8,128)(2,1)S(1)}, u32[]{:S(2)}, u32[]{:S(2)}) collective-permute-start(bf16[128,1024]{1,0:T(8,128)(2,1)S(1)} %constant_dynamic-update-slice_fusion.refs_0_), channel_id=1, source_target_pairs={{0,32},{1,33},{2,34},{3,35},{4,36},{5,37},{6,38},{7,39},{8,40},{9,... | collective-permute-start | bytes 786440 | tf_op jit(solution)/shard_map/ppermute | solution.py:26
  13.9 2.2 %collective-permute-start.5 = (bf16[128,1024]{1,0:T(8,128)(2,1)S(1)}, bf16[128,1024]{1,0:T(8,128)(2,1)S(1)}, u32[]{:S(2)}, u32[]{:S(2)}) collective-permute-start(bf16[128,1024]{1,0:T(8,128)(2,1)S(1)} %constant_dynamic-update-slice_fusion.refs_0_), channel_id=1, source_target_pairs={{0,96},{1,97},{2,98},{3,99},{4,100},{5,101},{6,102},{7,103},{8,104... | collective-permute-start | bytes 786440 | tf_op jit(solution)/shard_map/ppermute | solution.py:26
  16.1 1.6 %collective-permute-start.4 = (bf16[128,1024]{1,0:T(8,128)(2,1)S(1)}, bf16[128,1024]{1,0:T(8,128)(2,1)S(1)}, u32[]{:S(2)}, u32[]{:S(2)}) collective-permute-start(bf16[128,1024]{1,0:T(8,128)(2,1)S(1)} %pad_maximum_fusion.refs_0_), channel_id=1, source_target_pairs={{0,8},{1,9},{2,10},{3,11},{4,12},{5,13},{6,14},{7,15},{8,16},{9,17... | collective-permute-start | bytes 786440 | tf_op jit(solution)/shard_map/ppermute | solution.py:26
  17.7 1.7 %collective-permute-start.3 = (bf16[128,1024]{1,0:T(8,128)(2,1)S(1)}, bf16[128,1024]{1,0:T(8,128)(2,1)S(1)}, u32[]{:S(2)}, u32[]{:S(2)}) collective-permute-start(bf16[128,1024]{1,0:T(8,128)(2,1)S(1)} %pad_maximum_fusion.refs_0_), channel_id=1, source_target_pairs={{0,24},{1,25},{2,26},{3,27},{4,28},{5,29},{6,30},{7,31},{8,0},{9,1... | collective-permute-start | bytes 786440 | tf_op jit(solution)/shard_map/ppermute | solution.py:26
  19.4 0.2 collective-permute-start.9
  19.6 1.5 collective-permute-done.6.refs_3_
  21.1 2.9 %collective-permute-done.4.refs_3_ = bf16[128,1024]{1,0:T(8,128)(2,1)S(1)} collective-permute-done((bf16[128,1024]{1,0:T(8,128)(2,1)S(1)}, bf16[128,1024]{1,0:T(8,128)(2,1)S(1)}, u32[]{:S(2)}, u32[]{:S(2)}) %collective-permute-start.4) | collective-permute-done | bytes 262176 | tf_op jit(solution)/shard_map/ppermute | solution.py:26
  24.0 0.1 collective-permute-done.3.refs_1_
  24.1 2.9 %collective-permute-start.7 = (bf16[128,1024]{1,0:T(8,128)(2,1)S(1)}, bf16[128,1024]{1,0:T(8,128)(2,1)S(1)}, u32[]{:S(2)}, u32[]{:S(2)}) collective-permute-start(bf16[128,1024]{1,0:T(8,128)(2,1)S(1)} %collective-permute-done.3.refs_1_), channel_id=1, source_target_pairs={{0,24},{1,25},{2,26},{3,27},{4,28},{5,29},{6,30},{7,31},{8,0},{9,1... | collective-permute-start | bytes 786440 | tf_op jit(solution)/shard_map/ppermute | solution.py:26
  27.0 1.9 %collective-permute-start.8 = (bf16[128,1024]{1,0:T(8,128)(2,1)S(1)}, bf16[128,1024]{1,0:T(8,128)(2,1)S(1)}, u32[]{:S(2)}, u32[]{:S(2)}) collective-permute-start(bf16[128,1024]{1,0:T(8,128)(2,1)S(1)} %collective-permute-done.5.refs_1_), channel_id=1, source_target_pairs={{0,96},{1,97},{2,98},{3,99},{4,100},{5,101},{6,102},{7,103},{8,104... | collective-permute-start | bytes 786440 | tf_op jit(solution)/shard_map/ppermute | solution.py:26
  28.9 0.1 stack.23.at
  29.0 2.1 %collective-permute-start.14 = (bf16[256,1024]{1,0:T(8,128)(2,1)S(1)}, bf16[256,1024]{1,0:T(8,128)(2,1)S(1)}, u32[]{:S(2)}, u32[]{:S(2)}) collective-permute-start(bf16[256,1024]{1,0:T(8,128)(2,1)S(1)} %copy-done), channel_id=1, source_target_pairs={{0,6},{1,7},{2,4},{3,5},{4,2},{5,3},{6,0},{7,1},{8,14},{9,15},{10,... | collective-permute-start | bytes 1572872 | tf_op jit(solution)/shard_map/ppermute | solution.py:26
  31.1 0.1 collective-permute-done.9.refs_1_
  31.2 2.2 %collective-permute-done.8.refs_2_ = bf16[128,1024]{1,0:T(8,128)(2,1)S(1)} collective-permute-done((bf16[128,1024]{1,0:T(8,128)(2,1)S(1)}, bf16[128,1024]{1,0:T(8,128)(2,1)S(1)}, u32[]{:S(2)}, u32[]{:S(2)}) %collective-permute-start.8) | collective-permute-done | bytes 262176 | tf_op jit(solution)/shard_map/ppermute | solution.py:26
  33.4 0.7 shard_map.29.refs_7_.p0
  34.1 0.1 collective-permute-start.13
  34.1 3.2 %collective-permute-start.12 = (bf16[4,128,1024]{2,1,0:T(8,128)(2,1)S(1)}, bf16[4,128,1024]{2,1,0:T(8,128)(2,1)S(1)}, u32[]{:S(2)}, u32[]{:S(2)}) collective-permute-start(bf16[4,128,1024]{2,1,0:T(8,128)(2,1)S(1)} %shard_map.29.refs_7_.p0), channel_id=1, source_target_pairs={{0,24},{1,25},{2,26},{3,27},{4,28},{5,29},{6,30},{7,31},{8,0},{9,1... | collective-permute-start | bytes 3145736 | tf_op jit(solution)/shard_map/ppermute | solution.py:26
  37.4 0.7 shard_map.28.refs_4_.p0
  38.0 0.1 collective-permute-start.11
  38.1 3.2 %collective-permute-start.10 = (bf16[4,128,1024]{2,1,0:T(8,128)(2,1)S(1)}, bf16[4,128,1024]{2,1,0:T(8,128)(2,1)S(1)}, u32[]{:S(2)}, u32[]{:S(2)}) collective-permute-start(bf16[4,128,1024]{2,1,0:T(8,128)(2,1)S(1)} %shard_map.28.refs_4_.p0), channel_id=1, source_target_pairs={{0,96},{1,97},{2,98},{3,99},{4,100},{5,101},{6,102},{7,103},{8,104... | collective-permute-start | bytes 3145736 | tf_op jit(solution)/shard_map/ppermute | solution.py:26
  41.3 4.8 %collective-permute-done.14.refs_3_ = bf16[256,1024]{1,0:T(8,128)(2,1)S(1)} collective-permute-done((bf16[256,1024]{1,0:T(8,128)(2,1)S(1)}, bf16[256,1024]{1,0:T(8,128)(2,1)S(1)}, u32[]{:S(2)}, u32[]{:S(2)}) %collective-permute-start.14) | collective-permute-done | bytes 524320 | tf_op jit(solution)/shard_map/ppermute | solution.py:26
  46.2 10.7 %collective-permute-done.15.refs_2_ = bf16[256,1024]{1,0:T(8,128)(2,1)S(1)} collective-permute-done((bf16[256,1024]{1,0:T(8,128)(2,1)S(1)}, bf16[256,1024]{1,0:T(8,128)(2,1)S(1)}, u32[]{:S(2)}, u32[]{:S(2)}) %collective-permute-start.15) | collective-permute-done | bytes 524320 | tf_op jit(solution)/shard_map/ppermute | solution.py:26
  56.9 3.0 %collective-permute-done.11.refs_6_.last.p3 = bf16[4,128,1024]{2,1,0:T(8,128)(2,1)S(1)} collective-permute-done((bf16[4,128,1024]{2,1,0:T(8,128)(2,1)S(1)}, bf16[4,128,1024]{2,1,0:T(8,128)(2,1)S(1)}, u32[]{:S(2)}, u32[]{:S(2)}) %collective-permute-start.11) | collective-permute-done | bytes 1048608 | tf_op jit(solution)/shard_map/ppermute | solution.py:26
  59.9 0.4 collective-permute-done.10.refs_5_.next_.p1
  60.2 0.7 shard_map.31
  60.9 3.8 %collective-permute-start.16 = (bf16[2,128,1024]{2,1,0:T(8,128)(2,1)S(1)}, bf16[2,128,1024]{2,1,0:T(8,128)(2,1)S(1)}, u32[]{:S(2)}, u32[]{:S(2)}) collective-permute-start(bf16[2,128,1024]{2,1,0:T(8,128)(2,1)S(1)} %get-tuple-element.65), channel_id=1, source_target_pairs={{0,96},{1,97},{2,98},{3,99},{4,100},{5,101},{6,102},{7,103},{8,104... | collective-permute-start | bytes 1572872 | tf_op jit(solution)/shard_map/ppermute | solution.py:26
  64.7 0.7 shard_map.32
  65.3 0.1 collective-permute-start.18
  65.4 2.0 %collective-permute-start.19 = (bf16[2,128,1024]{2,1,0:T(8,128)(2,1)S(1)}, bf16[2,128,1024]{2,1,0:T(8,128)(2,1)S(1)}, u32[]{:S(2)}, u32[]{:S(2)}) collective-permute-start(bf16[2,128,1024]{2,1,0:T(8,128)(2,1)S(1)} %get-tuple-element.68), channel_id=1, source_target_pairs={{0,8},{1,9},{2,10},{3,11},{4,12},{5,13},{6,14},{7,15},{8,16},{9,17... | collective-permute-start | bytes 1572872 | tf_op jit(solution)/shard_map/ppermute | solution.py:26
  67.4 7.7 %shard_map.30 = (f32[4,4,512,128]{3,2,1,0:T(8,128)S(1)}, bf16[2,512,1024]{2,1,0:T(8,128)(2,1)S(1)}) custom-call(s32[5]{0:T(128)S(1)} %stack.23.at, bf16[256,1024]{1,0:T(8,128)(2,1)S(1)} %copy-done, bf16[256,1024]{1,0:T(8,128)(2,1)S(1)} %collective-permute-done.9.refs_1_, bf16[256,1024]{1,0:T(8,128)(2,1)S(1)} %collective-permute-done.15.refs_2_, ...), custom_call_target="tpu_custom_call" | custom-call | flops 3221225472 | bytes 14680084 | tf_op jit(solution)/shard_map/pallas_call | solution.py:76
  75.1 0.9 collective-permute-done.19.f_b.p2_b
  76.0 2.7 %shard_map.34 = f32[2,4,512,128]{3,2,1,0:T(8,128)S(1)} custom-call(s32[5]{0:T(128)S(1)} %stack.23.at, bf16[2,512,1024]{2,1,0:T(8,128)(2,1)S(1)} %get-tuple-element.63.x, f32[4,4,512,128]{3,2,1,0:T(8,128)S(1)} %get-tuple-element.64.acc, bf16[2,128,1024]{2,1,0:T(8,128)(2,1)S(1)} %collective-permute-done.16.n_a.p2_a, ...), custom_call_target="tpu_custom_call" | custom-call | flops 536870912 | bytes 10485780 | tf_op jit(solution)/shard_map/pallas_call | solution.py:76
  78.7 0.1 collective-permute-start.20
  78.8 1.7 %shard_map.33 = f32[2,4,512,128]{3,2,1,0:T(8,128)S(1)} custom-call(s32[5]{0:T(128)S(1)} %stack.23.at, bf16[2,512,1024]{2,1,0:T(8,128)(2,1)S(1)} %get-tuple-element.63.x, f32[4,4,512,128]{3,2,1,0:T(8,128)S(1)} %get-tuple-element.64.acc, bf16[2,128,1024]{2,1,0:T(8,128)(2,1)S(1)} %collective-permute-done.16.n_a.p2_a, ...), custom_call_target="tpu_custom_call" | custom-call | flops 536870912 | bytes 10485780 | tf_op jit(solution)/shard_map/pallas_call | solution.py:76
  80.6 2.4 %collective-permute-done.20.got = f32[8,512,128]{2,1,0:T(8,128)S(1)} collective-permute-done((f32[8,512,128]{2,1,0:T(8,128)S(1)}, f32[8,512,128]{2,1,0:T(8,128)S(1)}, u32[]{:S(2)}, u32[]{:S(2)}) %collective-permute-start.20) | collective-permute-done | bytes 2097184 | tf_op jit(solution)/shard_map/ppermute | solution.py:26
  83.0 2.0 %shard_map.35 = (f32[8,512,128]{2,1,0:T(8,128)S(1)}, f32[8,1,512]{2,1,0:T(1,128)S(1)}) custom-call(s32[5]{0:T(128)S(1)} %stack.23.at, f32[8,512,128]{2,1,0:T(8,128)S(1)} %bitcast.8, f32[8,512,128]{2,1,0:T(8,128)S(1)} %collective-permute-done.20.got), custom_call_target="tpu_custom_call" | custom-call | bytes 6307860 | tf_op jit(solution)/shard_map/pallas_call | solution.py:76
  85.0 8.7 %all_to_all.20.came = f32[8,1,512]{2,1,0:T(1,128)S(1)} all-to-all(f32[8,1,512]{2,1,0:T(1,128)S(1)} %get-tuple-element.69), channel_id=1, replica_groups=mesh['z'=4,'y'=4,'l'=2,'h'=2,'c'=2] {'l','h','c'}, dimensions={0} | all-to-all | bytes 32768 | tf_op jit(solution)/shard_map/all_to_all | solution.py:446
  93.7 1.3 shard_map.36
  95.0 11.1 %all_to_all.21.came = f32[16,8,128]{2,1,0:T(8,128)S(1)} all-to-all(f32[16,8,128]{2,1,0:T(8,128)S(1)} %get-tuple-element.71), channel_id=1, replica_groups=mesh['z'=4,'y'=4,'l'=2,'h'=2,'c'=2] {'z','y'}, dimensions={0} | all-to-all | bytes 131072 | tf_op jit(solution)/shard_map/all_to_all | solution.py:446
  106.1 1.3 shard_map.37
  107.4 0.0 collective-permute-start.21
  107.4 7.7 %all_to_all.22.came = f32[8,1,512]{2,1,0:T(1,128)S(1)} all-to-all(f32[8,1,512]{2,1,0:T(1,128)S(1)} %get-tuple-element.73), channel_id=1, replica_groups=mesh['z'=4,'y'=4,'l'=2,'h'=2,'c'=2] {'l','h','c'}, dimensions={0} | all-to-all | bytes 32768 | tf_op jit(solution)/shard_map/all_to_all | solution.py:446
  115.1 0.9 shard_map.38
  116.0 11.4 %all_to_all.23.came = f32[32,8,128]{2,1,0:T(8,128)S(1)} all-to-all(f32[32,8,128]{2,1,0:T(8,128)S(1)} %get-tuple-element.75), channel_id=1, replica_groups=mesh['z'=4,'y'=4,'l'=2,'h'=2,'c'=2] {'z','y','c'}, dimensions={0} | all-to-all | bytes 262144 | tf_op jit(solution)/shard_map/all_to_all | solution.py:446
  127.5 1.0 shard_map.39
  128.5 2.1 %shard_map.42 = (bf16[144,1024]{1,0:T(8,128)(2,1)S(1)}, bf16[144,1024]{1,0:T(8,128)(2,1)S(1)}) custom-call(s32[5]{0:T(128)S(1)} %stack.23.at, bf16[4,4,512,128]{3,2,1,0:T(8,128)(2,1)S(1)} %bitcast.9, bf16[4,128,1024]{2,1,0:T(8,128)(2,1)S(1)} %shard_map.29.refs_7_.p0, bf16[4,128,1024]{2,1,0:T(8,128)(2,1)S(1)} %collective-permute-done.12.refs_8_.next_.p1, ...), custom_call_target="tpu_custom_call" | custom-call | flops 2147483648 | bytes 6881300 | tf_op jit(solution)/shard_map/pallas_call | solution.py:76
  130.6 1.2 collective-permute-start.22
  131.8 2.1 %shard_map.44 = (f32[256,1024]{1,0:T(8,128)S(1)}, f32[8,256]{1,0:T(8,128)S(1)}) custom-call(s32[5]{0:T(128)S(1)} %stack.23.at, bf16[4,4,512,128]{3,2,1,0:T(8,128)(2,1)S(1)} %bitcast.10, bf16[4,128,1024]{2,1,0:T(8,128)(2,1)S(1)} %shard_map.29.refs_7_.p0, bf16[4,128,1024]{2,1,0:T(8,128)(2,1)S(1)} %collective-permute-done.12.refs_8_.next_.p1, ...), custom_call_target="tpu_custom_call" | custom-call | flops 2147483648 | bytes 7348244 | tf_op jit(solution)/shard_map/pallas_call | solution.py:76
  133.9 2.1 %shard_map.41 = (f32[256,1024]{1,0:T(8,128)S(1)}, f32[8,256]{1,0:T(8,128)S(1)}) custom-call(s32[5]{0:T(128)S(1)} %stack.23.at, bf16[4,4,512,128]{3,2,1,0:T(8,128)(2,1)S(1)} %bitcast.11, bf16[4,128,1024]{2,1,0:T(8,128)(2,1)S(1)} %shard_map.28.refs_4_.p0, bf16[4,128,1024]{2,1,0:T(8,128)(2,1)S(1)} %collective-permute-done.10.refs_5_.next_.p1, ...), custom_call_target="tpu_custom_call" | custom-call | flops 2147483648 | bytes 7348244 | tf_op jit(solution)/shard_map/pallas_call | solution.py:76
  136.0 4.6 %collective-permute-done.24.came = bf16[144,1024]{1,0:T(8,128)(2,1)S(1)} collective-permute-done((bf16[144,1024]{1,0:T(8,128)(2,1)S(1)}, bf16[144,1024]{1,0:T(8,128)(2,1)S(1)}, u32[]{:S(2)}, u32[]{:S(2)}) %collective-permute-start.24) | collective-permute-done | bytes 294944 | tf_op jit(solution)/shard_map/ppermute | solution.py:26
  140.5 0.6 shard_map.45
  141.2 2.1 %collective-permute-start.25 = (bf16[272,1024]{1,0:T(8,128)(2,1)S(1)}, bf16[272,1024]{1,0:T(8,128)(2,1)S(1)}, u32[]{:S(2)}, u32[]{:S(2)}) collective-permute-start(bf16[272,1024]{1,0:T(8,128)(2,1)S(1)} %shard_map.45), channel_id=1, source_target_pairs={{0,6},{1,7},{2,4},{3,5},{4,2},{5,3},{6,0},{7,1},{8,14},{9,15},{10,... | collective-permute-start | bytes 1671176 | tf_op jit(solution)/shard_map/ppermute | solution.py:26
  143.3 0.6 shard_map.43
  143.9 0.1 collective-permute-start.23
  144.0 2.1 %shard_map.40 = (f32[256,1024]{1,0:T(8,128)S(1)}, f32[8,256]{1,0:T(8,128)S(1)}) custom-call(s32[5]{0:T(128)S(1)} %stack.23.at, bf16[4,4,512,128]{3,2,1,0:T(8,128)(2,1)S(1)} %bitcast.12, bf16[4,128,1024]{2,1,0:T(8,128)(2,1)S(1)} %shard_map.28.refs_4_.p0, bf16[4,128,1024]{2,1,0:T(8,128)(2,1)S(1)} %collective-permute-done.10.refs_5_.next_.p1, ...), custom_call_target="tpu_custom_call" | custom-call | flops 2147483648 | bytes 7348244 | tf_op jit(solution)/shard_map/pallas_call | solution.py:76
  146.1 9.8 %collective-permute-done.25.b = bf16[272,1024]{1,0:T(8,128)(2,1)S(1)} collective-permute-done((bf16[272,1024]{1,0:T(8,128)(2,1)S(1)}, bf16[272,1024]{1,0:T(8,128)(2,1)S(1)}, u32[]{:S(2)}, u32[]{:S(2)}) %collective-permute-start.25) | collective-permute-done | bytes 557088 | tf_op jit(solution)/shard_map/ppermute | solution.py:26
  155.9 1.3 collective-permute-done.23.a
  157.2 1.7 %shard_map.46 = bf16[256,1024]{1,0:T(8,128)(2,1)} custom-call(s32[5]{0:T(128)S(1)} %stack.23.at, f32[256,1024]{1,0:T(8,128)S(1)} %get-tuple-element.77.own, f32[8,256]{1,0:T(8,128)S(1)} %get-tuple-element.78.own_total, bf16[272,1024]{1,0:T(8,128)(2,1)S(1)} %collective-permute-done.23.a, bf16[272,1024]{1,0:T(8,128)(2,1)S(1)} %collective-permute-done.25.b), custom_call_target="tpu_custom_call" | custom-call | bytes 2695188 | tf_op jit(solution)/shard_map/pallas_call | solution.py:76
  (18 shorter events, 0.1 us)
Async XLA Ops:
  0.0 19.4 %copy-start = (bf16[256,1024]{1,0:T(8,128)(2,1)S(1)}, bf16[256,1024]{1,0:T(8,128)(2,1)}, u32[]{:S(2)}) copy-start(bf16[256,1024]{1,0:T(8,128)(2,1)} %refs_0_) | copy-start | bytes 1572868
  1.2 5.2 %collective-permute-start = (bf16[64,1024]{1,0:T(8,128)(2,1)S(1)}, bf16[64,1024]{1,0:T(8,128)(2,1)S(1)}, u32[]{:S(2)}, u32[]{:S(2)}) collective-permute-start(bf16[64,1024]{1,0:T(8,128)(2,1)S(1)} %get-tuple-element.86), channel_id=1, source_target_pairs={{0,4},{1,5},{2,6},{3,7},{4,0},{5,1},{6,2},{7,3},{8,12},{9,13},{10,... | collective-permute-start | bytes 393224 | tf_op jit(solution)/shard_map/ppermute | solution.py:26
  2.8 9.0 %collective-permute-start.2 = (bf16[64,1024]{1,0:T(8,128)(2,1)S(1)}, bf16[64,1024]{1,0:T(8,128)(2,1)S(1)}, u32[]{:S(2)}, u32[]{:S(2)}) collective-permute-start(bf16[64,1024]{1,0:T(8,128)(2,1)S(1)} %get-tuple-element.87), channel_id=1, source_target_pairs={{0,6},{1,7},{2,4},{3,5},{4,2},{5,3},{6,0},{7,1},{8,14},{9,15},{10,... | collective-permute-start | bytes 393224 | tf_op jit(solution)/shard_map/ppermute | solution.py:26
  4.9 6.9 %collective-permute-start.1 = (bf16[64,1024]{1,0:T(8,128)(2,1)S(1)}, bf16[64,1024]{1,0:T(8,128)(2,1)S(1)}, u32[]{:S(2)}, u32[]{:S(2)}) collective-permute-start(bf16[64,1024]{1,0:T(8,128)(2,1)S(1)} %get-tuple-element.88), channel_id=1, source_target_pairs={{0,2},{1,3},{2,0},{3,1},{4,6},{5,7},{6,4},{7,5},{8,10},{9,11},{10,... | collective-permute-start | bytes 393224 | tf_op jit(solution)/shard_map/ppermute | solution.py:26
  11.9 9.2 %collective-permute-start.6 = (bf16[128,1024]{1,0:T(8,128)(2,1)S(1)}, bf16[128,1024]{1,0:T(8,128)(2,1)S(1)}, u32[]{:S(2)}, u32[]{:S(2)}) collective-permute-start(bf16[128,1024]{1,0:T(8,128)(2,1)S(1)} %constant_dynamic-update-slice_fusion.refs_0_), channel_id=1, source_target_pairs={{0,32},{1,33},{2,34},{3,35},{4,36},{5,37},{6,38},{7,39},{8,40},{9,... | collective-permute-start | bytes 786440 | tf_op jit(solution)/shard_map/ppermute | solution.py:26
  13.9 7.2 %collective-permute-start.5 = (bf16[128,1024]{1,0:T(8,128)(2,1)S(1)}, bf16[128,1024]{1,0:T(8,128)(2,1)S(1)}, u32[]{:S(2)}, u32[]{:S(2)}) collective-permute-start(bf16[128,1024]{1,0:T(8,128)(2,1)S(1)} %constant_dynamic-update-slice_fusion.refs_0_), channel_id=1, source_target_pairs={{0,96},{1,97},{2,98},{3,99},{4,100},{5,101},{6,102},{7,103},{8,104... | collective-permute-start | bytes 786440 | tf_op jit(solution)/shard_map/ppermute | solution.py:26
  16.1 7.9 %collective-permute-start.4 = (bf16[128,1024]{1,0:T(8,128)(2,1)S(1)}, bf16[128,1024]{1,0:T(8,128)(2,1)S(1)}, u32[]{:S(2)}, u32[]{:S(2)}) collective-permute-start(bf16[128,1024]{1,0:T(8,128)(2,1)S(1)} %pad_maximum_fusion.refs_0_), channel_id=1, source_target_pairs={{0,8},{1,9},{2,10},{3,11},{4,12},{5,13},{6,14},{7,15},{8,16},{9,17... | collective-permute-start | bytes 786440 | tf_op jit(solution)/shard_map/ppermute | solution.py:26
  17.7 6.4 %collective-permute-start.3 = (bf16[128,1024]{1,0:T(8,128)(2,1)S(1)}, bf16[128,1024]{1,0:T(8,128)(2,1)S(1)}, u32[]{:S(2)}, u32[]{:S(2)}) collective-permute-start(bf16[128,1024]{1,0:T(8,128)(2,1)S(1)} %pad_maximum_fusion.refs_0_), channel_id=1, source_target_pairs={{0,24},{1,25},{2,26},{3,27},{4,28},{5,29},{6,30},{7,31},{8,0},{9,1... | collective-permute-start | bytes 786440 | tf_op jit(solution)/shard_map/ppermute | solution.py:26
  19.4 11.8 %collective-permute-start.9 = (bf16[256,1024]{1,0:T(8,128)(2,1)S(1)}, bf16[256,1024]{1,0:T(8,128)(2,1)S(1)}, u32[]{:S(2)}, u32[]{:S(2)}) collective-permute-start(bf16[256,1024]{1,0:T(8,128)(2,1)S(1)} %copy-done), channel_id=1, source_target_pairs={{0,4},{1,5},{2,6},{3,7},{4,0},{5,1},{6,2},{7,3},{8,12},{9,13},{10,... | collective-permute-start | bytes 1572872 | tf_op jit(solution)/shard_map/ppermute | solution.py:26
  24.1 7.1 %collective-permute-start.7 = (bf16[128,1024]{1,0:T(8,128)(2,1)S(1)}, bf16[128,1024]{1,0:T(8,128)(2,1)S(1)}, u32[]{:S(2)}, u32[]{:S(2)}) collective-permute-start(bf16[128,1024]{1,0:T(8,128)(2,1)S(1)} %collective-permute-done.3.refs_1_), channel_id=1, source_target_pairs={{0,24},{1,25},{2,26},{3,27},{4,28},{5,29},{6,30},{7,31},{8,0},{9,1... | collective-permute-start | bytes 786440 | tf_op jit(solution)/shard_map/ppermute | solution.py:26
  27.0 6.4 %collective-permute-start.8 = (bf16[128,1024]{1,0:T(8,128)(2,1)S(1)}, bf16[128,1024]{1,0:T(8,128)(2,1)S(1)}, u32[]{:S(2)}, u32[]{:S(2)}) collective-permute-start(bf16[128,1024]{1,0:T(8,128)(2,1)S(1)} %collective-permute-done.5.refs_1_), channel_id=1, source_target_pairs={{0,96},{1,97},{2,98},{3,99},{4,100},{5,101},{6,102},{7,103},{8,104... | collective-permute-start | bytes 786440 | tf_op jit(solution)/shard_map/ppermute | solution.py:26
  29.0 17.2 %collective-permute-start.14 = (bf16[256,1024]{1,0:T(8,128)(2,1)S(1)}, bf16[256,1024]{1,0:T(8,128)(2,1)S(1)}, u32[]{:S(2)}, u32[]{:S(2)}) collective-permute-start(bf16[256,1024]{1,0:T(8,128)(2,1)S(1)} %copy-done), channel_id=1, source_target_pairs={{0,6},{1,7},{2,4},{3,5},{4,2},{5,3},{6,0},{7,1},{8,14},{9,15},{10,... | collective-permute-start | bytes 1572872 | tf_op jit(solution)/shard_map/ppermute | solution.py:26
  34.1 22.8 %collective-permute-start.13 = (bf16[4,128,1024]{2,1,0:T(8,128)(2,1)S(1)}, bf16[4,128,1024]{2,1,0:T(8,128)(2,1)S(1)}, u32[]{:S(2)}, u32[]{:S(2)}) collective-permute-start(bf16[4,128,1024]{2,1,0:T(8,128)(2,1)S(1)} %shard_map.29.refs_7_.p0), channel_id=1, source_target_pairs={{0,8},{1,9},{2,10},{3,11},{4,12},{5,13},{6,14},{7,15},{8,16},{9,17... | collective-permute-start | bytes 3145736 | tf_op jit(solution)/shard_map/ppermute | solution.py:26
  34.1 22.7 %collective-permute-start.12 = (bf16[4,128,1024]{2,1,0:T(8,128)(2,1)S(1)}, bf16[4,128,1024]{2,1,0:T(8,128)(2,1)S(1)}, u32[]{:S(2)}, u32[]{:S(2)}) collective-permute-start(bf16[4,128,1024]{2,1,0:T(8,128)(2,1)S(1)} %shard_map.29.refs_7_.p0), channel_id=1, source_target_pairs={{0,24},{1,25},{2,26},{3,27},{4,28},{5,29},{6,30},{7,31},{8,0},{9,1... | collective-permute-start | bytes 3145736 | tf_op jit(solution)/shard_map/ppermute | solution.py:26
  38.0 21.8 %collective-permute-start.11 = (bf16[4,128,1024]{2,1,0:T(8,128)(2,1)S(1)}, bf16[4,128,1024]{2,1,0:T(8,128)(2,1)S(1)}, u32[]{:S(2)}, u32[]{:S(2)}) collective-permute-start(bf16[4,128,1024]{2,1,0:T(8,128)(2,1)S(1)} %shard_map.28.refs_4_.p0), channel_id=1, source_target_pairs={{0,32},{1,33},{2,34},{3,35},{4,36},{5,37},{6,38},{7,39},{8,40},{9,... | collective-permute-start | bytes 3145736 | tf_op jit(solution)/shard_map/ppermute | solution.py:26
  38.1 22.1 %collective-permute-start.10 = (bf16[4,128,1024]{2,1,0:T(8,128)(2,1)S(1)}, bf16[4,128,1024]{2,1,0:T(8,128)(2,1)S(1)}, u32[]{:S(2)}, u32[]{:S(2)}) collective-permute-start(bf16[4,128,1024]{2,1,0:T(8,128)(2,1)S(1)} %shard_map.28.refs_4_.p0), channel_id=1, source_target_pairs={{0,96},{1,97},{2,98},{3,99},{4,100},{5,101},{6,102},{7,103},{8,104... | collective-permute-start | bytes 3145736 | tf_op jit(solution)/shard_map/ppermute | solution.py:26
  46.2 10.7 %collective-permute-start.15 = (bf16[256,1024]{1,0:T(8,128)(2,1)S(1)}, bf16[256,1024]{1,0:T(8,128)(2,1)S(1)}, u32[]{:S(2)}, u32[]{:S(2)}) collective-permute-start(bf16[256,1024]{1,0:T(8,128)(2,1)S(1)} %copy-done), channel_id=1, source_target_pairs={{0,2},{1,3},{2,0},{3,1},{4,6},{5,7},{6,4},{7,5},{8,10},{9,11},{10,... | collective-permute-start | bytes 1572872 | tf_op jit(solution)/shard_map/ppermute | solution.py:26
  60.9 14.2 %collective-permute-start.16 = (bf16[2,128,1024]{2,1,0:T(8,128)(2,1)S(1)}, bf16[2,128,1024]{2,1,0:T(8,128)(2,1)S(1)}, u32[]{:S(2)}, u32[]{:S(2)}) collective-permute-start(bf16[2,128,1024]{2,1,0:T(8,128)(2,1)S(1)} %get-tuple-element.65), channel_id=1, source_target_pairs={{0,96},{1,97},{2,98},{3,99},{4,100},{5,101},{6,102},{7,103},{8,104... | collective-permute-start | bytes 1572872 | tf_op jit(solution)/shard_map/ppermute | solution.py:26
  64.7 10.4 %collective-permute-start.17 = (bf16[2,128,1024]{2,1,0:T(8,128)(2,1)S(1)}, bf16[2,128,1024]{2,1,0:T(8,128)(2,1)S(1)}, u32[]{:S(2)}, u32[]{:S(2)}) collective-permute-start(bf16[2,128,1024]{2,1,0:T(8,128)(2,1)S(1)} %get-tuple-element.66), channel_id=1, source_target_pairs={{0,32},{1,33},{2,34},{3,35},{4,36},{5,37},{6,38},{7,39},{8,40},{9,... | collective-permute-start | bytes 1572872 | tf_op jit(solution)/shard_map/ppermute | solution.py:26
  65.3 9.8 %collective-permute-start.18 = (bf16[2,128,1024]{2,1,0:T(8,128)(2,1)S(1)}, bf16[2,128,1024]{2,1,0:T(8,128)(2,1)S(1)}, u32[]{:S(2)}, u32[]{:S(2)}) collective-permute-start(bf16[2,128,1024]{2,1,0:T(8,128)(2,1)S(1)} %get-tuple-element.67), channel_id=1, source_target_pairs={{0,24},{1,25},{2,26},{3,27},{4,28},{5,29},{6,30},{7,31},{8,0},{9,1... | collective-permute-start | bytes 1572872 | tf_op jit(solution)/shard_map/ppermute | solution.py:26
  65.4 10.6 %collective-permute-start.19 = (bf16[2,128,1024]{2,1,0:T(8,128)(2,1)S(1)}, bf16[2,128,1024]{2,1,0:T(8,128)(2,1)S(1)}, u32[]{:S(2)}, u32[]{:S(2)}) collective-permute-start(bf16[2,128,1024]{2,1,0:T(8,128)(2,1)S(1)} %get-tuple-element.68), channel_id=1, source_target_pairs={{0,8},{1,9},{2,10},{3,11},{4,12},{5,13},{6,14},{7,15},{8,16},{9,17... | collective-permute-start | bytes 1572872 | tf_op jit(solution)/shard_map/ppermute | solution.py:26
  78.7 4.2 %collective-permute-start.20 = (f32[8,512,128]{2,1,0:T(8,128)S(1)}, f32[8,512,128]{2,1,0:T(8,128)S(1)}, u32[]{:S(2)}, u32[]{:S(2)}) collective-permute-start(f32[8,512,128]{2,1,0:T(8,128)S(1)} %bitcast.13), channel_id=1, source_target_pairs={{0,1},{1,0},{2,3},{3,2},{4,5},{5,4},{6,7},{7,6},{8,9},{9,8},{10,11... | collective-permute-start | bytes 6291464 | tf_op jit(solution)/shard_map/ppermute | solution.py:26
  107.4 20.1 %collective-permute-start.21 = (f32[8,512,128]{2,1,0:T(8,128)S(1)}, f32[8,512,128]{2,1,0:T(8,128)S(1)}, u32[]{:S(2)}, u32[]{:S(2)}) collective-permute-start(f32[8,512,128]{2,1,0:T(8,128)S(1)} %get-tuple-element.74.plan), channel_id=1, source_target_pairs={{0,1},{1,0},{2,3},{3,2},{4,5},{5,4},{6,7},{7,6},{8,9},{9,8},{10,11... | collective-permute-start | bytes 6291464 | tf_op jit(solution)/shard_map/ppermute | solution.py:26
  130.6 12.8 %collective-permute-start.22 = (bf16[144,1024]{1,0:T(8,128)(2,1)S(1)}, bf16[144,1024]{1,0:T(8,128)(2,1)S(1)}, u32[]{:S(2)}, u32[]{:S(2)}) collective-permute-start(bf16[144,1024]{1,0:T(8,128)(2,1)S(1)} %get-tuple-element.81), channel_id=1, source_target_pairs={{0,6},{1,7},{2,4},{3,5},{4,2},{5,3},{6,0},{7,1},{8,14},{9,15},{10,... | collective-permute-start | bytes 884744 | tf_op jit(solution)/shard_map/ppermute | solution.py:26
  131.8 8.7 %collective-permute-start.24 = (bf16[144,1024]{1,0:T(8,128)(2,1)S(1)}, bf16[144,1024]{1,0:T(8,128)(2,1)S(1)}, u32[]{:S(2)}, u32[]{:S(2)}) collective-permute-start(bf16[144,1024]{1,0:T(8,128)(2,1)S(1)} %get-tuple-element.84), channel_id=1, source_target_pairs={{0,4},{1,5},{2,6},{3,7},{4,0},{5,1},{6,2},{7,3},{8,12},{9,13},{10,... | collective-permute-start | bytes 884744 | tf_op jit(solution)/shard_map/ppermute | solution.py:26
  141.2 14.8 %collective-permute-start.25 = (bf16[272,1024]{1,0:T(8,128)(2,1)S(1)}, bf16[272,1024]{1,0:T(8,128)(2,1)S(1)}, u32[]{:S(2)}, u32[]{:S(2)}) collective-permute-start(bf16[272,1024]{1,0:T(8,128)(2,1)S(1)} %shard_map.45), channel_id=1, source_target_pairs={{0,6},{1,7},{2,4},{3,5},{4,2},{5,3},{6,0},{7,1},{8,14},{9,15},{10,... | collective-permute-start | bytes 1671176 | tf_op jit(solution)/shard_map/ppermute | solution.py:26
  143.9 13.3 %collective-permute-start.23 = (bf16[272,1024]{1,0:T(8,128)(2,1)S(1)}, bf16[272,1024]{1,0:T(8,128)(2,1)S(1)}, u32[]{:S(2)}, u32[]{:S(2)}) collective-permute-start(bf16[272,1024]{1,0:T(8,128)(2,1)S(1)} %shard_map.43), channel_id=1, source_target_pairs={{0,4},{1,5},{2,6},{3,7},{4,0},{5,1},{6,2},{7,3},{8,12},{9,13},{10,... | collective-permute-start | bytes 1671176 | tf_op jit(solution)/shard_map/ppermute | solution.py:26

commit v2 on v1

--- a/solution.py
+++ b/solution.py
@@ -133,6 +133,14 @@
 
 def halves_kernel(at, next_, last, low, high, sems):
     for copy in started(sems, (next_.at[:2], low), (last.at[2:], high)):
+        copy.wait()
+
+
+def split_kernel(at, noise, near, far, sems):
+    mid = near.shape[0]
+    spans = [pl.ds(pl.multiple_of(n * mid, mid), mid) for n in (at[3], 1 - at[3])]
+    copies = started(sems, (noise.at[spans[0]], near), (noise.at[spans[1]], far))
+    for copy in copies:
         copy.wait()
 
 
@@ -238,36 +246,49 @@
         out[mid:, :mid] = terms_in_rows(total[:, n * mid : n * mid + mid])
 
 
-def target_2_kernel(place, own_rows, at, weights, p0, p1, p3, p2_a, p2_b, out, row_total):
-    parts, total = weights_of(at, weights, place, own_rows)
+def target_2_kernel(
+    place, half, at, weights, p0, p1, p3, p2_a, p2_b, message, values, row_total
+):
+    parts, total = weights_of(at, weights, place, False)
+    mid = values.shape[0]
+    kept, sent = (slice(n * mid, n * mid + mid) for n in (half, 1 - half))
     for first in range(0, p0.shape[-1], STEP):
-        out[:, first : first + STEP] = product(parts, (p0, p1, p3, p2_a, p2_b), first)
+        value = product(parts, (p0, p1, p3, p2_a, p2_b), first)
+        message[:mid, first : first + STEP] = value[sent].astype(message.dtype)
+        values[:, first : first + STEP] = value[kept]
+    message[mid:, :] = jnp.zeros((16, message.shape[1]), message.dtype)
+    message[mid:, :mid] = terms_in_rows(total[:, sent])
+    row_total[...] = jnp.broadcast_to(total[:, kept], row_total.shape)
+
+
+def target_3_kernel(at, weights, p0, p1, p3, p2_a, p2_b, values, row_total):
+    parts, total = weights_of(at, weights, near_place, True)
+    for first in range(0, p0.shape[-1], STEP):
+        values[:, first : first + STEP] = product(parts, (p0, p1, p3, p2_a, p2_b), first)
     row_total[...] = jnp.broadcast_to(total, row_total.shape)
 
 
-def add_kernel(part, at, values, row_total, came, out):
-    mid = came.shape[0] - 16
-    here = slice(part * mid, part * mid + mid)
-    there = slice(mid - part * mid, 2 * mid - part * mid)
-    out[here] = (values[here] + came[:mid].astype(jnp.float32)).astype(out.dtype)
-    out[there] = values[there].astype(out.dtype)
+def add_kernel(at, values, row_total, came, out):
+    mid = values.shape[0]
+    out[:mid, :] = (values[...] + came[:mid].astype(jnp.float32)).astype(out.dtype)
     terms = came[mid:, :mid].astype(jnp.float32)
-    total = [row_total[:1, :mid], row_total[:1, mid:]]
-    total[part] = total[part] + terms[0:1] + terms[1:2] + terms[2:3]
-    out[2 * mid :, :] = jnp.zeros((16, out.shape[1]), out.dtype)
-    out[2 * mid :, : 2 * mid] = terms_in_rows(jnp.concatenate(total, axis=1))
-
-
-def last_kernel(at, own, own_total, a, b, out):
-    rows = own.shape[0]
-    terms = [terms_in_rows(own_total[:1])] + [m[rows:, :rows] for m in (a, b)]
-    total = to_rows(jnp.concatenate(terms, axis=0))
-    for column in range(0, own.shape[1], 128):
-        span = slice(column, column + 128)
-        value = own[:, span]
-        for m in (a, b):
-            value = value + m[:rows, span].astype(jnp.float32)
-        out[:, span] = (value / total).astype(out.dtype)
+    total = row_total[:1] + terms[0:1] + terms[1:2] + terms[2:3]
+    out[mid:, :] = jnp.zeros((16, out.shape[1]), out.dtype)
+    out[mid:, :mid] = terms_in_rows(total)
+
+
+def last_kernel(at, own, own_total, l_low, l_high, lh_low, lh_high, out):
+    mid = own.shape[0] // 2
+    for n, messages in enumerate(((l_low, lh_low), (l_high, lh_high))):
+        here = slice(n * mid, n * mid + mid)
+        terms = [terms_in_rows(own_total[:1, here])] + [m[mid:, :mid] for m in messages]
+        total = to_rows(jnp.concatenate(terms, axis=0))
+        for column in range(0, own.shape[1], 128):
+            span = slice(column, column + 128)
+            value = own[here, span]
+            for m in messages:
+                value = value + m[:mid, span].astype(jnp.float32)
+            out[here, span] = (value / total).astype(out.dtype)
 
 
 TILE = 64
@@ -365,29 +386,23 @@
 
     at = jnp.stack([z, y, l, h, c])
 
-    def quarter(to_l, to_h):
-        return lax.dynamic_slice_in_dim(noise_rows, (2 * to_h + to_l) * piece, piece)
-
     wave = lax.optimization_barrier
-    near_other, far_own, far_other = wave(
-        (
-            flip(quarter(1 - l, h), "l"),
-            flip(quarter(l, 1 - h), "h"),
-            flip(quarter(1 - l, 1 - h), "lh"),
-        )
-    )
-    near = jnp.concatenate([quarter(l, h), near_other])
-    far = jnp.concatenate([far_own, far_other])
-
+    mid = rows // 2
+    sems = pltpu.SemaphoreType.DMA((4,))
+    near, far = call(
+        split_kernel,
+        [bfloat16(mid, part)] * 2,
+        0,
+        *(at, noise_rows),
+        anywhere=1,
+        spaces=pl.ANY,
+        scratch=[sems],
+    )
+    far = flip(far, "h")
+    near_1, near_2, near_3 = (from_y(near, k) for k in (1, 2, 3))
+    near_1, near_2, near_3, far, data_rows = wave((near_1, near_2, near_3, far, data_rows))
+    far_1, far_2, far_3 = (from_z(far, k) for k in (1, 2, 3))
     data_l = flip(data_rows, "l")
-    near_1, near_3, far_1, far_3, data_rows = wave(
-        (from_y(near, 1), from_y(near, 3), from_z(far, 1), from_z(far, 3), data_rows)
-    )
-    data_lh = flip(data_rows, "lh")
-    near_2, far_2, data_l, data_rows = wave(
-        (from_y(near_1, 1), from_z(far_1, 1), data_l, data_rows)
-    )
-    sems = pltpu.SemaphoreType.DMA((4,))
 
     def stacked(*blocks):
         out = [bfloat16(4, *blocks[0].shape)]
@@ -401,13 +416,15 @@
             halves_kernel, out, 0, at, next_, last, anywhere=2, spaces=pl.ANY, scratch=[sems]
         )
 
-    near, far = stacked(near, near_1, near_2, near_3), stacked(far, far_1, far_2, far_3)
+    near = stacked(near, near_1, near_2, near_3)
+    near, far_1, far_3 = wave((near, far_1, far_3))
     near_next, near_last = from_z(near, 1), from_z(near, 3)
+    far_2, data_l, data_rows = wave((far_2, data_l, data_rows))
+    far = stacked(far, far_1, far_2, far_3)
     far_next, far_last = from_y(far, 1), from_y(far, 3)
+    data_lh = flip(data_rows, "lh")
+    data_lh, data_rows = wave((data_lh, data_rows))
     data_h = flip(data_rows, "h")
-    near_next, near_last, far_next, far_last, data_lh, data_h = wave(
-        (near_next, near_last, far_next, far_last, data_lh, data_h)
-    )
     nears, fars = (near, near_next, near_last), (far, far_next, far_last)
     low, high = halves(near_next, near_last)
     near_two = from_z(low, 1), from_z(high, 3)
@@ -477,24 +494,28 @@
     weights = weights.reshape(4, 4, *blocks[1:])
 
     near_noise, far_noise = (*nears, *near_two), (*fars, *far_two)
-    low, high = call(
-        target_1_kernel, [bfloat16(rows // 2 + 16, part)] * 2, 8 * one, at, weights, *far_noise
-    )
+    message = bfloat16(mid + 16, part)
+    low, high = call(target_1_kernel, [message] * 2, 8 * one, at, weights, *far_noise)
     low, high = flip(low, "l"), flip(high, "lh")
 
-    def target(place, own_rows):
-        kernel = functools.partial(target_2_kernel, place, own_rows)
+    def other_rows(place, half, came, names):
         noise = near_noise if place is near_place else far_noise
-        return call(kernel, [float32(rows, part), float32(8, rows)], 8 * one, at, weights, *noise)
-
-    def message(half, came, values, row_total):
-        kernel = functools.partial(add_kernel, half)
-        return call(kernel, [bfloat16(rows + 16, part)], 0, at, values, row_total, came)[0]
-
-    to_lh = flip(message(0, low, *target(far_place, False)), "lh")
-    to_l = flip(message(1, high, *target(near_place, False)), "l")
-    own, own_total = target(near_place, True)
-    return call(last_kernel, [bfloat16(rows, part)], 0, at, own, own_total, to_l, to_lh)[0]
+        kernel = functools.partial(target_2_kernel, place, half)
+        outs = [message, float32(mid, part), float32(8, mid)]
+        sent, *kept = call(kernel, outs, 8 * one, at, weights, *noise)
+        added = call(add_kernel, [message], 0, at, *kept, came)[0]
+        return flip(sent, names), flip(added, names)
+
+    lh_high, lh_low = other_rows(far_place, 0, low, "lh")
+    l_low, l_high = other_rows(near_place, 1, high, "l")
+    own = call(
+        target_3_kernel,
+        [float32(rows, part), float32(8, rows)],
+        8 * one,
+        *(at, weights, *near_noise),
+    )
+    messages = l_low, l_high, lh_low, lh_high
+    return call(last_kernel, [bfloat16(rows, part)], 0, at, *own, *messages)[0]
 
 
 def solution(mesh):

time: 159 us -> 157 us (0.987)
  waiting for transfers between devices: 51 us -> 47.6 us
  starting transfers between devices: 35 us -> 37.2 us
    ppermute x26, waiting for transfers between devices: 51 us -> 47.6 us  [move(): return lax.ppermute(value, AXES, pairs)]
    ppermute x26, starting transfers between devices: 35 us -> 37.2 us  [move(): return lax.ppermute(value, AXES, pairs)]
    pallas_call x19 -> x20, Pallas kernels: 32.3 us -> 33 us  [call(): pl.pallas_call(kernel, out_shape=outs, in_specs=[pl.BlockSpec(memory_spac...]
  transfers between devices with their start and end apart: 26 -> 26, of which waited for: 16 -> 13; matrix products, arithmetic and copies ran while one was open for 0% -> 0% of each run, Pallas kernels for 12% -> 13%
where the time goes in v2:
time: 157 us
  waiting for transfers between devices  47.6 us (30%)
  blocking collectives  37.6 us (24%)
  starting transfers between devices  37.2 us (24%)
  Pallas kernels  33 us (21%)
    ppermute x26, waiting for transfers between devices, move(): return lax.ppermute(value, AXES, pairs)  47.6 us
    all_to_all x4, blocking collectives, exchange(): return lax.all_to_all(sent, axes, 0, 0, tiled=True)  37.6 us
    ppermute x26, starting transfers between devices, move(): return lax.ppermute(value, AXES, pairs)  37.2 us
    pallas_call x20, Pallas kernels, call(): pl.pallas_call(kernel, out_shape=outs, in_specs=[pl.BlockSpec(memory_spac...  33 us
  transfers between devices with their start and end apart: 26, of which 13 were waited for; matrix products, arithmetic and copies ran while one was open for 0% of the time, Pallas kernels for 13%

profile of v2, /device:TPU:0, one launch (start us, length us, event | category | flops | bytes accessed | tf_op | source)
XLA Modules:
  0.0 156.7 jit_solution(9557884620178601053)
XLA Ops:
  0.0 0.1 stack.23.at
  0.1 1.0 copy-done
  1.1 0.6 shard_map.28
  1.8 3.2 %collective-permute-start.3 = (bf16[128,1024]{1,0:T(8,128)(2,1)S(1)}, bf16[128,1024]{1,0:T(8,128)(2,1)S(1)}, u32[]{:S(2)}, u32[]{:S(2)}) collective-permute-start(bf16[128,1024]{1,0:T(8,128)(2,1)S(1)} %get-tuple-element.45), channel_id=1, source_target_pairs={{0,2},{1,3},{2,0},{3,1},{4,6},{5,7},{6,4},{7,5},{8,10},{9,11},{10,... | collective-permute-start | bytes 786440 | tf_op jit(solution)/shard_map/ppermute | solution.py:26
  4.9 1.6 %collective-permute-start.2 = (bf16[128,1024]{1,0:T(8,128)(2,1)S(1)}, bf16[128,1024]{1,0:T(8,128)(2,1)S(1)}, u32[]{:S(2)}, u32[]{:S(2)}) collective-permute-start(bf16[128,1024]{1,0:T(8,128)(2,1)S(1)} %get-tuple-element.44.refs_0_), channel_id=1, source_target_pairs={{0,8},{1,9},{2,10},{3,11},{4,12},{5,13},{6,14},{7,15},{8,16},{9,17... | collective-permute-start | bytes 786440 | tf_op jit(solution)/shard_map/ppermute | solution.py:26
  6.5 2.9 %collective-permute-start.1 = (bf16[128,1024]{1,0:T(8,128)(2,1)S(1)}, bf16[128,1024]{1,0:T(8,128)(2,1)S(1)}, u32[]{:S(2)}, u32[]{:S(2)}) collective-permute-start(bf16[128,1024]{1,0:T(8,128)(2,1)S(1)} %get-tuple-element.44.refs_0_), channel_id=1, source_target_pairs={{0,16},{1,17},{2,18},{3,19},{4,20},{5,21},{6,22},{7,23},{8,24},{9,... | collective-permute-start | bytes 786440 | tf_op jit(solution)/shard_map/ppermute | solution.py:26
  9.4 1.3 collective-permute-start
  10.8 0.5 collective-permute-done.3.refs_0_
  11.2 3.0 %collective-permute-done.2.refs_3_ = bf16[128,1024]{1,0:T(8,128)(2,1)S(1)} collective-permute-done((bf16[128,1024]{1,0:T(8,128)(2,1)S(1)}, bf16[128,1024]{1,0:T(8,128)(2,1)S(1)}, u32[]{:S(2)}, u32[]{:S(2)}) %collective-permute-start.2) | collective-permute-done | bytes 262176 | tf_op jit(solution)/shard_map/ppermute | solution.py:26
  14.3 6.5 %collective-permute-done.1.refs_2_ = bf16[128,1024]{1,0:T(8,128)(2,1)S(1)} collective-permute-done((bf16[128,1024]{1,0:T(8,128)(2,1)S(1)}, bf16[128,1024]{1,0:T(8,128)(2,1)S(1)}, u32[]{:S(2)}, u32[]{:S(2)}) %collective-permute-start.1) | collective-permute-done | bytes 262176 | tf_op jit(solution)/shard_map/ppermute | solution.py:26
  20.8 0.6 collective-permute-start.5
  21.4 1.9 %collective-permute-start.9 = (bf16[128,1024]{1,0:T(8,128)(2,1)S(1)}, bf16[128,1024]{1,0:T(8,128)(2,1)S(1)}, u32[]{:S(2)}, u32[]{:S(2)}) collective-permute-start(bf16[128,1024]{1,0:T(8,128)(2,1)S(1)} %collective-permute-done.3.refs_0_), channel_id=1, source_target_pairs={{0,32},{1,33},{2,34},{3,35},{4,36},{5,37},{6,38},{7,39},{8,40},{9,... | collective-permute-start | bytes 786440 | tf_op jit(solution)/shard_map/ppermute | solution.py:26
  23.3 2.1 %collective-permute-start.8 = (bf16[128,1024]{1,0:T(8,128)(2,1)S(1)}, bf16[128,1024]{1,0:T(8,128)(2,1)S(1)}, u32[]{:S(2)}, u32[]{:S(2)}) collective-permute-start(bf16[128,1024]{1,0:T(8,128)(2,1)S(1)} %collective-permute-done.3.refs_0_), channel_id=1, source_target_pairs={{0,96},{1,97},{2,98},{3,99},{4,100},{5,101},{6,102},{7,103},{8,104... | collective-permute-start | bytes 786440 | tf_op jit(solution)/shard_map/ppermute | solution.py:26
  25.4 1.9 %collective-permute-start.4 = (bf16[128,1024]{1,0:T(8,128)(2,1)S(1)}, bf16[128,1024]{1,0:T(8,128)(2,1)S(1)}, u32[]{:S(2)}, u32[]{:S(2)}) collective-permute-start(bf16[128,1024]{1,0:T(8,128)(2,1)S(1)} %collective-permute-done.3.refs_0_), channel_id=1, source_target_pairs={{0,64},{1,65},{2,66},{3,67},{4,68},{5,69},{6,70},{7,71},{8,72},{9,... | collective-permute-start | bytes 786440 | tf_op jit(solution)/shard_map/ppermute | solution.py:26
  27.3 0.7 shard_map.29.refs_4_.p0
  27.9 3.8 %collective-permute-done.9.refs_3_ = bf16[128,1024]{1,0:T(8,128)(2,1)S(1)} collective-permute-done((bf16[128,1024]{1,0:T(8,128)(2,1)S(1)}, bf16[128,1024]{1,0:T(8,128)(2,1)S(1)}, u32[]{:S(2)}, u32[]{:S(2)}) %collective-permute-start.9) | collective-permute-done | bytes 262176 | tf_op jit(solution)/shard_map/ppermute | solution.py:26
  31.7 1.7 %collective-permute-done.8.refs_1_ = bf16[128,1024]{1,0:T(8,128)(2,1)S(1)} collective-permute-done((bf16[128,1024]{1,0:T(8,128)(2,1)S(1)}, bf16[128,1024]{1,0:T(8,128)(2,1)S(1)}, u32[]{:S(2)}, u32[]{:S(2)}) %collective-permute-start.8) | collective-permute-done | bytes 262176 | tf_op jit(solution)/shard_map/ppermute | solution.py:26
  33.4 0.5 collective-permute-start.11
  34.0 3.7 %collective-permute-start.10 = (bf16[4,128,1024]{2,1,0:T(8,128)(2,1)S(1)}, bf16[4,128,1024]{2,1,0:T(8,128)(2,1)S(1)}, u32[]{:S(2)}, u32[]{:S(2)}) collective-permute-start(bf16[4,128,1024]{2,1,0:T(8,128)(2,1)S(1)} %shard_map.29.refs_4_.p0), channel_id=1, source_target_pairs={{0,96},{1,97},{2,98},{3,99},{4,100},{5,101},{6,102},{7,103},{8,104... | collective-permute-start | bytes 3145736 | tf_op jit(solution)/shard_map/ppermute | solution.py:26
  37.6 2.1 %collective-permute-done.4.refs_2_ = bf16[128,1024]{1,0:T(8,128)(2,1)S(1)} collective-permute-done((bf16[128,1024]{1,0:T(8,128)(2,1)S(1)}, bf16[128,1024]{1,0:T(8,128)(2,1)S(1)}, u32[]{:S(2)}, u32[]{:S(2)}) %collective-permute-start.4) | collective-permute-done | bytes 262176 | tf_op jit(solution)/shard_map/ppermute | solution.py:26
  39.7 0.7 shard_map.30.refs_7_.p0
  40.4 1.3 collective-permute-start.13
  41.6 2.1 %collective-permute-start.12 = (bf16[4,128,1024]{2,1,0:T(8,128)(2,1)S(1)}, bf16[4,128,1024]{2,1,0:T(8,128)(2,1)S(1)}, u32[]{:S(2)}, u32[]{:S(2)}) collective-permute-start(bf16[4,128,1024]{2,1,0:T(8,128)(2,1)S(1)} %shard_map.30.refs_7_.p0), channel_id=1, source_target_pairs={{0,24},{1,25},{2,26},{3,27},{4,28},{5,29},{6,30},{7,31},{8,0},{9,1... | collective-permute-start | bytes 3145736 | tf_op jit(solution)/shard_map/ppermute | solution.py:26
  43.7 0.8 collective-permute-start.6
  44.5 16.1 %collective-permute-done.6.refs_3_ = bf16[256,1024]{1,0:T(8,128)(2,1)S(1)} collective-permute-done((bf16[256,1024]{1,0:T(8,128)(2,1)S(1)}, bf16[256,1024]{1,0:T(8,128)(2,1)S(1)}, u32[]{:S(2)}, u32[]{:S(2)}) %collective-permute-start.6) | collective-permute-done | bytes 524320 | tf_op jit(solution)/shard_map/ppermute | solution.py:26
  60.6 0.8 collective-permute-start.7
  61.4 0.7 shard_map.32
  62.0 1.1 collective-permute-start.14
  63.2 1.0 collective-permute-start.15
  64.1 0.7 shard_map.33
  64.8 2.4 %collective-permute-start.16 = (bf16[2,128,1024]{2,1,0:T(8,128)(2,1)S(1)}, bf16[2,128,1024]{2,1,0:T(8,128)(2,1)S(1)}, u32[]{:S(2)}, u32[]{:S(2)}) collective-permute-start(bf16[2,128,1024]{2,1,0:T(8,128)(2,1)S(1)} %get-tuple-element.63), channel_id=1, source_target_pairs={{0,24},{1,25},{2,26},{3,27},{4,28},{5,29},{6,30},{7,31},{8,0},{9,1... | collective-permute-start | bytes 1572872 | tf_op jit(solution)/shard_map/ppermute | solution.py:26
  67.2 4.1 %collective-permute-done.7.refs_2_ = bf16[256,1024]{1,0:T(8,128)(2,1)S(1)} collective-permute-done((bf16[256,1024]{1,0:T(8,128)(2,1)S(1)}, bf16[256,1024]{1,0:T(8,128)(2,1)S(1)}, u32[]{:S(2)}, u32[]{:S(2)}) %collective-permute-start.7) | collective-permute-done | bytes 524320 | tf_op jit(solution)/shard_map/ppermute | solution.py:26
  71.3 7.7 %shard_map.31 = (f32[4,4,512,128]{3,2,1,0:T(8,128)S(1)}, bf16[2,512,1024]{2,1,0:T(8,128)(2,1)S(1)}) custom-call(s32[5]{0:T(128)S(1)} %stack.23.at, bf16[256,1024]{1,0:T(8,128)(2,1)S(1)} %copy-done.1, bf16[256,1024]{1,0:T(8,128)(2,1)S(1)} %collective-permute-done.5.refs_1_, bf16[256,1024]{1,0:T(8,128)(2,1)S(1)} %collective-permute-done.7.refs_2_, ...), custom_call_target="tpu_custom_call" | custom-call | flops 3221225472 | bytes 14680084 | tf_op jit(solution)/shard_map/pallas_call | solution.py:76
  79.0 2.7 %shard_map.35 = f32[2,4,512,128]{3,2,1,0:T(8,128)S(1)} custom-call(s32[5]{0:T(128)S(1)} %stack.23.at, bf16[2,512,1024]{2,1,0:T(8,128)(2,1)S(1)} %get-tuple-element.59.x, f32[4,4,512,128]{3,2,1,0:T(8,128)S(1)} %get-tuple-element.60.acc, bf16[2,128,1024]{2,1,0:T(8,128)(2,1)S(1)} %collective-permute-done.14.n_a.p2_a, ...), custom_call_target="tpu_custom_call" | custom-call | flops 536870912 | bytes 10485780 | tf_op jit(solution)/shard_map/pallas_call | solution.py:76
  81.7 0.1 collective-permute-start.18
  81.8 1.7 %shard_map.34 = f32[2,4,512,128]{3,2,1,0:T(8,128)S(1)} custom-call(s32[5]{0:T(128)S(1)} %stack.23.at, bf16[2,512,1024]{2,1,0:T(8,128)(2,1)S(1)} %get-tuple-element.59.x, f32[4,4,512,128]{3,2,1,0:T(8,128)S(1)} %get-tuple-element.60.acc, bf16[2,128,1024]{2,1,0:T(8,128)(2,1)S(1)} %collective-permute-done.14.n_a.p2_a, ...), custom_call_target="tpu_custom_call" | custom-call | flops 536870912 | bytes 10485780 | tf_op jit(solution)/shard_map/pallas_call | solution.py:76
  83.5 2.4 %collective-permute-done.18.got = f32[8,512,128]{2,1,0:T(8,128)S(1)} collective-permute-done((f32[8,512,128]{2,1,0:T(8,128)S(1)}, f32[8,512,128]{2,1,0:T(8,128)S(1)}, u32[]{:S(2)}, u32[]{:S(2)}) %collective-permute-start.18) | collective-permute-done | bytes 2097184 | tf_op jit(solution)/shard_map/ppermute | solution.py:26
  85.9 2.0 %shard_map.36 = (f32[8,512,128]{2,1,0:T(8,128)S(1)}, f32[8,1,512]{2,1,0:T(1,128)S(1)}) custom-call(s32[5]{0:T(128)S(1)} %stack.23.at, f32[8,512,128]{2,1,0:T(8,128)S(1)} %bitcast.8, f32[8,512,128]{2,1,0:T(8,128)S(1)} %collective-permute-done.18.got), custom_call_target="tpu_custom_call" | custom-call | bytes 6307860 | tf_op jit(solution)/shard_map/pallas_call | solution.py:76
  87.9 7.7 %all_to_all.20.came = f32[8,1,512]{2,1,0:T(1,128)S(1)} all-to-all(f32[8,1,512]{2,1,0:T(1,128)S(1)} %get-tuple-element.65), channel_id=1, replica_groups=mesh['z'=4,'y'=4,'l'=2,'h'=2,'c'=2] {'l','h','c'}, dimensions={0} | all-to-all | bytes 32768 | tf_op jit(solution)/shard_map/all_to_all | solution.py:463
  95.6 1.3 shard_map.37
  96.9 10.8 %all_to_all.21.came = f32[16,8,128]{2,1,0:T(8,128)S(1)} all-to-all(f32[16,8,128]{2,1,0:T(8,128)S(1)} %get-tuple-element.67), channel_id=1, replica_groups=mesh['z'=4,'y'=4,'l'=2,'h'=2,'c'=2] {'z','y'}, dimensions={0} | all-to-all | bytes 131072 | tf_op jit(solution)/shard_map/all_to_all | solution.py:463
  107.6 1.3 shard_map.38
  108.9 0.0 collective-permute-start.19
  108.9 7.7 %all_to_all.22.came = f32[8,1,512]{2,1,0:T(1,128)S(1)} all-to-all(f32[8,1,512]{2,1,0:T(1,128)S(1)} %get-tuple-element.69), channel_id=1, replica_groups=mesh['z'=4,'y'=4,'l'=2,'h'=2,'c'=2] {'l','h','c'}, dimensions={0} | all-to-all | bytes 32768 | tf_op jit(solution)/shard_map/all_to_all | solution.py:463
  116.6 0.9 shard_map.39
  117.5 11.4 %all_to_all.23.came = f32[32,8,128]{2,1,0:T(8,128)S(1)} all-to-all(f32[32,8,128]{2,1,0:T(8,128)S(1)} %get-tuple-element.71), channel_id=1, replica_groups=mesh['z'=4,'y'=4,'l'=2,'h'=2,'c'=2] {'z','y','c'}, dimensions={0} | all-to-all | bytes 262144 | tf_op jit(solution)/shard_map/all_to_all | solution.py:463
  129.0 1.0 shard_map.40
  130.0 2.1 %shard_map.43 = (bf16[144,1024]{1,0:T(8,128)(2,1)S(1)}, bf16[144,1024]{1,0:T(8,128)(2,1)S(1)}) custom-call(s32[5]{0:T(128)S(1)} %stack.23.at, bf16[4,4,512,128]{3,2,1,0:T(8,128)(2,1)S(1)} %bitcast.9, bf16[4,128,1024]{2,1,0:T(8,128)(2,1)S(1)} %shard_map.30.refs_7_.p0, bf16[4,128,1024]{2,1,0:T(8,128)(2,1)S(1)} %collective-permute-done.12.refs_8_.next_.p1, ...), custom_call_target="tpu_custom_call" | custom-call | flops 2147483648 | bytes 6881300 | tf_op jit(solution)/shard_map/pallas_call | solution.py:76
  132.1 1.2 collective-permute-start.21
  133.3 0.0 collective-permute-start.23
  133.3 2.1 %shard_map.45 = (bf16[144,1024]{1,0:T(8,128)(2,1)S(1)}, f32[128,1024]{1,0:T(8,128)S(1)}, f32[8,128]{1,0:T(8,128)S(1)}) custom-call(s32[5]{0:T(128)S(1)} %stack.23.at, bf16[4,4,512,128]{3,2,1,0:T(8,128)(2,1)S(1)} %bitcast.10, bf16[4,128,1024]{2,1,0:T(8,128)(2,1)S(1)} %shard_map.30.refs_7_.p0, ...), custom_call_target="tpu_custom_call" | custom-call | flops 2147483648 | bytes 7114772 | tf_op jit(solution)/shard_map/pallas_call | solution.py:76
  135.4 2.1 %collective-permute-start.25 = (bf16[144,1024]{1,0:T(8,128)(2,1)S(1)}, bf16[144,1024]{1,0:T(8,128)(2,1)S(1)}, u32[]{:S(2)}, u32[]{:S(2)}) collective-permute-start(bf16[144,1024]{1,0:T(8,128)(2,1)S(1)} %get-tuple-element.82), channel_id=1, source_target_pairs={{0,6},{1,7},{2,4},{3,5},{4,2},{5,3},{6,0},{7,1},{8,14},{9,15},{10,... | collective-permute-start | bytes 884744 | tf_op jit(solution)/shard_map/ppermute | solution.py:26
  137.5 2.1 %shard_map.42 = (bf16[144,1024]{1,0:T(8,128)(2,1)S(1)}, f32[128,1024]{1,0:T(8,128)S(1)}, f32[8,128]{1,0:T(8,128)S(1)}) custom-call(s32[5]{0:T(128)S(1)} %stack.23.at, bf16[4,4,512,128]{3,2,1,0:T(8,128)(2,1)S(1)} %bitcast.11, bf16[4,128,1024]{2,1,0:T(8,128)(2,1)S(1)} %shard_map.29.refs_4_.p0, ...), custom_call_target="tpu_custom_call" | custom-call | flops 2147483648 | bytes 7114772 | tf_op jit(solution)/shard_map/pallas_call | solution.py:76
  139.6 1.5 collective-permute-start.20
  141.1 1.1 collective-permute-done.23.came
  142.2 0.6 shard_map.46
  142.8 3.0 %collective-permute-start.24 = (bf16[144,1024]{1,0:T(8,128)(2,1)S(1)}, bf16[144,1024]{1,0:T(8,128)(2,1)S(1)}, u32[]{:S(2)}, u32[]{:S(2)}) collective-permute-start(bf16[144,1024]{1,0:T(8,128)(2,1)S(1)} %shard_map.46), channel_id=1, source_target_pairs={{0,6},{1,7},{2,4},{3,5},{4,2},{5,3},{6,0},{7,1},{8,14},{9,15},{10,... | collective-permute-start | bytes 884744 | tf_op jit(solution)/shard_map/ppermute | solution.py:26
  145.9 0.6 shard_map.44
  146.5 0.1 collective-permute-start.22
  146.6 2.1 %shard_map.41 = (f32[256,1024]{1,0:T(8,128)S(1)}, f32[8,256]{1,0:T(8,128)S(1)}) custom-call(s32[5]{0:T(128)S(1)} %stack.23.at, bf16[4,4,512,128]{3,2,1,0:T(8,128)(2,1)S(1)} %bitcast.12, bf16[4,128,1024]{2,1,0:T(8,128)(2,1)S(1)} %shard_map.29.refs_4_.p0, bf16[4,128,1024]{2,1,0:T(8,128)(2,1)S(1)} %collective-permute-done.10.refs_5_.next_.p1, ...), custom_call_target="tpu_custom_call" | custom-call | flops 2147483648 | bytes 7348244 | tf_op jit(solution)/shard_map/pallas_call | solution.py:76
  148.6 0.9 collective-permute-done.25.lh_high
  149.5 0.1 collective-permute-done.20.l_low
  149.6 5.4 %collective-permute-done.24.lh_low = bf16[144,1024]{1,0:T(8,128)(2,1)S(1)} collective-permute-done((bf16[144,1024]{1,0:T(8,128)(2,1)S(1)}, bf16[144,1024]{1,0:T(8,128)(2,1)S(1)}, u32[]{:S(2)}, u32[]{:S(2)}) %collective-permute-start.24) | collective-permute-done | bytes 294944 | tf_op jit(solution)/shard_map/ppermute | solution.py:26
  155.0 1.7 %shard_map.47 = bf16[256,1024]{1,0:T(8,128)(2,1)} custom-call(s32[5]{0:T(128)S(1)} %stack.23.at, f32[256,1024]{1,0:T(8,128)S(1)} %get-tuple-element.73.own, f32[8,256]{1,0:T(8,128)S(1)} %get-tuple-element.74.own_total, bf16[144,1024]{1,0:T(8,128)(2,1)S(1)} %collective-permute-done.20.l_low, bf16[144,1024]{1,0:T(8,128)(2,1)S(1)} %collective-permute-done.22.l_high, ...), custom_call_target="tpu_custom_call" | custom-call | bytes 2760724 | tf_op jit(solution)/shard_map/pallas_call | solution.py:76
  (17 shorter events, 0.0 us)
Async XLA Ops:
  0.1 1.0 copy-start
  1.8 9.5 %collective-permute-start.3 = (bf16[128,1024]{1,0:T(8,128)(2,1)S(1)}, bf16[128,1024]{1,0:T(8,128)(2,1)S(1)}, u32[]{:S(2)}, u32[]{:S(2)}) collective-permute-start(bf16[128,1024]{1,0:T(8,128)(2,1)S(1)} %get-tuple-element.45), channel_id=1, source_target_pairs={{0,2},{1,3},{2,0},{3,1},{4,6},{5,7},{6,4},{7,5},{8,10},{9,11},{10,... | collective-permute-start | bytes 786440 | tf_op jit(solution)/shard_map/ppermute | solution.py:26
  4.9 38.7 %copy-start.1 = (bf16[256,1024]{1,0:T(8,128)(2,1)S(1)}, bf16[256,1024]{1,0:T(8,128)(2,1)}, u32[]{:S(2)}) copy-start(bf16[256,1024]{1,0:T(8,128)(2,1)} %refs_0_) | copy-start | bytes 1572868
  4.9 9.3 %collective-permute-start.2 = (bf16[128,1024]{1,0:T(8,128)(2,1)S(1)}, bf16[128,1024]{1,0:T(8,128)(2,1)S(1)}, u32[]{:S(2)}, u32[]{:S(2)}) collective-permute-start(bf16[128,1024]{1,0:T(8,128)(2,1)S(1)} %get-tuple-element.44.refs_0_), channel_id=1, source_target_pairs={{0,8},{1,9},{2,10},{3,11},{4,12},{5,13},{6,14},{7,15},{8,16},{9,17... | collective-permute-start | bytes 786440 | tf_op jit(solution)/shard_map/ppermute | solution.py:26
  6.5 14.3 %collective-permute-start.1 = (bf16[128,1024]{1,0:T(8,128)(2,1)S(1)}, bf16[128,1024]{1,0:T(8,128)(2,1)S(1)}, u32[]{:S(2)}, u32[]{:S(2)}) collective-permute-start(bf16[128,1024]{1,0:T(8,128)(2,1)S(1)} %get-tuple-element.44.refs_0_), channel_id=1, source_target_pairs={{0,16},{1,17},{2,18},{3,19},{4,20},{5,21},{6,22},{7,23},{8,24},{9,... | collective-permute-start | bytes 786440 | tf_op jit(solution)/shard_map/ppermute | solution.py:26
  9.4 11.4 %collective-permute-start = (bf16[128,1024]{1,0:T(8,128)(2,1)S(1)}, bf16[128,1024]{1,0:T(8,128)(2,1)S(1)}, u32[]{:S(2)}, u32[]{:S(2)}) collective-permute-start(bf16[128,1024]{1,0:T(8,128)(2,1)S(1)} %get-tuple-element.44.refs_0_), channel_id=1, source_target_pairs={{0,24},{1,25},{2,26},{3,27},{4,28},{5,29},{6,30},{7,31},{8,0},{9,1... | collective-permute-start | bytes 786440 | tf_op jit(solution)/shard_map/ppermute | solution.py:26
  20.8 18.9 %collective-permute-start.5 = (bf16[256,1024]{1,0:T(8,128)(2,1)}, bf16[256,1024]{1,0:T(8,128)(2,1)S(1)}, u32[]{:S(2)}, u32[]{:S(2)}) collective-permute-start(bf16[256,1024]{1,0:T(8,128)(2,1)} %refs_0_), channel_id=1, source_target_pairs={{0,4},{1,5},{2,6},{3,7},{4,0},{5,1},{6,2},{7,3},{8,12},{9,13},{10,... | collective-permute-start | bytes 1572872 | tf_op jit(solution)/shard_map/ppermute | solution.py:26
  21.4 10.4 %collective-permute-start.9 = (bf16[128,1024]{1,0:T(8,128)(2,1)S(1)}, bf16[128,1024]{1,0:T(8,128)(2,1)S(1)}, u32[]{:S(2)}, u32[]{:S(2)}) collective-permute-start(bf16[128,1024]{1,0:T(8,128)(2,1)S(1)} %collective-permute-done.3.refs_0_), channel_id=1, source_target_pairs={{0,32},{1,33},{2,34},{3,35},{4,36},{5,37},{6,38},{7,39},{8,40},{9,... | collective-permute-start | bytes 786440 | tf_op jit(solution)/shard_map/ppermute | solution.py:26
  23.3 10.1 %collective-permute-start.8 = (bf16[128,1024]{1,0:T(8,128)(2,1)S(1)}, bf16[128,1024]{1,0:T(8,128)(2,1)S(1)}, u32[]{:S(2)}, u32[]{:S(2)}) collective-permute-start(bf16[128,1024]{1,0:T(8,128)(2,1)S(1)} %collective-permute-done.3.refs_0_), channel_id=1, source_target_pairs={{0,96},{1,97},{2,98},{3,99},{4,100},{5,101},{6,102},{7,103},{8,104... | collective-permute-start | bytes 786440 | tf_op jit(solution)/shard_map/ppermute | solution.py:26
  25.4 14.3 %collective-permute-start.4 = (bf16[128,1024]{1,0:T(8,128)(2,1)S(1)}, bf16[128,1024]{1,0:T(8,128)(2,1)S(1)}, u32[]{:S(2)}, u32[]{:S(2)}) collective-permute-start(bf16[128,1024]{1,0:T(8,128)(2,1)S(1)} %collective-permute-done.3.refs_0_), channel_id=1, source_target_pairs={{0,64},{1,65},{2,66},{3,67},{4,68},{5,69},{6,70},{7,71},{8,72},{9,... | collective-permute-start | bytes 786440 | tf_op jit(solution)/shard_map/ppermute | solution.py:26
  33.4 27.9 %collective-permute-start.11 = (bf16[4,128,1024]{2,1,0:T(8,128)(2,1)S(1)}, bf16[4,128,1024]{2,1,0:T(8,128)(2,1)S(1)}, u32[]{:S(2)}, u32[]{:S(2)}) collective-permute-start(bf16[4,128,1024]{2,1,0:T(8,128)(2,1)S(1)} %shard_map.29.refs_4_.p0), channel_id=1, source_target_pairs={{0,32},{1,33},{2,34},{3,35},{4,36},{5,37},{6,38},{7,39},{8,40},{9,... | collective-permute-start | bytes 3145736 | tf_op jit(solution)/shard_map/ppermute | solution.py:26
  34.0 27.4 %collective-permute-start.10 = (bf16[4,128,1024]{2,1,0:T(8,128)(2,1)S(1)}, bf16[4,128,1024]{2,1,0:T(8,128)(2,1)S(1)}, u32[]{:S(2)}, u32[]{:S(2)}) collective-permute-start(bf16[4,128,1024]{2,1,0:T(8,128)(2,1)S(1)} %shard_map.29.refs_4_.p0), channel_id=1, source_target_pairs={{0,96},{1,97},{2,98},{3,99},{4,100},{5,101},{6,102},{7,103},{8,104... | collective-permute-start | bytes 3145736 | tf_op jit(solution)/shard_map/ppermute | solution.py:26
  40.4 23.8 %collective-permute-start.13 = (bf16[4,128,1024]{2,1,0:T(8,128)(2,1)S(1)}, bf16[4,128,1024]{2,1,0:T(8,128)(2,1)S(1)}, u32[]{:S(2)}, u32[]{:S(2)}) collective-permute-start(bf16[4,128,1024]{2,1,0:T(8,128)(2,1)S(1)} %shard_map.30.refs_7_.p0), channel_id=1, source_target_pairs={{0,8},{1,9},{2,10},{3,11},{4,12},{5,13},{6,14},{7,15},{8,16},{9,17... | collective-permute-start | bytes 3145736 | tf_op jit(solution)/shard_map/ppermute | solution.py:26
  41.6 22.5 %collective-permute-start.12 = (bf16[4,128,1024]{2,1,0:T(8,128)(2,1)S(1)}, bf16[4,128,1024]{2,1,0:T(8,128)(2,1)S(1)}, u32[]{:S(2)}, u32[]{:S(2)}) collective-permute-start(bf16[4,128,1024]{2,1,0:T(8,128)(2,1)S(1)} %shard_map.30.refs_7_.p0), channel_id=1, source_target_pairs={{0,24},{1,25},{2,26},{3,27},{4,28},{5,29},{6,30},{7,31},{8,0},{9,1... | collective-permute-start | bytes 3145736 | tf_op jit(solution)/shard_map/ppermute | solution.py:26
  43.7 16.9 %collective-permute-start.6 = (bf16[256,1024]{1,0:T(8,128)(2,1)S(1)}, bf16[256,1024]{1,0:T(8,128)(2,1)S(1)}, u32[]{:S(2)}, u32[]{:S(2)}) collective-permute-start(bf16[256,1024]{1,0:T(8,128)(2,1)S(1)} %copy-done.1), channel_id=1, source_target_pairs={{0,6},{1,7},{2,4},{3,5},{4,2},{5,3},{6,0},{7,1},{8,14},{9,15},{10,... | collective-permute-start | bytes 1572872 | tf_op jit(solution)/shard_map/ppermute | solution.py:26
  60.6 10.7 %collective-permute-start.7 = (bf16[256,1024]{1,0:T(8,128)(2,1)S(1)}, bf16[256,1024]{1,0:T(8,128)(2,1)S(1)}, u32[]{:S(2)}, u32[]{:S(2)}) collective-permute-start(bf16[256,1024]{1,0:T(8,128)(2,1)S(1)} %copy-done.1), channel_id=1, source_target_pairs={{0,2},{1,3},{2,0},{3,1},{4,6},{5,7},{6,4},{7,5},{8,10},{9,11},{10,... | collective-permute-start | bytes 1572872 | tf_op jit(solution)/shard_map/ppermute | solution.py:26
  62.0 16.9 %collective-permute-start.14 = (bf16[2,128,1024]{2,1,0:T(8,128)(2,1)S(1)}, bf16[2,128,1024]{2,1,0:T(8,128)(2,1)S(1)}, u32[]{:S(2)}, u32[]{:S(2)}) collective-permute-start(bf16[2,128,1024]{2,1,0:T(8,128)(2,1)S(1)} %get-tuple-element.61), channel_id=1, source_target_pairs={{0,96},{1,97},{2,98},{3,99},{4,100},{5,101},{6,102},{7,103},{8,104... | collective-permute-start | bytes 1572872 | tf_op jit(solution)/shard_map/ppermute | solution.py:26
  63.2 15.8 %collective-permute-start.15 = (bf16[2,128,1024]{2,1,0:T(8,128)(2,1)S(1)}, bf16[2,128,1024]{2,1,0:T(8,128)(2,1)S(1)}, u32[]{:S(2)}, u32[]{:S(2)}) collective-permute-start(bf16[2,128,1024]{2,1,0:T(8,128)(2,1)S(1)} %get-tuple-element.62), channel_id=1, source_target_pairs={{0,32},{1,33},{2,34},{3,35},{4,36},{5,37},{6,38},{7,39},{8,40},{9,... | collective-permute-start | bytes 1572872 | tf_op jit(solution)/shard_map/ppermute | solution.py:26
  64.8 14.1 %collective-permute-start.16 = (bf16[2,128,1024]{2,1,0:T(8,128)(2,1)S(1)}, bf16[2,128,1024]{2,1,0:T(8,128)(2,1)S(1)}, u32[]{:S(2)}, u32[]{:S(2)}) collective-permute-start(bf16[2,128,1024]{2,1,0:T(8,128)(2,1)S(1)} %get-tuple-element.63), channel_id=1, source_target_pairs={{0,24},{1,25},{2,26},{3,27},{4,28},{5,29},{6,30},{7,31},{8,0},{9,1... | collective-permute-start | bytes 1572872 | tf_op jit(solution)/shard_map/ppermute | solution.py:26
  67.2 11.8 %collective-permute-start.17 = (bf16[2,128,1024]{2,1,0:T(8,128)(2,1)S(1)}, bf16[2,128,1024]{2,1,0:T(8,128)(2,1)S(1)}, u32[]{:S(2)}, u32[]{:S(2)}) collective-permute-start(bf16[2,128,1024]{2,1,0:T(8,128)(2,1)S(1)} %get-tuple-element.64), channel_id=1, source_target_pairs={{0,8},{1,9},{2,10},{3,11},{4,12},{5,13},{6,14},{7,15},{8,16},{9,17... | collective-permute-start | bytes 1572872 | tf_op jit(solution)/shard_map/ppermute | solution.py:26
  81.7 4.2 %collective-permute-start.18 = (f32[8,512,128]{2,1,0:T(8,128)S(1)}, f32[8,512,128]{2,1,0:T(8,128)S(1)}, u32[]{:S(2)}, u32[]{:S(2)}) collective-permute-start(f32[8,512,128]{2,1,0:T(8,128)S(1)} %bitcast.13), channel_id=1, source_target_pairs={{0,1},{1,0},{2,3},{3,2},{4,5},{5,4},{6,7},{7,6},{8,9},{9,8},{10,11... | collective-permute-start | bytes 6291464 | tf_op jit(solution)/shard_map/ppermute | solution.py:26
  108.9 20.1 %collective-permute-start.19 = (f32[8,512,128]{2,1,0:T(8,128)S(1)}, f32[8,512,128]{2,1,0:T(8,128)S(1)}, u32[]{:S(2)}, u32[]{:S(2)}) collective-permute-start(f32[8,512,128]{2,1,0:T(8,128)S(1)} %get-tuple-element.70.plan), channel_id=1, source_target_pairs={{0,1},{1,0},{2,3},{3,2},{4,5},{5,4},{6,7},{7,6},{8,9},{9,8},{10,11... | collective-permute-start | bytes 6291464 | tf_op jit(solution)/shard_map/ppermute | solution.py:26
  132.1 13.8 %collective-permute-start.21 = (bf16[144,1024]{1,0:T(8,128)(2,1)S(1)}, bf16[144,1024]{1,0:T(8,128)(2,1)S(1)}, u32[]{:S(2)}, u32[]{:S(2)}) collective-permute-start(bf16[144,1024]{1,0:T(8,128)(2,1)S(1)} %get-tuple-element.78), channel_id=1, source_target_pairs={{0,6},{1,7},{2,4},{3,5},{4,2},{5,3},{6,0},{7,1},{8,14},{9,15},{10,... | collective-permute-start | bytes 884744 | tf_op jit(solution)/shard_map/ppermute | solution.py:26
  133.3 8.9 %collective-permute-start.23 = (bf16[144,1024]{1,0:T(8,128)(2,1)S(1)}, bf16[144,1024]{1,0:T(8,128)(2,1)S(1)}, u32[]{:S(2)}, u32[]{:S(2)}) collective-permute-start(bf16[144,1024]{1,0:T(8,128)(2,1)S(1)} %get-tuple-element.81), channel_id=1, source_target_pairs={{0,4},{1,5},{2,6},{3,7},{4,0},{5,1},{6,2},{7,3},{8,12},{9,13},{10,... | collective-permute-start | bytes 884744 | tf_op jit(solution)/shard_map/ppermute | solution.py:26
  135.4 14.1 %collective-permute-start.25 = (bf16[144,1024]{1,0:T(8,128)(2,1)S(1)}, bf16[144,1024]{1,0:T(8,128)(2,1)S(1)}, u32[]{:S(2)}, u32[]{:S(2)}) collective-permute-start(bf16[144,1024]{1,0:T(8,128)(2,1)S(1)} %get-tuple-element.82), channel_id=1, source_target_pairs={{0,6},{1,7},{2,4},{3,5},{4,2},{5,3},{6,0},{7,1},{8,14},{9,15},{10,... | collective-permute-start | bytes 884744 | tf_op jit(solution)/shard_map/ppermute | solution.py:26
  139.6 10.0 %collective-permute-start.20 = (bf16[144,1024]{1,0:T(8,128)(2,1)S(1)}, bf16[144,1024]{1,0:T(8,128)(2,1)S(1)}, u32[]{:S(2)}, u32[]{:S(2)}) collective-permute-start(bf16[144,1024]{1,0:T(8,128)(2,1)S(1)} %get-tuple-element.75), channel_id=1, source_target_pairs={{0,4},{1,5},{2,6},{3,7},{4,0},{5,1},{6,2},{7,3},{8,12},{9,13},{10,... | collective-permute-start | bytes 884744 | tf_op jit(solution)/shard_map/ppermute | solution.py:26
  142.8 12.2 %collective-permute-start.24 = (bf16[144,1024]{1,0:T(8,128)(2,1)S(1)}, bf16[144,1024]{1,0:T(8,128)(2,1)S(1)}, u32[]{:S(2)}, u32[]{:S(2)}) collective-permute-start(bf16[144,1024]{1,0:T(8,128)(2,1)S(1)} %shard_map.46), channel_id=1, source_target_pairs={{0,6},{1,7},{2,4},{3,5},{4,2},{5,3},{6,0},{7,1},{8,14},{9,15},{10,... | collective-permute-start | bytes 884744 | tf_op jit(solution)/shard_map/ppermute | solution.py:26
  146.5 8.5 %collective-permute-start.22 = (bf16[144,1024]{1,0:T(8,128)(2,1)S(1)}, bf16[144,1024]{1,0:T(8,128)(2,1)S(1)}, u32[]{:S(2)}, u32[]{:S(2)}) collective-permute-start(bf16[144,1024]{1,0:T(8,128)(2,1)S(1)} %shard_map.44), channel_id=1, source_target_pairs={{0,4},{1,5},{2,6},{3,7},{4,0},{5,1},{6,2},{7,3},{8,12},{9,13},{10,... | collective-permute-start | bytes 884744 | tf_op jit(solution)/shard_map/ppermute | solution.py:26

commit v3 on v2

--- a/solution.py
+++ b/solution.py
@@ -133,14 +133,6 @@
 
 def halves_kernel(at, next_, last, low, high, sems):
     for copy in started(sems, (next_.at[:2], low), (last.at[2:], high)):
-        copy.wait()
-
-
-def split_kernel(at, noise, near, far, sems):
-    mid = near.shape[0]
-    spans = [pl.ds(pl.multiple_of(n * mid, mid), mid) for n in (at[3], 1 - at[3])]
-    copies = started(sems, (noise.at[spans[0]], near), (noise.at[spans[1]], far))
-    for copy in copies:
         copy.wait()
 
 
@@ -186,8 +178,8 @@
             out[far_place(at, k, r + 1)] += value[:, 128:]
 
 
-def second_kernel(half, at, x, acc, n_a, n_b, f_a, f_b, out, held, sems):
-    copies = started(sems, *((p, held.at[n]) for n, p in enumerate((n_a, n_b, f_a, f_b))))
+def second_kernel(half, at, x, acc, n_a, n_b, out, held, sems):
+    copies = started(sems, *((p, held.at[n]) for n, p in enumerate((n_a, n_b))))
     for block in range(2):
         for j in range(4):
             out[block, j] = acc[2 * half + block, j]
@@ -203,11 +195,15 @@
             out[block - 2 * half, near_place(at, 2, r)[1]] += value[:, :128]
             out[block - 2 * half, near_place(at, 2, r + 1)[1]] += value[:, 128:]
 
-    for block in range(2):
-        r = lax.rem(2 * at[4] + 2 * half + block - at[0] + 4, 4)
-        j = far_place(at, 2, 0)[1]
-        noise = held[2 + r // 2, lax.rem(r, 2)]
-        out[block, j] += cross(x[1], noise) - half_squares(noise)
+
+def third_kernel(at, x, f_a, f_b, keep, give, held, sems):
+    copies = started(sems, *((p, held.at[n]) for n, p in enumerate((f_a, f_b))))
+    for copy in copies:
+        copy.wait()
+    for block in range(4):
+        r = lax.rem(2 * at[4] + block - at[0] + 4, 4)
+        noise = held[r // 2, lax.rem(r, 2)]
+        (keep, give)[block // 2][block % 2] = cross(x[1], noise) - half_squares(noise)
 
 
 def weights_of(at, weights, place, own_rows):
@@ -254,11 +250,9 @@
     kept, sent = (slice(n * mid, n * mid + mid) for n in (half, 1 - half))
     for first in range(0, p0.shape[-1], STEP):
         value = product(parts, (p0, p1, p3, p2_a, p2_b), first)
-        message[:mid, first : first + STEP] = value[sent].astype(message.dtype)
+        message[:, first : first + STEP] = value[sent].astype(message.dtype)
         values[:, first : first + STEP] = value[kept]
-    message[mid:, :] = jnp.zeros((16, message.shape[1]), message.dtype)
-    message[mid:, :mid] = terms_in_rows(total[:, sent])
-    row_total[...] = jnp.broadcast_to(total[:, kept], row_total.shape)
+    row_total[...] = jnp.broadcast_to(total, row_total.shape)
 
 
 def target_3_kernel(at, weights, p0, p1, p3, p2_a, p2_b, values, row_total):
@@ -268,43 +262,45 @@
     row_total[...] = jnp.broadcast_to(total, row_total.shape)
 
 
-def add_kernel(at, values, row_total, came, out):
+def add_kernel(half, at, values, row_total, came, out):
     mid = values.shape[0]
     out[:mid, :] = (values[...] + came[:mid].astype(jnp.float32)).astype(out.dtype)
     terms = came[mid:, :mid].astype(jnp.float32)
-    total = row_total[:1] + terms[0:1] + terms[1:2] + terms[2:3]
+    total = [row_total[:1, :mid], row_total[:1, mid:]]
+    total[half] = total[half] + terms[0:1] + terms[1:2] + terms[2:3]
     out[mid:, :] = jnp.zeros((16, out.shape[1]), out.dtype)
-    out[mid:, :mid] = terms_in_rows(total)
+    out[mid:, : 2 * mid] = terms_in_rows(jnp.concatenate(total, axis=1))
 
 
 def last_kernel(at, own, own_total, l_low, l_high, lh_low, lh_high, out):
     mid = own.shape[0] // 2
+    terms = [m[mid:, : 2 * mid] for m in (l_high, lh_low)]
+    total = to_rows(jnp.concatenate([terms_in_rows(own_total[:1])] + terms, axis=0))
     for n, messages in enumerate(((l_low, lh_low), (l_high, lh_high))):
         here = slice(n * mid, n * mid + mid)
-        terms = [terms_in_rows(own_total[:1, here])] + [m[mid:, :mid] for m in messages]
-        total = to_rows(jnp.concatenate(terms, axis=0))
         for column in range(0, own.shape[1], 128):
             span = slice(column, column + 128)
             value = own[here, span]
             for m in messages:
                 value = value + m[:mid, span].astype(jnp.float32)
-            out[here, span] = (value / total).astype(out.dtype)
+            out[here, span] = (value / total[here]).astype(out.dtype)
 
 
 TILE = 64
 
 
-def rows_1_kernel(scale, at, keep, got, score, sent, tops, sums):
+def rows_1_kernel(scale, at, keep, got, far_keep, far_got, score, sent, tops, sums):
     blocks = keep.shape[0]
+    late = lax.rem(at[1] + 2, 4)
 
     @pl.loop(0, keep.shape[1] // TILE)
     def _(t):
         here = pl.ds(pl.multiple_of(t * TILE, TILE), TILE)
-        top = None
         for b in range(blocks):
-            value = (keep[b, here] + got[b, here]) * scale
-            score[b, here] = value
-            top = value if top is None else jnp.maximum(top, value)
+            score[b, here] = (keep[b, here] + got[b, here]) * scale
+        for b in range(2):
+            score[4 * b + late, here] += (far_keep[b, here] + far_got[b, here]) * scale
+        top = functools.reduce(jnp.maximum, [score[b, here] for b in range(blocks)])
         top = jnp.broadcast_to(jnp.max(top, axis=1, keepdims=True), top.shape)
         tops[here] = top
         sums[here] = sum(jnp.exp(score[b, here] - top) for b in range(blocks))
@@ -388,21 +384,15 @@
 
     wave = lax.optimization_barrier
     mid = rows // 2
+    near = lax.dynamic_slice_in_dim(noise_rows, h * mid, mid)
+    far = flip(lax.dynamic_slice_in_dim(noise_rows, (1 - h) * mid, mid), "h")
+    near_1, near_3 = from_y(near, 1), from_y(near, 3)
+    far, data_rows = wave((far, data_rows))
+    data_l, data_lh = flip(data_rows, "l"), flip(data_rows, "lh")
+    near_2 = from_y(near_1, 1)
+    near_3, far_1, far_3 = wave((near_3, from_z(far, 1), from_z(far, 3)))
+    far_2, data_l, data_lh, data_rows = wave((from_z(far_1, 1), data_l, data_lh, data_rows))
     sems = pltpu.SemaphoreType.DMA((4,))
-    near, far = call(
-        split_kernel,
-        [bfloat16(mid, part)] * 2,
-        0,
-        *(at, noise_rows),
-        anywhere=1,
-        spaces=pl.ANY,
-        scratch=[sems],
-    )
-    far = flip(far, "h")
-    near_1, near_2, near_3 = (from_y(near, k) for k in (1, 2, 3))
-    near_1, near_2, near_3, far, data_rows = wave((near_1, near_2, near_3, far, data_rows))
-    far_1, far_2, far_3 = (from_z(far, k) for k in (1, 2, 3))
-    data_l = flip(data_rows, "l")
 
     def stacked(*blocks):
         out = [bfloat16(4, *blocks[0].shape)]
@@ -416,15 +406,11 @@
             halves_kernel, out, 0, at, next_, last, anywhere=2, spaces=pl.ANY, scratch=[sems]
         )
 
-    near = stacked(near, near_1, near_2, near_3)
-    near, far_1, far_3 = wave((near, far_1, far_3))
+    near, far = stacked(near, near_1, near_2, near_3), stacked(far, far_1, far_2, far_3)
     near_next, near_last = from_z(near, 1), from_z(near, 3)
-    far_2, data_l, data_rows = wave((far_2, data_l, data_rows))
-    far = stacked(far, far_1, far_2, far_3)
     far_next, far_last = from_y(far, 1), from_y(far, 3)
-    data_lh = flip(data_rows, "lh")
-    data_lh, data_rows = wave((data_lh, data_rows))
     data_h = flip(data_rows, "h")
+    far_next, far_last, data_h = wave((far_next, far_last, data_h))
     nears, fars = (near, near_next, near_last), (far, far_next, far_last)
     low, high = halves(near_next, near_last)
     near_two = from_z(low, 1), from_z(high, 3)
@@ -445,12 +431,20 @@
         call(
             functools.partial(second_kernel, half),
             [float32(2, 4, 2 * rows, 2 * piece)],
-            2 * one,
-            *(at, x_all, scores, *near_two, *far_two),
-            anywhere=4,
-            scratch=[pltpu.VMEM((4, 2, *noise_shape[1:]), jnp.bfloat16), sems],
+            100 * one,
+            *(at, x_all, scores, *near_two),
+            anywhere=2,
+            scratch=[pltpu.VMEM((2, 2, *noise_shape[1:]), jnp.bfloat16), sems],
         )[0]
         for half in (1, 0)
+    )
+    far_keep, far_give = call(
+        third_kernel,
+        [float32(2, 2 * rows, 2 * piece)] * 2,
+        2 * one,
+        *(at, x_all, *far_two),
+        anywhere=2,
+        scratch=[pltpu.VMEM((2, 2, *noise_shape[1:]), jnp.bfloat16), sems],
     )
 
     blocks = (8, 2 * rows, 2 * piece)
@@ -465,7 +459,11 @@
     keep, give = keep.reshape(blocks), give.reshape(blocks)
     kernel = functools.partial(rows_1_kernel, 2.0 / (width * eps))
     score, sent = call(
-        kernel, [float32(*blocks), row_sent], 0, at, keep, flip(give, "c"), scratch=[pltpu.VMEM(tall, jnp.float32)] * 2
+        kernel,
+        [float32(*blocks), row_sent],
+        0,
+        *(at, keep, flip(give, "c"), far_keep, flip(far_give, "c")),
+        scratch=[pltpu.VMEM(tall, jnp.float32)] * 2,
     )
     kernel = functools.partial(columns_1_kernel, log_count)
     row_pot, sent = call(
@@ -501,9 +499,9 @@
     def other_rows(place, half, came, names):
         noise = near_noise if place is near_place else far_noise
         kernel = functools.partial(target_2_kernel, place, half)
-        outs = [message, float32(mid, part), float32(8, mid)]
+        outs = [bfloat16(mid, part), float32(mid, part), float32(8, rows)]
         sent, *kept = call(kernel, outs, 8 * one, at, weights, *noise)
-        added = call(add_kernel, [message], 0, at, *kept, came)[0]
+        added = call(functools.partial(add_kernel, half), [message], 0, at, *kept, came)[0]
         return flip(sent, names), flip(added, names)
 
     lh_high, lh_low = other_rows(far_place, 0, low, "lh")
@@ -511,7 +509,7 @@
     own = call(
         target_3_kernel,
         [float32(rows, part), float32(8, rows)],
-        8 * one,
+        64 * one,
         *(at, weights, *near_noise),
     )
     messages = l_low, l_high, lh_low, lh_high

time: 157 us -> 148 us (0.943)
  waiting for transfers between devices: 47.6 us -> 32.3 us
  starting transfers between devices: 37.2 us -> 41.5 us
  blocking collectives: 37.6 us -> 39.5 us
    ppermute x26 -> x27, waiting for transfers between devices: 47.6 us -> 32.3 us  [move(): return lax.ppermute(value, AXES, pairs)]
    ppermute x26 -> x27, starting transfers between devices: 37.2 us -> 41.5 us  [move(): return lax.ppermute(value, AXES, pairs)]
    all_to_all x4, blocking collectives: 37.6 us -> 39.5 us  [exchange(): return lax.all_to_all(sent, axes, 0, 0, tiled=True)]
  transfers between devices with their start and end apart: 26 -> 27, of which waited for: 13 -> 15; matrix products, arithmetic and copies ran while one was open for 0% -> 0% of each run, Pallas kernels for 13% -> 16%
where the time goes in v3:
time: 148 us; the launch traced here: 147 us
  starting transfers between devices  41.5 us (28%)
  blocking collectives  39.5 us (27%)
  Pallas kernels  32.9 us (22%)
  waiting for transfers between devices  32.3 us (22%)
    ppermute x27, starting transfers between devices, move(): return lax.ppermute(value, AXES, pairs)  41.5 us
    all_to_all x4, blocking collectives, exchange(): return lax.all_to_all(sent, axes, 0, 0, tiled=True)  39.5 us
    pallas_call x20, Pallas kernels, call(): pl.pallas_call(kernel, out_shape=outs, in_specs=[pl.BlockSpec(memory_spac...  32.9 us
    ppermute x27, waiting for transfers between devices, move(): return lax.ppermute(value, AXES, pairs)  32.3 us
  transfers between devices with their start and end apart: 27, of which 15 were waited for; matrix products, arithmetic and copies ran while one was open for 0% of the time, Pallas kernels for 16%

profile of v3, /device:TPU:0, one launch (start us, length us, event | category | flops | bytes accessed | tf_op | source)
XLA Modules:
  0.0 147.4 jit_solution(2938045828994498968)
XLA Ops:
  0.0 1.1 constant_dynamic-slice_fusion
  1.1 3.2 %collective-permute-start.1 = (bf16[128,1024]{1,0:T(8,128)(2,1)S(1)}, bf16[128,1024]{1,0:T(8,128)(2,1)S(1)}, u32[]{:S(2)}, u32[]{:S(2)}) collective-permute-start(bf16[128,1024]{1,0:T(8,128)(2,1)S(1)} %get-tuple-element.81), channel_id=1, source_target_pairs={{0,2},{1,3},{2,0},{3,1},{4,6},{5,7},{6,4},{7,5},{8,10},{9,11},{10,... | collective-permute-start | bytes 786440 | tf_op jit(solution)/shard_map/ppermute | solution.py:26
  4.3 1.6 %collective-permute-start = (bf16[128,1024]{1,0:T(8,128)(2,1)S(1)}, bf16[128,1024]{1,0:T(8,128)(2,1)S(1)}, u32[]{:S(2)}, u32[]{:S(2)}) collective-permute-start(bf16[128,1024]{1,0:T(8,128)(2,1)S(1)} %get-tuple-element.82.refs_0_), channel_id=1, source_target_pairs={{0,8},{1,9},{2,10},{3,11},{4,12},{5,13},{6,14},{7,15},{8,16},{9,17... | collective-permute-start | bytes 786440 | tf_op jit(solution)/shard_map/ppermute | solution.py:26
  5.8 1.7 %collective-permute-start.10 = (bf16[128,1024]{1,0:T(8,128)(2,1)S(1)}, bf16[128,1024]{1,0:T(8,128)(2,1)S(1)}, u32[]{:S(2)}, u32[]{:S(2)}) collective-permute-start(bf16[128,1024]{1,0:T(8,128)(2,1)S(1)} %get-tuple-element.82.refs_0_), channel_id=1, source_target_pairs={{0,24},{1,25},{2,26},{3,27},{4,28},{5,29},{6,30},{7,31},{8,0},{9,1... | collective-permute-start | bytes 786440 | tf_op jit(solution)/shard_map/ppermute | solution.py:26
  7.5 3.1 %collective-permute-done.1.refs_0_ = bf16[128,1024]{1,0:T(8,128)(2,1)S(1)} collective-permute-done((bf16[128,1024]{1,0:T(8,128)(2,1)S(1)}, bf16[128,1024]{1,0:T(8,128)(2,1)S(1)}, u32[]{:S(2)}, u32[]{:S(2)}) %collective-permute-start.1) | collective-permute-done | bytes 262176 | tf_op jit(solution)/shard_map/ppermute | solution.py:26
  10.6 4.3 %collective-permute-start.2 = (bf16[128,1024]{1,0:T(8,128)(2,1)S(1)}, bf16[128,1024]{1,0:T(8,128)(2,1)S(1)}, u32[]{:S(2)}, u32[]{:S(2)}) collective-permute-start(bf16[128,1024]{1,0:T(8,128)(2,1)S(1)} %collective-permute-done.1.refs_0_), channel_id=1, source_target_pairs={{0,96},{1,97},{2,98},{3,99},{4,100},{5,101},{6,102},{7,103},{8,104... | collective-permute-start | bytes 786440 | tf_op jit(solution)/shard_map/ppermute | solution.py:26
  14.8 1.5 %collective-permute-start.5 = (bf16[256,1024]{1,0:T(8,128)(2,1)}, bf16[256,1024]{1,0:T(8,128)(2,1)S(1)}, u32[]{:S(2)}, u32[]{:S(2)}) collective-permute-start(bf16[256,1024]{1,0:T(8,128)(2,1)} %refs_0_), channel_id=1, source_target_pairs={{0,4},{1,5},{2,6},{3,7},{4,0},{5,1},{6,2},{7,3},{8,12},{9,13},{10,... | collective-permute-start | bytes 1572872 | tf_op jit(solution)/shard_map/ppermute | solution.py:26
  16.3 2.1 %collective-permute-start.6 = (bf16[256,1024]{1,0:T(8,128)(2,1)}, bf16[256,1024]{1,0:T(8,128)(2,1)S(1)}, u32[]{:S(2)}, u32[]{:S(2)}) collective-permute-start(bf16[256,1024]{1,0:T(8,128)(2,1)} %refs_0_), channel_id=1, source_target_pairs={{0,6},{1,7},{2,4},{3,5},{4,2},{5,3},{6,0},{7,1},{8,14},{9,15},{10,... | collective-permute-start | bytes 1572872 | tf_op jit(solution)/shard_map/ppermute | solution.py:26
  18.4 3.0 %collective-permute-start.11 = (bf16[128,1024]{1,0:T(8,128)(2,1)S(1)}, bf16[128,1024]{1,0:T(8,128)(2,1)S(1)}, u32[]{:S(2)}, u32[]{:S(2)}) collective-permute-start(bf16[128,1024]{1,0:T(8,128)(2,1)S(1)} %collective-permute-done.10.refs_1_), channel_id=1, source_target_pairs={{0,24},{1,25},{2,26},{3,27},{4,28},{5,29},{6,30},{7,31},{8,0},{9,1... | collective-permute-start | bytes 786440 | tf_op jit(solution)/shard_map/ppermute | solution.py:26
  21.4 1.5 %collective-permute-done.3.refs_3_ = bf16[128,1024]{1,0:T(8,128)(2,1)S(1)} collective-permute-done((bf16[128,1024]{1,0:T(8,128)(2,1)S(1)}, bf16[128,1024]{1,0:T(8,128)(2,1)S(1)}, u32[]{:S(2)}, u32[]{:S(2)}) %collective-permute-start.3) | collective-permute-done | bytes 262176 | tf_op jit(solution)/shard_map/ppermute | solution.py:26
  22.9 1.7 %collective-permute-start.4 = (bf16[128,1024]{1,0:T(8,128)(2,1)S(1)}, bf16[128,1024]{1,0:T(8,128)(2,1)S(1)}, u32[]{:S(2)}, u32[]{:S(2)}) collective-permute-start(bf16[128,1024]{1,0:T(8,128)(2,1)S(1)} %collective-permute-done.2.refs_1_), channel_id=1, source_target_pairs={{0,96},{1,97},{2,98},{3,99},{4,100},{5,101},{6,102},{7,103},{8,104... | collective-permute-start | bytes 786440 | tf_op jit(solution)/shard_map/ppermute | solution.py:26
  24.7 0.1 stack.23.at
  24.8 0.6 collective-permute-done.11.refs_2_
  25.3 0.7 shard_map.29.refs_4_.p0
  26.0 3.3 %collective-permute-start.12 = (bf16[4,128,1024]{2,1,0:T(8,128)(2,1)S(1)}, bf16[4,128,1024]{2,1,0:T(8,128)(2,1)S(1)}, u32[]{:S(2)}, u32[]{:S(2)}) collective-permute-start(bf16[4,128,1024]{2,1,0:T(8,128)(2,1)S(1)} %shard_map.29.refs_4_.p0), channel_id=1, source_target_pairs={{0,96},{1,97},{2,98},{3,99},{4,100},{5,101},{6,102},{7,103},{8,104... | collective-permute-start | bytes 3145736 | tf_op jit(solution)/shard_map/ppermute | solution.py:26
  29.3 2.9 %collective-permute-done.4.refs_2_ = bf16[128,1024]{1,0:T(8,128)(2,1)S(1)} collective-permute-done((bf16[128,1024]{1,0:T(8,128)(2,1)S(1)}, bf16[128,1024]{1,0:T(8,128)(2,1)S(1)}, u32[]{:S(2)}, u32[]{:S(2)}) %collective-permute-start.4) | collective-permute-done | bytes 262176 | tf_op jit(solution)/shard_map/ppermute | solution.py:26
  32.2 0.7 shard_map.28.refs_7_.p0
  32.8 2.9 %collective-permute-start.7 = (bf16[4,128,1024]{2,1,0:T(8,128)(2,1)S(1)}, bf16[4,128,1024]{2,1,0:T(8,128)(2,1)S(1)}, u32[]{:S(2)}, u32[]{:S(2)}) collective-permute-start(bf16[4,128,1024]{2,1,0:T(8,128)(2,1)S(1)} %shard_map.28.refs_7_.p0), channel_id=1, source_target_pairs={{0,24},{1,25},{2,26},{3,27},{4,28},{5,29},{6,30},{7,31},{8,0},{9,1... | collective-permute-start | bytes 3145736 | tf_op jit(solution)/shard_map/ppermute | solution.py:26
  35.8 3.2 %collective-permute-start.9 = (bf16[256,1024]{1,0:T(8,128)(2,1)S(1)}, bf16[256,1024]{1,0:T(8,128)(2,1)S(1)}, u32[]{:S(2)}, u32[]{:S(2)}) collective-permute-start(bf16[256,1024]{1,0:T(8,128)(2,1)S(1)} %copy-done), channel_id=1, source_target_pairs={{0,2},{1,3},{2,0},{3,1},{4,6},{5,7},{6,4},{7,5},{8,10},{9,11},{10,... | collective-permute-start | bytes 1572872 | tf_op jit(solution)/shard_map/ppermute | solution.py:26
  39.0 12.4 %collective-permute-done.12.refs_5_.next_.p1 = bf16[4,128,1024]{2,1,0:T(8,128)(2,1)S(1)} collective-permute-done((bf16[4,128,1024]{2,1,0:T(8,128)(2,1)S(1)}, bf16[4,128,1024]{2,1,0:T(8,128)(2,1)S(1)}, u32[]{:S(2)}, u32[]{:S(2)}) %collective-permute-start.12) | collective-permute-done | bytes 1048608 | tf_op jit(solution)/shard_map/ppermute | solution.py:26
  51.4 0.9 collective-permute-done.13.refs_6_.last.p3
  52.3 0.7 shard_map.31
  52.9 2.5 %collective-permute-start.14 = (bf16[2,128,1024]{2,1,0:T(8,128)(2,1)S(1)}, bf16[2,128,1024]{2,1,0:T(8,128)(2,1)S(1)}, u32[]{:S(2)}, u32[]{:S(2)}) collective-permute-start(bf16[2,128,1024]{2,1,0:T(8,128)(2,1)S(1)} %get-tuple-element.57), channel_id=1, source_target_pairs={{0,96},{1,97},{2,98},{3,99},{4,100},{5,101},{6,102},{7,103},{8,104... | collective-permute-start | bytes 1572872 | tf_op jit(solution)/shard_map/ppermute | solution.py:26
  55.5 1.7 %collective-permute-done.8.refs_9_.last.p3 = bf16[4,128,1024]{2,1,0:T(8,128)(2,1)S(1)} collective-permute-done((bf16[4,128,1024]{2,1,0:T(8,128)(2,1)S(1)}, bf16[4,128,1024]{2,1,0:T(8,128)(2,1)S(1)}, u32[]{:S(2)}, u32[]{:S(2)}) %collective-permute-start.8) | collective-permute-done | bytes 1048608 | tf_op jit(solution)/shard_map/ppermute | solution.py:26
  57.2 0.7 shard_map.34
  57.9 1.6 %collective-permute-start.17 = (bf16[2,128,1024]{2,1,0:T(8,128)(2,1)S(1)}, bf16[2,128,1024]{2,1,0:T(8,128)(2,1)S(1)}, u32[]{:S(2)}, u32[]{:S(2)}) collective-permute-start(bf16[2,128,1024]{2,1,0:T(8,128)(2,1)S(1)} %get-tuple-element.59), channel_id=1, source_target_pairs={{0,24},{1,25},{2,26},{3,27},{4,28},{5,29},{6,30},{7,31},{8,0},{9,1... | collective-permute-start | bytes 1572872 | tf_op jit(solution)/shard_map/ppermute | solution.py:26
  59.5 0.5 collective-permute-start.18
  60.0 7.7 %shard_map.30 = (f32[4,4,512,128]{3,2,1,0:T(8,128)S(1)}, bf16[2,512,1024]{2,1,0:T(8,128)(2,1)S(1)}) custom-call(s32[5]{0:T(128)S(1)} %stack.23.at, bf16[256,1024]{1,0:T(8,128)(2,1)S(1)} %copy-done, bf16[256,1024]{1,0:T(8,128)(2,1)S(1)} %collective-permute-done.5.refs_1_, bf16[256,1024]{1,0:T(8,128)(2,1)S(1)} %collective-permute-done.9.refs_2_, ...), custom_call_target="tpu_custom_call" | custom-call | flops 3221225472 | bytes 14680084 | tf_op jit(solution)/shard_map/pallas_call | solution.py:76
  67.6 0.5 collective-permute-done.15.n_b.p2_b
  68.1 1.8 %shard_map.33 = f32[2,4,512,128]{3,2,1,0:T(8,128)S(1)} custom-call(s32[5]{0:T(128)S(1)} %stack.23.at, bf16[2,512,1024]{2,1,0:T(8,128)(2,1)S(1)} %get-tuple-element.55.x, f32[4,4,512,128]{3,2,1,0:T(8,128)S(1)} %get-tuple-element.56.acc, bf16[2,128,1024]{2,1,0:T(8,128)(2,1)S(1)} %collective-permute-done.14.n_a.p2_a, ...), custom_call_target="tpu_custom_call" | custom-call | flops 26843545600 | bytes 9437204 | tf_op jit(solution)/shard_map/pallas_call | solution.py:76
  69.9 0.1 collective-permute-start.16
  70.0 2.2 %shard_map.35 = (f32[2,512,128]{2,1,0:T(8,128)S(1)}, f32[2,512,128]{2,1,0:T(8,128)S(1)}) custom-call(s32[5]{0:T(128)S(1)} %stack.23.at, bf16[2,512,1024]{2,1,0:T(8,128)(2,1)S(1)} %get-tuple-element.55.x, bf16[2,128,1024]{2,1,0:T(8,128)(2,1)S(1)} %collective-permute-done.17.f_a.p2_a, bf16[2,128,1024]{2,1,0:T(8,128)(2,1)S(1)} %collective-permute-done.18.f_b.p2_b), custom_call_target="tpu_custom_call" | custom-call | flops 536870912 | bytes 4194324 | tf_op jit(solution)/shard_map/pallas_call | solution.py:76
  72.2 0.6 collective-permute-start.19
  72.7 0.8 shard_map.32
  73.5 1.3 collective-permute-done.19.far_got
  74.9 2.2 %shard_map.36 = (f32[8,512,128]{2,1,0:T(8,128)S(1)}, f32[8,1,512]{2,1,0:T(1,128)S(1)}) custom-call(s32[5]{0:T(128)S(1)} %stack.23.at, f32[8,512,128]{2,1,0:T(8,128)S(1)} %bitcast.12, f32[8,512,128]{2,1,0:T(8,128)S(1)} %collective-permute-done.16.got, f32[2,512,128]{2,1,0:T(8,128)S(1)} %get-tuple-element.61.far_keep, ...), custom_call_target="tpu_custom_call" | custom-call | bytes 7356436 | tf_op jit(solution)/shard_map/pallas_call | solution.py:76
  77.1 8.6 %all_to_all.20.came = f32[8,1,512]{2,1,0:T(1,128)S(1)} all-to-all(f32[8,1,512]{2,1,0:T(1,128)S(1)} %get-tuple-element.63), channel_id=1, replica_groups=mesh['z'=4,'y'=4,'l'=2,'h'=2,'c'=2] {'l','h','c'}, dimensions={0} | all-to-all | bytes 32768 | tf_op jit(solution)/shard_map/all_to_all | solution.py:457
  85.7 1.3 shard_map.37
  87.0 11.9 %all_to_all.21.came = f32[16,8,128]{2,1,0:T(8,128)S(1)} all-to-all(f32[16,8,128]{2,1,0:T(8,128)S(1)} %get-tuple-element.65), channel_id=1, replica_groups=mesh['z'=4,'y'=4,'l'=2,'h'=2,'c'=2] {'z','y'}, dimensions={0} | all-to-all | bytes 131072 | tf_op jit(solution)/shard_map/all_to_all | solution.py:457
  98.9 1.3 shard_map.38
  100.2 0.0 collective-permute-start.20
  100.2 7.7 %all_to_all.22.came = f32[8,1,512]{2,1,0:T(1,128)S(1)} all-to-all(f32[8,1,512]{2,1,0:T(1,128)S(1)} %get-tuple-element.67), channel_id=1, replica_groups=mesh['z'=4,'y'=4,'l'=2,'h'=2,'c'=2] {'l','h','c'}, dimensions={0} | all-to-all | bytes 32768 | tf_op jit(solution)/shard_map/all_to_all | solution.py:457
  107.9 0.9 shard_map.39
  108.8 11.2 %all_to_all.23.came = f32[32,8,128]{2,1,0:T(8,128)S(1)} all-to-all(f32[32,8,128]{2,1,0:T(8,128)S(1)} %get-tuple-element.69), channel_id=1, replica_groups=mesh['z'=4,'y'=4,'l'=2,'h'=2,'c'=2] {'z','y','c'}, dimensions={0} | all-to-all | bytes 262144 | tf_op jit(solution)/shard_map/all_to_all | solution.py:457
  120.1 1.0 shard_map.40
  121.1 2.1 %shard_map.43 = (bf16[144,1024]{1,0:T(8,128)(2,1)S(1)}, bf16[144,1024]{1,0:T(8,128)(2,1)S(1)}) custom-call(s32[5]{0:T(128)S(1)} %stack.23.at, bf16[4,4,512,128]{3,2,1,0:T(8,128)(2,1)S(1)} %bitcast.8, bf16[4,128,1024]{2,1,0:T(8,128)(2,1)S(1)} %shard_map.28.refs_7_.p0, bf16[4,128,1024]{2,1,0:T(8,128)(2,1)S(1)} %collective-permute-done.7.refs_8_.next_.p1, ...), custom_call_target="tpu_custom_call" | custom-call | flops 2147483648 | bytes 6881300 | tf_op jit(solution)/shard_map/pallas_call | solution.py:76
  123.2 1.2 collective-permute-start.22
  124.4 0.0 collective-permute-start.24
  124.4 2.1 %shard_map.42 = (bf16[128,1024]{1,0:T(8,128)(2,1)S(1)}, f32[128,1024]{1,0:T(8,128)S(1)}, f32[8,256]{1,0:T(8,128)S(1)}) custom-call(s32[5]{0:T(128)S(1)} %stack.23.at, bf16[4,4,512,128]{3,2,1,0:T(8,128)(2,1)S(1)} %bitcast.9, bf16[4,128,1024]{2,1,0:T(8,128)(2,1)S(1)} %shard_map.29.refs_4_.p0, ...), custom_call_target="tpu_custom_call" | custom-call | flops 2147483648 | bytes 7086100 | tf_op jit(solution)/shard_map/pallas_call | solution.py:76
  126.5 2.1 %collective-permute-start.21 = (bf16[128,1024]{1,0:T(8,128)(2,1)S(1)}, bf16[128,1024]{1,0:T(8,128)(2,1)S(1)}, u32[]{:S(2)}, u32[]{:S(2)}) collective-permute-start(bf16[128,1024]{1,0:T(8,128)(2,1)S(1)} %get-tuple-element.73), channel_id=1, source_target_pairs={{0,4},{1,5},{2,6},{3,7},{4,0},{5,1},{6,2},{7,3},{8,12},{9,13},{10,... | collective-permute-start | bytes 786440 | tf_op jit(solution)/shard_map/ppermute | solution.py:26
  128.6 2.1 %shard_map.45 = (bf16[128,1024]{1,0:T(8,128)(2,1)S(1)}, f32[128,1024]{1,0:T(8,128)S(1)}, f32[8,256]{1,0:T(8,128)S(1)}) custom-call(s32[5]{0:T(128)S(1)} %stack.23.at, bf16[4,4,512,128]{3,2,1,0:T(8,128)(2,1)S(1)} %bitcast.10, bf16[4,128,1024]{2,1,0:T(8,128)(2,1)S(1)} %shard_map.28.refs_7_.p0, ...), custom_call_target="tpu_custom_call" | custom-call | flops 2147483648 | bytes 7086100 | tf_op jit(solution)/shard_map/pallas_call | solution.py:76
  130.7 2.1 %collective-permute-start.26 = (bf16[128,1024]{1,0:T(8,128)(2,1)S(1)}, bf16[128,1024]{1,0:T(8,128)(2,1)S(1)}, u32[]{:S(2)}, u32[]{:S(2)}) collective-permute-start(bf16[128,1024]{1,0:T(8,128)(2,1)S(1)} %get-tuple-element.80), channel_id=1, source_target_pairs={{0,6},{1,7},{2,4},{3,5},{4,2},{5,3},{6,0},{7,1},{8,14},{9,15},{10,... | collective-permute-start | bytes 786440 | tf_op jit(solution)/shard_map/ppermute | solution.py:26
  132.8 0.7 collective-permute-done.22.came
  133.5 0.6 shard_map.44
  134.1 0.1 collective-permute-start.23
  134.2 0.1 collective-permute-done.24.came
  134.3 0.6 shard_map.46
  134.9 2.1 %collective-permute-start.25 = (bf16[144,1024]{1,0:T(8,128)(2,1)S(1)}, bf16[144,1024]{1,0:T(8,128)(2,1)S(1)}, u32[]{:S(2)}, u32[]{:S(2)}) collective-permute-start(bf16[144,1024]{1,0:T(8,128)(2,1)S(1)} %shard_map.46), channel_id=1, source_target_pairs={{0,6},{1,7},{2,4},{3,5},{4,2},{5,3},{6,0},{7,1},{8,14},{9,15},{10,... | collective-permute-start | bytes 884744 | tf_op jit(solution)/shard_map/ppermute | solution.py:26
  137.1 2.1 %shard_map.41 = (f32[256,1024]{1,0:T(8,128)S(1)}, f32[8,256]{1,0:T(8,128)S(1)}) custom-call(s32[5]{0:T(128)S(1)} %stack.23.at, bf16[4,4,512,128]{3,2,1,0:T(8,128)(2,1)S(1)} %bitcast.11, bf16[4,128,1024]{2,1,0:T(8,128)(2,1)S(1)} %shard_map.29.refs_4_.p0, bf16[4,128,1024]{2,1,0:T(8,128)(2,1)S(1)} %collective-permute-done.12.refs_5_.next_.p1, ...), custom_call_target="tpu_custom_call" | custom-call | flops 17179869184 | bytes 7348244 | tf_op jit(solution)/shard_map/pallas_call | solution.py:76
  139.1 0.8 collective-permute-done.21.l_low
  139.9 0.9 collective-permute-done.26.lh_high
  140.8 4.2 %collective-permute-done.23.l_high = bf16[144,1024]{1,0:T(8,128)(2,1)S(1)} collective-permute-done((bf16[144,1024]{1,0:T(8,128)(2,1)S(1)}, bf16[144,1024]{1,0:T(8,128)(2,1)S(1)}, u32[]{:S(2)}, u32[]{:S(2)}) %collective-permute-start.23) | collective-permute-done | bytes 294944 | tf_op jit(solution)/shard_map/ppermute | solution.py:26
  145.1 0.7 collective-permute-done.25.lh_low
  145.8 1.7 %shard_map.47 = bf16[256,1024]{1,0:T(8,128)(2,1)} custom-call(s32[5]{0:T(128)S(1)} %stack.23.at, f32[256,1024]{1,0:T(8,128)S(1)} %get-tuple-element.71.own, f32[8,256]{1,0:T(8,128)S(1)} %get-tuple-element.72.own_total, bf16[128,1024]{1,0:T(8,128)(2,1)S(1)} %collective-permute-done.21.l_low, bf16[144,1024]{1,0:T(8,128)(2,1)S(1)} %collective-permute-done.23.l_high, ...), custom_call_target="tpu_custom_call" | custom-call | bytes 2695188 | tf_op jit(solution)/shard_map/pallas_call | solution.py:76
  (18 shorter events, 0.0 us)
Async XLA Ops:
  1.1 9.5 %collective-permute-start.1 = (bf16[128,1024]{1,0:T(8,128)(2,1)S(1)}, bf16[128,1024]{1,0:T(8,128)(2,1)S(1)}, u32[]{:S(2)}, u32[]{:S(2)}) collective-permute-start(bf16[128,1024]{1,0:T(8,128)(2,1)S(1)} %get-tuple-element.81), channel_id=1, source_target_pairs={{0,2},{1,3},{2,0},{3,1},{4,6},{5,7},{6,4},{7,5},{8,10},{9,11},{10,... | collective-permute-start | bytes 786440 | tf_op jit(solution)/shard_map/ppermute | solution.py:26
  4.3 12.1 %collective-permute-start = (bf16[128,1024]{1,0:T(8,128)(2,1)S(1)}, bf16[128,1024]{1,0:T(8,128)(2,1)S(1)}, u32[]{:S(2)}, u32[]{:S(2)}) collective-permute-start(bf16[128,1024]{1,0:T(8,128)(2,1)S(1)} %get-tuple-element.82.refs_0_), channel_id=1, source_target_pairs={{0,8},{1,9},{2,10},{3,11},{4,12},{5,13},{6,14},{7,15},{8,16},{9,17... | collective-permute-start | bytes 786440 | tf_op jit(solution)/shard_map/ppermute | solution.py:26
  5.8 12.6 %collective-permute-start.10 = (bf16[128,1024]{1,0:T(8,128)(2,1)S(1)}, bf16[128,1024]{1,0:T(8,128)(2,1)S(1)}, u32[]{:S(2)}, u32[]{:S(2)}) collective-permute-start(bf16[128,1024]{1,0:T(8,128)(2,1)S(1)} %get-tuple-element.82.refs_0_), channel_id=1, source_target_pairs={{0,24},{1,25},{2,26},{3,27},{4,28},{5,29},{6,30},{7,31},{8,0},{9,1... | collective-permute-start | bytes 786440 | tf_op jit(solution)/shard_map/ppermute | solution.py:26
  10.6 10.9 %collective-permute-start.2 = (bf16[128,1024]{1,0:T(8,128)(2,1)S(1)}, bf16[128,1024]{1,0:T(8,128)(2,1)S(1)}, u32[]{:S(2)}, u32[]{:S(2)}) collective-permute-start(bf16[128,1024]{1,0:T(8,128)(2,1)S(1)} %collective-permute-done.1.refs_0_), channel_id=1, source_target_pairs={{0,96},{1,97},{2,98},{3,99},{4,100},{5,101},{6,102},{7,103},{8,104... | collective-permute-start | bytes 786440 | tf_op jit(solution)/shard_map/ppermute | solution.py:26
  14.8 8.1 %collective-permute-start.3 = (bf16[128,1024]{1,0:T(8,128)(2,1)S(1)}, bf16[128,1024]{1,0:T(8,128)(2,1)S(1)}, u32[]{:S(2)}, u32[]{:S(2)}) collective-permute-start(bf16[128,1024]{1,0:T(8,128)(2,1)S(1)} %collective-permute-done.1.refs_0_), channel_id=1, source_target_pairs={{0,32},{1,33},{2,34},{3,35},{4,36},{5,37},{6,38},{7,39},{8,40},{9,... | collective-permute-start | bytes 786440 | tf_op jit(solution)/shard_map/ppermute | solution.py:26
  14.8 17.3 %collective-permute-start.5 = (bf16[256,1024]{1,0:T(8,128)(2,1)}, bf16[256,1024]{1,0:T(8,128)(2,1)S(1)}, u32[]{:S(2)}, u32[]{:S(2)}) collective-permute-start(bf16[256,1024]{1,0:T(8,128)(2,1)} %refs_0_), channel_id=1, source_target_pairs={{0,4},{1,5},{2,6},{3,7},{4,0},{5,1},{6,2},{7,3},{8,12},{9,13},{10,... | collective-permute-start | bytes 1572872 | tf_op jit(solution)/shard_map/ppermute | solution.py:26
  16.3 15.9 %collective-permute-start.6 = (bf16[256,1024]{1,0:T(8,128)(2,1)}, bf16[256,1024]{1,0:T(8,128)(2,1)S(1)}, u32[]{:S(2)}, u32[]{:S(2)}) collective-permute-start(bf16[256,1024]{1,0:T(8,128)(2,1)} %refs_0_), channel_id=1, source_target_pairs={{0,6},{1,7},{2,4},{3,5},{4,2},{5,3},{6,0},{7,1},{8,14},{9,15},{10,... | collective-permute-start | bytes 1572872 | tf_op jit(solution)/shard_map/ppermute | solution.py:26
  18.4 6.9 %collective-permute-start.11 = (bf16[128,1024]{1,0:T(8,128)(2,1)S(1)}, bf16[128,1024]{1,0:T(8,128)(2,1)S(1)}, u32[]{:S(2)}, u32[]{:S(2)}) collective-permute-start(bf16[128,1024]{1,0:T(8,128)(2,1)S(1)} %collective-permute-done.10.refs_1_), channel_id=1, source_target_pairs={{0,24},{1,25},{2,26},{3,27},{4,28},{5,29},{6,30},{7,31},{8,0},{9,1... | collective-permute-start | bytes 786440 | tf_op jit(solution)/shard_map/ppermute | solution.py:26
  22.9 9.2 %collective-permute-start.4 = (bf16[128,1024]{1,0:T(8,128)(2,1)S(1)}, bf16[128,1024]{1,0:T(8,128)(2,1)S(1)}, u32[]{:S(2)}, u32[]{:S(2)}) collective-permute-start(bf16[128,1024]{1,0:T(8,128)(2,1)S(1)} %collective-permute-done.2.refs_1_), channel_id=1, source_target_pairs={{0,96},{1,97},{2,98},{3,99},{4,100},{5,101},{6,102},{7,103},{8,104... | collective-permute-start | bytes 786440 | tf_op jit(solution)/shard_map/ppermute | solution.py:26
  24.8 11.0 %copy-start = (bf16[256,1024]{1,0:T(8,128)(2,1)S(1)}, bf16[256,1024]{1,0:T(8,128)(2,1)}, u32[]{:S(2)}) copy-start(bf16[256,1024]{1,0:T(8,128)(2,1)} %refs_0_) | copy-start | bytes 1572868
  26.0 25.4 %collective-permute-start.12 = (bf16[4,128,1024]{2,1,0:T(8,128)(2,1)S(1)}, bf16[4,128,1024]{2,1,0:T(8,128)(2,1)S(1)}, u32[]{:S(2)}, u32[]{:S(2)}) collective-permute-start(bf16[4,128,1024]{2,1,0:T(8,128)(2,1)S(1)} %shard_map.29.refs_4_.p0), channel_id=1, source_target_pairs={{0,96},{1,97},{2,98},{3,99},{4,100},{5,101},{6,102},{7,103},{8,104... | collective-permute-start | bytes 3145736 | tf_op jit(solution)/shard_map/ppermute | solution.py:26
  29.3 23.0 %collective-permute-start.13 = (bf16[4,128,1024]{2,1,0:T(8,128)(2,1)S(1)}, bf16[4,128,1024]{2,1,0:T(8,128)(2,1)S(1)}, u32[]{:S(2)}, u32[]{:S(2)}) collective-permute-start(bf16[4,128,1024]{2,1,0:T(8,128)(2,1)S(1)} %shard_map.29.refs_4_.p0), channel_id=1, source_target_pairs={{0,32},{1,33},{2,34},{3,35},{4,36},{5,37},{6,38},{7,39},{8,40},{9,... | collective-permute-start | bytes 3145736 | tf_op jit(solution)/shard_map/ppermute | solution.py:26
  32.8 22.6 %collective-permute-start.7 = (bf16[4,128,1024]{2,1,0:T(8,128)(2,1)S(1)}, bf16[4,128,1024]{2,1,0:T(8,128)(2,1)S(1)}, u32[]{:S(2)}, u32[]{:S(2)}) collective-permute-start(bf16[4,128,1024]{2,1,0:T(8,128)(2,1)S(1)} %shard_map.28.refs_7_.p0), channel_id=1, source_target_pairs={{0,24},{1,25},{2,26},{3,27},{4,28},{5,29},{6,30},{7,31},{8,0},{9,1... | collective-permute-start | bytes 3145736 | tf_op jit(solution)/shard_map/ppermute | solution.py:26
  35.8 21.4 %collective-permute-start.8 = (bf16[4,128,1024]{2,1,0:T(8,128)(2,1)S(1)}, bf16[4,128,1024]{2,1,0:T(8,128)(2,1)S(1)}, u32[]{:S(2)}, u32[]{:S(2)}) collective-permute-start(bf16[4,128,1024]{2,1,0:T(8,128)(2,1)S(1)} %shard_map.28.refs_7_.p0), channel_id=1, source_target_pairs={{0,8},{1,9},{2,10},{3,11},{4,12},{5,13},{6,14},{7,15},{8,16},{9,17... | collective-permute-start | bytes 3145736 | tf_op jit(solution)/shard_map/ppermute | solution.py:26
  35.8 19.7 %collective-permute-start.9 = (bf16[256,1024]{1,0:T(8,128)(2,1)S(1)}, bf16[256,1024]{1,0:T(8,128)(2,1)S(1)}, u32[]{:S(2)}, u32[]{:S(2)}) collective-permute-start(bf16[256,1024]{1,0:T(8,128)(2,1)S(1)} %copy-done), channel_id=1, source_target_pairs={{0,2},{1,3},{2,0},{3,1},{4,6},{5,7},{6,4},{7,5},{8,10},{9,11},{10,... | collective-permute-start | bytes 1572872 | tf_op jit(solution)/shard_map/ppermute | solution.py:26
  52.9 14.7 %collective-permute-start.14 = (bf16[2,128,1024]{2,1,0:T(8,128)(2,1)S(1)}, bf16[2,128,1024]{2,1,0:T(8,128)(2,1)S(1)}, u32[]{:S(2)}, u32[]{:S(2)}) collective-permute-start(bf16[2,128,1024]{2,1,0:T(8,128)(2,1)S(1)} %get-tuple-element.57), channel_id=1, source_target_pairs={{0,96},{1,97},{2,98},{3,99},{4,100},{5,101},{6,102},{7,103},{8,104... | collective-permute-start | bytes 1572872 | tf_op jit(solution)/shard_map/ppermute | solution.py:26
  55.5 12.6 %collective-permute-start.15 = (bf16[2,128,1024]{2,1,0:T(8,128)(2,1)S(1)}, bf16[2,128,1024]{2,1,0:T(8,128)(2,1)S(1)}, u32[]{:S(2)}, u32[]{:S(2)}) collective-permute-start(bf16[2,128,1024]{2,1,0:T(8,128)(2,1)S(1)} %get-tuple-element.58), channel_id=1, source_target_pairs={{0,32},{1,33},{2,34},{3,35},{4,36},{5,37},{6,38},{7,39},{8,40},{9,... | collective-permute-start | bytes 1572872 | tf_op jit(solution)/shard_map/ppermute | solution.py:26
  57.9 12.1 %collective-permute-start.17 = (bf16[2,128,1024]{2,1,0:T(8,128)(2,1)S(1)}, bf16[2,128,1024]{2,1,0:T(8,128)(2,1)S(1)}, u32[]{:S(2)}, u32[]{:S(2)}) collective-permute-start(bf16[2,128,1024]{2,1,0:T(8,128)(2,1)S(1)} %get-tuple-element.59), channel_id=1, source_target_pairs={{0,24},{1,25},{2,26},{3,27},{4,28},{5,29},{6,30},{7,31},{8,0},{9,1... | collective-permute-start | bytes 1572872 | tf_op jit(solution)/shard_map/ppermute | solution.py:26
  59.5 10.5 %collective-permute-start.18 = (bf16[2,128,1024]{2,1,0:T(8,128)(2,1)S(1)}, bf16[2,128,1024]{2,1,0:T(8,128)(2,1)S(1)}, u32[]{:S(2)}, u32[]{:S(2)}) collective-permute-start(bf16[2,128,1024]{2,1,0:T(8,128)(2,1)S(1)} %get-tuple-element.60), channel_id=1, source_target_pairs={{0,8},{1,9},{2,10},{3,11},{4,12},{5,13},{6,14},{7,15},{8,16},{9,17... | collective-permute-start | bytes 1572872 | tf_op jit(solution)/shard_map/ppermute | solution.py:26
  69.9 5.0 %collective-permute-start.16 = (f32[8,512,128]{2,1,0:T(8,128)S(1)}, f32[8,512,128]{2,1,0:T(8,128)S(1)}, u32[]{:S(2)}, u32[]{:S(2)}) collective-permute-start(f32[8,512,128]{2,1,0:T(8,128)S(1)} %bitcast.13), channel_id=1, source_target_pairs={{0,1},{1,0},{2,3},{3,2},{4,5},{5,4},{6,7},{7,6},{8,9},{9,8},{10,11... | collective-permute-start | bytes 6291464 | tf_op jit(solution)/shard_map/ppermute | solution.py:26
  72.2 2.7 %collective-permute-start.19 = (f32[2,512,128]{2,1,0:T(8,128)S(1)}, f32[2,512,128]{2,1,0:T(8,128)S(1)}, u32[]{:S(2)}, u32[]{:S(2)}) collective-permute-start(f32[2,512,128]{2,1,0:T(8,128)S(1)} %get-tuple-element.62), channel_id=1, source_target_pairs={{0,1},{1,0},{2,3},{3,2},{4,5},{5,4},{6,7},{7,6},{8,9},{9,8},{10,11... | collective-permute-start | bytes 1572872 | tf_op jit(solution)/shard_map/ppermute | solution.py:26
  100.2 19.9 %collective-permute-start.20 = (f32[8,512,128]{2,1,0:T(8,128)S(1)}, f32[8,512,128]{2,1,0:T(8,128)S(1)}, u32[]{:S(2)}, u32[]{:S(2)}) collective-permute-start(f32[8,512,128]{2,1,0:T(8,128)S(1)} %get-tuple-element.68.plan), channel_id=1, source_target_pairs={{0,1},{1,0},{2,3},{3,2},{4,5},{5,4},{6,7},{7,6},{8,9},{9,8},{10,11... | collective-permute-start | bytes 6291464 | tf_op jit(solution)/shard_map/ppermute | solution.py:26
  123.2 10.3 %collective-permute-start.22 = (bf16[144,1024]{1,0:T(8,128)(2,1)S(1)}, bf16[144,1024]{1,0:T(8,128)(2,1)S(1)}, u32[]{:S(2)}, u32[]{:S(2)}) collective-permute-start(bf16[144,1024]{1,0:T(8,128)(2,1)S(1)} %get-tuple-element.76), channel_id=1, source_target_pairs={{0,6},{1,7},{2,4},{3,5},{4,2},{5,3},{6,0},{7,1},{8,14},{9,15},{10,... | collective-permute-start | bytes 884744 | tf_op jit(solution)/shard_map/ppermute | solution.py:26
  124.4 9.9 %collective-permute-start.24 = (bf16[144,1024]{1,0:T(8,128)(2,1)S(1)}, bf16[144,1024]{1,0:T(8,128)(2,1)S(1)}, u32[]{:S(2)}, u32[]{:S(2)}) collective-permute-start(bf16[144,1024]{1,0:T(8,128)(2,1)S(1)} %get-tuple-element.79), channel_id=1, source_target_pairs={{0,4},{1,5},{2,6},{3,7},{4,0},{5,1},{6,2},{7,3},{8,12},{9,13},{10,... | collective-permute-start | bytes 884744 | tf_op jit(solution)/shard_map/ppermute | solution.py:26
  126.5 13.4 %collective-permute-start.21 = (bf16[128,1024]{1,0:T(8,128)(2,1)S(1)}, bf16[128,1024]{1,0:T(8,128)(2,1)S(1)}, u32[]{:S(2)}, u32[]{:S(2)}) collective-permute-start(bf16[128,1024]{1,0:T(8,128)(2,1)S(1)} %get-tuple-element.73), channel_id=1, source_target_pairs={{0,4},{1,5},{2,6},{3,7},{4,0},{5,1},{6,2},{7,3},{8,12},{9,13},{10,... | collective-permute-start | bytes 786440 | tf_op jit(solution)/shard_map/ppermute | solution.py:26
  130.7 10.2 %collective-permute-start.26 = (bf16[128,1024]{1,0:T(8,128)(2,1)S(1)}, bf16[128,1024]{1,0:T(8,128)(2,1)S(1)}, u32[]{:S(2)}, u32[]{:S(2)}) collective-permute-start(bf16[128,1024]{1,0:T(8,128)(2,1)S(1)} %get-tuple-element.80), channel_id=1, source_target_pairs={{0,6},{1,7},{2,4},{3,5},{4,2},{5,3},{6,0},{7,1},{8,14},{9,15},{10,... | collective-permute-start | bytes 786440 | tf_op jit(solution)/shard_map/ppermute | solution.py:26
  134.1 11.0 %collective-permute-start.23 = (bf16[144,1024]{1,0:T(8,128)(2,1)S(1)}, bf16[144,1024]{1,0:T(8,128)(2,1)S(1)}, u32[]{:S(2)}, u32[]{:S(2)}) collective-permute-start(bf16[144,1024]{1,0:T(8,128)(2,1)S(1)} %shard_map.44), channel_id=1, source_target_pairs={{0,4},{1,5},{2,6},{3,7},{4,0},{5,1},{6,2},{7,3},{8,12},{9,13},{10,... | collective-permute-start | bytes 884744 | tf_op jit(solution)/shard_map/ppermute | solution.py:26
  134.9 10.8 %collective-permute-start.25 = (bf16[144,1024]{1,0:T(8,128)(2,1)S(1)}, bf16[144,1024]{1,0:T(8,128)(2,1)S(1)}, u32[]{:S(2)}, u32[]{:S(2)}) collective-permute-start(bf16[144,1024]{1,0:T(8,128)(2,1)S(1)} %shard_map.46), channel_id=1, source_target_pairs={{0,6},{1,7},{2,4},{3,5},{4,2},{5,3},{6,0},{7,1},{8,14},{9,15},{10,... | collective-permute-start | bytes 884744 | tf_op jit(solution)/shard_map/ppermute | solution.py:26

commit v4 on v3

--- a/solution.py
+++ b/solution.py
@@ -388,10 +388,11 @@
     far = flip(lax.dynamic_slice_in_dim(noise_rows, (1 - h) * mid, mid), "h")
     near_1, near_3 = from_y(near, 1), from_y(near, 3)
     far, data_rows = wave((far, data_rows))
-    data_l, data_lh = flip(data_rows, "l"), flip(data_rows, "lh")
+    data_l = flip(data_rows, "l")
     near_2 = from_y(near_1, 1)
-    near_3, far_1, far_3 = wave((near_3, from_z(far, 1), from_z(far, 3)))
-    far_2, data_l, data_lh, data_rows = wave((from_z(far_1, 1), data_l, data_lh, data_rows))
+    near_3, far_1, far_3, data_rows = wave((near_3, from_z(far, 1), from_z(far, 3), data_rows))
+    data_lh = flip(data_rows, "lh")
+    far_2, data_l, data_rows = wave((from_z(far_1, 1), data_l, data_rows))
     sems = pltpu.SemaphoreType.DMA((4,))
 
     def stacked(*blocks):
@@ -409,6 +410,7 @@
     near, far = stacked(near, near_1, near_2, near_3), stacked(far, far_1, far_2, far_3)
     near_next, near_last = from_z(near, 1), from_z(near, 3)
     far_next, far_last = from_y(far, 1), from_y(far, 3)
+    data_lh, data_rows = wave((data_lh, data_rows))
     data_h = flip(data_rows, "h")
     far_next, far_last, data_h = wave((far_next, far_last, data_h))
     nears, fars = (near, near_next, near_last), (far, far_next, far_last)

time: 148 us -> 148 us (level)
  starting transfers between devices: 41.5 us -> 37.9 us
  waiting for transfers between devices: 32.3 us -> 35.3 us
    ppermute x27, starting transfers between devices: 41.5 us -> 37.9 us  [move(): return lax.ppermute(value, AXES, pairs)]
    ppermute x27, waiting for transfers between devices: 32.3 us -> 35.3 us  [move(): return lax.ppermute(value, AXES, pairs)]
  transfers between devices with their start and end apart: 27 -> 27, of which waited for: 15 -> 16; matrix products, arithmetic and copies ran while one was open for 0% -> 0% of each run, Pallas kernels for 16% -> 16%
where the time goes in v4:
time: 148 us
  blocking collectives  40.7 us (28%)
  starting transfers between devices  37.9 us (26%)
  waiting for transfers between devices  35.3 us (24%)
  Pallas kernels  32.9 us (22%)
    all_to_all x4, blocking collectives, exchange(): return lax.all_to_all(sent, axes, 0, 0, tiled=True)  40.7 us
    ppermute x27, starting transfers between devices, move(): return lax.ppermute(value, AXES, pairs)  37.9 us
    ppermute x27, waiting for transfers between devices, move(): return lax.ppermute(value, AXES, pairs)  35.3 us
    pallas_call x20, Pallas kernels, call(): pl.pallas_call(kernel, out_shape=outs, in_specs=[pl.BlockSpec(memory_spac...  32.9 us
  transfers between devices with their start and end apart: 27, of which 16 were waited for; matrix products, arithmetic and copies ran while one was open for 0% of the time, Pallas kernels for 16%

profile of v4, /device:TPU:0, one launch (start us, length us, event | category | flops | bytes accessed | tf_op | source)
XLA Modules:
  0.0 148.2 jit_solution(2281796196592858071)
XLA Ops:
  0.0 1.1 constant_dynamic-slice_fusion
  1.1 3.2 %collective-permute-start.1 = (bf16[128,1024]{1,0:T(8,128)(2,1)S(1)}, bf16[128,1024]{1,0:T(8,128)(2,1)S(1)}, u32[]{:S(2)}, u32[]{:S(2)}) collective-permute-start(bf16[128,1024]{1,0:T(8,128)(2,1)S(1)} %get-tuple-element.85), channel_id=1, source_target_pairs={{0,2},{1,3},{2,0},{3,1},{4,6},{5,7},{6,4},{7,5},{8,10},{9,11},{10,... | collective-permute-start | bytes 786440 | tf_op jit(solution)/shard_map/ppermute | solution.py:26
  4.3 3.0 %collective-permute-start.10 = (bf16[128,1024]{1,0:T(8,128)(2,1)S(1)}, bf16[128,1024]{1,0:T(8,128)(2,1)S(1)}, u32[]{:S(2)}, u32[]{:S(2)}) collective-permute-start(bf16[128,1024]{1,0:T(8,128)(2,1)S(1)} %get-tuple-element.86.refs_0_), channel_id=1, source_target_pairs={{0,24},{1,25},{2,26},{3,27},{4,28},{5,29},{6,30},{7,31},{8,0},{9,1... | collective-permute-start | bytes 786440 | tf_op jit(solution)/shard_map/ppermute | solution.py:26
  7.3 3.3 %collective-permute-done.1.refs_0_ = bf16[128,1024]{1,0:T(8,128)(2,1)S(1)} collective-permute-done((bf16[128,1024]{1,0:T(8,128)(2,1)S(1)}, bf16[128,1024]{1,0:T(8,128)(2,1)S(1)}, u32[]{:S(2)}, u32[]{:S(2)}) %collective-permute-start.1) | collective-permute-done | bytes 262176 | tf_op jit(solution)/shard_map/ppermute | solution.py:26
  10.6 4.3 %collective-permute-start.2 = (bf16[128,1024]{1,0:T(8,128)(2,1)S(1)}, bf16[128,1024]{1,0:T(8,128)(2,1)S(1)}, u32[]{:S(2)}, u32[]{:S(2)}) collective-permute-start(bf16[128,1024]{1,0:T(8,128)(2,1)S(1)} %collective-permute-done.1.refs_0_), channel_id=1, source_target_pairs={{0,96},{1,97},{2,98},{3,99},{4,100},{5,101},{6,102},{7,103},{8,104... | collective-permute-start | bytes 786440 | tf_op jit(solution)/shard_map/ppermute | solution.py:26
  14.9 1.5 %collective-permute-start.6 = (bf16[256,1024]{1,0:T(8,128)(2,1)}, bf16[256,1024]{1,0:T(8,128)(2,1)S(1)}, u32[]{:S(2)}, u32[]{:S(2)}) collective-permute-start(bf16[256,1024]{1,0:T(8,128)(2,1)} %refs_0_), channel_id=1, source_target_pairs={{0,4},{1,5},{2,6},{3,7},{4,0},{5,1},{6,2},{7,3},{8,12},{9,13},{10,... | collective-permute-start | bytes 1572872 | tf_op jit(solution)/shard_map/ppermute | solution.py:26
  16.4 3.0 %collective-permute-start.11 = (bf16[128,1024]{1,0:T(8,128)(2,1)S(1)}, bf16[128,1024]{1,0:T(8,128)(2,1)S(1)}, u32[]{:S(2)}, u32[]{:S(2)}) collective-permute-start(bf16[128,1024]{1,0:T(8,128)(2,1)S(1)} %collective-permute-done.10.refs_1_), channel_id=1, source_target_pairs={{0,24},{1,25},{2,26},{3,27},{4,28},{5,29},{6,30},{7,31},{8,0},{9,1... | collective-permute-start | bytes 786440 | tf_op jit(solution)/shard_map/ppermute | solution.py:26
  19.4 0.2 collective-permute-done.2.refs_1_
  19.6 3.4 %collective-permute-done.3.refs_3_ = bf16[128,1024]{1,0:T(8,128)(2,1)S(1)} collective-permute-done((bf16[128,1024]{1,0:T(8,128)(2,1)S(1)}, bf16[128,1024]{1,0:T(8,128)(2,1)S(1)}, u32[]{:S(2)}, u32[]{:S(2)}) %collective-permute-start.3) | collective-permute-done | bytes 262176 | tf_op jit(solution)/shard_map/ppermute | solution.py:26
  23.0 0.3 collective-permute-start.5
  23.3 0.1 stack.23.at
  23.4 0.2 collective-permute-done.11.refs_2_
  23.5 0.7 shard_map.29.refs_4_.p0
  24.2 3.1 %collective-permute-start.12 = (bf16[4,128,1024]{2,1,0:T(8,128)(2,1)S(1)}, bf16[4,128,1024]{2,1,0:T(8,128)(2,1)S(1)}, u32[]{:S(2)}, u32[]{:S(2)}) collective-permute-start(bf16[4,128,1024]{2,1,0:T(8,128)(2,1)S(1)} %shard_map.29.refs_4_.p0), channel_id=1, source_target_pairs={{0,96},{1,97},{2,98},{3,99},{4,100},{5,101},{6,102},{7,103},{8,104... | collective-permute-start | bytes 3145736 | tf_op jit(solution)/shard_map/ppermute | solution.py:26
  27.3 2.1 %collective-permute-start.4 = (bf16[256,1024]{1,0:T(8,128)(2,1)S(1)}, bf16[256,1024]{1,0:T(8,128)(2,1)S(1)}, u32[]{:S(2)}, u32[]{:S(2)}) collective-permute-start(bf16[256,1024]{1,0:T(8,128)(2,1)S(1)} %copy-done), channel_id=1, source_target_pairs={{0,6},{1,7},{2,4},{3,5},{4,2},{5,3},{6,0},{7,1},{8,14},{9,15},{10,... | collective-permute-start | bytes 1572872 | tf_op jit(solution)/shard_map/ppermute | solution.py:26
  29.4 2.9 %collective-permute-done.5.refs_2_ = bf16[128,1024]{1,0:T(8,128)(2,1)S(1)} collective-permute-done((bf16[128,1024]{1,0:T(8,128)(2,1)S(1)}, bf16[128,1024]{1,0:T(8,128)(2,1)S(1)}, u32[]{:S(2)}, u32[]{:S(2)}) %collective-permute-start.5) | collective-permute-done | bytes 262176 | tf_op jit(solution)/shard_map/ppermute | solution.py:26
  32.2 0.7 shard_map.28.refs_7_.p0
  32.9 3.1 %collective-permute-start.7 = (bf16[4,128,1024]{2,1,0:T(8,128)(2,1)S(1)}, bf16[4,128,1024]{2,1,0:T(8,128)(2,1)S(1)}, u32[]{:S(2)}, u32[]{:S(2)}) collective-permute-start(bf16[4,128,1024]{2,1,0:T(8,128)(2,1)S(1)} %shard_map.28.refs_7_.p0), channel_id=1, source_target_pairs={{0,24},{1,25},{2,26},{3,27},{4,28},{5,29},{6,30},{7,31},{8,0},{9,1... | collective-permute-start | bytes 3145736 | tf_op jit(solution)/shard_map/ppermute | solution.py:26
  36.0 3.3 %collective-permute-done.4.refs_3_ = bf16[256,1024]{1,0:T(8,128)(2,1)S(1)} collective-permute-done((bf16[256,1024]{1,0:T(8,128)(2,1)S(1)}, bf16[256,1024]{1,0:T(8,128)(2,1)S(1)}, u32[]{:S(2)}, u32[]{:S(2)}) %collective-permute-start.4) | collective-permute-done | bytes 524320 | tf_op jit(solution)/shard_map/ppermute | solution.py:26
  39.3 1.5 %collective-permute-start.9 = (bf16[256,1024]{1,0:T(8,128)(2,1)S(1)}, bf16[256,1024]{1,0:T(8,128)(2,1)S(1)}, u32[]{:S(2)}, u32[]{:S(2)}) collective-permute-start(bf16[256,1024]{1,0:T(8,128)(2,1)S(1)} %copy-done), channel_id=1, source_target_pairs={{0,2},{1,3},{2,0},{3,1},{4,6},{5,7},{6,4},{7,5},{8,10},{9,11},{10,... | collective-permute-start | bytes 1572872 | tf_op jit(solution)/shard_map/ppermute | solution.py:26
  40.8 10.6 %collective-permute-done.12.refs_5_.next_.p1 = bf16[4,128,1024]{2,1,0:T(8,128)(2,1)S(1)} collective-permute-done((bf16[4,128,1024]{2,1,0:T(8,128)(2,1)S(1)}, bf16[4,128,1024]{2,1,0:T(8,128)(2,1)S(1)}, u32[]{:S(2)}, u32[]{:S(2)}) %collective-permute-start.12) | collective-permute-done | bytes 1048608 | tf_op jit(solution)/shard_map/ppermute | solution.py:26
  51.4 0.7 shard_map.31
  52.1 2.0 %collective-permute-start.14 = (bf16[2,128,1024]{2,1,0:T(8,128)(2,1)S(1)}, bf16[2,128,1024]{2,1,0:T(8,128)(2,1)S(1)}, u32[]{:S(2)}, u32[]{:S(2)}) collective-permute-start(bf16[2,128,1024]{2,1,0:T(8,128)(2,1)S(1)} %get-tuple-element.61), channel_id=1, source_target_pairs={{0,96},{1,97},{2,98},{3,99},{4,100},{5,101},{6,102},{7,103},{8,104... | collective-permute-start | bytes 1572872 | tf_op jit(solution)/shard_map/ppermute | solution.py:26
  54.1 0.1 collective-permute-start.15
  54.2 2.0 %collective-permute-done.8.refs_9_.last.p3 = bf16[4,128,1024]{2,1,0:T(8,128)(2,1)S(1)} collective-permute-done((bf16[4,128,1024]{2,1,0:T(8,128)(2,1)S(1)}, bf16[4,128,1024]{2,1,0:T(8,128)(2,1)S(1)}, u32[]{:S(2)}, u32[]{:S(2)}) %collective-permute-start.8) | collective-permute-done | bytes 1048608 | tf_op jit(solution)/shard_map/ppermute | solution.py:26
  56.2 0.7 shard_map.34
  56.9 2.9 %collective-permute-start.17 = (bf16[2,128,1024]{2,1,0:T(8,128)(2,1)S(1)}, bf16[2,128,1024]{2,1,0:T(8,128)(2,1)S(1)}, u32[]{:S(2)}, u32[]{:S(2)}) collective-permute-start(bf16[2,128,1024]{2,1,0:T(8,128)(2,1)S(1)} %get-tuple-element.63), channel_id=1, source_target_pairs={{0,24},{1,25},{2,26},{3,27},{4,28},{5,29},{6,30},{7,31},{8,0},{9,1... | collective-permute-start | bytes 1572872 | tf_op jit(solution)/shard_map/ppermute | solution.py:26
  59.7 7.7 %shard_map.30 = (f32[4,4,512,128]{3,2,1,0:T(8,128)S(1)}, bf16[2,512,1024]{2,1,0:T(8,128)(2,1)S(1)}) custom-call(s32[5]{0:T(128)S(1)} %stack.23.at, bf16[256,1024]{1,0:T(8,128)(2,1)S(1)} %copy-done, bf16[256,1024]{1,0:T(8,128)(2,1)S(1)} %collective-permute-done.6.refs_1_, bf16[256,1024]{1,0:T(8,128)(2,1)S(1)} %collective-permute-done.9.refs_2_, ...), custom_call_target="tpu_custom_call" | custom-call | flops 3221225472 | bytes 14680084 | tf_op jit(solution)/shard_map/pallas_call | solution.py:76
  67.4 1.8 %shard_map.33 = f32[2,4,512,128]{3,2,1,0:T(8,128)S(1)} custom-call(s32[5]{0:T(128)S(1)} %stack.23.at, bf16[2,512,1024]{2,1,0:T(8,128)(2,1)S(1)} %get-tuple-element.59.x, f32[4,4,512,128]{3,2,1,0:T(8,128)S(1)} %get-tuple-element.60.acc, bf16[2,128,1024]{2,1,0:T(8,128)(2,1)S(1)} %collective-permute-done.14.n_a.p2_a, ...), custom_call_target="tpu_custom_call" | custom-call | flops 26843545600 | bytes 9437204 | tf_op jit(solution)/shard_map/pallas_call | solution.py:76
  69.2 0.1 collective-permute-start.16
  69.3 0.9 collective-permute-done.18.f_b.p2_b
  70.2 2.2 %shard_map.35 = (f32[2,512,128]{2,1,0:T(8,128)S(1)}, f32[2,512,128]{2,1,0:T(8,128)S(1)}) custom-call(s32[5]{0:T(128)S(1)} %stack.23.at, bf16[2,512,1024]{2,1,0:T(8,128)(2,1)S(1)} %get-tuple-element.59.x, bf16[2,128,1024]{2,1,0:T(8,128)(2,1)S(1)} %collective-permute-done.17.f_a.p2_a, bf16[2,128,1024]{2,1,0:T(8,128)(2,1)S(1)} %collective-permute-done.18.f_b.p2_b), custom_call_target="tpu_custom_call" | custom-call | flops 536870912 | bytes 4194324 | tf_op jit(solution)/shard_map/pallas_call | solution.py:76
  72.4 0.1 collective-permute-start.19
  72.5 0.8 shard_map.32
  73.3 1.1 collective-permute-done.19.far_got
  74.4 2.2 %shard_map.36 = (f32[8,512,128]{2,1,0:T(8,128)S(1)}, f32[8,1,512]{2,1,0:T(1,128)S(1)}) custom-call(s32[5]{0:T(128)S(1)} %stack.23.at, f32[8,512,128]{2,1,0:T(8,128)S(1)} %bitcast.12, f32[8,512,128]{2,1,0:T(8,128)S(1)} %collective-permute-done.16.got, f32[2,512,128]{2,1,0:T(8,128)S(1)} %get-tuple-element.65.far_keep, ...), custom_call_target="tpu_custom_call" | custom-call | bytes 7356436 | tf_op jit(solution)/shard_map/pallas_call | solution.py:76
  76.6 9.1 %all_to_all.20.came = f32[8,1,512]{2,1,0:T(1,128)S(1)} all-to-all(f32[8,1,512]{2,1,0:T(1,128)S(1)} %get-tuple-element.67), channel_id=1, replica_groups=mesh['z'=4,'y'=4,'l'=2,'h'=2,'c'=2] {'l','h','c'}, dimensions={0} | all-to-all | bytes 32768 | tf_op jit(solution)/shard_map/all_to_all | solution.py:459
  85.7 1.3 shard_map.37
  87.0 12.7 %all_to_all.21.came = f32[16,8,128]{2,1,0:T(8,128)S(1)} all-to-all(f32[16,8,128]{2,1,0:T(8,128)S(1)} %get-tuple-element.69), channel_id=1, replica_groups=mesh['z'=4,'y'=4,'l'=2,'h'=2,'c'=2] {'z','y'}, dimensions={0} | all-to-all | bytes 131072 | tf_op jit(solution)/shard_map/all_to_all | solution.py:459
  99.7 1.3 shard_map.38
  101.0 0.0 collective-permute-start.20
  101.0 7.7 %all_to_all.22.came = f32[8,1,512]{2,1,0:T(1,128)S(1)} all-to-all(f32[8,1,512]{2,1,0:T(1,128)S(1)} %get-tuple-element.71), channel_id=1, replica_groups=mesh['z'=4,'y'=4,'l'=2,'h'=2,'c'=2] {'l','h','c'}, dimensions={0} | all-to-all | bytes 32768 | tf_op jit(solution)/shard_map/all_to_all | solution.py:459
  108.7 0.9 shard_map.39
  109.6 11.2 %all_to_all.23.came = f32[32,8,128]{2,1,0:T(8,128)S(1)} all-to-all(f32[32,8,128]{2,1,0:T(8,128)S(1)} %get-tuple-element.73), channel_id=1, replica_groups=mesh['z'=4,'y'=4,'l'=2,'h'=2,'c'=2] {'z','y','c'}, dimensions={0} | all-to-all | bytes 262144 | tf_op jit(solution)/shard_map/all_to_all | solution.py:459
  120.8 1.0 shard_map.40
  121.8 2.1 %shard_map.43 = (bf16[144,1024]{1,0:T(8,128)(2,1)S(1)}, bf16[144,1024]{1,0:T(8,128)(2,1)S(1)}) custom-call(s32[5]{0:T(128)S(1)} %stack.23.at, bf16[4,4,512,128]{3,2,1,0:T(8,128)(2,1)S(1)} %bitcast.8, bf16[4,128,1024]{2,1,0:T(8,128)(2,1)S(1)} %shard_map.28.refs_7_.p0, bf16[4,128,1024]{2,1,0:T(8,128)(2,1)S(1)} %collective-permute-done.7.refs_8_.next_.p1, ...), custom_call_target="tpu_custom_call" | custom-call | flops 2147483648 | bytes 6881300 | tf_op jit(solution)/shard_map/pallas_call | solution.py:76
  123.9 1.2 collective-permute-start.22
  125.2 0.0 collective-permute-start.24
  125.2 2.1 %shard_map.42 = (bf16[128,1024]{1,0:T(8,128)(2,1)S(1)}, f32[128,1024]{1,0:T(8,128)S(1)}, f32[8,256]{1,0:T(8,128)S(1)}) custom-call(s32[5]{0:T(128)S(1)} %stack.23.at, bf16[4,4,512,128]{3,2,1,0:T(8,128)(2,1)S(1)} %bitcast.9, bf16[4,128,1024]{2,1,0:T(8,128)(2,1)S(1)} %shard_map.29.refs_4_.p0, ...), custom_call_target="tpu_custom_call" | custom-call | flops 2147483648 | bytes 7086100 | tf_op jit(solution)/shard_map/pallas_call | solution.py:76
  127.2 2.1 %collective-permute-start.21 = (bf16[128,1024]{1,0:T(8,128)(2,1)S(1)}, bf16[128,1024]{1,0:T(8,128)(2,1)S(1)}, u32[]{:S(2)}, u32[]{:S(2)}) collective-permute-start(bf16[128,1024]{1,0:T(8,128)(2,1)S(1)} %get-tuple-element.77), channel_id=1, source_target_pairs={{0,4},{1,5},{2,6},{3,7},{4,0},{5,1},{6,2},{7,3},{8,12},{9,13},{10,... | collective-permute-start | bytes 786440 | tf_op jit(solution)/shard_map/ppermute | solution.py:26
  129.3 2.1 %shard_map.45 = (bf16[128,1024]{1,0:T(8,128)(2,1)S(1)}, f32[128,1024]{1,0:T(8,128)S(1)}, f32[8,256]{1,0:T(8,128)S(1)}) custom-call(s32[5]{0:T(128)S(1)} %stack.23.at, bf16[4,4,512,128]{3,2,1,0:T(8,128)(2,1)S(1)} %bitcast.10, bf16[4,128,1024]{2,1,0:T(8,128)(2,1)S(1)} %shard_map.28.refs_7_.p0, ...), custom_call_target="tpu_custom_call" | custom-call | flops 2147483648 | bytes 7086100 | tf_op jit(solution)/shard_map/pallas_call | solution.py:76
  131.4 2.1 %collective-permute-start.26 = (bf16[128,1024]{1,0:T(8,128)(2,1)S(1)}, bf16[128,1024]{1,0:T(8,128)(2,1)S(1)}, u32[]{:S(2)}, u32[]{:S(2)}) collective-permute-start(bf16[128,1024]{1,0:T(8,128)(2,1)S(1)} %get-tuple-element.84), channel_id=1, source_target_pairs={{0,6},{1,7},{2,4},{3,5},{4,2},{5,3},{6,0},{7,1},{8,14},{9,15},{10,... | collective-permute-start | bytes 786440 | tf_op jit(solution)/shard_map/ppermute | solution.py:26
  133.6 0.7 collective-permute-done.22.came
  134.2 0.6 shard_map.44
  134.8 0.1 collective-permute-start.23
  134.9 0.1 collective-permute-done.24.came
  135.1 0.6 shard_map.46
  135.7 2.1 %collective-permute-start.25 = (bf16[144,1024]{1,0:T(8,128)(2,1)S(1)}, bf16[144,1024]{1,0:T(8,128)(2,1)S(1)}, u32[]{:S(2)}, u32[]{:S(2)}) collective-permute-start(bf16[144,1024]{1,0:T(8,128)(2,1)S(1)} %shard_map.46), channel_id=1, source_target_pairs={{0,6},{1,7},{2,4},{3,5},{4,2},{5,3},{6,0},{7,1},{8,14},{9,15},{10,... | collective-permute-start | bytes 884744 | tf_op jit(solution)/shard_map/ppermute | solution.py:26
  137.8 2.1 %shard_map.41 = (f32[256,1024]{1,0:T(8,128)S(1)}, f32[8,256]{1,0:T(8,128)S(1)}) custom-call(s32[5]{0:T(128)S(1)} %stack.23.at, bf16[4,4,512,128]{3,2,1,0:T(8,128)(2,1)S(1)} %bitcast.11, bf16[4,128,1024]{2,1,0:T(8,128)(2,1)S(1)} %shard_map.29.refs_4_.p0, bf16[4,128,1024]{2,1,0:T(8,128)(2,1)S(1)} %collective-permute-done.12.refs_5_.next_.p1, ...), custom_call_target="tpu_custom_call" | custom-call | flops 17179869184 | bytes 7348244 | tf_op jit(solution)/shard_map/pallas_call | solution.py:76
  139.9 0.8 collective-permute-done.21.l_low
  140.7 0.9 collective-permute-done.26.lh_high
  141.6 4.2 %collective-permute-done.23.l_high = bf16[144,1024]{1,0:T(8,128)(2,1)S(1)} collective-permute-done((bf16[144,1024]{1,0:T(8,128)(2,1)S(1)}, bf16[144,1024]{1,0:T(8,128)(2,1)S(1)}, u32[]{:S(2)}, u32[]{:S(2)}) %collective-permute-start.23) | collective-permute-done | bytes 294944 | tf_op jit(solution)/shard_map/ppermute | solution.py:26
  145.8 0.7 collective-permute-done.25.lh_low
  146.5 1.7 %shard_map.47 = bf16[256,1024]{1,0:T(8,128)(2,1)} custom-call(s32[5]{0:T(128)S(1)} %stack.23.at, f32[256,1024]{1,0:T(8,128)S(1)} %get-tuple-element.75.own, f32[8,256]{1,0:T(8,128)S(1)} %get-tuple-element.76.own_total, bf16[128,1024]{1,0:T(8,128)(2,1)S(1)} %collective-permute-done.21.l_low, bf16[144,1024]{1,0:T(8,128)(2,1)S(1)} %collective-permute-done.23.l_high, ...), custom_call_target="tpu_custom_call" | custom-call | bytes 2695188 | tf_op jit(solution)/shard_map/pallas_call | solution.py:76
  (18 shorter events, 0.0 us)
Async XLA Ops:
  0.0 27.3 %copy-start = (bf16[256,1024]{1,0:T(8,128)(2,1)S(1)}, bf16[256,1024]{1,0:T(8,128)(2,1)}, u32[]{:S(2)}) copy-start(bf16[256,1024]{1,0:T(8,128)(2,1)} %refs_0_) | copy-start | bytes 1572868
  1.1 9.5 %collective-permute-start.1 = (bf16[128,1024]{1,0:T(8,128)(2,1)S(1)}, bf16[128,1024]{1,0:T(8,128)(2,1)S(1)}, u32[]{:S(2)}, u32[]{:S(2)}) collective-permute-start(bf16[128,1024]{1,0:T(8,128)(2,1)S(1)} %get-tuple-element.85), channel_id=1, source_target_pairs={{0,2},{1,3},{2,0},{3,1},{4,6},{5,7},{6,4},{7,5},{8,10},{9,11},{10,... | collective-permute-start | bytes 786440 | tf_op jit(solution)/shard_map/ppermute | solution.py:26
  4.3 12.1 %collective-permute-start.10 = (bf16[128,1024]{1,0:T(8,128)(2,1)S(1)}, bf16[128,1024]{1,0:T(8,128)(2,1)S(1)}, u32[]{:S(2)}, u32[]{:S(2)}) collective-permute-start(bf16[128,1024]{1,0:T(8,128)(2,1)S(1)} %get-tuple-element.86.refs_0_), channel_id=1, source_target_pairs={{0,24},{1,25},{2,26},{3,27},{4,28},{5,29},{6,30},{7,31},{8,0},{9,1... | collective-permute-start | bytes 786440 | tf_op jit(solution)/shard_map/ppermute | solution.py:26
  7.3 12.1 %collective-permute-start = (bf16[128,1024]{1,0:T(8,128)(2,1)S(1)}, bf16[128,1024]{1,0:T(8,128)(2,1)S(1)}, u32[]{:S(2)}, u32[]{:S(2)}) collective-permute-start(bf16[128,1024]{1,0:T(8,128)(2,1)S(1)} %get-tuple-element.86.refs_0_), channel_id=1, source_target_pairs={{0,8},{1,9},{2,10},{3,11},{4,12},{5,13},{6,14},{7,15},{8,16},{9,17... | collective-permute-start | bytes 786440 | tf_op jit(solution)/shard_map/ppermute | solution.py:26
  10.6 9.0 %collective-permute-start.2 = (bf16[128,1024]{1,0:T(8,128)(2,1)S(1)}, bf16[128,1024]{1,0:T(8,128)(2,1)S(1)}, u32[]{:S(2)}, u32[]{:S(2)}) collective-permute-start(bf16[128,1024]{1,0:T(8,128)(2,1)S(1)} %collective-permute-done.1.refs_0_), channel_id=1, source_target_pairs={{0,96},{1,97},{2,98},{3,99},{4,100},{5,101},{6,102},{7,103},{8,104... | collective-permute-start | bytes 786440 | tf_op jit(solution)/shard_map/ppermute | solution.py:26
  14.9 8.1 %collective-permute-start.3 = (bf16[128,1024]{1,0:T(8,128)(2,1)S(1)}, bf16[128,1024]{1,0:T(8,128)(2,1)S(1)}, u32[]{:S(2)}, u32[]{:S(2)}) collective-permute-start(bf16[128,1024]{1,0:T(8,128)(2,1)S(1)} %collective-permute-done.1.refs_0_), channel_id=1, source_target_pairs={{0,32},{1,33},{2,34},{3,35},{4,36},{5,37},{6,38},{7,39},{8,40},{9,... | collective-permute-start | bytes 786440 | tf_op jit(solution)/shard_map/ppermute | solution.py:26
  14.9 17.3 %collective-permute-start.6 = (bf16[256,1024]{1,0:T(8,128)(2,1)}, bf16[256,1024]{1,0:T(8,128)(2,1)S(1)}, u32[]{:S(2)}, u32[]{:S(2)}) collective-permute-start(bf16[256,1024]{1,0:T(8,128)(2,1)} %refs_0_), channel_id=1, source_target_pairs={{0,4},{1,5},{2,6},{3,7},{4,0},{5,1},{6,2},{7,3},{8,12},{9,13},{10,... | collective-permute-start | bytes 1572872 | tf_op jit(solution)/shard_map/ppermute | solution.py:26
  16.4 7.1 %collective-permute-start.11 = (bf16[128,1024]{1,0:T(8,128)(2,1)S(1)}, bf16[128,1024]{1,0:T(8,128)(2,1)S(1)}, u32[]{:S(2)}, u32[]{:S(2)}) collective-permute-start(bf16[128,1024]{1,0:T(8,128)(2,1)S(1)} %collective-permute-done.10.refs_1_), channel_id=1, source_target_pairs={{0,24},{1,25},{2,26},{3,27},{4,28},{5,29},{6,30},{7,31},{8,0},{9,1... | collective-permute-start | bytes 786440 | tf_op jit(solution)/shard_map/ppermute | solution.py:26
  23.0 9.2 %collective-permute-start.5 = (bf16[128,1024]{1,0:T(8,128)(2,1)S(1)}, bf16[128,1024]{1,0:T(8,128)(2,1)S(1)}, u32[]{:S(2)}, u32[]{:S(2)}) collective-permute-start(bf16[128,1024]{1,0:T(8,128)(2,1)S(1)} %collective-permute-done.2.refs_1_), channel_id=1, source_target_pairs={{0,96},{1,97},{2,98},{3,99},{4,100},{5,101},{6,102},{7,103},{8,104... | collective-permute-start | bytes 786440 | tf_op jit(solution)/shard_map/ppermute | solution.py:26
  24.2 27.2 %collective-permute-start.12 = (bf16[4,128,1024]{2,1,0:T(8,128)(2,1)S(1)}, bf16[4,128,1024]{2,1,0:T(8,128)(2,1)S(1)}, u32[]{:S(2)}, u32[]{:S(2)}) collective-permute-start(bf16[4,128,1024]{2,1,0:T(8,128)(2,1)S(1)} %shard_map.29.refs_4_.p0), channel_id=1, source_target_pairs={{0,96},{1,97},{2,98},{3,99},{4,100},{5,101},{6,102},{7,103},{8,104... | collective-permute-start | bytes 3145736 | tf_op jit(solution)/shard_map/ppermute | solution.py:26
  27.2 24.2 %collective-permute-start.13 = (bf16[4,128,1024]{2,1,0:T(8,128)(2,1)S(1)}, bf16[4,128,1024]{2,1,0:T(8,128)(2,1)S(1)}, u32[]{:S(2)}, u32[]{:S(2)}) collective-permute-start(bf16[4,128,1024]{2,1,0:T(8,128)(2,1)S(1)} %shard_map.29.refs_4_.p0), channel_id=1, source_target_pairs={{0,32},{1,33},{2,34},{3,35},{4,36},{5,37},{6,38},{7,39},{8,40},{9,... | collective-permute-start | bytes 3145736 | tf_op jit(solution)/shard_map/ppermute | solution.py:26
  27.3 12.0 %collective-permute-start.4 = (bf16[256,1024]{1,0:T(8,128)(2,1)S(1)}, bf16[256,1024]{1,0:T(8,128)(2,1)S(1)}, u32[]{:S(2)}, u32[]{:S(2)}) collective-permute-start(bf16[256,1024]{1,0:T(8,128)(2,1)S(1)} %copy-done), channel_id=1, source_target_pairs={{0,6},{1,7},{2,4},{3,5},{4,2},{5,3},{6,0},{7,1},{8,14},{9,15},{10,... | collective-permute-start | bytes 1572872 | tf_op jit(solution)/shard_map/ppermute | solution.py:26
  32.9 21.3 %collective-permute-start.7 = (bf16[4,128,1024]{2,1,0:T(8,128)(2,1)S(1)}, bf16[4,128,1024]{2,1,0:T(8,128)(2,1)S(1)}, u32[]{:S(2)}, u32[]{:S(2)}) collective-permute-start(bf16[4,128,1024]{2,1,0:T(8,128)(2,1)S(1)} %shard_map.28.refs_7_.p0), channel_id=1, source_target_pairs={{0,24},{1,25},{2,26},{3,27},{4,28},{5,29},{6,30},{7,31},{8,0},{9,1... | collective-permute-start | bytes 3145736 | tf_op jit(solution)/shard_map/ppermute | solution.py:26
  36.0 20.2 %collective-permute-start.8 = (bf16[4,128,1024]{2,1,0:T(8,128)(2,1)S(1)}, bf16[4,128,1024]{2,1,0:T(8,128)(2,1)S(1)}, u32[]{:S(2)}, u32[]{:S(2)}) collective-permute-start(bf16[4,128,1024]{2,1,0:T(8,128)(2,1)S(1)} %shard_map.28.refs_7_.p0), channel_id=1, source_target_pairs={{0,8},{1,9},{2,10},{3,11},{4,12},{5,13},{6,14},{7,15},{8,16},{9,17... | collective-permute-start | bytes 3145736 | tf_op jit(solution)/shard_map/ppermute | solution.py:26
  39.3 14.9 %collective-permute-start.9 = (bf16[256,1024]{1,0:T(8,128)(2,1)S(1)}, bf16[256,1024]{1,0:T(8,128)(2,1)S(1)}, u32[]{:S(2)}, u32[]{:S(2)}) collective-permute-start(bf16[256,1024]{1,0:T(8,128)(2,1)S(1)} %copy-done), channel_id=1, source_target_pairs={{0,2},{1,3},{2,0},{3,1},{4,6},{5,7},{6,4},{7,5},{8,10},{9,11},{10,... | collective-permute-start | bytes 1572872 | tf_op jit(solution)/shard_map/ppermute | solution.py:26
  52.1 15.3 %collective-permute-start.14 = (bf16[2,128,1024]{2,1,0:T(8,128)(2,1)S(1)}, bf16[2,128,1024]{2,1,0:T(8,128)(2,1)S(1)}, u32[]{:S(2)}, u32[]{:S(2)}) collective-permute-start(bf16[2,128,1024]{2,1,0:T(8,128)(2,1)S(1)} %get-tuple-element.61), channel_id=1, source_target_pairs={{0,96},{1,97},{2,98},{3,99},{4,100},{5,101},{6,102},{7,103},{8,104... | collective-permute-start | bytes 1572872 | tf_op jit(solution)/shard_map/ppermute | solution.py:26
  54.1 13.4 %collective-permute-start.15 = (bf16[2,128,1024]{2,1,0:T(8,128)(2,1)S(1)}, bf16[2,128,1024]{2,1,0:T(8,128)(2,1)S(1)}, u32[]{:S(2)}, u32[]{:S(2)}) collective-permute-start(bf16[2,128,1024]{2,1,0:T(8,128)(2,1)S(1)} %get-tuple-element.62), channel_id=1, source_target_pairs={{0,32},{1,33},{2,34},{3,35},{4,36},{5,37},{6,38},{7,39},{8,40},{9,... | collective-permute-start | bytes 1572872 | tf_op jit(solution)/shard_map/ppermute | solution.py:26
  56.9 12.4 %collective-permute-start.17 = (bf16[2,128,1024]{2,1,0:T(8,128)(2,1)S(1)}, bf16[2,128,1024]{2,1,0:T(8,128)(2,1)S(1)}, u32[]{:S(2)}, u32[]{:S(2)}) collective-permute-start(bf16[2,128,1024]{2,1,0:T(8,128)(2,1)S(1)} %get-tuple-element.63), channel_id=1, source_target_pairs={{0,24},{1,25},{2,26},{3,27},{4,28},{5,29},{6,30},{7,31},{8,0},{9,1... | collective-permute-start | bytes 1572872 | tf_op jit(solution)/shard_map/ppermute | solution.py:26
  59.7 10.5 %collective-permute-start.18 = (bf16[2,128,1024]{2,1,0:T(8,128)(2,1)S(1)}, bf16[2,128,1024]{2,1,0:T(8,128)(2,1)S(1)}, u32[]{:S(2)}, u32[]{:S(2)}) collective-permute-start(bf16[2,128,1024]{2,1,0:T(8,128)(2,1)S(1)} %get-tuple-element.64), channel_id=1, source_target_pairs={{0,8},{1,9},{2,10},{3,11},{4,12},{5,13},{6,14},{7,15},{8,16},{9,17... | collective-permute-start | bytes 1572872 | tf_op jit(solution)/shard_map/ppermute | solution.py:26
  69.2 5.2 %collective-permute-start.16 = (f32[8,512,128]{2,1,0:T(8,128)S(1)}, f32[8,512,128]{2,1,0:T(8,128)S(1)}, u32[]{:S(2)}, u32[]{:S(2)}) collective-permute-start(f32[8,512,128]{2,1,0:T(8,128)S(1)} %bitcast.13), channel_id=1, source_target_pairs={{0,1},{1,0},{2,3},{3,2},{4,5},{5,4},{6,7},{7,6},{8,9},{9,8},{10,11... | collective-permute-start | bytes 6291464 | tf_op jit(solution)/shard_map/ppermute | solution.py:26
  72.4 2.0 %collective-permute-start.19 = (f32[2,512,128]{2,1,0:T(8,128)S(1)}, f32[2,512,128]{2,1,0:T(8,128)S(1)}, u32[]{:S(2)}, u32[]{:S(2)}) collective-permute-start(f32[2,512,128]{2,1,0:T(8,128)S(1)} %get-tuple-element.66), channel_id=1, source_target_pairs={{0,1},{1,0},{2,3},{3,2},{4,5},{5,4},{6,7},{7,6},{8,9},{9,8},{10,11... | collective-permute-start | bytes 1572872 | tf_op jit(solution)/shard_map/ppermute | solution.py:26
  101.0 19.9 %collective-permute-start.20 = (f32[8,512,128]{2,1,0:T(8,128)S(1)}, f32[8,512,128]{2,1,0:T(8,128)S(1)}, u32[]{:S(2)}, u32[]{:S(2)}) collective-permute-start(f32[8,512,128]{2,1,0:T(8,128)S(1)} %get-tuple-element.72.plan), channel_id=1, source_target_pairs={{0,1},{1,0},{2,3},{3,2},{4,5},{5,4},{6,7},{7,6},{8,9},{9,8},{10,11... | collective-permute-start | bytes 6291464 | tf_op jit(solution)/shard_map/ppermute | solution.py:26
  123.9 10.3 %collective-permute-start.22 = (bf16[144,1024]{1,0:T(8,128)(2,1)S(1)}, bf16[144,1024]{1,0:T(8,128)(2,1)S(1)}, u32[]{:S(2)}, u32[]{:S(2)}) collective-permute-start(bf16[144,1024]{1,0:T(8,128)(2,1)S(1)} %get-tuple-element.80), channel_id=1, source_target_pairs={{0,6},{1,7},{2,4},{3,5},{4,2},{5,3},{6,0},{7,1},{8,14},{9,15},{10,... | collective-permute-start | bytes 884744 | tf_op jit(solution)/shard_map/ppermute | solution.py:26
  125.2 9.9 %collective-permute-start.24 = (bf16[144,1024]{1,0:T(8,128)(2,1)S(1)}, bf16[144,1024]{1,0:T(8,128)(2,1)S(1)}, u32[]{:S(2)}, u32[]{:S(2)}) collective-permute-start(bf16[144,1024]{1,0:T(8,128)(2,1)S(1)} %get-tuple-element.83), channel_id=1, source_target_pairs={{0,4},{1,5},{2,6},{3,7},{4,0},{5,1},{6,2},{7,3},{8,12},{9,13},{10,... | collective-permute-start | bytes 884744 | tf_op jit(solution)/shard_map/ppermute | solution.py:26
  127.2 13.4 %collective-permute-start.21 = (bf16[128,1024]{1,0:T(8,128)(2,1)S(1)}, bf16[128,1024]{1,0:T(8,128)(2,1)S(1)}, u32[]{:S(2)}, u32[]{:S(2)}) collective-permute-start(bf16[128,1024]{1,0:T(8,128)(2,1)S(1)} %get-tuple-element.77), channel_id=1, source_target_pairs={{0,4},{1,5},{2,6},{3,7},{4,0},{5,1},{6,2},{7,3},{8,12},{9,13},{10,... | collective-permute-start | bytes 786440 | tf_op jit(solution)/shard_map/ppermute | solution.py:26
  131.4 10.2 %collective-permute-start.26 = (bf16[128,1024]{1,0:T(8,128)(2,1)S(1)}, bf16[128,1024]{1,0:T(8,128)(2,1)S(1)}, u32[]{:S(2)}, u32[]{:S(2)}) collective-permute-start(bf16[128,1024]{1,0:T(8,128)(2,1)S(1)} %get-tuple-element.84), channel_id=1, source_target_pairs={{0,6},{1,7},{2,4},{3,5},{4,2},{5,3},{6,0},{7,1},{8,14},{9,15},{10,... | collective-permute-start | bytes 786440 | tf_op jit(solution)/shard_map/ppermute | solution.py:26
  134.8 11.0 %collective-permute-start.23 = (bf16[144,1024]{1,0:T(8,128)(2,1)S(1)}, bf16[144,1024]{1,0:T(8,128)(2,1)S(1)}, u32[]{:S(2)}, u32[]{:S(2)}) collective-permute-start(bf16[144,1024]{1,0:T(8,128)(2,1)S(1)} %shard_map.44), channel_id=1, source_target_pairs={{0,4},{1,5},{2,6},{3,7},{4,0},{5,1},{6,2},{7,3},{8,12},{9,13},{10,... | collective-permute-start | bytes 884744 | tf_op jit(solution)/shard_map/ppermute | solution.py:26
  135.7 10.8 %collective-permute-start.25 = (bf16[144,1024]{1,0:T(8,128)(2,1)S(1)}, bf16[144,1024]{1,0:T(8,128)(2,1)S(1)}, u32[]{:S(2)}, u32[]{:S(2)}) collective-permute-start(bf16[144,1024]{1,0:T(8,128)(2,1)S(1)} %shard_map.46), channel_id=1, source_target_pairs={{0,6},{1,7},{2,4},{3,5},{4,2},{5,3},{6,0},{7,1},{8,14},{9,15},{10,... | collective-permute-start | bytes 884744 | tf_op jit(solution)/shard_map/ppermute | solution.py:26

commit v5 on v4

--- a/solution.py
+++ b/solution.py
@@ -392,7 +392,7 @@
     near_2 = from_y(near_1, 1)
     near_3, far_1, far_3, data_rows = wave((near_3, from_z(far, 1), from_z(far, 3), data_rows))
     data_lh = flip(data_rows, "lh")
-    far_2, data_l, data_rows = wave((from_z(far_1, 1), data_l, data_rows))
+    far_2, data_l, data_rows = wave((from_z(far, 2), data_l, data_rows))
     sems = pltpu.SemaphoreType.DMA((4,))
 
     def stacked(*blocks):

time: 148 us -> 151 us (1.020)
  waiting for transfers between devices: 35.3 us -> 38 us
    ppermute x27, waiting for transfers between devices: 35.3 us -> 38 us  [move(): return lax.ppermute(value, AXES, pairs)]
  transfers between devices with their start and end apart: 27 -> 27, of which waited for: 16 -> 13; matrix products, arithmetic and copies ran while one was open for 0% -> 0% of each run, Pallas kernels for 16% -> 15%
where the time goes in v5:
time: 151 us
  blocking collectives  39.8 us (26%)
  starting transfers between devices  39 us (26%)
  waiting for transfers between devices  38 us (25%)
  Pallas kernels  32.9 us (22%)
    all_to_all x4, blocking collectives, exchange(): return lax.all_to_all(sent, axes, 0, 0, tiled=True)  39.8 us
    ppermute x27, starting transfers between devices, move(): return lax.ppermute(value, AXES, pairs)  39 us
    ppermute x27, waiting for transfers between devices, move(): return lax.ppermute(value, AXES, pairs)  38 us
    pallas_call x20, Pallas kernels, call(): pl.pallas_call(kernel, out_shape=outs, in_specs=[pl.BlockSpec(memory_spac...  32.9 us
  transfers between devices with their start and end apart: 27, of which 13 were waited for; matrix products, arithmetic and copies ran while one was open for 0% of the time, Pallas kernels for 15%

profile of v5, /device:TPU:0, one launch (start us, length us, event | category | flops | bytes accessed | tf_op | source)
XLA Modules:
  0.0 151.1 jit_solution(10298605935175345313)
XLA Ops:
  0.0 1.1 constant_dynamic-slice_fusion
  1.1 3.2 %collective-permute-start.1 = (bf16[128,1024]{1,0:T(8,128)(2,1)S(1)}, bf16[128,1024]{1,0:T(8,128)(2,1)S(1)}, u32[]{:S(2)}, u32[]{:S(2)}) collective-permute-start(bf16[128,1024]{1,0:T(8,128)(2,1)S(1)} %get-tuple-element.85), channel_id=1, source_target_pairs={{0,2},{1,3},{2,0},{3,1},{4,6},{5,7},{6,4},{7,5},{8,10},{9,11},{10,... | collective-permute-start | bytes 786440 | tf_op jit(solution)/shard_map/ppermute | solution.py:26
  4.3 3.0 %collective-permute-start.10 = (bf16[128,1024]{1,0:T(8,128)(2,1)S(1)}, bf16[128,1024]{1,0:T(8,128)(2,1)S(1)}, u32[]{:S(2)}, u32[]{:S(2)}) collective-permute-start(bf16[128,1024]{1,0:T(8,128)(2,1)S(1)} %get-tuple-element.86.refs_0_), channel_id=1, source_target_pairs={{0,24},{1,25},{2,26},{3,27},{4,28},{5,29},{6,30},{7,31},{8,0},{9,1... | collective-permute-start | bytes 786440 | tf_op jit(solution)/shard_map/ppermute | solution.py:26
  7.3 3.3 %collective-permute-done.1.refs_0_ = bf16[128,1024]{1,0:T(8,128)(2,1)S(1)} collective-permute-done((bf16[128,1024]{1,0:T(8,128)(2,1)S(1)}, bf16[128,1024]{1,0:T(8,128)(2,1)S(1)}, u32[]{:S(2)}, u32[]{:S(2)}) %collective-permute-start.1) | collective-permute-done | bytes 262176 | tf_op jit(solution)/shard_map/ppermute | solution.py:26
  10.6 1.7 %collective-permute-start.6 = (bf16[256,1024]{1,0:T(8,128)(2,1)}, bf16[256,1024]{1,0:T(8,128)(2,1)S(1)}, u32[]{:S(2)}, u32[]{:S(2)}) collective-permute-start(bf16[256,1024]{1,0:T(8,128)(2,1)} %refs_0_), channel_id=1, source_target_pairs={{0,4},{1,5},{2,6},{3,7},{4,0},{5,1},{6,2},{7,3},{8,12},{9,13},{10,... | collective-permute-start | bytes 1572872 | tf_op jit(solution)/shard_map/ppermute | solution.py:26
  12.3 4.0 %collective-permute-start.2 = (bf16[128,1024]{1,0:T(8,128)(2,1)S(1)}, bf16[128,1024]{1,0:T(8,128)(2,1)S(1)}, u32[]{:S(2)}, u32[]{:S(2)}) collective-permute-start(bf16[128,1024]{1,0:T(8,128)(2,1)S(1)} %collective-permute-done.1.refs_0_), channel_id=1, source_target_pairs={{0,96},{1,97},{2,98},{3,99},{4,100},{5,101},{6,102},{7,103},{8,104... | collective-permute-start | bytes 786440 | tf_op jit(solution)/shard_map/ppermute | solution.py:26
  16.4 0.0 collective-permute-start.3
  16.4 3.0 %collective-permute-start.11 = (bf16[128,1024]{1,0:T(8,128)(2,1)S(1)}, bf16[128,1024]{1,0:T(8,128)(2,1)S(1)}, u32[]{:S(2)}, u32[]{:S(2)}) collective-permute-start(bf16[128,1024]{1,0:T(8,128)(2,1)S(1)} %collective-permute-done.10.refs_1_), channel_id=1, source_target_pairs={{0,24},{1,25},{2,26},{3,27},{4,28},{5,29},{6,30},{7,31},{8,0},{9,1... | collective-permute-start | bytes 786440 | tf_op jit(solution)/shard_map/ppermute | solution.py:26
  19.4 1.9 %collective-permute-start.5 = (bf16[128,1024]{1,0:T(8,128)(2,1)S(1)}, bf16[128,1024]{1,0:T(8,128)(2,1)S(1)}, u32[]{:S(2)}, u32[]{:S(2)}) collective-permute-start(bf16[128,1024]{1,0:T(8,128)(2,1)S(1)} %collective-permute-done.1.refs_0_), channel_id=1, source_target_pairs={{0,64},{1,65},{2,66},{3,67},{4,68},{5,69},{6,70},{7,71},{8,72},{9,... | collective-permute-start | bytes 786440 | tf_op jit(solution)/shard_map/ppermute | solution.py:26
  21.3 0.1 stack.23.at
  21.3 9.1 %collective-permute-done.3.refs_3_ = bf16[128,1024]{1,0:T(8,128)(2,1)S(1)} collective-permute-done((bf16[128,1024]{1,0:T(8,128)(2,1)S(1)}, bf16[128,1024]{1,0:T(8,128)(2,1)S(1)}, u32[]{:S(2)}, u32[]{:S(2)}) %collective-permute-start.3) | collective-permute-done | bytes 262176 | tf_op jit(solution)/shard_map/ppermute | solution.py:26
  30.4 0.7 shard_map.29.refs_4_.p0
  31.1 0.1 collective-permute-start.12
  31.2 2.0 %collective-permute-start.13 = (bf16[4,128,1024]{2,1,0:T(8,128)(2,1)S(1)}, bf16[4,128,1024]{2,1,0:T(8,128)(2,1)S(1)}, u32[]{:S(2)}, u32[]{:S(2)}) collective-permute-start(bf16[4,128,1024]{2,1,0:T(8,128)(2,1)S(1)} %shard_map.29.refs_4_.p0), channel_id=1, source_target_pairs={{0,32},{1,33},{2,34},{3,35},{4,36},{5,37},{6,38},{7,39},{8,40},{9,... | collective-permute-start | bytes 3145736 | tf_op jit(solution)/shard_map/ppermute | solution.py:26
  33.2 2.1 %collective-permute-start.4 = (bf16[256,1024]{1,0:T(8,128)(2,1)S(1)}, bf16[256,1024]{1,0:T(8,128)(2,1)S(1)}, u32[]{:S(2)}, u32[]{:S(2)}) collective-permute-start(bf16[256,1024]{1,0:T(8,128)(2,1)S(1)} %copy-done), channel_id=1, source_target_pairs={{0,6},{1,7},{2,4},{3,5},{4,2},{5,3},{6,0},{7,1},{8,14},{9,15},{10,... | collective-permute-start | bytes 1572872 | tf_op jit(solution)/shard_map/ppermute | solution.py:26
  35.3 0.7 shard_map.28.refs_7_.p0
  36.0 3.0 %collective-permute-start.7 = (bf16[4,128,1024]{2,1,0:T(8,128)(2,1)S(1)}, bf16[4,128,1024]{2,1,0:T(8,128)(2,1)S(1)}, u32[]{:S(2)}, u32[]{:S(2)}) collective-permute-start(bf16[4,128,1024]{2,1,0:T(8,128)(2,1)S(1)} %shard_map.28.refs_7_.p0), channel_id=1, source_target_pairs={{0,24},{1,25},{2,26},{3,27},{4,28},{5,29},{6,30},{7,31},{8,0},{9,1... | collective-permute-start | bytes 3145736 | tf_op jit(solution)/shard_map/ppermute | solution.py:26
  39.0 9.8 %collective-permute-done.4.refs_3_ = bf16[256,1024]{1,0:T(8,128)(2,1)S(1)} collective-permute-done((bf16[256,1024]{1,0:T(8,128)(2,1)S(1)}, bf16[256,1024]{1,0:T(8,128)(2,1)S(1)}, u32[]{:S(2)}, u32[]{:S(2)}) %collective-permute-start.4) | collective-permute-done | bytes 524320 | tf_op jit(solution)/shard_map/ppermute | solution.py:26
  48.8 1.5 %collective-permute-start.9 = (bf16[256,1024]{1,0:T(8,128)(2,1)S(1)}, bf16[256,1024]{1,0:T(8,128)(2,1)S(1)}, u32[]{:S(2)}, u32[]{:S(2)}) collective-permute-start(bf16[256,1024]{1,0:T(8,128)(2,1)S(1)} %copy-done), channel_id=1, source_target_pairs={{0,2},{1,3},{2,0},{3,1},{4,6},{5,7},{6,4},{7,5},{8,10},{9,11},{10,... | collective-permute-start | bytes 1572872 | tf_op jit(solution)/shard_map/ppermute | solution.py:26
  50.3 1.9 %collective-permute-done.13.refs_6_.last.p3 = bf16[4,128,1024]{2,1,0:T(8,128)(2,1)S(1)} collective-permute-done((bf16[4,128,1024]{2,1,0:T(8,128)(2,1)S(1)}, bf16[4,128,1024]{2,1,0:T(8,128)(2,1)S(1)}, u32[]{:S(2)}, u32[]{:S(2)}) %collective-permute-start.13) | collective-permute-done | bytes 1048608 | tf_op jit(solution)/shard_map/ppermute | solution.py:26
  52.3 0.7 shard_map.31
  52.9 1.6 %collective-permute-start.14 = (bf16[2,128,1024]{2,1,0:T(8,128)(2,1)S(1)}, bf16[2,128,1024]{2,1,0:T(8,128)(2,1)S(1)}, u32[]{:S(2)}, u32[]{:S(2)}) collective-permute-start(bf16[2,128,1024]{2,1,0:T(8,128)(2,1)S(1)} %get-tuple-element.61), channel_id=1, source_target_pairs={{0,96},{1,97},{2,98},{3,99},{4,100},{5,101},{6,102},{7,103},{8,104... | collective-permute-start | bytes 1572872 | tf_op jit(solution)/shard_map/ppermute | solution.py:26
  54.5 0.5 collective-permute-start.15
  55.0 4.5 %collective-permute-done.9.refs_2_ = bf16[256,1024]{1,0:T(8,128)(2,1)S(1)} collective-permute-done((bf16[256,1024]{1,0:T(8,128)(2,1)S(1)}, bf16[256,1024]{1,0:T(8,128)(2,1)S(1)}, u32[]{:S(2)}, u32[]{:S(2)}) %collective-permute-start.9) | collective-permute-done | bytes 524320 | tf_op jit(solution)/shard_map/ppermute | solution.py:26
  59.5 0.7 shard_map.34
  60.2 3.4 %collective-permute-start.17 = (bf16[2,128,1024]{2,1,0:T(8,128)(2,1)S(1)}, bf16[2,128,1024]{2,1,0:T(8,128)(2,1)S(1)}, u32[]{:S(2)}, u32[]{:S(2)}) collective-permute-start(bf16[2,128,1024]{2,1,0:T(8,128)(2,1)S(1)} %get-tuple-element.63), channel_id=1, source_target_pairs={{0,24},{1,25},{2,26},{3,27},{4,28},{5,29},{6,30},{7,31},{8,0},{9,1... | collective-permute-start | bytes 1572872 | tf_op jit(solution)/shard_map/ppermute | solution.py:26
  63.6 0.0 collective-permute-start.18
  63.6 7.7 %shard_map.30 = (f32[4,4,512,128]{3,2,1,0:T(8,128)S(1)}, bf16[2,512,1024]{2,1,0:T(8,128)(2,1)S(1)}) custom-call(s32[5]{0:T(128)S(1)} %stack.23.at, bf16[256,1024]{1,0:T(8,128)(2,1)S(1)} %copy-done, bf16[256,1024]{1,0:T(8,128)(2,1)S(1)} %collective-permute-done.6.refs_1_, bf16[256,1024]{1,0:T(8,128)(2,1)S(1)} %collective-permute-done.9.refs_2_, ...), custom_call_target="tpu_custom_call" | custom-call | flops 3221225472 | bytes 14680084 | tf_op jit(solution)/shard_map/pallas_call | solution.py:76
  71.3 1.8 %shard_map.33 = f32[2,4,512,128]{3,2,1,0:T(8,128)S(1)} custom-call(s32[5]{0:T(128)S(1)} %stack.23.at, bf16[2,512,1024]{2,1,0:T(8,128)(2,1)S(1)} %get-tuple-element.59.x, f32[4,4,512,128]{3,2,1,0:T(8,128)S(1)} %get-tuple-element.60.acc, bf16[2,128,1024]{2,1,0:T(8,128)(2,1)S(1)} %collective-permute-done.14.n_a.p2_a, ...), custom_call_target="tpu_custom_call" | custom-call | flops 26843545600 | bytes 9437204 | tf_op jit(solution)/shard_map/pallas_call | solution.py:76
  73.1 0.1 collective-permute-start.16
  73.2 0.8 collective-permute-done.18.f_b.p2_b
  74.0 2.2 %shard_map.35 = (f32[2,512,128]{2,1,0:T(8,128)S(1)}, f32[2,512,128]{2,1,0:T(8,128)S(1)}) custom-call(s32[5]{0:T(128)S(1)} %stack.23.at, bf16[2,512,1024]{2,1,0:T(8,128)(2,1)S(1)} %get-tuple-element.59.x, bf16[2,128,1024]{2,1,0:T(8,128)(2,1)S(1)} %collective-permute-done.17.f_a.p2_a, bf16[2,128,1024]{2,1,0:T(8,128)(2,1)S(1)} %collective-permute-done.18.f_b.p2_b), custom_call_target="tpu_custom_call" | custom-call | flops 536870912 | bytes 4194324 | tf_op jit(solution)/shard_map/pallas_call | solution.py:76
  76.2 0.1 collective-permute-start.19
  76.3 0.8 shard_map.32
  77.1 1.1 collective-permute-done.19.far_got
  78.2 2.2 %shard_map.36 = (f32[8,512,128]{2,1,0:T(8,128)S(1)}, f32[8,1,512]{2,1,0:T(1,128)S(1)}) custom-call(s32[5]{0:T(128)S(1)} %stack.23.at, f32[8,512,128]{2,1,0:T(8,128)S(1)} %bitcast.12, f32[8,512,128]{2,1,0:T(8,128)S(1)} %collective-permute-done.16.got, f32[2,512,128]{2,1,0:T(8,128)S(1)} %get-tuple-element.65.far_keep, ...), custom_call_target="tpu_custom_call" | custom-call | bytes 7356436 | tf_op jit(solution)/shard_map/pallas_call | solution.py:76
  80.4 8.5 %all_to_all.20.came = f32[8,1,512]{2,1,0:T(1,128)S(1)} all-to-all(f32[8,1,512]{2,1,0:T(1,128)S(1)} %get-tuple-element.67), channel_id=1, replica_groups=mesh['z'=4,'y'=4,'l'=2,'h'=2,'c'=2] {'l','h','c'}, dimensions={0} | all-to-all | bytes 32768 | tf_op jit(solution)/shard_map/all_to_all | solution.py:459
  88.9 1.3 shard_map.37
  90.2 12.4 %all_to_all.21.came = f32[16,8,128]{2,1,0:T(8,128)S(1)} all-to-all(f32[16,8,128]{2,1,0:T(8,128)S(1)} %get-tuple-element.69), channel_id=1, replica_groups=mesh['z'=4,'y'=4,'l'=2,'h'=2,'c'=2] {'z','y'}, dimensions={0} | all-to-all | bytes 131072 | tf_op jit(solution)/shard_map/all_to_all | solution.py:459
  102.6 1.3 shard_map.38
  103.8 0.0 collective-permute-start.20
  103.9 7.7 %all_to_all.22.came = f32[8,1,512]{2,1,0:T(1,128)S(1)} all-to-all(f32[8,1,512]{2,1,0:T(1,128)S(1)} %get-tuple-element.71), channel_id=1, replica_groups=mesh['z'=4,'y'=4,'l'=2,'h'=2,'c'=2] {'l','h','c'}, dimensions={0} | all-to-all | bytes 32768 | tf_op jit(solution)/shard_map/all_to_all | solution.py:459
  111.6 0.9 shard_map.39
  112.5 11.2 %all_to_all.23.came = f32[32,8,128]{2,1,0:T(8,128)S(1)} all-to-all(f32[32,8,128]{2,1,0:T(8,128)S(1)} %get-tuple-element.73), channel_id=1, replica_groups=mesh['z'=4,'y'=4,'l'=2,'h'=2,'c'=2] {'z','y','c'}, dimensions={0} | all-to-all | bytes 262144 | tf_op jit(solution)/shard_map/all_to_all | solution.py:459
  123.7 1.0 shard_map.40
  124.7 2.1 %shard_map.43 = (bf16[144,1024]{1,0:T(8,128)(2,1)S(1)}, bf16[144,1024]{1,0:T(8,128)(2,1)S(1)}) custom-call(s32[5]{0:T(128)S(1)} %stack.23.at, bf16[4,4,512,128]{3,2,1,0:T(8,128)(2,1)S(1)} %bitcast.8, bf16[4,128,1024]{2,1,0:T(8,128)(2,1)S(1)} %shard_map.28.refs_7_.p0, bf16[4,128,1024]{2,1,0:T(8,128)(2,1)S(1)} %collective-permute-done.7.refs_8_.next_.p1, ...), custom_call_target="tpu_custom_call" | custom-call | flops 2147483648 | bytes 6881300 | tf_op jit(solution)/shard_map/pallas_call | solution.py:76
  126.8 1.2 collective-permute-start.22
  128.0 0.0 collective-permute-start.24
  128.0 2.1 %shard_map.42 = (bf16[128,1024]{1,0:T(8,128)(2,1)S(1)}, f32[128,1024]{1,0:T(8,128)S(1)}, f32[8,256]{1,0:T(8,128)S(1)}) custom-call(s32[5]{0:T(128)S(1)} %stack.23.at, bf16[4,4,512,128]{3,2,1,0:T(8,128)(2,1)S(1)} %bitcast.9, bf16[4,128,1024]{2,1,0:T(8,128)(2,1)S(1)} %shard_map.29.refs_4_.p0, ...), custom_call_target="tpu_custom_call" | custom-call | flops 2147483648 | bytes 7086100 | tf_op jit(solution)/shard_map/pallas_call | solution.py:76
  130.1 2.1 %collective-permute-start.21 = (bf16[128,1024]{1,0:T(8,128)(2,1)S(1)}, bf16[128,1024]{1,0:T(8,128)(2,1)S(1)}, u32[]{:S(2)}, u32[]{:S(2)}) collective-permute-start(bf16[128,1024]{1,0:T(8,128)(2,1)S(1)} %get-tuple-element.77), channel_id=1, source_target_pairs={{0,4},{1,5},{2,6},{3,7},{4,0},{5,1},{6,2},{7,3},{8,12},{9,13},{10,... | collective-permute-start | bytes 786440 | tf_op jit(solution)/shard_map/ppermute | solution.py:26
  132.2 2.1 %shard_map.45 = (bf16[128,1024]{1,0:T(8,128)(2,1)S(1)}, f32[128,1024]{1,0:T(8,128)S(1)}, f32[8,256]{1,0:T(8,128)S(1)}) custom-call(s32[5]{0:T(128)S(1)} %stack.23.at, bf16[4,4,512,128]{3,2,1,0:T(8,128)(2,1)S(1)} %bitcast.10, bf16[4,128,1024]{2,1,0:T(8,128)(2,1)S(1)} %shard_map.28.refs_7_.p0, ...), custom_call_target="tpu_custom_call" | custom-call | flops 2147483648 | bytes 7086100 | tf_op jit(solution)/shard_map/pallas_call | solution.py:76
  134.3 2.1 %collective-permute-start.26 = (bf16[128,1024]{1,0:T(8,128)(2,1)S(1)}, bf16[128,1024]{1,0:T(8,128)(2,1)S(1)}, u32[]{:S(2)}, u32[]{:S(2)}) collective-permute-start(bf16[128,1024]{1,0:T(8,128)(2,1)S(1)} %get-tuple-element.84), channel_id=1, source_target_pairs={{0,6},{1,7},{2,4},{3,5},{4,2},{5,3},{6,0},{7,1},{8,14},{9,15},{10,... | collective-permute-start | bytes 786440 | tf_op jit(solution)/shard_map/ppermute | solution.py:26
  136.4 0.7 collective-permute-done.22.came
  137.1 0.6 shard_map.44
  137.7 0.1 collective-permute-start.23
  137.8 0.1 collective-permute-done.24.came
  137.9 0.6 shard_map.46
  138.5 2.1 %collective-permute-start.25 = (bf16[144,1024]{1,0:T(8,128)(2,1)S(1)}, bf16[144,1024]{1,0:T(8,128)(2,1)S(1)}, u32[]{:S(2)}, u32[]{:S(2)}) collective-permute-start(bf16[144,1024]{1,0:T(8,128)(2,1)S(1)} %shard_map.46), channel_id=1, source_target_pairs={{0,6},{1,7},{2,4},{3,5},{4,2},{5,3},{6,0},{7,1},{8,14},{9,15},{10,... | collective-permute-start | bytes 884744 | tf_op jit(solution)/shard_map/ppermute | solution.py:26
  140.7 2.1 %shard_map.41 = (f32[256,1024]{1,0:T(8,128)S(1)}, f32[8,256]{1,0:T(8,128)S(1)}) custom-call(s32[5]{0:T(128)S(1)} %stack.23.at, bf16[4,4,512,128]{3,2,1,0:T(8,128)(2,1)S(1)} %bitcast.11, bf16[4,128,1024]{2,1,0:T(8,128)(2,1)S(1)} %shard_map.29.refs_4_.p0, bf16[4,128,1024]{2,1,0:T(8,128)(2,1)S(1)} %collective-permute-done.12.refs_5_.next_.p1, ...), custom_call_target="tpu_custom_call" | custom-call | flops 17179869184 | bytes 7348244 | tf_op jit(solution)/shard_map/pallas_call | solution.py:76
  142.8 0.8 collective-permute-done.21.l_low
  143.6 0.9 collective-permute-done.26.lh_high
  144.5 4.2 %collective-permute-done.23.l_high = bf16[144,1024]{1,0:T(8,128)(2,1)S(1)} collective-permute-done((bf16[144,1024]{1,0:T(8,128)(2,1)S(1)}, bf16[144,1024]{1,0:T(8,128)(2,1)S(1)}, u32[]{:S(2)}, u32[]{:S(2)}) %collective-permute-start.23) | collective-permute-done | bytes 294944 | tf_op jit(solution)/shard_map/ppermute | solution.py:26
  148.7 0.7 collective-permute-done.25.lh_low
  149.4 1.7 %shard_map.47 = bf16[256,1024]{1,0:T(8,128)(2,1)} custom-call(s32[5]{0:T(128)S(1)} %stack.23.at, f32[256,1024]{1,0:T(8,128)S(1)} %get-tuple-element.75.own, f32[8,256]{1,0:T(8,128)S(1)} %get-tuple-element.76.own_total, bf16[128,1024]{1,0:T(8,128)(2,1)S(1)} %collective-permute-done.21.l_low, bf16[144,1024]{1,0:T(8,128)(2,1)S(1)} %collective-permute-done.23.l_high, ...), custom_call_target="tpu_custom_call" | custom-call | bytes 2695188 | tf_op jit(solution)/shard_map/pallas_call | solution.py:76
  (18 shorter events, 0.0 us)
Async XLA Ops:
  0.0 33.2 %copy-start = (bf16[256,1024]{1,0:T(8,128)(2,1)S(1)}, bf16[256,1024]{1,0:T(8,128)(2,1)}, u32[]{:S(2)}) copy-start(bf16[256,1024]{1,0:T(8,128)(2,1)} %refs_0_) | copy-start | bytes 1572868
  1.1 9.5 %collective-permute-start.1 = (bf16[128,1024]{1,0:T(8,128)(2,1)S(1)}, bf16[128,1024]{1,0:T(8,128)(2,1)S(1)}, u32[]{:S(2)}, u32[]{:S(2)}) collective-permute-start(bf16[128,1024]{1,0:T(8,128)(2,1)S(1)} %get-tuple-element.85), channel_id=1, source_target_pairs={{0,2},{1,3},{2,0},{3,1},{4,6},{5,7},{6,4},{7,5},{8,10},{9,11},{10,... | collective-permute-start | bytes 786440 | tf_op jit(solution)/shard_map/ppermute | solution.py:26
  4.3 12.1 %collective-permute-start.10 = (bf16[128,1024]{1,0:T(8,128)(2,1)S(1)}, bf16[128,1024]{1,0:T(8,128)(2,1)S(1)}, u32[]{:S(2)}, u32[]{:S(2)}) collective-permute-start(bf16[128,1024]{1,0:T(8,128)(2,1)S(1)} %get-tuple-element.86.refs_0_), channel_id=1, source_target_pairs={{0,24},{1,25},{2,26},{3,27},{4,28},{5,29},{6,30},{7,31},{8,0},{9,1... | collective-permute-start | bytes 786440 | tf_op jit(solution)/shard_map/ppermute | solution.py:26
  7.3 12.1 %collective-permute-start = (bf16[128,1024]{1,0:T(8,128)(2,1)S(1)}, bf16[128,1024]{1,0:T(8,128)(2,1)S(1)}, u32[]{:S(2)}, u32[]{:S(2)}) collective-permute-start(bf16[128,1024]{1,0:T(8,128)(2,1)S(1)} %get-tuple-element.86.refs_0_), channel_id=1, source_target_pairs={{0,8},{1,9},{2,10},{3,11},{4,12},{5,13},{6,14},{7,15},{8,16},{9,17... | collective-permute-start | bytes 786440 | tf_op jit(solution)/shard_map/ppermute | solution.py:26
  10.6 24.7 %collective-permute-start.6 = (bf16[256,1024]{1,0:T(8,128)(2,1)}, bf16[256,1024]{1,0:T(8,128)(2,1)S(1)}, u32[]{:S(2)}, u32[]{:S(2)}) collective-permute-start(bf16[256,1024]{1,0:T(8,128)(2,1)} %refs_0_), channel_id=1, source_target_pairs={{0,4},{1,5},{2,6},{3,7},{4,0},{5,1},{6,2},{7,3},{8,12},{9,13},{10,... | collective-permute-start | bytes 1572872 | tf_op jit(solution)/shard_map/ppermute | solution.py:26
  12.3 9.0 %collective-permute-start.2 = (bf16[128,1024]{1,0:T(8,128)(2,1)S(1)}, bf16[128,1024]{1,0:T(8,128)(2,1)S(1)}, u32[]{:S(2)}, u32[]{:S(2)}) collective-permute-start(bf16[128,1024]{1,0:T(8,128)(2,1)S(1)} %collective-permute-done.1.refs_0_), channel_id=1, source_target_pairs={{0,96},{1,97},{2,98},{3,99},{4,100},{5,101},{6,102},{7,103},{8,104... | collective-permute-start | bytes 786440 | tf_op jit(solution)/shard_map/ppermute | solution.py:26
  16.4 14.1 %collective-permute-start.3 = (bf16[128,1024]{1,0:T(8,128)(2,1)S(1)}, bf16[128,1024]{1,0:T(8,128)(2,1)S(1)}, u32[]{:S(2)}, u32[]{:S(2)}) collective-permute-start(bf16[128,1024]{1,0:T(8,128)(2,1)S(1)} %collective-permute-done.1.refs_0_), channel_id=1, source_target_pairs={{0,32},{1,33},{2,34},{3,35},{4,36},{5,37},{6,38},{7,39},{8,40},{9,... | collective-permute-start | bytes 786440 | tf_op jit(solution)/shard_map/ppermute | solution.py:26
  16.4 14.1 %collective-permute-start.11 = (bf16[128,1024]{1,0:T(8,128)(2,1)S(1)}, bf16[128,1024]{1,0:T(8,128)(2,1)S(1)}, u32[]{:S(2)}, u32[]{:S(2)}) collective-permute-start(bf16[128,1024]{1,0:T(8,128)(2,1)S(1)} %collective-permute-done.10.refs_1_), channel_id=1, source_target_pairs={{0,24},{1,25},{2,26},{3,27},{4,28},{5,29},{6,30},{7,31},{8,0},{9,1... | collective-permute-start | bytes 786440 | tf_op jit(solution)/shard_map/ppermute | solution.py:26
  19.4 15.9 %collective-permute-start.5 = (bf16[128,1024]{1,0:T(8,128)(2,1)S(1)}, bf16[128,1024]{1,0:T(8,128)(2,1)S(1)}, u32[]{:S(2)}, u32[]{:S(2)}) collective-permute-start(bf16[128,1024]{1,0:T(8,128)(2,1)S(1)} %collective-permute-done.1.refs_0_), channel_id=1, source_target_pairs={{0,64},{1,65},{2,66},{3,67},{4,68},{5,69},{6,70},{7,71},{8,72},{9,... | collective-permute-start | bytes 786440 | tf_op jit(solution)/shard_map/ppermute | solution.py:26
  31.1 19.2 %collective-permute-start.12 = (bf16[4,128,1024]{2,1,0:T(8,128)(2,1)S(1)}, bf16[4,128,1024]{2,1,0:T(8,128)(2,1)S(1)}, u32[]{:S(2)}, u32[]{:S(2)}) collective-permute-start(bf16[4,128,1024]{2,1,0:T(8,128)(2,1)S(1)} %shard_map.29.refs_4_.p0), channel_id=1, source_target_pairs={{0,96},{1,97},{2,98},{3,99},{4,100},{5,101},{6,102},{7,103},{8,104... | collective-permute-start | bytes 3145736 | tf_op jit(solution)/shard_map/ppermute | solution.py:26
  31.2 21.1 %collective-permute-start.13 = (bf16[4,128,1024]{2,1,0:T(8,128)(2,1)S(1)}, bf16[4,128,1024]{2,1,0:T(8,128)(2,1)S(1)}, u32[]{:S(2)}, u32[]{:S(2)}) collective-permute-start(bf16[4,128,1024]{2,1,0:T(8,128)(2,1)S(1)} %shard_map.29.refs_4_.p0), channel_id=1, source_target_pairs={{0,32},{1,33},{2,34},{3,35},{4,36},{5,37},{6,38},{7,39},{8,40},{9,... | collective-permute-start | bytes 3145736 | tf_op jit(solution)/shard_map/ppermute | solution.py:26
  33.2 15.6 %collective-permute-start.4 = (bf16[256,1024]{1,0:T(8,128)(2,1)S(1)}, bf16[256,1024]{1,0:T(8,128)(2,1)S(1)}, u32[]{:S(2)}, u32[]{:S(2)}) collective-permute-start(bf16[256,1024]{1,0:T(8,128)(2,1)S(1)} %copy-done), channel_id=1, source_target_pairs={{0,6},{1,7},{2,4},{3,5},{4,2},{5,3},{6,0},{7,1},{8,14},{9,15},{10,... | collective-permute-start | bytes 1572872 | tf_op jit(solution)/shard_map/ppermute | solution.py:26
  36.0 23.5 %collective-permute-start.7 = (bf16[4,128,1024]{2,1,0:T(8,128)(2,1)S(1)}, bf16[4,128,1024]{2,1,0:T(8,128)(2,1)S(1)}, u32[]{:S(2)}, u32[]{:S(2)}) collective-permute-start(bf16[4,128,1024]{2,1,0:T(8,128)(2,1)S(1)} %shard_map.28.refs_7_.p0), channel_id=1, source_target_pairs={{0,24},{1,25},{2,26},{3,27},{4,28},{5,29},{6,30},{7,31},{8,0},{9,1... | collective-permute-start | bytes 3145736 | tf_op jit(solution)/shard_map/ppermute | solution.py:26
  39.0 20.5 %collective-permute-start.8 = (bf16[4,128,1024]{2,1,0:T(8,128)(2,1)S(1)}, bf16[4,128,1024]{2,1,0:T(8,128)(2,1)S(1)}, u32[]{:S(2)}, u32[]{:S(2)}) collective-permute-start(bf16[4,128,1024]{2,1,0:T(8,128)(2,1)S(1)} %shard_map.28.refs_7_.p0), channel_id=1, source_target_pairs={{0,8},{1,9},{2,10},{3,11},{4,12},{5,13},{6,14},{7,15},{8,16},{9,17... | collective-permute-start | bytes 3145736 | tf_op jit(solution)/shard_map/ppermute | solution.py:26
  48.8 10.7 %collective-permute-start.9 = (bf16[256,1024]{1,0:T(8,128)(2,1)S(1)}, bf16[256,1024]{1,0:T(8,128)(2,1)S(1)}, u32[]{:S(2)}, u32[]{:S(2)}) collective-permute-start(bf16[256,1024]{1,0:T(8,128)(2,1)S(1)} %copy-done), channel_id=1, source_target_pairs={{0,2},{1,3},{2,0},{3,1},{4,6},{5,7},{6,4},{7,5},{8,10},{9,11},{10,... | collective-permute-start | bytes 1572872 | tf_op jit(solution)/shard_map/ppermute | solution.py:26
  52.9 18.3 %collective-permute-start.14 = (bf16[2,128,1024]{2,1,0:T(8,128)(2,1)S(1)}, bf16[2,128,1024]{2,1,0:T(8,128)(2,1)S(1)}, u32[]{:S(2)}, u32[]{:S(2)}) collective-permute-start(bf16[2,128,1024]{2,1,0:T(8,128)(2,1)S(1)} %get-tuple-element.61), channel_id=1, source_target_pairs={{0,96},{1,97},{2,98},{3,99},{4,100},{5,101},{6,102},{7,103},{8,104... | collective-permute-start | bytes 1572872 | tf_op jit(solution)/shard_map/ppermute | solution.py:26
  54.5 16.8 %collective-permute-start.15 = (bf16[2,128,1024]{2,1,0:T(8,128)(2,1)S(1)}, bf16[2,128,1024]{2,1,0:T(8,128)(2,1)S(1)}, u32[]{:S(2)}, u32[]{:S(2)}) collective-permute-start(bf16[2,128,1024]{2,1,0:T(8,128)(2,1)S(1)} %get-tuple-element.62), channel_id=1, source_target_pairs={{0,32},{1,33},{2,34},{3,35},{4,36},{5,37},{6,38},{7,39},{8,40},{9,... | collective-permute-start | bytes 1572872 | tf_op jit(solution)/shard_map/ppermute | solution.py:26
  60.2 13.0 %collective-permute-start.17 = (bf16[2,128,1024]{2,1,0:T(8,128)(2,1)S(1)}, bf16[2,128,1024]{2,1,0:T(8,128)(2,1)S(1)}, u32[]{:S(2)}, u32[]{:S(2)}) collective-permute-start(bf16[2,128,1024]{2,1,0:T(8,128)(2,1)S(1)} %get-tuple-element.63), channel_id=1, source_target_pairs={{0,24},{1,25},{2,26},{3,27},{4,28},{5,29},{6,30},{7,31},{8,0},{9,1... | collective-permute-start | bytes 1572872 | tf_op jit(solution)/shard_map/ppermute | solution.py:26
  63.6 10.4 %collective-permute-start.18 = (bf16[2,128,1024]{2,1,0:T(8,128)(2,1)S(1)}, bf16[2,128,1024]{2,1,0:T(8,128)(2,1)S(1)}, u32[]{:S(2)}, u32[]{:S(2)}) collective-permute-start(bf16[2,128,1024]{2,1,0:T(8,128)(2,1)S(1)} %get-tuple-element.64), channel_id=1, source_target_pairs={{0,8},{1,9},{2,10},{3,11},{4,12},{5,13},{6,14},{7,15},{8,16},{9,17... | collective-permute-start | bytes 1572872 | tf_op jit(solution)/shard_map/ppermute | solution.py:26
  73.1 5.1 %collective-permute-start.16 = (f32[8,512,128]{2,1,0:T(8,128)S(1)}, f32[8,512,128]{2,1,0:T(8,128)S(1)}, u32[]{:S(2)}, u32[]{:S(2)}) collective-permute-start(f32[8,512,128]{2,1,0:T(8,128)S(1)} %bitcast.13), channel_id=1, source_target_pairs={{0,1},{1,0},{2,3},{3,2},{4,5},{5,4},{6,7},{7,6},{8,9},{9,8},{10,11... | collective-permute-start | bytes 6291464 | tf_op jit(solution)/shard_map/ppermute | solution.py:26
  76.2 2.0 %collective-permute-start.19 = (f32[2,512,128]{2,1,0:T(8,128)S(1)}, f32[2,512,128]{2,1,0:T(8,128)S(1)}, u32[]{:S(2)}, u32[]{:S(2)}) collective-permute-start(f32[2,512,128]{2,1,0:T(8,128)S(1)} %get-tuple-element.66), channel_id=1, source_target_pairs={{0,1},{1,0},{2,3},{3,2},{4,5},{5,4},{6,7},{7,6},{8,9},{9,8},{10,11... | collective-permute-start | bytes 1572872 | tf_op jit(solution)/shard_map/ppermute | solution.py:26
  103.8 19.9 %collective-permute-start.20 = (f32[8,512,128]{2,1,0:T(8,128)S(1)}, f32[8,512,128]{2,1,0:T(8,128)S(1)}, u32[]{:S(2)}, u32[]{:S(2)}) collective-permute-start(f32[8,512,128]{2,1,0:T(8,128)S(1)} %get-tuple-element.72.plan), channel_id=1, source_target_pairs={{0,1},{1,0},{2,3},{3,2},{4,5},{5,4},{6,7},{7,6},{8,9},{9,8},{10,11... | collective-permute-start | bytes 6291464 | tf_op jit(solution)/shard_map/ppermute | solution.py:26
  126.8 10.3 %collective-permute-start.22 = (bf16[144,1024]{1,0:T(8,128)(2,1)S(1)}, bf16[144,1024]{1,0:T(8,128)(2,1)S(1)}, u32[]{:S(2)}, u32[]{:S(2)}) collective-permute-start(bf16[144,1024]{1,0:T(8,128)(2,1)S(1)} %get-tuple-element.80), channel_id=1, source_target_pairs={{0,6},{1,7},{2,4},{3,5},{4,2},{5,3},{6,0},{7,1},{8,14},{9,15},{10,... | collective-permute-start | bytes 884744 | tf_op jit(solution)/shard_map/ppermute | solution.py:26
  128.0 9.9 %collective-permute-start.24 = (bf16[144,1024]{1,0:T(8,128)(2,1)S(1)}, bf16[144,1024]{1,0:T(8,128)(2,1)S(1)}, u32[]{:S(2)}, u32[]{:S(2)}) collective-permute-start(bf16[144,1024]{1,0:T(8,128)(2,1)S(1)} %get-tuple-element.83), channel_id=1, source_target_pairs={{0,4},{1,5},{2,6},{3,7},{4,0},{5,1},{6,2},{7,3},{8,12},{9,13},{10,... | collective-permute-start | bytes 884744 | tf_op jit(solution)/shard_map/ppermute | solution.py:26
  130.1 13.4 %collective-permute-start.21 = (bf16[128,1024]{1,0:T(8,128)(2,1)S(1)}, bf16[128,1024]{1,0:T(8,128)(2,1)S(1)}, u32[]{:S(2)}, u32[]{:S(2)}) collective-permute-start(bf16[128,1024]{1,0:T(8,128)(2,1)S(1)} %get-tuple-element.77), channel_id=1, source_target_pairs={{0,4},{1,5},{2,6},{3,7},{4,0},{5,1},{6,2},{7,3},{8,12},{9,13},{10,... | collective-permute-start | bytes 786440 | tf_op jit(solution)/shard_map/ppermute | solution.py:26
  134.3 10.2 %collective-permute-start.26 = (bf16[128,1024]{1,0:T(8,128)(2,1)S(1)}, bf16[128,1024]{1,0:T(8,128)(2,1)S(1)}, u32[]{:S(2)}, u32[]{:S(2)}) collective-permute-start(bf16[128,1024]{1,0:T(8,128)(2,1)S(1)} %get-tuple-element.84), channel_id=1, source_target_pairs={{0,6},{1,7},{2,4},{3,5},{4,2},{5,3},{6,0},{7,1},{8,14},{9,15},{10,... | collective-permute-start | bytes 786440 | tf_op jit(solution)/shard_map/ppermute | solution.py:26
  137.7 11.0 %collective-permute-start.23 = (bf16[144,1024]{1,0:T(8,128)(2,1)S(1)}, bf16[144,1024]{1,0:T(8,128)(2,1)S(1)}, u32[]{:S(2)}, u32[]{:S(2)}) collective-permute-start(bf16[144,1024]{1,0:T(8,128)(2,1)S(1)} %shard_map.44), channel_id=1, source_target_pairs={{0,4},{1,5},{2,6},{3,7},{4,0},{5,1},{6,2},{7,3},{8,12},{9,13},{10,... | collective-permute-start | bytes 884744 | tf_op jit(solution)/shard_map/ppermute | solution.py:26
  138.5 10.8 %collective-permute-start.25 = (bf16[144,1024]{1,0:T(8,128)(2,1)S(1)}, bf16[144,1024]{1,0:T(8,128)(2,1)S(1)}, u32[]{:S(2)}, u32[]{:S(2)}) collective-permute-start(bf16[144,1024]{1,0:T(8,128)(2,1)S(1)} %shard_map.46), channel_id=1, source_target_pairs={{0,6},{1,7},{2,4},{3,5},{4,2},{5,3},{6,0},{7,1},{8,14},{9,15},{10,... | collective-permute-start | bytes 884744 | tf_op jit(solution)/shard_map/ppermute | solution.py:26

commit v6 on v3

--- a/solution.py
+++ b/solution.py
@@ -198,12 +198,21 @@
 
 def third_kernel(at, x, f_a, f_b, keep, give, held, sems):
     copies = started(sems, *((p, held.at[n]) for n, p in enumerate((f_a, f_b))))
-    for copy in copies:
+    for n, copy in enumerate(copies):
         copy.wait()
-    for block in range(4):
-        r = lax.rem(2 * at[4] + block - at[0] + 4, 4)
-        noise = held[r // 2, lax.rem(r, 2)]
-        (keep, give)[block // 2][block % 2] = cross(x[1], noise) - half_squares(noise)
+        noise = flat(held[n])
+        value = cross(x[1], noise) - half_squares(noise)
+        for side in range(2):
+            block, _ = far_place(at, 2, 2 * n + side)
+            part = value[:, 128 * side : 128 * side + 128]
+
+            @pl.when(block < 2)
+            def _():
+                keep[block] = part
+
+            @pl.when(block >= 2)
+            def _():
+                give[block - 2] = part
 
 
 def weights_of(at, weights, place, own_rows):
@@ -230,7 +239,17 @@
     return sum(dot(w, flat(p[:, :, span])) for w, p in zip(parts, noise))
 
 
-def target_1_kernel(at, weights, p0, p1, p3, p2_a, p2_b, low, high):
+def target_1_kernel(
+    least, at, came, plan, other, row_scale, p0, p1, p3, p2_a, p2_b, weights, low, high
+):
+    c = at[4]
+    mine = sum(came[2 * n + c] for n in range(came.shape[0] // 2))
+    theirs = sum(came[2 * n + 1 - c] for n in range(came.shape[0] // 2))
+    for half, (values, total) in enumerate(((plan, mine), (other, theirs))):
+        scale = 1.0 / jnp.maximum(total, least)
+        for b in range(values.shape[0]):
+            value = values[b] * row_scale[...] * scale[b : b + 1]
+            weights[2 * half + b // 4, b % 4] = value.astype(weights.dtype)
     parts, total = weights_of(at, weights, far_place, True)
     mid = low.shape[0] - 16
     for first in range(0, p0.shape[-1], STEP):
@@ -275,7 +294,7 @@
 def last_kernel(at, own, own_total, l_low, l_high, lh_low, lh_high, out):
     mid = own.shape[0] // 2
     terms = [m[mid:, : 2 * mid] for m in (l_high, lh_low)]
-    total = to_rows(jnp.concatenate([terms_in_rows(own_total[:1])] + terms, axis=0))
+    total = 1.0 / to_rows(jnp.concatenate([terms_in_rows(own_total[:1])] + terms, axis=0))
     for n, messages in enumerate(((l_low, lh_low), (l_high, lh_high))):
         here = slice(n * mid, n * mid + mid)
         for column in range(0, own.shape[1], 128):
@@ -283,27 +302,29 @@
             value = own[here, span]
             for m in messages:
                 value = value + m[:mid, span].astype(jnp.float32)
-            out[here, span] = (value / total[here]).astype(out.dtype)
-
-
-TILE = 64
+            out[here, span] = (value * total[here]).astype(out.dtype)
+
+
+TILE = 32
 
 
 def rows_1_kernel(scale, at, keep, got, far_keep, far_got, score, sent, tops, sums):
-    blocks = keep.shape[0]
     late = lax.rem(at[1] + 2, 4)
+    scales = [jnp.where(late == j, scale, 0.0) for j in range(4)]
 
     @pl.loop(0, keep.shape[1] // TILE)
     def _(t):
         here = pl.ds(pl.multiple_of(t * TILE, TILE), TILE)
-        for b in range(blocks):
-            score[b, here] = (keep[b, here] + got[b, here]) * scale
-        for b in range(2):
-            score[4 * b + late, here] += (far_keep[b, here] + far_got[b, here]) * scale
-        top = functools.reduce(jnp.maximum, [score[b, here] for b in range(blocks)])
+        far = [far_keep[b, here] + far_got[b, here] for b in range(2)]
+        values = []
+        for b in range(keep.shape[0]):
+            value = (keep[b, here] + got[b, here]) * scale + far[b // 4] * scales[b % 4]
+            score[b, here] = value
+            values.append(value)
+        top = functools.reduce(jnp.maximum, values)
         top = jnp.broadcast_to(jnp.max(top, axis=1, keepdims=True), top.shape)
         tops[here] = top
-        sums[here] = sum(jnp.exp(score[b, here] - top) for b in range(blocks))
+        sums[here] = sum(jnp.exp(value - top) for value in values)
 
     log_row = first_lanes(tops[...]) + jnp.log(lane_sums(sums[...]))
     for n in range(sent.shape[0]):
@@ -354,17 +375,6 @@
         sent[n] = sums
 
 
-def weights_kernel(least, at, came, plan, other, row_scale, weights):
-    c = at[4]
-    mine = sum(came[2 * n + c] for n in range(came.shape[0] // 2))
-    theirs = sum(came[2 * n + 1 - c] for n in range(came.shape[0] // 2))
-    for half, (values, total) in enumerate(((plan, mine), (other, theirs))):
-        scale = 1.0 / jnp.maximum(total, least)
-        for b in range(values.shape[0]):
-            value = values[b] * row_scale[...] * scale[b : b + 1]
-            weights[values.shape[0] * half + b] = value.astype(weights.dtype)
-
-
 def per_device(data_rows, noise_rows):
     z, y, l, h, c = (lax.axis_index(name) for name in AXES)
     rows, part = data_rows.shape
@@ -482,18 +492,14 @@
     row_scale, sent = call(
         kernel, [float32(*tall), col_sent], 0, at, exchange(sent, row_axes), plan
     )
-    kernel = functools.partial(weights_kernel, least)
-    (weights,) = call(
-        kernel,
-        [bfloat16(16, *blocks[1:])],
-        0,
-        *(at, exchange(sent, ("z", "y", "c")), plan, plan_other, row_scale),
-    )
-    weights = weights.reshape(4, 4, *blocks[1:])
-
     near_noise, far_noise = (*nears, *near_two), (*fars, *far_two)
     message = bfloat16(mid + 16, part)
-    low, high = call(target_1_kernel, [message] * 2, 8 * one, at, weights, *far_noise)
+    weights, low, high = call(
+        functools.partial(target_1_kernel, least),
+        [bfloat16(4, 4, *blocks[1:]), message, message],
+        8 * one,
+        *(at, exchange(sent, ("z", "y", "c")), plan, plan_other, row_scale, *far_noise),
+    )
     low, high = flip(low, "l"), flip(high, "lh")
 
     def other_rows(place, half, came, names):

time: 148 us -> 148 us (level)
    pallas_call x20 -> x19, Pallas kernels: 32.9 us -> 33.3 us  [call(): pl.pallas_call(kernel, out_shape=outs, in_specs=[pl.BlockSpec(memory_spac...]
where the time goes in v6:
time: 148 us
  starting transfers between devices  41.5 us (28%)
  blocking collectives  39.7 us (27%)
  Pallas kernels  33.3 us (22%)
  waiting for transfers between devices  32.2 us (22%)
    ppermute x27, starting transfers between devices, move(): return lax.ppermute(value, AXES, pairs)  41.5 us
    all_to_all x4, blocking collectives, exchange(): return lax.all_to_all(sent, axes, 0, 0, tiled=True)  39.7 us
    pallas_call x19, Pallas kernels, call(): pl.pallas_call(kernel, out_shape=outs, in_specs=[pl.BlockSpec(memory_spac...  33.3 us
    ppermute x27, waiting for transfers between devices, move(): return lax.ppermute(value, AXES, pairs)  32.2 us
  transfers between devices with their start and end apart: 27, of which 15 were waited for; matrix products, arithmetic and copies ran while one was open for 0% of the time, Pallas kernels for 16%

profile of v6, /device:TPU:0, one launch (start us, length us, event | category | flops | bytes accessed | tf_op | source)
XLA Modules:
  0.0 148.0 jit_solution(7235840837680817565)
XLA Ops:
  0.0 1.1 constant_dynamic-slice_fusion
  1.1 3.2 %collective-permute-start.1 = (bf16[128,1024]{1,0:T(8,128)(2,1)S(1)}, bf16[128,1024]{1,0:T(8,128)(2,1)S(1)}, u32[]{:S(2)}, u32[]{:S(2)}) collective-permute-start(bf16[128,1024]{1,0:T(8,128)(2,1)S(1)} %get-tuple-element.83), channel_id=1, source_target_pairs={{0,2},{1,3},{2,0},{3,1},{4,6},{5,7},{6,4},{7,5},{8,10},{9,11},{10,... | collective-permute-start | bytes 786440 | tf_op jit(solution)/shard_map/ppermute | solution.py:26
  4.3 1.6 %collective-permute-start = (bf16[128,1024]{1,0:T(8,128)(2,1)S(1)}, bf16[128,1024]{1,0:T(8,128)(2,1)S(1)}, u32[]{:S(2)}, u32[]{:S(2)}) collective-permute-start(bf16[128,1024]{1,0:T(8,128)(2,1)S(1)} %get-tuple-element.84.refs_0_), channel_id=1, source_target_pairs={{0,8},{1,9},{2,10},{3,11},{4,12},{5,13},{6,14},{7,15},{8,16},{9,17... | collective-permute-start | bytes 786440 | tf_op jit(solution)/shard_map/ppermute | solution.py:26
  5.8 1.7 %collective-permute-start.10 = (bf16[128,1024]{1,0:T(8,128)(2,1)S(1)}, bf16[128,1024]{1,0:T(8,128)(2,1)S(1)}, u32[]{:S(2)}, u32[]{:S(2)}) collective-permute-start(bf16[128,1024]{1,0:T(8,128)(2,1)S(1)} %get-tuple-element.84.refs_0_), channel_id=1, source_target_pairs={{0,24},{1,25},{2,26},{3,27},{4,28},{5,29},{6,30},{7,31},{8,0},{9,1... | collective-permute-start | bytes 786440 | tf_op jit(solution)/shard_map/ppermute | solution.py:26
  7.5 3.1 %collective-permute-done.1.refs_0_ = bf16[128,1024]{1,0:T(8,128)(2,1)S(1)} collective-permute-done((bf16[128,1024]{1,0:T(8,128)(2,1)S(1)}, bf16[128,1024]{1,0:T(8,128)(2,1)S(1)}, u32[]{:S(2)}, u32[]{:S(2)}) %collective-permute-start.1) | collective-permute-done | bytes 262176 | tf_op jit(solution)/shard_map/ppermute | solution.py:26
  10.6 4.3 %collective-permute-start.2 = (bf16[128,1024]{1,0:T(8,128)(2,1)S(1)}, bf16[128,1024]{1,0:T(8,128)(2,1)S(1)}, u32[]{:S(2)}, u32[]{:S(2)}) collective-permute-start(bf16[128,1024]{1,0:T(8,128)(2,1)S(1)} %collective-permute-done.1.refs_0_), channel_id=1, source_target_pairs={{0,96},{1,97},{2,98},{3,99},{4,100},{5,101},{6,102},{7,103},{8,104... | collective-permute-start | bytes 786440 | tf_op jit(solution)/shard_map/ppermute | solution.py:26
  14.8 0.0 collective-permute-start.3
  14.8 1.5 %collective-permute-start.5 = (bf16[256,1024]{1,0:T(8,128)(2,1)}, bf16[256,1024]{1,0:T(8,128)(2,1)S(1)}, u32[]{:S(2)}, u32[]{:S(2)}) collective-permute-start(bf16[256,1024]{1,0:T(8,128)(2,1)} %refs_0_), channel_id=1, source_target_pairs={{0,4},{1,5},{2,6},{3,7},{4,0},{5,1},{6,2},{7,3},{8,12},{9,13},{10,... | collective-permute-start | bytes 1572872 | tf_op jit(solution)/shard_map/ppermute | solution.py:26
  16.3 0.0 collective-permute-done.refs_3_
  16.3 2.1 %collective-permute-start.6 = (bf16[256,1024]{1,0:T(8,128)(2,1)}, bf16[256,1024]{1,0:T(8,128)(2,1)S(1)}, u32[]{:S(2)}, u32[]{:S(2)}) collective-permute-start(bf16[256,1024]{1,0:T(8,128)(2,1)} %refs_0_), channel_id=1, source_target_pairs={{0,6},{1,7},{2,4},{3,5},{4,2},{5,3},{6,0},{7,1},{8,14},{9,15},{10,... | collective-permute-start | bytes 1572872 | tf_op jit(solution)/shard_map/ppermute | solution.py:26
  18.4 3.0 %collective-permute-start.11 = (bf16[128,1024]{1,0:T(8,128)(2,1)S(1)}, bf16[128,1024]{1,0:T(8,128)(2,1)S(1)}, u32[]{:S(2)}, u32[]{:S(2)}) collective-permute-start(bf16[128,1024]{1,0:T(8,128)(2,1)S(1)} %collective-permute-done.10.refs_1_), channel_id=1, source_target_pairs={{0,24},{1,25},{2,26},{3,27},{4,28},{5,29},{6,30},{7,31},{8,0},{9,1... | collective-permute-start | bytes 786440 | tf_op jit(solution)/shard_map/ppermute | solution.py:26
  21.4 1.5 %collective-permute-done.3.refs_3_ = bf16[128,1024]{1,0:T(8,128)(2,1)S(1)} collective-permute-done((bf16[128,1024]{1,0:T(8,128)(2,1)S(1)}, bf16[128,1024]{1,0:T(8,128)(2,1)S(1)}, u32[]{:S(2)}, u32[]{:S(2)}) %collective-permute-start.3) | collective-permute-done | bytes 262176 | tf_op jit(solution)/shard_map/ppermute | solution.py:26
  22.9 1.7 %collective-permute-start.4 = (bf16[128,1024]{1,0:T(8,128)(2,1)S(1)}, bf16[128,1024]{1,0:T(8,128)(2,1)S(1)}, u32[]{:S(2)}, u32[]{:S(2)}) collective-permute-start(bf16[128,1024]{1,0:T(8,128)(2,1)S(1)} %collective-permute-done.2.refs_1_), channel_id=1, source_target_pairs={{0,96},{1,97},{2,98},{3,99},{4,100},{5,101},{6,102},{7,103},{8,104... | collective-permute-start | bytes 786440 | tf_op jit(solution)/shard_map/ppermute | solution.py:26
  24.7 0.1 stack.23.at
  24.8 0.6 collective-permute-done.11.refs_2_
  25.3 0.7 shard_map.29.refs_4_.p0
  26.0 3.3 %collective-permute-start.12 = (bf16[4,128,1024]{2,1,0:T(8,128)(2,1)S(1)}, bf16[4,128,1024]{2,1,0:T(8,128)(2,1)S(1)}, u32[]{:S(2)}, u32[]{:S(2)}) collective-permute-start(bf16[4,128,1024]{2,1,0:T(8,128)(2,1)S(1)} %shard_map.29.refs_4_.p0), channel_id=1, source_target_pairs={{0,96},{1,97},{2,98},{3,99},{4,100},{5,101},{6,102},{7,103},{8,104... | collective-permute-start | bytes 3145736 | tf_op jit(solution)/shard_map/ppermute | solution.py:26
  29.3 2.9 %collective-permute-done.4.refs_2_ = bf16[128,1024]{1,0:T(8,128)(2,1)S(1)} collective-permute-done((bf16[128,1024]{1,0:T(8,128)(2,1)S(1)}, bf16[128,1024]{1,0:T(8,128)(2,1)S(1)}, u32[]{:S(2)}, u32[]{:S(2)}) %collective-permute-start.4) | collective-permute-done | bytes 262176 | tf_op jit(solution)/shard_map/ppermute | solution.py:26
  32.2 0.7 shard_map.28.refs_7_.p0
  32.8 2.9 %collective-permute-start.7 = (bf16[4,128,1024]{2,1,0:T(8,128)(2,1)S(1)}, bf16[4,128,1024]{2,1,0:T(8,128)(2,1)S(1)}, u32[]{:S(2)}, u32[]{:S(2)}) collective-permute-start(bf16[4,128,1024]{2,1,0:T(8,128)(2,1)S(1)} %shard_map.28.refs_7_.p0), channel_id=1, source_target_pairs={{0,24},{1,25},{2,26},{3,27},{4,28},{5,29},{6,30},{7,31},{8,0},{9,1... | collective-permute-start | bytes 3145736 | tf_op jit(solution)/shard_map/ppermute | solution.py:26
  35.8 3.2 %collective-permute-start.9 = (bf16[256,1024]{1,0:T(8,128)(2,1)S(1)}, bf16[256,1024]{1,0:T(8,128)(2,1)S(1)}, u32[]{:S(2)}, u32[]{:S(2)}) collective-permute-start(bf16[256,1024]{1,0:T(8,128)(2,1)S(1)} %copy-done), channel_id=1, source_target_pairs={{0,2},{1,3},{2,0},{3,1},{4,6},{5,7},{6,4},{7,5},{8,10},{9,11},{10,... | collective-permute-start | bytes 1572872 | tf_op jit(solution)/shard_map/ppermute | solution.py:26
  39.0 12.4 %collective-permute-done.12.refs_5_.next_.p1 = bf16[4,128,1024]{2,1,0:T(8,128)(2,1)S(1)} collective-permute-done((bf16[4,128,1024]{2,1,0:T(8,128)(2,1)S(1)}, bf16[4,128,1024]{2,1,0:T(8,128)(2,1)S(1)}, u32[]{:S(2)}, u32[]{:S(2)}) %collective-permute-start.12) | collective-permute-done | bytes 1048608 | tf_op jit(solution)/shard_map/ppermute | solution.py:26
  51.4 0.9 collective-permute-done.13.refs_6_.last.p3
  52.3 0.7 shard_map.31
  52.9 2.5 %collective-permute-start.14 = (bf16[2,128,1024]{2,1,0:T(8,128)(2,1)S(1)}, bf16[2,128,1024]{2,1,0:T(8,128)(2,1)S(1)}, u32[]{:S(2)}, u32[]{:S(2)}) collective-permute-start(bf16[2,128,1024]{2,1,0:T(8,128)(2,1)S(1)} %get-tuple-element.58), channel_id=1, source_target_pairs={{0,96},{1,97},{2,98},{3,99},{4,100},{5,101},{6,102},{7,103},{8,104... | collective-permute-start | bytes 1572872 | tf_op jit(solution)/shard_map/ppermute | solution.py:26
  55.5 1.7 %collective-permute-done.8.refs_9_.last.p3 = bf16[4,128,1024]{2,1,0:T(8,128)(2,1)S(1)} collective-permute-done((bf16[4,128,1024]{2,1,0:T(8,128)(2,1)S(1)}, bf16[4,128,1024]{2,1,0:T(8,128)(2,1)S(1)}, u32[]{:S(2)}, u32[]{:S(2)}) %collective-permute-start.8) | collective-permute-done | bytes 1048608 | tf_op jit(solution)/shard_map/ppermute | solution.py:26
  57.2 0.7 shard_map.34
  57.9 1.6 %collective-permute-start.17 = (bf16[2,128,1024]{2,1,0:T(8,128)(2,1)S(1)}, bf16[2,128,1024]{2,1,0:T(8,128)(2,1)S(1)}, u32[]{:S(2)}, u32[]{:S(2)}) collective-permute-start(bf16[2,128,1024]{2,1,0:T(8,128)(2,1)S(1)} %get-tuple-element.60), channel_id=1, source_target_pairs={{0,24},{1,25},{2,26},{3,27},{4,28},{5,29},{6,30},{7,31},{8,0},{9,1... | collective-permute-start | bytes 1572872 | tf_op jit(solution)/shard_map/ppermute | solution.py:26
  59.5 0.5 collective-permute-start.18
  60.0 7.7 %shard_map.30 = (f32[4,4,512,128]{3,2,1,0:T(8,128)S(1)}, bf16[2,512,1024]{2,1,0:T(8,128)(2,1)S(1)}) custom-call(s32[5]{0:T(128)S(1)} %stack.23.at, bf16[256,1024]{1,0:T(8,128)(2,1)S(1)} %copy-done, bf16[256,1024]{1,0:T(8,128)(2,1)S(1)} %collective-permute-done.5.refs_1_, bf16[256,1024]{1,0:T(8,128)(2,1)S(1)} %collective-permute-done.9.refs_2_, ...), custom_call_target="tpu_custom_call" | custom-call | flops 3221225472 | bytes 14680084 | tf_op jit(solution)/shard_map/pallas_call | solution.py:76
  67.6 0.5 collective-permute-done.15.n_b.p2_b
  68.1 1.8 %shard_map.33 = f32[2,4,512,128]{3,2,1,0:T(8,128)S(1)} custom-call(s32[5]{0:T(128)S(1)} %stack.23.at, bf16[2,512,1024]{2,1,0:T(8,128)(2,1)S(1)} %get-tuple-element.56.x, f32[4,4,512,128]{3,2,1,0:T(8,128)S(1)} %get-tuple-element.57.acc, bf16[2,128,1024]{2,1,0:T(8,128)(2,1)S(1)} %collective-permute-done.14.n_a.p2_a, ...), custom_call_target="tpu_custom_call" | custom-call | flops 26843545600 | bytes 9437204 | tf_op jit(solution)/shard_map/pallas_call | solution.py:76
  69.9 0.1 collective-permute-start.16
  70.0 2.2 %shard_map.35 = (f32[2,512,128]{2,1,0:T(8,128)S(1)}, f32[2,512,128]{2,1,0:T(8,128)S(1)}) custom-call(s32[5]{0:T(128)S(1)} %stack.23.at, bf16[2,512,1024]{2,1,0:T(8,128)(2,1)S(1)} %get-tuple-element.56.x, bf16[2,128,1024]{2,1,0:T(8,128)(2,1)S(1)} %collective-permute-done.17.f_a.p2_a, bf16[2,128,1024]{2,1,0:T(8,128)(2,1)S(1)} %collective-permute-done.18.f_b.p2_b), custom_call_target="tpu_custom_call" | custom-call | flops 536870912 | bytes 4194324 | tf_op jit(solution)/shard_map/pallas_call | solution.py:76
  72.2 0.6 collective-permute-start.19
  72.8 0.8 shard_map.32
  73.6 1.3 collective-permute-done.19.far_got
  74.9 2.8 %shard_map.36 = (f32[8,512,128]{2,1,0:T(8,128)S(1)}, f32[8,1,512]{2,1,0:T(1,128)S(1)}) custom-call(s32[5]{0:T(128)S(1)} %stack.23.at, f32[8,512,128]{2,1,0:T(8,128)S(1)} %bitcast.7, f32[8,512,128]{2,1,0:T(8,128)S(1)} %collective-permute-done.16.got, f32[2,512,128]{2,1,0:T(8,128)S(1)} %get-tuple-element.62.far_keep, ...), custom_call_target="tpu_custom_call" | custom-call | bytes 7356436 | tf_op jit(solution)/shard_map/pallas_call | solution.py:76
  77.7 8.7 %all_to_all.20.came = f32[8,1,512]{2,1,0:T(1,128)S(1)} all-to-all(f32[8,1,512]{2,1,0:T(1,128)S(1)} %get-tuple-element.64), channel_id=1, replica_groups=mesh['z'=4,'y'=4,'l'=2,'h'=2,'c'=2] {'l','h','c'}, dimensions={0} | all-to-all | bytes 32768 | tf_op jit(solution)/shard_map/all_to_all | solution.py:467
  86.4 1.3 shard_map.37
  87.7 11.8 %all_to_all.21.came = f32[16,8,128]{2,1,0:T(8,128)S(1)} all-to-all(f32[16,8,128]{2,1,0:T(8,128)S(1)} %get-tuple-element.66), channel_id=1, replica_groups=mesh['z'=4,'y'=4,'l'=2,'h'=2,'c'=2] {'z','y'}, dimensions={0} | all-to-all | bytes 131072 | tf_op jit(solution)/shard_map/all_to_all | solution.py:467
  99.6 1.3 shard_map.38
  100.9 0.0 collective-permute-start.20
  100.9 7.7 %all_to_all.22.came = f32[8,1,512]{2,1,0:T(1,128)S(1)} all-to-all(f32[8,1,512]{2,1,0:T(1,128)S(1)} %get-tuple-element.68), channel_id=1, replica_groups=mesh['z'=4,'y'=4,'l'=2,'h'=2,'c'=2] {'l','h','c'}, dimensions={0} | all-to-all | bytes 32768 | tf_op jit(solution)/shard_map/all_to_all | solution.py:467
  108.6 0.9 shard_map.39
  109.5 11.4 %all_to_all.23.came = f32[32,8,128]{2,1,0:T(8,128)S(1)} all-to-all(f32[32,8,128]{2,1,0:T(8,128)S(1)} %get-tuple-element.70), channel_id=1, replica_groups=mesh['z'=4,'y'=4,'l'=2,'h'=2,'c'=2] {'z','y','c'}, dimensions={0} | all-to-all | bytes 262144 | tf_op jit(solution)/shard_map/all_to_all | solution.py:467
  121.0 2.8 %shard_map.40 = (bf16[4,4,512,128]{3,2,1,0:T(8,128)(2,1)S(1)}, bf16[144,1024]{1,0:T(8,128)(2,1)S(1)}, bf16[144,1024]{1,0:T(8,128)(2,1)S(1)}) custom-call(s32[5]{0:T(128)S(1)} %stack.23.at, f32[32,8,128]{2,1,0:T(8,128)S(1)} %all_to_all.23.came, f32[8,512,128]{2,1,0:T(8,128)S(1)} %get-tuple-element.69.plan, f32[8,512,128]{2,1,0:T(8,128)S(1)} %collective-permute-done.20.other, ...), custom_call_target="tpu_custom_call" | custom-call | flops 2147483648 | bytes 11468820 | tf_op jit(solution)/shard_map/pallas_call | solution.py:76
  123.8 1.2 collective-permute-start.22
  125.0 2.1 %shard_map.42 = (bf16[128,1024]{1,0:T(8,128)(2,1)S(1)}, f32[128,1024]{1,0:T(8,128)S(1)}, f32[8,256]{1,0:T(8,128)S(1)}) custom-call(s32[5]{0:T(128)S(1)} %stack.23.at, bf16[4,4,512,128]{3,2,1,0:T(8,128)(2,1)S(1)} %get-tuple-element.72.weights, bf16[4,128,1024]{2,1,0:T(8,128)(2,1)S(1)} %shard_map.29.refs_4_.p0, ...), custom_call_target="tpu_custom_call" | custom-call | flops 2147483648 | bytes 7086100 | tf_op jit(solution)/shard_map/pallas_call | solution.py:76
  127.1 2.1 %collective-permute-start.21 = (bf16[128,1024]{1,0:T(8,128)(2,1)S(1)}, bf16[128,1024]{1,0:T(8,128)(2,1)S(1)}, u32[]{:S(2)}, u32[]{:S(2)}) collective-permute-start(bf16[128,1024]{1,0:T(8,128)(2,1)S(1)} %get-tuple-element.75), channel_id=1, source_target_pairs={{0,4},{1,5},{2,6},{3,7},{4,0},{5,1},{6,2},{7,3},{8,12},{9,13},{10,... | collective-permute-start | bytes 786440 | tf_op jit(solution)/shard_map/ppermute | solution.py:26
  129.2 2.1 %shard_map.44 = (bf16[128,1024]{1,0:T(8,128)(2,1)S(1)}, f32[128,1024]{1,0:T(8,128)S(1)}, f32[8,256]{1,0:T(8,128)S(1)}) custom-call(s32[5]{0:T(128)S(1)} %stack.23.at, bf16[4,4,512,128]{3,2,1,0:T(8,128)(2,1)S(1)} %get-tuple-element.72.weights, bf16[4,128,1024]{2,1,0:T(8,128)(2,1)S(1)} %shard_map.28.refs_7_.p0, ...), custom_call_target="tpu_custom_call" | custom-call | flops 2147483648 | bytes 7086100 | tf_op jit(solution)/shard_map/pallas_call | solution.py:76
  131.3 2.1 %collective-permute-start.26 = (bf16[128,1024]{1,0:T(8,128)(2,1)S(1)}, bf16[128,1024]{1,0:T(8,128)(2,1)S(1)}, u32[]{:S(2)}, u32[]{:S(2)}) collective-permute-start(bf16[128,1024]{1,0:T(8,128)(2,1)S(1)} %get-tuple-element.82), channel_id=1, source_target_pairs={{0,6},{1,7},{2,4},{3,5},{4,2},{5,3},{6,0},{7,1},{8,14},{9,15},{10,... | collective-permute-start | bytes 786440 | tf_op jit(solution)/shard_map/ppermute | solution.py:26
  133.4 0.7 collective-permute-done.22.came
  134.1 0.6 shard_map.43
  134.7 0.1 collective-permute-start.23
  134.8 0.1 collective-permute-done.24.came
  134.9 0.6 shard_map.45
  135.5 2.1 %collective-permute-start.25 = (bf16[144,1024]{1,0:T(8,128)(2,1)S(1)}, bf16[144,1024]{1,0:T(8,128)(2,1)S(1)}, u32[]{:S(2)}, u32[]{:S(2)}) collective-permute-start(bf16[144,1024]{1,0:T(8,128)(2,1)S(1)} %shard_map.45), channel_id=1, source_target_pairs={{0,6},{1,7},{2,4},{3,5},{4,2},{5,3},{6,0},{7,1},{8,14},{9,15},{10,... | collective-permute-start | bytes 884744 | tf_op jit(solution)/shard_map/ppermute | solution.py:26
  137.7 2.1 %shard_map.41 = (f32[256,1024]{1,0:T(8,128)S(1)}, f32[8,256]{1,0:T(8,128)S(1)}) custom-call(s32[5]{0:T(128)S(1)} %stack.23.at, bf16[4,4,512,128]{3,2,1,0:T(8,128)(2,1)S(1)} %get-tuple-element.72.weights, bf16[4,128,1024]{2,1,0:T(8,128)(2,1)S(1)} %shard_map.29.refs_4_.p0, bf16[4,128,1024]{2,1,0:T(8,128)(2,1)S(1)} %collective-permute-done.12.refs_5_.next_.p1, ...), custom_call_target="tpu_custom_call" | custom-call | flops 17179869184 | bytes 7348244 | tf_op jit(solution)/shard_map/pallas_call | solution.py:76
  139.8 0.8 collective-permute-done.21.l_low
  140.5 0.9 collective-permute-done.26.lh_high
  141.5 4.2 %collective-permute-done.23.l_high = bf16[144,1024]{1,0:T(8,128)(2,1)S(1)} collective-permute-done((bf16[144,1024]{1,0:T(8,128)(2,1)S(1)}, bf16[144,1024]{1,0:T(8,128)(2,1)S(1)}, u32[]{:S(2)}, u32[]{:S(2)}) %collective-permute-start.23) | collective-permute-done | bytes 294944 | tf_op jit(solution)/shard_map/ppermute | solution.py:26
  145.7 0.7 collective-permute-done.25.lh_low
  146.4 1.7 %shard_map.46 = bf16[256,1024]{1,0:T(8,128)(2,1)} custom-call(s32[5]{0:T(128)S(1)} %stack.23.at, f32[256,1024]{1,0:T(8,128)S(1)} %get-tuple-element.73.own, f32[8,256]{1,0:T(8,128)S(1)} %get-tuple-element.74.own_total, bf16[128,1024]{1,0:T(8,128)(2,1)S(1)} %collective-permute-done.21.l_low, bf16[144,1024]{1,0:T(8,128)(2,1)S(1)} %collective-permute-done.23.l_high, ...), custom_call_target="tpu_custom_call" | custom-call | bytes 2695188 | tf_op jit(solution)/shard_map/pallas_call | solution.py:76
  (17 shorter events, 0.0 us)
Async XLA Ops:
  1.1 9.5 %collective-permute-start.1 = (bf16[128,1024]{1,0:T(8,128)(2,1)S(1)}, bf16[128,1024]{1,0:T(8,128)(2,1)S(1)}, u32[]{:S(2)}, u32[]{:S(2)}) collective-permute-start(bf16[128,1024]{1,0:T(8,128)(2,1)S(1)} %get-tuple-element.83), channel_id=1, source_target_pairs={{0,2},{1,3},{2,0},{3,1},{4,6},{5,7},{6,4},{7,5},{8,10},{9,11},{10,... | collective-permute-start | bytes 786440 | tf_op jit(solution)/shard_map/ppermute | solution.py:26
  4.3 12.1 %collective-permute-start = (bf16[128,1024]{1,0:T(8,128)(2,1)S(1)}, bf16[128,1024]{1,0:T(8,128)(2,1)S(1)}, u32[]{:S(2)}, u32[]{:S(2)}) collective-permute-start(bf16[128,1024]{1,0:T(8,128)(2,1)S(1)} %get-tuple-element.84.refs_0_), channel_id=1, source_target_pairs={{0,8},{1,9},{2,10},{3,11},{4,12},{5,13},{6,14},{7,15},{8,16},{9,17... | collective-permute-start | bytes 786440 | tf_op jit(solution)/shard_map/ppermute | solution.py:26
  5.8 12.6 %collective-permute-start.10 = (bf16[128,1024]{1,0:T(8,128)(2,1)S(1)}, bf16[128,1024]{1,0:T(8,128)(2,1)S(1)}, u32[]{:S(2)}, u32[]{:S(2)}) collective-permute-start(bf16[128,1024]{1,0:T(8,128)(2,1)S(1)} %get-tuple-element.84.refs_0_), channel_id=1, source_target_pairs={{0,24},{1,25},{2,26},{3,27},{4,28},{5,29},{6,30},{7,31},{8,0},{9,1... | collective-permute-start | bytes 786440 | tf_op jit(solution)/shard_map/ppermute | solution.py:26
  10.6 10.9 %collective-permute-start.2 = (bf16[128,1024]{1,0:T(8,128)(2,1)S(1)}, bf16[128,1024]{1,0:T(8,128)(2,1)S(1)}, u32[]{:S(2)}, u32[]{:S(2)}) collective-permute-start(bf16[128,1024]{1,0:T(8,128)(2,1)S(1)} %collective-permute-done.1.refs_0_), channel_id=1, source_target_pairs={{0,96},{1,97},{2,98},{3,99},{4,100},{5,101},{6,102},{7,103},{8,104... | collective-permute-start | bytes 786440 | tf_op jit(solution)/shard_map/ppermute | solution.py:26
  14.8 8.1 %collective-permute-start.3 = (bf16[128,1024]{1,0:T(8,128)(2,1)S(1)}, bf16[128,1024]{1,0:T(8,128)(2,1)S(1)}, u32[]{:S(2)}, u32[]{:S(2)}) collective-permute-start(bf16[128,1024]{1,0:T(8,128)(2,1)S(1)} %collective-permute-done.1.refs_0_), channel_id=1, source_target_pairs={{0,32},{1,33},{2,34},{3,35},{4,36},{5,37},{6,38},{7,39},{8,40},{9,... | collective-permute-start | bytes 786440 | tf_op jit(solution)/shard_map/ppermute | solution.py:26
  14.8 17.3 %collective-permute-start.5 = (bf16[256,1024]{1,0:T(8,128)(2,1)}, bf16[256,1024]{1,0:T(8,128)(2,1)S(1)}, u32[]{:S(2)}, u32[]{:S(2)}) collective-permute-start(bf16[256,1024]{1,0:T(8,128)(2,1)} %refs_0_), channel_id=1, source_target_pairs={{0,4},{1,5},{2,6},{3,7},{4,0},{5,1},{6,2},{7,3},{8,12},{9,13},{10,... | collective-permute-start | bytes 1572872 | tf_op jit(solution)/shard_map/ppermute | solution.py:26
  16.3 15.9 %collective-permute-start.6 = (bf16[256,1024]{1,0:T(8,128)(2,1)}, bf16[256,1024]{1,0:T(8,128)(2,1)S(1)}, u32[]{:S(2)}, u32[]{:S(2)}) collective-permute-start(bf16[256,1024]{1,0:T(8,128)(2,1)} %refs_0_), channel_id=1, source_target_pairs={{0,6},{1,7},{2,4},{3,5},{4,2},{5,3},{6,0},{7,1},{8,14},{9,15},{10,... | collective-permute-start | bytes 1572872 | tf_op jit(solution)/shard_map/ppermute | solution.py:26
  18.4 6.9 %collective-permute-start.11 = (bf16[128,1024]{1,0:T(8,128)(2,1)S(1)}, bf16[128,1024]{1,0:T(8,128)(2,1)S(1)}, u32[]{:S(2)}, u32[]{:S(2)}) collective-permute-start(bf16[128,1024]{1,0:T(8,128)(2,1)S(1)} %collective-permute-done.10.refs_1_), channel_id=1, source_target_pairs={{0,24},{1,25},{2,26},{3,27},{4,28},{5,29},{6,30},{7,31},{8,0},{9,1... | collective-permute-start | bytes 786440 | tf_op jit(solution)/shard_map/ppermute | solution.py:26
  22.9 9.2 %collective-permute-start.4 = (bf16[128,1024]{1,0:T(8,128)(2,1)S(1)}, bf16[128,1024]{1,0:T(8,128)(2,1)S(1)}, u32[]{:S(2)}, u32[]{:S(2)}) collective-permute-start(bf16[128,1024]{1,0:T(8,128)(2,1)S(1)} %collective-permute-done.2.refs_1_), channel_id=1, source_target_pairs={{0,96},{1,97},{2,98},{3,99},{4,100},{5,101},{6,102},{7,103},{8,104... | collective-permute-start | bytes 786440 | tf_op jit(solution)/shard_map/ppermute | solution.py:26
  24.8 11.0 %copy-start = (bf16[256,1024]{1,0:T(8,128)(2,1)S(1)}, bf16[256,1024]{1,0:T(8,128)(2,1)}, u32[]{:S(2)}) copy-start(bf16[256,1024]{1,0:T(8,128)(2,1)} %refs_0_) | copy-start | bytes 1572868
  26.0 25.4 %collective-permute-start.12 = (bf16[4,128,1024]{2,1,0:T(8,128)(2,1)S(1)}, bf16[4,128,1024]{2,1,0:T(8,128)(2,1)S(1)}, u32[]{:S(2)}, u32[]{:S(2)}) collective-permute-start(bf16[4,128,1024]{2,1,0:T(8,128)(2,1)S(1)} %shard_map.29.refs_4_.p0), channel_id=1, source_target_pairs={{0,96},{1,97},{2,98},{3,99},{4,100},{5,101},{6,102},{7,103},{8,104... | collective-permute-start | bytes 3145736 | tf_op jit(solution)/shard_map/ppermute | solution.py:26
  29.3 23.0 %collective-permute-start.13 = (bf16[4,128,1024]{2,1,0:T(8,128)(2,1)S(1)}, bf16[4,128,1024]{2,1,0:T(8,128)(2,1)S(1)}, u32[]{:S(2)}, u32[]{:S(2)}) collective-permute-start(bf16[4,128,1024]{2,1,0:T(8,128)(2,1)S(1)} %shard_map.29.refs_4_.p0), channel_id=1, source_target_pairs={{0,32},{1,33},{2,34},{3,35},{4,36},{5,37},{6,38},{7,39},{8,40},{9,... | collective-permute-start | bytes 3145736 | tf_op jit(solution)/shard_map/ppermute | solution.py:26
  32.8 22.6 %collective-permute-start.7 = (bf16[4,128,1024]{2,1,0:T(8,128)(2,1)S(1)}, bf16[4,128,1024]{2,1,0:T(8,128)(2,1)S(1)}, u32[]{:S(2)}, u32[]{:S(2)}) collective-permute-start(bf16[4,128,1024]{2,1,0:T(8,128)(2,1)S(1)} %shard_map.28.refs_7_.p0), channel_id=1, source_target_pairs={{0,24},{1,25},{2,26},{3,27},{4,28},{5,29},{6,30},{7,31},{8,0},{9,1... | collective-permute-start | bytes 3145736 | tf_op jit(solution)/shard_map/ppermute | solution.py:26
  35.8 21.4 %collective-permute-start.8 = (bf16[4,128,1024]{2,1,0:T(8,128)(2,1)S(1)}, bf16[4,128,1024]{2,1,0:T(8,128)(2,1)S(1)}, u32[]{:S(2)}, u32[]{:S(2)}) collective-permute-start(bf16[4,128,1024]{2,1,0:T(8,128)(2,1)S(1)} %shard_map.28.refs_7_.p0), channel_id=1, source_target_pairs={{0,8},{1,9},{2,10},{3,11},{4,12},{5,13},{6,14},{7,15},{8,16},{9,17... | collective-permute-start | bytes 3145736 | tf_op jit(solution)/shard_map/ppermute | solution.py:26
  35.8 19.7 %collective-permute-start.9 = (bf16[256,1024]{1,0:T(8,128)(2,1)S(1)}, bf16[256,1024]{1,0:T(8,128)(2,1)S(1)}, u32[]{:S(2)}, u32[]{:S(2)}) collective-permute-start(bf16[256,1024]{1,0:T(8,128)(2,1)S(1)} %copy-done), channel_id=1, source_target_pairs={{0,2},{1,3},{2,0},{3,1},{4,6},{5,7},{6,4},{7,5},{8,10},{9,11},{10,... | collective-permute-start | bytes 1572872 | tf_op jit(solution)/shard_map/ppermute | solution.py:26
  52.9 14.7 %collective-permute-start.14 = (bf16[2,128,1024]{2,1,0:T(8,128)(2,1)S(1)}, bf16[2,128,1024]{2,1,0:T(8,128)(2,1)S(1)}, u32[]{:S(2)}, u32[]{:S(2)}) collective-permute-start(bf16[2,128,1024]{2,1,0:T(8,128)(2,1)S(1)} %get-tuple-element.58), channel_id=1, source_target_pairs={{0,96},{1,97},{2,98},{3,99},{4,100},{5,101},{6,102},{7,103},{8,104... | collective-permute-start | bytes 1572872 | tf_op jit(solution)/shard_map/ppermute | solution.py:26
  55.5 12.6 %collective-permute-start.15 = (bf16[2,128,1024]{2,1,0:T(8,128)(2,1)S(1)}, bf16[2,128,1024]{2,1,0:T(8,128)(2,1)S(1)}, u32[]{:S(2)}, u32[]{:S(2)}) collective-permute-start(bf16[2,128,1024]{2,1,0:T(8,128)(2,1)S(1)} %get-tuple-element.59), channel_id=1, source_target_pairs={{0,32},{1,33},{2,34},{3,35},{4,36},{5,37},{6,38},{7,39},{8,40},{9,... | collective-permute-start | bytes 1572872 | tf_op jit(solution)/shard_map/ppermute | solution.py:26
  57.9 12.1 %collective-permute-start.17 = (bf16[2,128,1024]{2,1,0:T(8,128)(2,1)S(1)}, bf16[2,128,1024]{2,1,0:T(8,128)(2,1)S(1)}, u32[]{:S(2)}, u32[]{:S(2)}) collective-permute-start(bf16[2,128,1024]{2,1,0:T(8,128)(2,1)S(1)} %get-tuple-element.60), channel_id=1, source_target_pairs={{0,24},{1,25},{2,26},{3,27},{4,28},{5,29},{6,30},{7,31},{8,0},{9,1... | collective-permute-start | bytes 1572872 | tf_op jit(solution)/shard_map/ppermute | solution.py:26
  59.5 10.5 %collective-permute-start.18 = (bf16[2,128,1024]{2,1,0:T(8,128)(2,1)S(1)}, bf16[2,128,1024]{2,1,0:T(8,128)(2,1)S(1)}, u32[]{:S(2)}, u32[]{:S(2)}) collective-permute-start(bf16[2,128,1024]{2,1,0:T(8,128)(2,1)S(1)} %get-tuple-element.61), channel_id=1, source_target_pairs={{0,8},{1,9},{2,10},{3,11},{4,12},{5,13},{6,14},{7,15},{8,16},{9,17... | collective-permute-start | bytes 1572872 | tf_op jit(solution)/shard_map/ppermute | solution.py:26
  69.9 5.0 %collective-permute-start.16 = (f32[8,512,128]{2,1,0:T(8,128)S(1)}, f32[8,512,128]{2,1,0:T(8,128)S(1)}, u32[]{:S(2)}, u32[]{:S(2)}) collective-permute-start(f32[8,512,128]{2,1,0:T(8,128)S(1)} %bitcast.8), channel_id=1, source_target_pairs={{0,1},{1,0},{2,3},{3,2},{4,5},{5,4},{6,7},{7,6},{8,9},{9,8},{10,11... | collective-permute-start | bytes 6291464 | tf_op jit(solution)/shard_map/ppermute | solution.py:26
  72.2 2.7 %collective-permute-start.19 = (f32[2,512,128]{2,1,0:T(8,128)S(1)}, f32[2,512,128]{2,1,0:T(8,128)S(1)}, u32[]{:S(2)}, u32[]{:S(2)}) collective-permute-start(f32[2,512,128]{2,1,0:T(8,128)S(1)} %get-tuple-element.63), channel_id=1, source_target_pairs={{0,1},{1,0},{2,3},{3,2},{4,5},{5,4},{6,7},{7,6},{8,9},{9,8},{10,11... | collective-permute-start | bytes 1572872 | tf_op jit(solution)/shard_map/ppermute | solution.py:26
  100.9 20.1 %collective-permute-start.20 = (f32[8,512,128]{2,1,0:T(8,128)S(1)}, f32[8,512,128]{2,1,0:T(8,128)S(1)}, u32[]{:S(2)}, u32[]{:S(2)}) collective-permute-start(f32[8,512,128]{2,1,0:T(8,128)S(1)} %get-tuple-element.69.plan), channel_id=1, source_target_pairs={{0,1},{1,0},{2,3},{3,2},{4,5},{5,4},{6,7},{7,6},{8,9},{9,8},{10,11... | collective-permute-start | bytes 6291464 | tf_op jit(solution)/shard_map/ppermute | solution.py:26
  123.8 10.3 %collective-permute-start.22 = (bf16[144,1024]{1,0:T(8,128)(2,1)S(1)}, bf16[144,1024]{1,0:T(8,128)(2,1)S(1)}, u32[]{:S(2)}, u32[]{:S(2)}) collective-permute-start(bf16[144,1024]{1,0:T(8,128)(2,1)S(1)} %get-tuple-element.78), channel_id=1, source_target_pairs={{0,6},{1,7},{2,4},{3,5},{4,2},{5,3},{6,0},{7,1},{8,14},{9,15},{10,... | collective-permute-start | bytes 884744 | tf_op jit(solution)/shard_map/ppermute | solution.py:26
  125.0 9.9 %collective-permute-start.24 = (bf16[144,1024]{1,0:T(8,128)(2,1)S(1)}, bf16[144,1024]{1,0:T(8,128)(2,1)S(1)}, u32[]{:S(2)}, u32[]{:S(2)}) collective-permute-start(bf16[144,1024]{1,0:T(8,128)(2,1)S(1)} %get-tuple-element.81), channel_id=1, source_target_pairs={{0,4},{1,5},{2,6},{3,7},{4,0},{5,1},{6,2},{7,3},{8,12},{9,13},{10,... | collective-permute-start | bytes 884744 | tf_op jit(solution)/shard_map/ppermute | solution.py:26
  127.1 13.4 %collective-permute-start.21 = (bf16[128,1024]{1,0:T(8,128)(2,1)S(1)}, bf16[128,1024]{1,0:T(8,128)(2,1)S(1)}, u32[]{:S(2)}, u32[]{:S(2)}) collective-permute-start(bf16[128,1024]{1,0:T(8,128)(2,1)S(1)} %get-tuple-element.75), channel_id=1, source_target_pairs={{0,4},{1,5},{2,6},{3,7},{4,0},{5,1},{6,2},{7,3},{8,12},{9,13},{10,... | collective-permute-start | bytes 786440 | tf_op jit(solution)/shard_map/ppermute | solution.py:26
  131.3 10.2 %collective-permute-start.26 = (bf16[128,1024]{1,0:T(8,128)(2,1)S(1)}, bf16[128,1024]{1,0:T(8,128)(2,1)S(1)}, u32[]{:S(2)}, u32[]{:S(2)}) collective-permute-start(bf16[128,1024]{1,0:T(8,128)(2,1)S(1)} %get-tuple-element.82), channel_id=1, source_target_pairs={{0,6},{1,7},{2,4},{3,5},{4,2},{5,3},{6,0},{7,1},{8,14},{9,15},{10,... | collective-permute-start | bytes 786440 | tf_op jit(solution)/shard_map/ppermute | solution.py:26
  134.7 11.0 %collective-permute-start.23 = (bf16[144,1024]{1,0:T(8,128)(2,1)S(1)}, bf16[144,1024]{1,0:T(8,128)(2,1)S(1)}, u32[]{:S(2)}, u32[]{:S(2)}) collective-permute-start(bf16[144,1024]{1,0:T(8,128)(2,1)S(1)} %shard_map.43), channel_id=1, source_target_pairs={{0,4},{1,5},{2,6},{3,7},{4,0},{5,1},{6,2},{7,3},{8,12},{9,13},{10,... | collective-permute-start | bytes 884744 | tf_op jit(solution)/shard_map/ppermute | solution.py:26
  135.5 10.8 %collective-permute-start.25 = (bf16[144,1024]{1,0:T(8,128)(2,1)S(1)}, bf16[144,1024]{1,0:T(8,128)(2,1)S(1)}, u32[]{:S(2)}, u32[]{:S(2)}) collective-permute-start(bf16[144,1024]{1,0:T(8,128)(2,1)S(1)} %shard_map.45), channel_id=1, source_target_pairs={{0,6},{1,7},{2,4},{3,5},{4,2},{5,3},{6,0},{7,1},{8,14},{9,15},{10,... | collective-permute-start | bytes 884744 | tf_op jit(solution)/shard_map/ppermute | solution.py:26

commit v7 on v6

--- a/solution.py
+++ b/solution.py
@@ -154,19 +154,19 @@
     )
     for copy in copies[:4]:
         copy.wait()
+    for n, k in enumerate((0, 1, 3)):
+        copies[4 + n].wait()
+        for r in (0, 2):
+            noise = flat(held[n, r : r + 2])
+            value = cross(x[0], noise) - half_squares(noise)
+            out[near_place(at, k, r)] = value[:, :128]
+            out[near_place(at, k, r + 1)] = value[:, 128:]
     x_sq = 0.0
     for side in range(2):
         for span in range(0, x.shape[2], 128):
             wide = x[side, :, span : span + 128].astype(jnp.float32)
             x_sq = x_sq + wide * wide
     x_sq = jnp.broadcast_to(0.5 * jnp.sum(x_sq, axis=1, keepdims=True), x_sq.shape)
-    for n, k in enumerate((0, 1, 3)):
-        copies[4 + n].wait()
-        for r in (0, 2):
-            noise = flat(held[n, r : r + 2])
-            value = cross(x[0], noise) - half_squares(noise)
-            out[near_place(at, k, r)] = value[:, :128] - x_sq
-            out[near_place(at, k, r + 1)] = value[:, 128:] - x_sq
     for r in range(4):
         out[near_place(at, 2, r)] = -x_sq
     for n, k in enumerate((0, 1, 3)):
@@ -176,6 +176,9 @@
             value = cross(x[1], noise) - half_squares(noise)
             out[far_place(at, k, r)] += value[:, :128]
             out[far_place(at, k, r + 1)] += value[:, 128:]
+    for n, k in enumerate((0, 1, 3)):
+        for r in range(4):
+            out[near_place(at, k, r)] -= x_sq
 
 
 def second_kernel(half, at, x, acc, n_a, n_b, out, held, sems):
@@ -305,26 +308,32 @@
             out[here, span] = (value * total[here]).astype(out.dtype)
 
 
-TILE = 32
+TILE = 64
 
 
 def rows_1_kernel(scale, at, keep, got, far_keep, far_got, score, sent, tops, sums):
     late = lax.rem(at[1] + 2, 4)
     scales = [jnp.where(late == j, scale, 0.0) for j in range(4)]
+    blocks = range(keep.shape[0])
 
     @pl.loop(0, keep.shape[1] // TILE)
     def _(t):
         here = pl.ds(pl.multiple_of(t * TILE, TILE), TILE)
         far = [far_keep[b, here] + far_got[b, here] for b in range(2)]
-        values = []
-        for b in range(keep.shape[0]):
+        top = None
+        for b in blocks:
             value = (keep[b, here] + got[b, here]) * scale + far[b // 4] * scales[b % 4]
             score[b, here] = value
-            values.append(value)
-        top = functools.reduce(jnp.maximum, values)
-        top = jnp.broadcast_to(jnp.max(top, axis=1, keepdims=True), top.shape)
+            top = value if top is None else jnp.maximum(top, value)
         tops[here] = top
-        sums[here] = sum(jnp.exp(value - top) for value in values)
+
+    tops[...] = jnp.broadcast_to(jnp.max(tops[...], axis=1, keepdims=True), tops.shape)
+
+    @pl.loop(0, keep.shape[1] // TILE)
+    def _(t):
+        here = pl.ds(pl.multiple_of(t * TILE, TILE), TILE)
+        top = tops[here]
+        sums[here] = sum(jnp.exp(score[b, here] - top) for b in blocks)
 
     log_row = first_lanes(tops[...]) + jnp.log(lane_sums(sums[...]))
     for n in range(sent.shape[0]):
@@ -398,10 +407,11 @@
     far = flip(lax.dynamic_slice_in_dim(noise_rows, (1 - h) * mid, mid), "h")
     near_1, near_3 = from_y(near, 1), from_y(near, 3)
     far, data_rows = wave((far, data_rows))
-    data_l, data_lh = flip(data_rows, "l"), flip(data_rows, "lh")
+    data_l = flip(data_rows, "l")
     near_2 = from_y(near_1, 1)
-    near_3, far_1, far_3 = wave((near_3, from_z(far, 1), from_z(far, 3)))
-    far_2, data_l, data_lh, data_rows = wave((from_z(far_1, 1), data_l, data_lh, data_rows))
+    near_3, far_1, far_3, data_rows = wave((near_3, from_z(far, 1), from_z(far, 3), data_rows))
+    data_lh = flip(data_rows, "lh")
+    far_2, data_l, data_rows = wave((from_z(far_1, 1), data_l, data_rows))
     sems = pltpu.SemaphoreType.DMA((4,))
 
     def stacked(*blocks):
@@ -419,6 +429,7 @@
     near, far = stacked(near, near_1, near_2, near_3), stacked(far, far_1, far_2, far_3)
     near_next, near_last = from_z(near, 1), from_z(near, 3)
     far_next, far_last = from_y(far, 1), from_y(far, 3)
+    data_lh, data_rows = wave((data_lh, data_rows))
     data_h = flip(data_rows, "h")
     far_next, far_last, data_h = wave((far_next, far_last, data_h))
     nears, fars = (near, near_next, near_last), (far, far_next, far_last)

time: 148 us -> 148 us (level)
  starting transfers between devices: 41.5 us -> 37.9 us
  waiting for transfers between devices: 32.2 us -> 35.3 us
    ppermute x27, starting transfers between devices: 41.5 us -> 37.9 us  [move(): return lax.ppermute(value, AXES, pairs)]
    ppermute x27, waiting for transfers between devices: 32.2 us -> 35.3 us  [move(): return lax.ppermute(value, AXES, pairs)]
  transfers between devices with their start and end apart: 27 -> 27, of which waited for: 15 -> 16; matrix products, arithmetic and copies ran while one was open for 0% -> 0% of each run, Pallas kernels for 16% -> 16%
where the time goes in v7:
time: 148 us; the launch traced here: 147 us
  blocking collectives  40.7 us (28%)
  starting transfers between devices  37.9 us (26%)
  waiting for transfers between devices  35.3 us (24%)
  Pallas kernels  32.2 us (22%)
    all_to_all x4, blocking collectives, exchange(): return lax.all_to_all(sent, axes, 0, 0, tiled=True)  40.7 us
    ppermute x27, starting transfers between devices, move(): return lax.ppermute(value, AXES, pairs)  37.9 us
    ppermute x27, waiting for transfers between devices, move(): return lax.ppermute(value, AXES, pairs)  35.3 us
    pallas_call x19, Pallas kernels, call(): pl.pallas_call(kernel, out_shape=outs, in_specs=[pl.BlockSpec(memory_spac...  32.2 us
  transfers between devices with their start and end apart: 27, of which 16 were waited for; matrix products, arithmetic and copies ran while one was open for 0% of the time, Pallas kernels for 16%

profile of v7, /device:TPU:0, one launch (start us, length us, event | category | flops | bytes accessed | tf_op | source)
XLA Modules:
  0.0 147.5 jit_solution(2773955990307996186)
XLA Ops:
  0.0 1.1 constant_dynamic-slice_fusion
  1.1 3.2 %collective-permute-start.1 = (bf16[128,1024]{1,0:T(8,128)(2,1)S(1)}, bf16[128,1024]{1,0:T(8,128)(2,1)S(1)}, u32[]{:S(2)}, u32[]{:S(2)}) collective-permute-start(bf16[128,1024]{1,0:T(8,128)(2,1)S(1)} %get-tuple-element.87), channel_id=1, source_target_pairs={{0,2},{1,3},{2,0},{3,1},{4,6},{5,7},{6,4},{7,5},{8,10},{9,11},{10,... | collective-permute-start | bytes 786440 | tf_op jit(solution)/shard_map/ppermute | solution.py:26
  4.3 3.0 %collective-permute-start.10 = (bf16[128,1024]{1,0:T(8,128)(2,1)S(1)}, bf16[128,1024]{1,0:T(8,128)(2,1)S(1)}, u32[]{:S(2)}, u32[]{:S(2)}) collective-permute-start(bf16[128,1024]{1,0:T(8,128)(2,1)S(1)} %get-tuple-element.88.refs_0_), channel_id=1, source_target_pairs={{0,24},{1,25},{2,26},{3,27},{4,28},{5,29},{6,30},{7,31},{8,0},{9,1... | collective-permute-start | bytes 786440 | tf_op jit(solution)/shard_map/ppermute | solution.py:26
  7.3 3.3 %collective-permute-done.1.refs_0_ = bf16[128,1024]{1,0:T(8,128)(2,1)S(1)} collective-permute-done((bf16[128,1024]{1,0:T(8,128)(2,1)S(1)}, bf16[128,1024]{1,0:T(8,128)(2,1)S(1)}, u32[]{:S(2)}, u32[]{:S(2)}) %collective-permute-start.1) | collective-permute-done | bytes 262176 | tf_op jit(solution)/shard_map/ppermute | solution.py:26
  10.6 4.3 %collective-permute-start.2 = (bf16[128,1024]{1,0:T(8,128)(2,1)S(1)}, bf16[128,1024]{1,0:T(8,128)(2,1)S(1)}, u32[]{:S(2)}, u32[]{:S(2)}) collective-permute-start(bf16[128,1024]{1,0:T(8,128)(2,1)S(1)} %collective-permute-done.1.refs_0_), channel_id=1, source_target_pairs={{0,96},{1,97},{2,98},{3,99},{4,100},{5,101},{6,102},{7,103},{8,104... | collective-permute-start | bytes 786440 | tf_op jit(solution)/shard_map/ppermute | solution.py:26
  14.9 1.5 %collective-permute-start.6 = (bf16[256,1024]{1,0:T(8,128)(2,1)}, bf16[256,1024]{1,0:T(8,128)(2,1)S(1)}, u32[]{:S(2)}, u32[]{:S(2)}) collective-permute-start(bf16[256,1024]{1,0:T(8,128)(2,1)} %refs_0_), channel_id=1, source_target_pairs={{0,4},{1,5},{2,6},{3,7},{4,0},{5,1},{6,2},{7,3},{8,12},{9,13},{10,... | collective-permute-start | bytes 1572872 | tf_op jit(solution)/shard_map/ppermute | solution.py:26
  16.4 3.0 %collective-permute-start.11 = (bf16[128,1024]{1,0:T(8,128)(2,1)S(1)}, bf16[128,1024]{1,0:T(8,128)(2,1)S(1)}, u32[]{:S(2)}, u32[]{:S(2)}) collective-permute-start(bf16[128,1024]{1,0:T(8,128)(2,1)S(1)} %collective-permute-done.10.refs_1_), channel_id=1, source_target_pairs={{0,24},{1,25},{2,26},{3,27},{4,28},{5,29},{6,30},{7,31},{8,0},{9,1... | collective-permute-start | bytes 786440 | tf_op jit(solution)/shard_map/ppermute | solution.py:26
  19.4 0.2 collective-permute-done.2.refs_1_
  19.6 3.4 %collective-permute-done.3.refs_3_ = bf16[128,1024]{1,0:T(8,128)(2,1)S(1)} collective-permute-done((bf16[128,1024]{1,0:T(8,128)(2,1)S(1)}, bf16[128,1024]{1,0:T(8,128)(2,1)S(1)}, u32[]{:S(2)}, u32[]{:S(2)}) %collective-permute-start.3) | collective-permute-done | bytes 262176 | tf_op jit(solution)/shard_map/ppermute | solution.py:26
  23.0 0.3 collective-permute-start.5
  23.3 0.1 stack.23.at
  23.4 0.2 collective-permute-done.11.refs_2_
  23.5 0.7 shard_map.29.refs_4_.p0
  24.2 3.1 %collective-permute-start.12 = (bf16[4,128,1024]{2,1,0:T(8,128)(2,1)S(1)}, bf16[4,128,1024]{2,1,0:T(8,128)(2,1)S(1)}, u32[]{:S(2)}, u32[]{:S(2)}) collective-permute-start(bf16[4,128,1024]{2,1,0:T(8,128)(2,1)S(1)} %shard_map.29.refs_4_.p0), channel_id=1, source_target_pairs={{0,96},{1,97},{2,98},{3,99},{4,100},{5,101},{6,102},{7,103},{8,104... | collective-permute-start | bytes 3145736 | tf_op jit(solution)/shard_map/ppermute | solution.py:26
  27.3 2.1 %collective-permute-start.4 = (bf16[256,1024]{1,0:T(8,128)(2,1)S(1)}, bf16[256,1024]{1,0:T(8,128)(2,1)S(1)}, u32[]{:S(2)}, u32[]{:S(2)}) collective-permute-start(bf16[256,1024]{1,0:T(8,128)(2,1)S(1)} %copy-done), channel_id=1, source_target_pairs={{0,6},{1,7},{2,4},{3,5},{4,2},{5,3},{6,0},{7,1},{8,14},{9,15},{10,... | collective-permute-start | bytes 1572872 | tf_op jit(solution)/shard_map/ppermute | solution.py:26
  29.4 2.9 %collective-permute-done.5.refs_2_ = bf16[128,1024]{1,0:T(8,128)(2,1)S(1)} collective-permute-done((bf16[128,1024]{1,0:T(8,128)(2,1)S(1)}, bf16[128,1024]{1,0:T(8,128)(2,1)S(1)}, u32[]{:S(2)}, u32[]{:S(2)}) %collective-permute-start.5) | collective-permute-done | bytes 262176 | tf_op jit(solution)/shard_map/ppermute | solution.py:26
  32.2 0.7 shard_map.28.refs_7_.p0
  32.9 3.1 %collective-permute-start.7 = (bf16[4,128,1024]{2,1,0:T(8,128)(2,1)S(1)}, bf16[4,128,1024]{2,1,0:T(8,128)(2,1)S(1)}, u32[]{:S(2)}, u32[]{:S(2)}) collective-permute-start(bf16[4,128,1024]{2,1,0:T(8,128)(2,1)S(1)} %shard_map.28.refs_7_.p0), channel_id=1, source_target_pairs={{0,24},{1,25},{2,26},{3,27},{4,28},{5,29},{6,30},{7,31},{8,0},{9,1... | collective-permute-start | bytes 3145736 | tf_op jit(solution)/shard_map/ppermute | solution.py:26
  36.0 3.3 %collective-permute-done.4.refs_3_ = bf16[256,1024]{1,0:T(8,128)(2,1)S(1)} collective-permute-done((bf16[256,1024]{1,0:T(8,128)(2,1)S(1)}, bf16[256,1024]{1,0:T(8,128)(2,1)S(1)}, u32[]{:S(2)}, u32[]{:S(2)}) %collective-permute-start.4) | collective-permute-done | bytes 524320 | tf_op jit(solution)/shard_map/ppermute | solution.py:26
  39.3 1.5 %collective-permute-start.9 = (bf16[256,1024]{1,0:T(8,128)(2,1)S(1)}, bf16[256,1024]{1,0:T(8,128)(2,1)S(1)}, u32[]{:S(2)}, u32[]{:S(2)}) collective-permute-start(bf16[256,1024]{1,0:T(8,128)(2,1)S(1)} %copy-done), channel_id=1, source_target_pairs={{0,2},{1,3},{2,0},{3,1},{4,6},{5,7},{6,4},{7,5},{8,10},{9,11},{10,... | collective-permute-start | bytes 1572872 | tf_op jit(solution)/shard_map/ppermute | solution.py:26
  40.8 10.6 %collective-permute-done.12.refs_5_.next_.p1 = bf16[4,128,1024]{2,1,0:T(8,128)(2,1)S(1)} collective-permute-done((bf16[4,128,1024]{2,1,0:T(8,128)(2,1)S(1)}, bf16[4,128,1024]{2,1,0:T(8,128)(2,1)S(1)}, u32[]{:S(2)}, u32[]{:S(2)}) %collective-permute-start.12) | collective-permute-done | bytes 1048608 | tf_op jit(solution)/shard_map/ppermute | solution.py:26
  51.4 0.7 shard_map.31
  52.1 2.0 %collective-permute-start.14 = (bf16[2,128,1024]{2,1,0:T(8,128)(2,1)S(1)}, bf16[2,128,1024]{2,1,0:T(8,128)(2,1)S(1)}, u32[]{:S(2)}, u32[]{:S(2)}) collective-permute-start(bf16[2,128,1024]{2,1,0:T(8,128)(2,1)S(1)} %get-tuple-element.62), channel_id=1, source_target_pairs={{0,96},{1,97},{2,98},{3,99},{4,100},{5,101},{6,102},{7,103},{8,104... | collective-permute-start | bytes 1572872 | tf_op jit(solution)/shard_map/ppermute | solution.py:26
  54.1 0.1 collective-permute-start.15
  54.2 2.0 %collective-permute-done.8.refs_9_.last.p3 = bf16[4,128,1024]{2,1,0:T(8,128)(2,1)S(1)} collective-permute-done((bf16[4,128,1024]{2,1,0:T(8,128)(2,1)S(1)}, bf16[4,128,1024]{2,1,0:T(8,128)(2,1)S(1)}, u32[]{:S(2)}, u32[]{:S(2)}) %collective-permute-start.8) | collective-permute-done | bytes 1048608 | tf_op jit(solution)/shard_map/ppermute | solution.py:26
  56.2 0.7 shard_map.34
  56.9 2.9 %collective-permute-start.17 = (bf16[2,128,1024]{2,1,0:T(8,128)(2,1)S(1)}, bf16[2,128,1024]{2,1,0:T(8,128)(2,1)S(1)}, u32[]{:S(2)}, u32[]{:S(2)}) collective-permute-start(bf16[2,128,1024]{2,1,0:T(8,128)(2,1)S(1)} %get-tuple-element.64), channel_id=1, source_target_pairs={{0,24},{1,25},{2,26},{3,27},{4,28},{5,29},{6,30},{7,31},{8,0},{9,1... | collective-permute-start | bytes 1572872 | tf_op jit(solution)/shard_map/ppermute | solution.py:26
  59.7 0.0 collective-permute-start.18
  59.7 7.7 %shard_map.30 = (f32[4,4,512,128]{3,2,1,0:T(8,128)S(1)}, bf16[2,512,1024]{2,1,0:T(8,128)(2,1)S(1)}) custom-call(s32[5]{0:T(128)S(1)} %stack.23.at, bf16[256,1024]{1,0:T(8,128)(2,1)S(1)} %copy-done, bf16[256,1024]{1,0:T(8,128)(2,1)S(1)} %collective-permute-done.6.refs_1_, bf16[256,1024]{1,0:T(8,128)(2,1)S(1)} %collective-permute-done.9.refs_2_, ...), custom_call_target="tpu_custom_call" | custom-call | flops 3221225472 | bytes 14680084 | tf_op jit(solution)/shard_map/pallas_call | solution.py:76
  67.4 1.8 %shard_map.33 = f32[2,4,512,128]{3,2,1,0:T(8,128)S(1)} custom-call(s32[5]{0:T(128)S(1)} %stack.23.at, bf16[2,512,1024]{2,1,0:T(8,128)(2,1)S(1)} %get-tuple-element.60.x, f32[4,4,512,128]{3,2,1,0:T(8,128)S(1)} %get-tuple-element.61.acc, bf16[2,128,1024]{2,1,0:T(8,128)(2,1)S(1)} %collective-permute-done.14.n_a.p2_a, ...), custom_call_target="tpu_custom_call" | custom-call | flops 26843545600 | bytes 9437204 | tf_op jit(solution)/shard_map/pallas_call | solution.py:76
  69.2 0.1 collective-permute-start.16
  69.3 0.9 collective-permute-done.18.f_b.p2_b
  70.2 2.2 %shard_map.35 = (f32[2,512,128]{2,1,0:T(8,128)S(1)}, f32[2,512,128]{2,1,0:T(8,128)S(1)}) custom-call(s32[5]{0:T(128)S(1)} %stack.23.at, bf16[2,512,1024]{2,1,0:T(8,128)(2,1)S(1)} %get-tuple-element.60.x, bf16[2,128,1024]{2,1,0:T(8,128)(2,1)S(1)} %collective-permute-done.17.f_a.p2_a, bf16[2,128,1024]{2,1,0:T(8,128)(2,1)S(1)} %collective-permute-done.18.f_b.p2_b), custom_call_target="tpu_custom_call" | custom-call | flops 536870912 | bytes 4194324 | tf_op jit(solution)/shard_map/pallas_call | solution.py:76
  72.4 0.1 collective-permute-start.19
  72.5 0.8 shard_map.32
  73.3 1.1 collective-permute-done.19.far_got
  74.4 1.8 %shard_map.36 = (f32[8,512,128]{2,1,0:T(8,128)S(1)}, f32[8,1,512]{2,1,0:T(1,128)S(1)}) custom-call(s32[5]{0:T(128)S(1)} %stack.23.at, f32[8,512,128]{2,1,0:T(8,128)S(1)} %bitcast.7, f32[8,512,128]{2,1,0:T(8,128)S(1)} %collective-permute-done.16.got, f32[2,512,128]{2,1,0:T(8,128)S(1)} %get-tuple-element.66.far_keep, ...), custom_call_target="tpu_custom_call" | custom-call | bytes 7356436 | tf_op jit(solution)/shard_map/pallas_call | solution.py:76
  76.2 9.1 %all_to_all.20.came = f32[8,1,512]{2,1,0:T(1,128)S(1)} all-to-all(f32[8,1,512]{2,1,0:T(1,128)S(1)} %get-tuple-element.68), channel_id=1, replica_groups=mesh['z'=4,'y'=4,'l'=2,'h'=2,'c'=2] {'l','h','c'}, dimensions={0} | all-to-all | bytes 32768 | tf_op jit(solution)/shard_map/all_to_all | solution.py:478
  85.3 1.3 shard_map.37
  86.6 12.6 %all_to_all.21.came = f32[16,8,128]{2,1,0:T(8,128)S(1)} all-to-all(f32[16,8,128]{2,1,0:T(8,128)S(1)} %get-tuple-element.70), channel_id=1, replica_groups=mesh['z'=4,'y'=4,'l'=2,'h'=2,'c'=2] {'z','y'}, dimensions={0} | all-to-all | bytes 131072 | tf_op jit(solution)/shard_map/all_to_all | solution.py:478
  99.3 1.3 shard_map.38
  100.5 0.0 collective-permute-start.20
  100.6 7.7 %all_to_all.22.came = f32[8,1,512]{2,1,0:T(1,128)S(1)} all-to-all(f32[8,1,512]{2,1,0:T(1,128)S(1)} %get-tuple-element.72), channel_id=1, replica_groups=mesh['z'=4,'y'=4,'l'=2,'h'=2,'c'=2] {'l','h','c'}, dimensions={0} | all-to-all | bytes 32768 | tf_op jit(solution)/shard_map/all_to_all | solution.py:478
  108.3 0.9 shard_map.39
  109.2 11.2 %all_to_all.23.came = f32[32,8,128]{2,1,0:T(8,128)S(1)} all-to-all(f32[32,8,128]{2,1,0:T(8,128)S(1)} %get-tuple-element.74), channel_id=1, replica_groups=mesh['z'=4,'y'=4,'l'=2,'h'=2,'c'=2] {'z','y','c'}, dimensions={0} | all-to-all | bytes 262144 | tf_op jit(solution)/shard_map/all_to_all | solution.py:478
  120.4 2.8 %shard_map.40 = (bf16[4,4,512,128]{3,2,1,0:T(8,128)(2,1)S(1)}, bf16[144,1024]{1,0:T(8,128)(2,1)S(1)}, bf16[144,1024]{1,0:T(8,128)(2,1)S(1)}) custom-call(s32[5]{0:T(128)S(1)} %stack.23.at, f32[32,8,128]{2,1,0:T(8,128)S(1)} %all_to_all.23.came, f32[8,512,128]{2,1,0:T(8,128)S(1)} %get-tuple-element.73.plan, f32[8,512,128]{2,1,0:T(8,128)S(1)} %collective-permute-done.20.other, ...), custom_call_target="tpu_custom_call" | custom-call | flops 2147483648 | bytes 11468820 | tf_op jit(solution)/shard_map/pallas_call | solution.py:76
  123.2 1.2 collective-permute-start.22
  124.5 0.0 collective-permute-start.24
  124.5 2.1 %shard_map.42 = (bf16[128,1024]{1,0:T(8,128)(2,1)S(1)}, f32[128,1024]{1,0:T(8,128)S(1)}, f32[8,256]{1,0:T(8,128)S(1)}) custom-call(s32[5]{0:T(128)S(1)} %stack.23.at, bf16[4,4,512,128]{3,2,1,0:T(8,128)(2,1)S(1)} %get-tuple-element.76.weights, bf16[4,128,1024]{2,1,0:T(8,128)(2,1)S(1)} %shard_map.29.refs_4_.p0, ...), custom_call_target="tpu_custom_call" | custom-call | flops 2147483648 | bytes 7086100 | tf_op jit(solution)/shard_map/pallas_call | solution.py:76
  126.5 2.1 %collective-permute-start.21 = (bf16[128,1024]{1,0:T(8,128)(2,1)S(1)}, bf16[128,1024]{1,0:T(8,128)(2,1)S(1)}, u32[]{:S(2)}, u32[]{:S(2)}) collective-permute-start(bf16[128,1024]{1,0:T(8,128)(2,1)S(1)} %get-tuple-element.79), channel_id=1, source_target_pairs={{0,4},{1,5},{2,6},{3,7},{4,0},{5,1},{6,2},{7,3},{8,12},{9,13},{10,... | collective-permute-start | bytes 786440 | tf_op jit(solution)/shard_map/ppermute | solution.py:26
  128.6 2.1 %shard_map.44 = (bf16[128,1024]{1,0:T(8,128)(2,1)S(1)}, f32[128,1024]{1,0:T(8,128)S(1)}, f32[8,256]{1,0:T(8,128)S(1)}) custom-call(s32[5]{0:T(128)S(1)} %stack.23.at, bf16[4,4,512,128]{3,2,1,0:T(8,128)(2,1)S(1)} %get-tuple-element.76.weights, bf16[4,128,1024]{2,1,0:T(8,128)(2,1)S(1)} %shard_map.28.refs_7_.p0, ...), custom_call_target="tpu_custom_call" | custom-call | flops 2147483648 | bytes 7086100 | tf_op jit(solution)/shard_map/pallas_call | solution.py:76
  130.7 2.1 %collective-permute-start.26 = (bf16[128,1024]{1,0:T(8,128)(2,1)S(1)}, bf16[128,1024]{1,0:T(8,128)(2,1)S(1)}, u32[]{:S(2)}, u32[]{:S(2)}) collective-permute-start(bf16[128,1024]{1,0:T(8,128)(2,1)S(1)} %get-tuple-element.86), channel_id=1, source_target_pairs={{0,6},{1,7},{2,4},{3,5},{4,2},{5,3},{6,0},{7,1},{8,14},{9,15},{10,... | collective-permute-start | bytes 786440 | tf_op jit(solution)/shard_map/ppermute | solution.py:26
  132.9 0.7 collective-permute-done.22.came
  133.5 0.6 shard_map.43
  134.1 0.1 collective-permute-start.23
  134.2 0.1 collective-permute-done.24.came
  134.4 0.6 shard_map.45
  135.0 2.1 %collective-permute-start.25 = (bf16[144,1024]{1,0:T(8,128)(2,1)S(1)}, bf16[144,1024]{1,0:T(8,128)(2,1)S(1)}, u32[]{:S(2)}, u32[]{:S(2)}) collective-permute-start(bf16[144,1024]{1,0:T(8,128)(2,1)S(1)} %shard_map.45), channel_id=1, source_target_pairs={{0,6},{1,7},{2,4},{3,5},{4,2},{5,3},{6,0},{7,1},{8,14},{9,15},{10,... | collective-permute-start | bytes 884744 | tf_op jit(solution)/shard_map/ppermute | solution.py:26
  137.1 2.1 %shard_map.41 = (f32[256,1024]{1,0:T(8,128)S(1)}, f32[8,256]{1,0:T(8,128)S(1)}) custom-call(s32[5]{0:T(128)S(1)} %stack.23.at, bf16[4,4,512,128]{3,2,1,0:T(8,128)(2,1)S(1)} %get-tuple-element.76.weights, bf16[4,128,1024]{2,1,0:T(8,128)(2,1)S(1)} %shard_map.29.refs_4_.p0, bf16[4,128,1024]{2,1,0:T(8,128)(2,1)S(1)} %collective-permute-done.12.refs_5_.next_.p1, ...), custom_call_target="tpu_custom_call" | custom-call | flops 17179869184 | bytes 7348244 | tf_op jit(solution)/shard_map/pallas_call | solution.py:76
  139.2 0.8 collective-permute-done.21.l_low
  140.0 0.9 collective-permute-done.26.lh_high
  140.9 4.2 %collective-permute-done.23.l_high = bf16[144,1024]{1,0:T(8,128)(2,1)S(1)} collective-permute-done((bf16[144,1024]{1,0:T(8,128)(2,1)S(1)}, bf16[144,1024]{1,0:T(8,128)(2,1)S(1)}, u32[]{:S(2)}, u32[]{:S(2)}) %collective-permute-start.23) | collective-permute-done | bytes 294944 | tf_op jit(solution)/shard_map/ppermute | solution.py:26
  145.1 0.7 collective-permute-done.25.lh_low
  145.8 1.7 %shard_map.46 = bf16[256,1024]{1,0:T(8,128)(2,1)} custom-call(s32[5]{0:T(128)S(1)} %stack.23.at, f32[256,1024]{1,0:T(8,128)S(1)} %get-tuple-element.77.own, f32[8,256]{1,0:T(8,128)S(1)} %get-tuple-element.78.own_total, bf16[128,1024]{1,0:T(8,128)(2,1)S(1)} %collective-permute-done.21.l_low, bf16[144,1024]{1,0:T(8,128)(2,1)S(1)} %collective-permute-done.23.l_high, ...), custom_call_target="tpu_custom_call" | custom-call | bytes 2695188 | tf_op jit(solution)/shard_map/pallas_call | solution.py:76
  (17 shorter events, 0.0 us)
Async XLA Ops:
  0.0 27.3 %copy-start = (bf16[256,1024]{1,0:T(8,128)(2,1)S(1)}, bf16[256,1024]{1,0:T(8,128)(2,1)}, u32[]{:S(2)}) copy-start(bf16[256,1024]{1,0:T(8,128)(2,1)} %refs_0_) | copy-start | bytes 1572868
  1.1 9.5 %collective-permute-start.1 = (bf16[128,1024]{1,0:T(8,128)(2,1)S(1)}, bf16[128,1024]{1,0:T(8,128)(2,1)S(1)}, u32[]{:S(2)}, u32[]{:S(2)}) collective-permute-start(bf16[128,1024]{1,0:T(8,128)(2,1)S(1)} %get-tuple-element.87), channel_id=1, source_target_pairs={{0,2},{1,3},{2,0},{3,1},{4,6},{5,7},{6,4},{7,5},{8,10},{9,11},{10,... | collective-permute-start | bytes 786440 | tf_op jit(solution)/shard_map/ppermute | solution.py:26
  4.3 12.1 %collective-permute-start.10 = (bf16[128,1024]{1,0:T(8,128)(2,1)S(1)}, bf16[128,1024]{1,0:T(8,128)(2,1)S(1)}, u32[]{:S(2)}, u32[]{:S(2)}) collective-permute-start(bf16[128,1024]{1,0:T(8,128)(2,1)S(1)} %get-tuple-element.88.refs_0_), channel_id=1, source_target_pairs={{0,24},{1,25},{2,26},{3,27},{4,28},{5,29},{6,30},{7,31},{8,0},{9,1... | collective-permute-start | bytes 786440 | tf_op jit(solution)/shard_map/ppermute | solution.py:26
  7.3 12.1 %collective-permute-start = (bf16[128,1024]{1,0:T(8,128)(2,1)S(1)}, bf16[128,1024]{1,0:T(8,128)(2,1)S(1)}, u32[]{:S(2)}, u32[]{:S(2)}) collective-permute-start(bf16[128,1024]{1,0:T(8,128)(2,1)S(1)} %get-tuple-element.88.refs_0_), channel_id=1, source_target_pairs={{0,8},{1,9},{2,10},{3,11},{4,12},{5,13},{6,14},{7,15},{8,16},{9,17... | collective-permute-start | bytes 786440 | tf_op jit(solution)/shard_map/ppermute | solution.py:26
  10.6 9.0 %collective-permute-start.2 = (bf16[128,1024]{1,0:T(8,128)(2,1)S(1)}, bf16[128,1024]{1,0:T(8,128)(2,1)S(1)}, u32[]{:S(2)}, u32[]{:S(2)}) collective-permute-start(bf16[128,1024]{1,0:T(8,128)(2,1)S(1)} %collective-permute-done.1.refs_0_), channel_id=1, source_target_pairs={{0,96},{1,97},{2,98},{3,99},{4,100},{5,101},{6,102},{7,103},{8,104... | collective-permute-start | bytes 786440 | tf_op jit(solution)/shard_map/ppermute | solution.py:26
  14.9 8.1 %collective-permute-start.3 = (bf16[128,1024]{1,0:T(8,128)(2,1)S(1)}, bf16[128,1024]{1,0:T(8,128)(2,1)S(1)}, u32[]{:S(2)}, u32[]{:S(2)}) collective-permute-start(bf16[128,1024]{1,0:T(8,128)(2,1)S(1)} %collective-permute-done.1.refs_0_), channel_id=1, source_target_pairs={{0,32},{1,33},{2,34},{3,35},{4,36},{5,37},{6,38},{7,39},{8,40},{9,... | collective-permute-start | bytes 786440 | tf_op jit(solution)/shard_map/ppermute | solution.py:26
  14.9 17.3 %collective-permute-start.6 = (bf16[256,1024]{1,0:T(8,128)(2,1)}, bf16[256,1024]{1,0:T(8,128)(2,1)S(1)}, u32[]{:S(2)}, u32[]{:S(2)}) collective-permute-start(bf16[256,1024]{1,0:T(8,128)(2,1)} %refs_0_), channel_id=1, source_target_pairs={{0,4},{1,5},{2,6},{3,7},{4,0},{5,1},{6,2},{7,3},{8,12},{9,13},{10,... | collective-permute-start | bytes 1572872 | tf_op jit(solution)/shard_map/ppermute | solution.py:26
  16.4 7.1 %collective-permute-start.11 = (bf16[128,1024]{1,0:T(8,128)(2,1)S(1)}, bf16[128,1024]{1,0:T(8,128)(2,1)S(1)}, u32[]{:S(2)}, u32[]{:S(2)}) collective-permute-start(bf16[128,1024]{1,0:T(8,128)(2,1)S(1)} %collective-permute-done.10.refs_1_), channel_id=1, source_target_pairs={{0,24},{1,25},{2,26},{3,27},{4,28},{5,29},{6,30},{7,31},{8,0},{9,1... | collective-permute-start | bytes 786440 | tf_op jit(solution)/shard_map/ppermute | solution.py:26
  23.0 9.2 %collective-permute-start.5 = (bf16[128,1024]{1,0:T(8,128)(2,1)S(1)}, bf16[128,1024]{1,0:T(8,128)(2,1)S(1)}, u32[]{:S(2)}, u32[]{:S(2)}) collective-permute-start(bf16[128,1024]{1,0:T(8,128)(2,1)S(1)} %collective-permute-done.2.refs_1_), channel_id=1, source_target_pairs={{0,96},{1,97},{2,98},{3,99},{4,100},{5,101},{6,102},{7,103},{8,104... | collective-permute-start | bytes 786440 | tf_op jit(solution)/shard_map/ppermute | solution.py:26
  24.2 27.2 %collective-permute-start.12 = (bf16[4,128,1024]{2,1,0:T(8,128)(2,1)S(1)}, bf16[4,128,1024]{2,1,0:T(8,128)(2,1)S(1)}, u32[]{:S(2)}, u32[]{:S(2)}) collective-permute-start(bf16[4,128,1024]{2,1,0:T(8,128)(2,1)S(1)} %shard_map.29.refs_4_.p0), channel_id=1, source_target_pairs={{0,96},{1,97},{2,98},{3,99},{4,100},{5,101},{6,102},{7,103},{8,104... | collective-permute-start | bytes 3145736 | tf_op jit(solution)/shard_map/ppermute | solution.py:26
  27.2 24.2 %collective-permute-start.13 = (bf16[4,128,1024]{2,1,0:T(8,128)(2,1)S(1)}, bf16[4,128,1024]{2,1,0:T(8,128)(2,1)S(1)}, u32[]{:S(2)}, u32[]{:S(2)}) collective-permute-start(bf16[4,128,1024]{2,1,0:T(8,128)(2,1)S(1)} %shard_map.29.refs_4_.p0), channel_id=1, source_target_pairs={{0,32},{1,33},{2,34},{3,35},{4,36},{5,37},{6,38},{7,39},{8,40},{9,... | collective-permute-start | bytes 3145736 | tf_op jit(solution)/shard_map/ppermute | solution.py:26
  27.3 12.0 %collective-permute-start.4 = (bf16[256,1024]{1,0:T(8,128)(2,1)S(1)}, bf16[256,1024]{1,0:T(8,128)(2,1)S(1)}, u32[]{:S(2)}, u32[]{:S(2)}) collective-permute-start(bf16[256,1024]{1,0:T(8,128)(2,1)S(1)} %copy-done), channel_id=1, source_target_pairs={{0,6},{1,7},{2,4},{3,5},{4,2},{5,3},{6,0},{7,1},{8,14},{9,15},{10,... | collective-permute-start | bytes 1572872 | tf_op jit(solution)/shard_map/ppermute | solution.py:26
  32.9 21.3 %collective-permute-start.7 = (bf16[4,128,1024]{2,1,0:T(8,128)(2,1)S(1)}, bf16[4,128,1024]{2,1,0:T(8,128)(2,1)S(1)}, u32[]{:S(2)}, u32[]{:S(2)}) collective-permute-start(bf16[4,128,1024]{2,1,0:T(8,128)(2,1)S(1)} %shard_map.28.refs_7_.p0), channel_id=1, source_target_pairs={{0,24},{1,25},{2,26},{3,27},{4,28},{5,29},{6,30},{7,31},{8,0},{9,1... | collective-permute-start | bytes 3145736 | tf_op jit(solution)/shard_map/ppermute | solution.py:26
  36.0 20.2 %collective-permute-start.8 = (bf16[4,128,1024]{2,1,0:T(8,128)(2,1)S(1)}, bf16[4,128,1024]{2,1,0:T(8,128)(2,1)S(1)}, u32[]{:S(2)}, u32[]{:S(2)}) collective-permute-start(bf16[4,128,1024]{2,1,0:T(8,128)(2,1)S(1)} %shard_map.28.refs_7_.p0), channel_id=1, source_target_pairs={{0,8},{1,9},{2,10},{3,11},{4,12},{5,13},{6,14},{7,15},{8,16},{9,17... | collective-permute-start | bytes 3145736 | tf_op jit(solution)/shard_map/ppermute | solution.py:26
  39.3 14.9 %collective-permute-start.9 = (bf16[256,1024]{1,0:T(8,128)(2,1)S(1)}, bf16[256,1024]{1,0:T(8,128)(2,1)S(1)}, u32[]{:S(2)}, u32[]{:S(2)}) collective-permute-start(bf16[256,1024]{1,0:T(8,128)(2,1)S(1)} %copy-done), channel_id=1, source_target_pairs={{0,2},{1,3},{2,0},{3,1},{4,6},{5,7},{6,4},{7,5},{8,10},{9,11},{10,... | collective-permute-start | bytes 1572872 | tf_op jit(solution)/shard_map/ppermute | solution.py:26
  52.1 15.3 %collective-permute-start.14 = (bf16[2,128,1024]{2,1,0:T(8,128)(2,1)S(1)}, bf16[2,128,1024]{2,1,0:T(8,128)(2,1)S(1)}, u32[]{:S(2)}, u32[]{:S(2)}) collective-permute-start(bf16[2,128,1024]{2,1,0:T(8,128)(2,1)S(1)} %get-tuple-element.62), channel_id=1, source_target_pairs={{0,96},{1,97},{2,98},{3,99},{4,100},{5,101},{6,102},{7,103},{8,104... | collective-permute-start | bytes 1572872 | tf_op jit(solution)/shard_map/ppermute | solution.py:26
  54.1 13.4 %collective-permute-start.15 = (bf16[2,128,1024]{2,1,0:T(8,128)(2,1)S(1)}, bf16[2,128,1024]{2,1,0:T(8,128)(2,1)S(1)}, u32[]{:S(2)}, u32[]{:S(2)}) collective-permute-start(bf16[2,128,1024]{2,1,0:T(8,128)(2,1)S(1)} %get-tuple-element.63), channel_id=1, source_target_pairs={{0,32},{1,33},{2,34},{3,35},{4,36},{5,37},{6,38},{7,39},{8,40},{9,... | collective-permute-start | bytes 1572872 | tf_op jit(solution)/shard_map/ppermute | solution.py:26
  56.9 12.4 %collective-permute-start.17 = (bf16[2,128,1024]{2,1,0:T(8,128)(2,1)S(1)}, bf16[2,128,1024]{2,1,0:T(8,128)(2,1)S(1)}, u32[]{:S(2)}, u32[]{:S(2)}) collective-permute-start(bf16[2,128,1024]{2,1,0:T(8,128)(2,1)S(1)} %get-tuple-element.64), channel_id=1, source_target_pairs={{0,24},{1,25},{2,26},{3,27},{4,28},{5,29},{6,30},{7,31},{8,0},{9,1... | collective-permute-start | bytes 1572872 | tf_op jit(solution)/shard_map/ppermute | solution.py:26
  59.7 10.5 %collective-permute-start.18 = (bf16[2,128,1024]{2,1,0:T(8,128)(2,1)S(1)}, bf16[2,128,1024]{2,1,0:T(8,128)(2,1)S(1)}, u32[]{:S(2)}, u32[]{:S(2)}) collective-permute-start(bf16[2,128,1024]{2,1,0:T(8,128)(2,1)S(1)} %get-tuple-element.65), channel_id=1, source_target_pairs={{0,8},{1,9},{2,10},{3,11},{4,12},{5,13},{6,14},{7,15},{8,16},{9,17... | collective-permute-start | bytes 1572872 | tf_op jit(solution)/shard_map/ppermute | solution.py:26
  69.2 5.2 %collective-permute-start.16 = (f32[8,512,128]{2,1,0:T(8,128)S(1)}, f32[8,512,128]{2,1,0:T(8,128)S(1)}, u32[]{:S(2)}, u32[]{:S(2)}) collective-permute-start(f32[8,512,128]{2,1,0:T(8,128)S(1)} %bitcast.8), channel_id=1, source_target_pairs={{0,1},{1,0},{2,3},{3,2},{4,5},{5,4},{6,7},{7,6},{8,9},{9,8},{10,11... | collective-permute-start | bytes 6291464 | tf_op jit(solution)/shard_map/ppermute | solution.py:26
  72.4 2.0 %collective-permute-start.19 = (f32[2,512,128]{2,1,0:T(8,128)S(1)}, f32[2,512,128]{2,1,0:T(8,128)S(1)}, u32[]{:S(2)}, u32[]{:S(2)}) collective-permute-start(f32[2,512,128]{2,1,0:T(8,128)S(1)} %get-tuple-element.67), channel_id=1, source_target_pairs={{0,1},{1,0},{2,3},{3,2},{4,5},{5,4},{6,7},{7,6},{8,9},{9,8},{10,11... | collective-permute-start | bytes 1572872 | tf_op jit(solution)/shard_map/ppermute | solution.py:26
  100.5 19.9 %collective-permute-start.20 = (f32[8,512,128]{2,1,0:T(8,128)S(1)}, f32[8,512,128]{2,1,0:T(8,128)S(1)}, u32[]{:S(2)}, u32[]{:S(2)}) collective-permute-start(f32[8,512,128]{2,1,0:T(8,128)S(1)} %get-tuple-element.73.plan), channel_id=1, source_target_pairs={{0,1},{1,0},{2,3},{3,2},{4,5},{5,4},{6,7},{7,6},{8,9},{9,8},{10,11... | collective-permute-start | bytes 6291464 | tf_op jit(solution)/shard_map/ppermute | solution.py:26
  123.2 10.3 %collective-permute-start.22 = (bf16[144,1024]{1,0:T(8,128)(2,1)S(1)}, bf16[144,1024]{1,0:T(8,128)(2,1)S(1)}, u32[]{:S(2)}, u32[]{:S(2)}) collective-permute-start(bf16[144,1024]{1,0:T(8,128)(2,1)S(1)} %get-tuple-element.82), channel_id=1, source_target_pairs={{0,6},{1,7},{2,4},{3,5},{4,2},{5,3},{6,0},{7,1},{8,14},{9,15},{10,... | collective-permute-start | bytes 884744 | tf_op jit(solution)/shard_map/ppermute | solution.py:26
  124.5 9.9 %collective-permute-start.24 = (bf16[144,1024]{1,0:T(8,128)(2,1)S(1)}, bf16[144,1024]{1,0:T(8,128)(2,1)S(1)}, u32[]{:S(2)}, u32[]{:S(2)}) collective-permute-start(bf16[144,1024]{1,0:T(8,128)(2,1)S(1)} %get-tuple-element.85), channel_id=1, source_target_pairs={{0,4},{1,5},{2,6},{3,7},{4,0},{5,1},{6,2},{7,3},{8,12},{9,13},{10,... | collective-permute-start | bytes 884744 | tf_op jit(solution)/shard_map/ppermute | solution.py:26
  126.5 13.4 %collective-permute-start.21 = (bf16[128,1024]{1,0:T(8,128)(2,1)S(1)}, bf16[128,1024]{1,0:T(8,128)(2,1)S(1)}, u32[]{:S(2)}, u32[]{:S(2)}) collective-permute-start(bf16[128,1024]{1,0:T(8,128)(2,1)S(1)} %get-tuple-element.79), channel_id=1, source_target_pairs={{0,4},{1,5},{2,6},{3,7},{4,0},{5,1},{6,2},{7,3},{8,12},{9,13},{10,... | collective-permute-start | bytes 786440 | tf_op jit(solution)/shard_map/ppermute | solution.py:26
  130.7 10.2 %collective-permute-start.26 = (bf16[128,1024]{1,0:T(8,128)(2,1)S(1)}, bf16[128,1024]{1,0:T(8,128)(2,1)S(1)}, u32[]{:S(2)}, u32[]{:S(2)}) collective-permute-start(bf16[128,1024]{1,0:T(8,128)(2,1)S(1)} %get-tuple-element.86), channel_id=1, source_target_pairs={{0,6},{1,7},{2,4},{3,5},{4,2},{5,3},{6,0},{7,1},{8,14},{9,15},{10,... | collective-permute-start | bytes 786440 | tf_op jit(solution)/shard_map/ppermute | solution.py:26
  134.1 11.0 %collective-permute-start.23 = (bf16[144,1024]{1,0:T(8,128)(2,1)S(1)}, bf16[144,1024]{1,0:T(8,128)(2,1)S(1)}, u32[]{:S(2)}, u32[]{:S(2)}) collective-permute-start(bf16[144,1024]{1,0:T(8,128)(2,1)S(1)} %shard_map.43), channel_id=1, source_target_pairs={{0,4},{1,5},{2,6},{3,7},{4,0},{5,1},{6,2},{7,3},{8,12},{9,13},{10,... | collective-permute-start | bytes 884744 | tf_op jit(solution)/shard_map/ppermute | solution.py:26
  135.0 10.8 %collective-permute-start.25 = (bf16[144,1024]{1,0:T(8,128)(2,1)S(1)}, bf16[144,1024]{1,0:T(8,128)(2,1)S(1)}, u32[]{:S(2)}, u32[]{:S(2)}) collective-permute-start(bf16[144,1024]{1,0:T(8,128)(2,1)S(1)} %shard_map.45), channel_id=1, source_target_pairs={{0,6},{1,7},{2,4},{3,5},{4,2},{5,3},{6,0},{7,1},{8,14},{9,15},{10,... | collective-permute-start | bytes 884744 | tf_op jit(solution)/shard_map/ppermute | solution.py:26

commit v8 on v7

--- a/solution.py
+++ b/solution.py
@@ -409,7 +409,8 @@
     far, data_rows = wave((far, data_rows))
     data_l = flip(data_rows, "l")
     near_2 = from_y(near_1, 1)
-    near_3, far_1, far_3, data_rows = wave((near_3, from_z(far, 1), from_z(far, 3), data_rows))
+    far_3 = from_z(far, 3)
+    near_3, far_1, data_rows = wave((near_3, from_z(far, 1), data_rows))
     data_lh = flip(data_rows, "lh")
     far_2, data_l, data_rows = wave((from_z(far_1, 1), data_l, data_rows))
     sems = pltpu.SemaphoreType.DMA((4,))

time: 148 us -> 149 us (level)
  starting transfers between devices: 37.9 us -> 41.6 us
  waiting for transfers between devices: 35.3 us -> 33 us
    ppermute x27, starting transfers between devices: 37.9 us -> 41.6 us  [move(): return lax.ppermute(value, AXES, pairs)]
    ppermute x27, waiting for transfers between devices: 35.3 us -> 33 us  [move(): return lax.ppermute(value, AXES, pairs)]
  transfers between devices with their start and end apart: 27 -> 27, of which waited for: 16 -> 18; matrix products, arithmetic and copies ran while one was open for 0% -> 0% of each run, Pallas kernels for 16% -> 16%
where the time goes in v8:
time: 149 us
  starting transfers between devices  41.6 us (28%)
  blocking collectives  40.8 us (27%)
  waiting for transfers between devices  33 us (22%)
  Pallas kernels  32.2 us (22%)
    ppermute x27, starting transfers between devices, move(): return lax.ppermute(value, AXES, pairs)  41.6 us
    all_to_all x4, blocking collectives, exchange(): return lax.all_to_all(sent, axes, 0, 0, tiled=True)  40.8 us
    ppermute x27, waiting for transfers between devices, move(): return lax.ppermute(value, AXES, pairs)  33 us
    pallas_call x19, Pallas kernels, call(): pl.pallas_call(kernel, out_shape=outs, in_specs=[pl.BlockSpec(memory_spac...  32.2 us
  transfers between devices with their start and end apart: 27, of which 18 were waited for; matrix products, arithmetic and copies ran while one was open for 0% of the time, Pallas kernels for 16%

profile of v8, /device:TPU:0, one launch (start us, length us, event | category | flops | bytes accessed | tf_op | source)
XLA Modules:
  0.0 149.1 jit_solution(1146623593939432068)
XLA Ops:
  0.0 1.1 constant_dynamic-slice_fusion
  1.1 3.2 %collective-permute-start.1 = (bf16[128,1024]{1,0:T(8,128)(2,1)S(1)}, bf16[128,1024]{1,0:T(8,128)(2,1)S(1)}, u32[]{:S(2)}, u32[]{:S(2)}) collective-permute-start(bf16[128,1024]{1,0:T(8,128)(2,1)S(1)} %get-tuple-element.85), channel_id=1, source_target_pairs={{0,2},{1,3},{2,0},{3,1},{4,6},{5,7},{6,4},{7,5},{8,10},{9,11},{10,... | collective-permute-start | bytes 786440 | tf_op jit(solution)/shard_map/ppermute | solution.py:26
  4.3 3.0 %collective-permute-start.10 = (bf16[128,1024]{1,0:T(8,128)(2,1)S(1)}, bf16[128,1024]{1,0:T(8,128)(2,1)S(1)}, u32[]{:S(2)}, u32[]{:S(2)}) collective-permute-start(bf16[128,1024]{1,0:T(8,128)(2,1)S(1)} %get-tuple-element.86.refs_0_), channel_id=1, source_target_pairs={{0,24},{1,25},{2,26},{3,27},{4,28},{5,29},{6,30},{7,31},{8,0},{9,1... | collective-permute-start | bytes 786440 | tf_op jit(solution)/shard_map/ppermute | solution.py:26
  7.3 3.3 %collective-permute-done.1.refs_0_ = bf16[128,1024]{1,0:T(8,128)(2,1)S(1)} collective-permute-done((bf16[128,1024]{1,0:T(8,128)(2,1)S(1)}, bf16[128,1024]{1,0:T(8,128)(2,1)S(1)}, u32[]{:S(2)}, u32[]{:S(2)}) %collective-permute-start.1) | collective-permute-done | bytes 262176 | tf_op jit(solution)/shard_map/ppermute | solution.py:26
  10.6 4.3 %collective-permute-start.2 = (bf16[128,1024]{1,0:T(8,128)(2,1)S(1)}, bf16[128,1024]{1,0:T(8,128)(2,1)S(1)}, u32[]{:S(2)}, u32[]{:S(2)}) collective-permute-start(bf16[128,1024]{1,0:T(8,128)(2,1)S(1)} %collective-permute-done.1.refs_0_), channel_id=1, source_target_pairs={{0,96},{1,97},{2,98},{3,99},{4,100},{5,101},{6,102},{7,103},{8,104... | collective-permute-start | bytes 786440 | tf_op jit(solution)/shard_map/ppermute | solution.py:26
  14.9 1.5 %collective-permute-start.5 = (bf16[256,1024]{1,0:T(8,128)(2,1)}, bf16[256,1024]{1,0:T(8,128)(2,1)S(1)}, u32[]{:S(2)}, u32[]{:S(2)}) collective-permute-start(bf16[256,1024]{1,0:T(8,128)(2,1)} %refs_0_), channel_id=1, source_target_pairs={{0,4},{1,5},{2,6},{3,7},{4,0},{5,1},{6,2},{7,3},{8,12},{9,13},{10,... | collective-permute-start | bytes 1572872 | tf_op jit(solution)/shard_map/ppermute | solution.py:26
  16.4 3.0 %collective-permute-start.11 = (bf16[128,1024]{1,0:T(8,128)(2,1)S(1)}, bf16[128,1024]{1,0:T(8,128)(2,1)S(1)}, u32[]{:S(2)}, u32[]{:S(2)}) collective-permute-start(bf16[128,1024]{1,0:T(8,128)(2,1)S(1)} %collective-permute-done.10.refs_1_), channel_id=1, source_target_pairs={{0,24},{1,25},{2,26},{3,27},{4,28},{5,29},{6,30},{7,31},{8,0},{9,1... | collective-permute-start | bytes 786440 | tf_op jit(solution)/shard_map/ppermute | solution.py:26
  19.4 0.2 collective-permute-done.2.refs_1_
  19.6 3.7 %collective-permute-start.4 = (bf16[128,1024]{1,0:T(8,128)(2,1)S(1)}, bf16[128,1024]{1,0:T(8,128)(2,1)S(1)}, u32[]{:S(2)}, u32[]{:S(2)}) collective-permute-start(bf16[128,1024]{1,0:T(8,128)(2,1)S(1)} %collective-permute-done.2.refs_1_), channel_id=1, source_target_pairs={{0,96},{1,97},{2,98},{3,99},{4,100},{5,101},{6,102},{7,103},{8,104... | collective-permute-start | bytes 786440 | tf_op jit(solution)/shard_map/ppermute | solution.py:26
  23.3 0.1 stack.23.at
  23.4 0.2 collective-permute-done.11.refs_2_
  23.5 0.7 shard_map.29.refs_4_.p0
  24.2 3.1 %collective-permute-start.12 = (bf16[4,128,1024]{2,1,0:T(8,128)(2,1)S(1)}, bf16[4,128,1024]{2,1,0:T(8,128)(2,1)S(1)}, u32[]{:S(2)}, u32[]{:S(2)}) collective-permute-start(bf16[4,128,1024]{2,1,0:T(8,128)(2,1)S(1)} %shard_map.29.refs_4_.p0), channel_id=1, source_target_pairs={{0,96},{1,97},{2,98},{3,99},{4,100},{5,101},{6,102},{7,103},{8,104... | collective-permute-start | bytes 3145736 | tf_op jit(solution)/shard_map/ppermute | solution.py:26
  27.3 2.1 %collective-permute-done.4.refs_2_ = bf16[128,1024]{1,0:T(8,128)(2,1)S(1)} collective-permute-done((bf16[128,1024]{1,0:T(8,128)(2,1)S(1)}, bf16[128,1024]{1,0:T(8,128)(2,1)S(1)}, u32[]{:S(2)}, u32[]{:S(2)}) %collective-permute-start.4) | collective-permute-done | bytes 262176 | tf_op jit(solution)/shard_map/ppermute | solution.py:26
  29.5 2.8 %collective-permute-start.3 = (bf16[256,1024]{1,0:T(8,128)(2,1)S(1)}, bf16[256,1024]{1,0:T(8,128)(2,1)S(1)}, u32[]{:S(2)}, u32[]{:S(2)}) collective-permute-start(bf16[256,1024]{1,0:T(8,128)(2,1)S(1)} %copy-done), channel_id=1, source_target_pairs={{0,6},{1,7},{2,4},{3,5},{4,2},{5,3},{6,0},{7,1},{8,14},{9,15},{10,... | collective-permute-start | bytes 1572872 | tf_op jit(solution)/shard_map/ppermute | solution.py:26
  32.2 1.1 collective-permute-done.6.refs_3_
  33.4 0.7 shard_map.28.refs_7_.p0
  34.0 3.1 %collective-permute-start.7 = (bf16[4,128,1024]{2,1,0:T(8,128)(2,1)S(1)}, bf16[4,128,1024]{2,1,0:T(8,128)(2,1)S(1)}, u32[]{:S(2)}, u32[]{:S(2)}) collective-permute-start(bf16[4,128,1024]{2,1,0:T(8,128)(2,1)S(1)} %shard_map.28.refs_7_.p0), channel_id=1, source_target_pairs={{0,24},{1,25},{2,26},{3,27},{4,28},{5,29},{6,30},{7,31},{8,0},{9,1... | collective-permute-start | bytes 3145736 | tf_op jit(solution)/shard_map/ppermute | solution.py:26
  37.1 8.3 %collective-permute-done.3.refs_3_ = bf16[256,1024]{1,0:T(8,128)(2,1)S(1)} collective-permute-done((bf16[256,1024]{1,0:T(8,128)(2,1)S(1)}, bf16[256,1024]{1,0:T(8,128)(2,1)S(1)}, u32[]{:S(2)}, u32[]{:S(2)}) %collective-permute-start.3) | collective-permute-done | bytes 524320 | tf_op jit(solution)/shard_map/ppermute | solution.py:26
  45.5 1.8 %collective-permute-start.9 = (bf16[256,1024]{1,0:T(8,128)(2,1)S(1)}, bf16[256,1024]{1,0:T(8,128)(2,1)S(1)}, u32[]{:S(2)}, u32[]{:S(2)}) collective-permute-start(bf16[256,1024]{1,0:T(8,128)(2,1)S(1)} %copy-done), channel_id=1, source_target_pairs={{0,2},{1,3},{2,0},{3,1},{4,6},{5,7},{6,4},{7,5},{8,10},{9,11},{10,... | collective-permute-start | bytes 1572872 | tf_op jit(solution)/shard_map/ppermute | solution.py:26
  47.3 2.3 %collective-permute-done.12.refs_5_.next_.p1 = bf16[4,128,1024]{2,1,0:T(8,128)(2,1)S(1)} collective-permute-done((bf16[4,128,1024]{2,1,0:T(8,128)(2,1)S(1)}, bf16[4,128,1024]{2,1,0:T(8,128)(2,1)S(1)}, u32[]{:S(2)}, u32[]{:S(2)}) %collective-permute-start.12) | collective-permute-done | bytes 1048608 | tf_op jit(solution)/shard_map/ppermute | solution.py:26
  49.6 3.7 %collective-permute-done.13.refs_6_.last.p3 = bf16[4,128,1024]{2,1,0:T(8,128)(2,1)S(1)} collective-permute-done((bf16[4,128,1024]{2,1,0:T(8,128)(2,1)S(1)}, bf16[4,128,1024]{2,1,0:T(8,128)(2,1)S(1)}, u32[]{:S(2)}, u32[]{:S(2)}) %collective-permute-start.13) | collective-permute-done | bytes 1048608 | tf_op jit(solution)/shard_map/ppermute | solution.py:26
  53.3 0.7 shard_map.31
  54.0 0.1 collective-permute-start.14
  54.1 2.0 %collective-permute-start.15 = (bf16[2,128,1024]{2,1,0:T(8,128)(2,1)S(1)}, bf16[2,128,1024]{2,1,0:T(8,128)(2,1)S(1)}, u32[]{:S(2)}, u32[]{:S(2)}) collective-permute-start(bf16[2,128,1024]{2,1,0:T(8,128)(2,1)S(1)} %get-tuple-element.61), channel_id=1, source_target_pairs={{0,32},{1,33},{2,34},{3,35},{4,36},{5,37},{6,38},{7,39},{8,40},{9,... | collective-permute-start | bytes 1572872 | tf_op jit(solution)/shard_map/ppermute | solution.py:26
  56.1 0.1 collective-permute-done.9.refs_2_
  56.2 1.0 collective-permute-done.8.refs_9_.last.p3
  57.2 0.7 shard_map.34
  57.9 2.0 %collective-permute-start.17 = (bf16[2,128,1024]{2,1,0:T(8,128)(2,1)S(1)}, bf16[2,128,1024]{2,1,0:T(8,128)(2,1)S(1)}, u32[]{:S(2)}, u32[]{:S(2)}) collective-permute-start(bf16[2,128,1024]{2,1,0:T(8,128)(2,1)S(1)} %get-tuple-element.62), channel_id=1, source_target_pairs={{0,24},{1,25},{2,26},{3,27},{4,28},{5,29},{6,30},{7,31},{8,0},{9,1... | collective-permute-start | bytes 1572872 | tf_op jit(solution)/shard_map/ppermute | solution.py:26
  59.9 0.1 collective-permute-start.18
  60.0 7.7 %shard_map.30 = (f32[4,4,512,128]{3,2,1,0:T(8,128)S(1)}, bf16[2,512,1024]{2,1,0:T(8,128)(2,1)S(1)}) custom-call(s32[5]{0:T(128)S(1)} %stack.23.at, bf16[256,1024]{1,0:T(8,128)(2,1)S(1)} %copy-done, bf16[256,1024]{1,0:T(8,128)(2,1)S(1)} %collective-permute-done.5.refs_1_, bf16[256,1024]{1,0:T(8,128)(2,1)S(1)} %collective-permute-done.9.refs_2_, ...), custom_call_target="tpu_custom_call" | custom-call | flops 3221225472 | bytes 14680084 | tf_op jit(solution)/shard_map/pallas_call | solution.py:76
  67.6 1.8 %shard_map.33 = f32[2,4,512,128]{3,2,1,0:T(8,128)S(1)} custom-call(s32[5]{0:T(128)S(1)} %stack.23.at, bf16[2,512,1024]{2,1,0:T(8,128)(2,1)S(1)} %get-tuple-element.58.x, f32[4,4,512,128]{3,2,1,0:T(8,128)S(1)} %get-tuple-element.59.acc, bf16[2,128,1024]{2,1,0:T(8,128)(2,1)S(1)} %collective-permute-done.14.n_a.p2_a, ...), custom_call_target="tpu_custom_call" | custom-call | flops 26843545600 | bytes 9437204 | tf_op jit(solution)/shard_map/pallas_call | solution.py:76
  69.4 0.1 collective-permute-start.16
  69.5 2.1 %collective-permute-done.18.f_b.p2_b = bf16[2,128,1024]{2,1,0:T(8,128)(2,1)S(1)} collective-permute-done((bf16[2,128,1024]{2,1,0:T(8,128)(2,1)S(1)}, bf16[2,128,1024]{2,1,0:T(8,128)(2,1)S(1)}, u32[]{:S(2)}, u32[]{:S(2)}) %collective-permute-start.18) | collective-permute-done | bytes 524320 | tf_op jit(solution)/shard_map/ppermute | solution.py:26
  71.6 2.2 %shard_map.35 = (f32[2,512,128]{2,1,0:T(8,128)S(1)}, f32[2,512,128]{2,1,0:T(8,128)S(1)}) custom-call(s32[5]{0:T(128)S(1)} %stack.23.at, bf16[2,512,1024]{2,1,0:T(8,128)(2,1)S(1)} %get-tuple-element.58.x, bf16[2,128,1024]{2,1,0:T(8,128)(2,1)S(1)} %collective-permute-done.17.f_a.p2_a, bf16[2,128,1024]{2,1,0:T(8,128)(2,1)S(1)} %collective-permute-done.18.f_b.p2_b), custom_call_target="tpu_custom_call" | custom-call | flops 536870912 | bytes 4194324 | tf_op jit(solution)/shard_map/pallas_call | solution.py:76
  73.8 0.1 collective-permute-start.19
  73.9 0.8 shard_map.32
  74.7 1.1 collective-permute-done.19.far_got
  75.8 1.8 %shard_map.36 = (f32[8,512,128]{2,1,0:T(8,128)S(1)}, f32[8,1,512]{2,1,0:T(1,128)S(1)}) custom-call(s32[5]{0:T(128)S(1)} %stack.23.at, f32[8,512,128]{2,1,0:T(8,128)S(1)} %bitcast.7, f32[8,512,128]{2,1,0:T(8,128)S(1)} %collective-permute-done.16.got, f32[2,512,128]{2,1,0:T(8,128)S(1)} %get-tuple-element.64.far_keep, ...), custom_call_target="tpu_custom_call" | custom-call | bytes 7356436 | tf_op jit(solution)/shard_map/pallas_call | solution.py:76
  77.6 9.4 %all_to_all.20.came = f32[8,1,512]{2,1,0:T(1,128)S(1)} all-to-all(f32[8,1,512]{2,1,0:T(1,128)S(1)} %get-tuple-element.66), channel_id=1, replica_groups=mesh['z'=4,'y'=4,'l'=2,'h'=2,'c'=2] {'l','h','c'}, dimensions={0} | all-to-all | bytes 32768 | tf_op jit(solution)/shard_map/all_to_all | solution.py:479
  87.1 1.3 shard_map.37
  88.4 12.5 %all_to_all.21.came = f32[16,8,128]{2,1,0:T(8,128)S(1)} all-to-all(f32[16,8,128]{2,1,0:T(8,128)S(1)} %get-tuple-element.68), channel_id=1, replica_groups=mesh['z'=4,'y'=4,'l'=2,'h'=2,'c'=2] {'z','y'}, dimensions={0} | all-to-all | bytes 131072 | tf_op jit(solution)/shard_map/all_to_all | solution.py:479
  100.9 1.3 shard_map.38
  102.1 7.7 %all_to_all.22.came = f32[8,1,512]{2,1,0:T(1,128)S(1)} all-to-all(f32[8,1,512]{2,1,0:T(1,128)S(1)} %get-tuple-element.70), channel_id=1, replica_groups=mesh['z'=4,'y'=4,'l'=2,'h'=2,'c'=2] {'l','h','c'}, dimensions={0} | all-to-all | bytes 32768 | tf_op jit(solution)/shard_map/all_to_all | solution.py:479
  109.8 0.9 shard_map.39
  110.8 11.2 %all_to_all.23.came = f32[32,8,128]{2,1,0:T(8,128)S(1)} all-to-all(f32[32,8,128]{2,1,0:T(8,128)S(1)} %get-tuple-element.72), channel_id=1, replica_groups=mesh['z'=4,'y'=4,'l'=2,'h'=2,'c'=2] {'z','y','c'}, dimensions={0} | all-to-all | bytes 262144 | tf_op jit(solution)/shard_map/all_to_all | solution.py:479
  122.0 2.8 %shard_map.40 = (bf16[4,4,512,128]{3,2,1,0:T(8,128)(2,1)S(1)}, bf16[144,1024]{1,0:T(8,128)(2,1)S(1)}, bf16[144,1024]{1,0:T(8,128)(2,1)S(1)}) custom-call(s32[5]{0:T(128)S(1)} %stack.23.at, f32[32,8,128]{2,1,0:T(8,128)S(1)} %all_to_all.23.came, f32[8,512,128]{2,1,0:T(8,128)S(1)} %get-tuple-element.71.plan, f32[8,512,128]{2,1,0:T(8,128)S(1)} %collective-permute-done.20.other, ...), custom_call_target="tpu_custom_call" | custom-call | flops 2147483648 | bytes 11468820 | tf_op jit(solution)/shard_map/pallas_call | solution.py:76
  124.8 1.2 collective-permute-start.22
  126.1 2.1 %shard_map.42 = (bf16[128,1024]{1,0:T(8,128)(2,1)S(1)}, f32[128,1024]{1,0:T(8,128)S(1)}, f32[8,256]{1,0:T(8,128)S(1)}) custom-call(s32[5]{0:T(128)S(1)} %stack.23.at, bf16[4,4,512,128]{3,2,1,0:T(8,128)(2,1)S(1)} %get-tuple-element.74.weights, bf16[4,128,1024]{2,1,0:T(8,128)(2,1)S(1)} %shard_map.29.refs_4_.p0, ...), custom_call_target="tpu_custom_call" | custom-call | flops 2147483648 | bytes 7086100 | tf_op jit(solution)/shard_map/pallas_call | solution.py:76
  128.1 2.1 %collective-permute-start.21 = (bf16[128,1024]{1,0:T(8,128)(2,1)S(1)}, bf16[128,1024]{1,0:T(8,128)(2,1)S(1)}, u32[]{:S(2)}, u32[]{:S(2)}) collective-permute-start(bf16[128,1024]{1,0:T(8,128)(2,1)S(1)} %get-tuple-element.77), channel_id=1, source_target_pairs={{0,4},{1,5},{2,6},{3,7},{4,0},{5,1},{6,2},{7,3},{8,12},{9,13},{10,... | collective-permute-start | bytes 786440 | tf_op jit(solution)/shard_map/ppermute | solution.py:26
  130.2 2.1 %shard_map.44 = (bf16[128,1024]{1,0:T(8,128)(2,1)S(1)}, f32[128,1024]{1,0:T(8,128)S(1)}, f32[8,256]{1,0:T(8,128)S(1)}) custom-call(s32[5]{0:T(128)S(1)} %stack.23.at, bf16[4,4,512,128]{3,2,1,0:T(8,128)(2,1)S(1)} %get-tuple-element.74.weights, bf16[4,128,1024]{2,1,0:T(8,128)(2,1)S(1)} %shard_map.28.refs_7_.p0, ...), custom_call_target="tpu_custom_call" | custom-call | flops 2147483648 | bytes 7086100 | tf_op jit(solution)/shard_map/pallas_call | solution.py:76
  132.3 2.1 %collective-permute-start.26 = (bf16[128,1024]{1,0:T(8,128)(2,1)S(1)}, bf16[128,1024]{1,0:T(8,128)(2,1)S(1)}, u32[]{:S(2)}, u32[]{:S(2)}) collective-permute-start(bf16[128,1024]{1,0:T(8,128)(2,1)S(1)} %get-tuple-element.84), channel_id=1, source_target_pairs={{0,6},{1,7},{2,4},{3,5},{4,2},{5,3},{6,0},{7,1},{8,14},{9,15},{10,... | collective-permute-start | bytes 786440 | tf_op jit(solution)/shard_map/ppermute | solution.py:26
  134.5 0.7 collective-permute-done.22.came
  135.1 0.6 shard_map.43
  135.7 0.1 collective-permute-start.23
  135.8 0.1 collective-permute-done.24.came
  135.9 0.6 shard_map.45
  136.6 2.1 %collective-permute-start.25 = (bf16[144,1024]{1,0:T(8,128)(2,1)S(1)}, bf16[144,1024]{1,0:T(8,128)(2,1)S(1)}, u32[]{:S(2)}, u32[]{:S(2)}) collective-permute-start(bf16[144,1024]{1,0:T(8,128)(2,1)S(1)} %shard_map.45), channel_id=1, source_target_pairs={{0,6},{1,7},{2,4},{3,5},{4,2},{5,3},{6,0},{7,1},{8,14},{9,15},{10,... | collective-permute-start | bytes 884744 | tf_op jit(solution)/shard_map/ppermute | solution.py:26
  138.7 2.1 %shard_map.41 = (f32[256,1024]{1,0:T(8,128)S(1)}, f32[8,256]{1,0:T(8,128)S(1)}) custom-call(s32[5]{0:T(128)S(1)} %stack.23.at, bf16[4,4,512,128]{3,2,1,0:T(8,128)(2,1)S(1)} %get-tuple-element.74.weights, bf16[4,128,1024]{2,1,0:T(8,128)(2,1)S(1)} %shard_map.29.refs_4_.p0, bf16[4,128,1024]{2,1,0:T(8,128)(2,1)S(1)} %collective-permute-done.12.refs_5_.next_.p1, ...), custom_call_target="tpu_custom_call" | custom-call | flops 17179869184 | bytes 7348244 | tf_op jit(solution)/shard_map/pallas_call | solution.py:76
  140.8 0.8 collective-permute-done.21.l_low
  141.6 0.9 collective-permute-done.26.lh_high
  142.5 4.2 %collective-permute-done.23.l_high = bf16[144,1024]{1,0:T(8,128)(2,1)S(1)} collective-permute-done((bf16[144,1024]{1,0:T(8,128)(2,1)S(1)}, bf16[144,1024]{1,0:T(8,128)(2,1)S(1)}, u32[]{:S(2)}, u32[]{:S(2)}) %collective-permute-start.23) | collective-permute-done | bytes 294944 | tf_op jit(solution)/shard_map/ppermute | solution.py:26
  146.7 0.7 collective-permute-done.25.lh_low
  147.4 1.7 %shard_map.46 = bf16[256,1024]{1,0:T(8,128)(2,1)} custom-call(s32[5]{0:T(128)S(1)} %stack.23.at, f32[256,1024]{1,0:T(8,128)S(1)} %get-tuple-element.75.own, f32[8,256]{1,0:T(8,128)S(1)} %get-tuple-element.76.own_total, bf16[128,1024]{1,0:T(8,128)(2,1)S(1)} %collective-permute-done.21.l_low, bf16[144,1024]{1,0:T(8,128)(2,1)S(1)} %collective-permute-done.23.l_high, ...), custom_call_target="tpu_custom_call" | custom-call | bytes 2695188 | tf_op jit(solution)/shard_map/pallas_call | solution.py:76
  (17 shorter events, 0.1 us)
Async XLA Ops:
  0.0 29.5 %copy-start = (bf16[256,1024]{1,0:T(8,128)(2,1)S(1)}, bf16[256,1024]{1,0:T(8,128)(2,1)}, u32[]{:S(2)}) copy-start(bf16[256,1024]{1,0:T(8,128)(2,1)} %refs_0_) | copy-start | bytes 1572868
  1.1 9.5 %collective-permute-start.1 = (bf16[128,1024]{1,0:T(8,128)(2,1)S(1)}, bf16[128,1024]{1,0:T(8,128)(2,1)S(1)}, u32[]{:S(2)}, u32[]{:S(2)}) collective-permute-start(bf16[128,1024]{1,0:T(8,128)(2,1)S(1)} %get-tuple-element.85), channel_id=1, source_target_pairs={{0,2},{1,3},{2,0},{3,1},{4,6},{5,7},{6,4},{7,5},{8,10},{9,11},{10,... | collective-permute-start | bytes 786440 | tf_op jit(solution)/shard_map/ppermute | solution.py:26
  4.3 12.1 %collective-permute-start.10 = (bf16[128,1024]{1,0:T(8,128)(2,1)S(1)}, bf16[128,1024]{1,0:T(8,128)(2,1)S(1)}, u32[]{:S(2)}, u32[]{:S(2)}) collective-permute-start(bf16[128,1024]{1,0:T(8,128)(2,1)S(1)} %get-tuple-element.86.refs_0_), channel_id=1, source_target_pairs={{0,24},{1,25},{2,26},{3,27},{4,28},{5,29},{6,30},{7,31},{8,0},{9,1... | collective-permute-start | bytes 786440 | tf_op jit(solution)/shard_map/ppermute | solution.py:26
  7.3 12.1 %collective-permute-start = (bf16[128,1024]{1,0:T(8,128)(2,1)S(1)}, bf16[128,1024]{1,0:T(8,128)(2,1)S(1)}, u32[]{:S(2)}, u32[]{:S(2)}) collective-permute-start(bf16[128,1024]{1,0:T(8,128)(2,1)S(1)} %get-tuple-element.86.refs_0_), channel_id=1, source_target_pairs={{0,8},{1,9},{2,10},{3,11},{4,12},{5,13},{6,14},{7,15},{8,16},{9,17... | collective-permute-start | bytes 786440 | tf_op jit(solution)/shard_map/ppermute | solution.py:26
  10.6 9.0 %collective-permute-start.2 = (bf16[128,1024]{1,0:T(8,128)(2,1)S(1)}, bf16[128,1024]{1,0:T(8,128)(2,1)S(1)}, u32[]{:S(2)}, u32[]{:S(2)}) collective-permute-start(bf16[128,1024]{1,0:T(8,128)(2,1)S(1)} %collective-permute-done.1.refs_0_), channel_id=1, source_target_pairs={{0,96},{1,97},{2,98},{3,99},{4,100},{5,101},{6,102},{7,103},{8,104... | collective-permute-start | bytes 786440 | tf_op jit(solution)/shard_map/ppermute | solution.py:26
  14.9 17.3 %collective-permute-start.5 = (bf16[256,1024]{1,0:T(8,128)(2,1)}, bf16[256,1024]{1,0:T(8,128)(2,1)S(1)}, u32[]{:S(2)}, u32[]{:S(2)}) collective-permute-start(bf16[256,1024]{1,0:T(8,128)(2,1)} %refs_0_), channel_id=1, source_target_pairs={{0,4},{1,5},{2,6},{3,7},{4,0},{5,1},{6,2},{7,3},{8,12},{9,13},{10,... | collective-permute-start | bytes 1572872 | tf_op jit(solution)/shard_map/ppermute | solution.py:26
  16.4 7.1 %collective-permute-start.11 = (bf16[128,1024]{1,0:T(8,128)(2,1)S(1)}, bf16[128,1024]{1,0:T(8,128)(2,1)S(1)}, u32[]{:S(2)}, u32[]{:S(2)}) collective-permute-start(bf16[128,1024]{1,0:T(8,128)(2,1)S(1)} %collective-permute-done.10.refs_1_), channel_id=1, source_target_pairs={{0,24},{1,25},{2,26},{3,27},{4,28},{5,29},{6,30},{7,31},{8,0},{9,1... | collective-permute-start | bytes 786440 | tf_op jit(solution)/shard_map/ppermute | solution.py:26
  19.6 9.9 %collective-permute-start.4 = (bf16[128,1024]{1,0:T(8,128)(2,1)S(1)}, bf16[128,1024]{1,0:T(8,128)(2,1)S(1)}, u32[]{:S(2)}, u32[]{:S(2)}) collective-permute-start(bf16[128,1024]{1,0:T(8,128)(2,1)S(1)} %collective-permute-done.2.refs_1_), channel_id=1, source_target_pairs={{0,96},{1,97},{2,98},{3,99},{4,100},{5,101},{6,102},{7,103},{8,104... | collective-permute-start | bytes 786440 | tf_op jit(solution)/shard_map/ppermute | solution.py:26
  23.3 10.1 %collective-permute-start.6 = (bf16[128,1024]{1,0:T(8,128)(2,1)S(1)}, bf16[128,1024]{1,0:T(8,128)(2,1)S(1)}, u32[]{:S(2)}, u32[]{:S(2)}) collective-permute-start(bf16[128,1024]{1,0:T(8,128)(2,1)S(1)} %collective-permute-done.1.refs_0_), channel_id=1, source_target_pairs={{0,32},{1,33},{2,34},{3,35},{4,36},{5,37},{6,38},{7,39},{8,40},{9,... | collective-permute-start | bytes 786440 | tf_op jit(solution)/shard_map/ppermute | solution.py:26
  24.2 25.4 %collective-permute-start.12 = (bf16[4,128,1024]{2,1,0:T(8,128)(2,1)S(1)}, bf16[4,128,1024]{2,1,0:T(8,128)(2,1)S(1)}, u32[]{:S(2)}, u32[]{:S(2)}) collective-permute-start(bf16[4,128,1024]{2,1,0:T(8,128)(2,1)S(1)} %shard_map.29.refs_4_.p0), channel_id=1, source_target_pairs={{0,96},{1,97},{2,98},{3,99},{4,100},{5,101},{6,102},{7,103},{8,104... | collective-permute-start | bytes 3145736 | tf_op jit(solution)/shard_map/ppermute | solution.py:26
  27.3 26.0 %collective-permute-start.13 = (bf16[4,128,1024]{2,1,0:T(8,128)(2,1)S(1)}, bf16[4,128,1024]{2,1,0:T(8,128)(2,1)S(1)}, u32[]{:S(2)}, u32[]{:S(2)}) collective-permute-start(bf16[4,128,1024]{2,1,0:T(8,128)(2,1)S(1)} %shard_map.29.refs_4_.p0), channel_id=1, source_target_pairs={{0,32},{1,33},{2,34},{3,35},{4,36},{5,37},{6,38},{7,39},{8,40},{9,... | collective-permute-start | bytes 3145736 | tf_op jit(solution)/shard_map/ppermute | solution.py:26
  29.5 16.0 %collective-permute-start.3 = (bf16[256,1024]{1,0:T(8,128)(2,1)S(1)}, bf16[256,1024]{1,0:T(8,128)(2,1)S(1)}, u32[]{:S(2)}, u32[]{:S(2)}) collective-permute-start(bf16[256,1024]{1,0:T(8,128)(2,1)S(1)} %copy-done), channel_id=1, source_target_pairs={{0,6},{1,7},{2,4},{3,5},{4,2},{5,3},{6,0},{7,1},{8,14},{9,15},{10,... | collective-permute-start | bytes 1572872 | tf_op jit(solution)/shard_map/ppermute | solution.py:26
  34.0 22.1 %collective-permute-start.7 = (bf16[4,128,1024]{2,1,0:T(8,128)(2,1)S(1)}, bf16[4,128,1024]{2,1,0:T(8,128)(2,1)S(1)}, u32[]{:S(2)}, u32[]{:S(2)}) collective-permute-start(bf16[4,128,1024]{2,1,0:T(8,128)(2,1)S(1)} %shard_map.28.refs_7_.p0), channel_id=1, source_target_pairs={{0,24},{1,25},{2,26},{3,27},{4,28},{5,29},{6,30},{7,31},{8,0},{9,1... | collective-permute-start | bytes 3145736 | tf_op jit(solution)/shard_map/ppermute | solution.py:26
  37.1 20.1 %collective-permute-start.8 = (bf16[4,128,1024]{2,1,0:T(8,128)(2,1)S(1)}, bf16[4,128,1024]{2,1,0:T(8,128)(2,1)S(1)}, u32[]{:S(2)}, u32[]{:S(2)}) collective-permute-start(bf16[4,128,1024]{2,1,0:T(8,128)(2,1)S(1)} %shard_map.28.refs_7_.p0), channel_id=1, source_target_pairs={{0,8},{1,9},{2,10},{3,11},{4,12},{5,13},{6,14},{7,15},{8,16},{9,17... | collective-permute-start | bytes 3145736 | tf_op jit(solution)/shard_map/ppermute | solution.py:26
  45.5 10.7 %collective-permute-start.9 = (bf16[256,1024]{1,0:T(8,128)(2,1)S(1)}, bf16[256,1024]{1,0:T(8,128)(2,1)S(1)}, u32[]{:S(2)}, u32[]{:S(2)}) collective-permute-start(bf16[256,1024]{1,0:T(8,128)(2,1)S(1)} %copy-done), channel_id=1, source_target_pairs={{0,2},{1,3},{2,0},{3,1},{4,6},{5,7},{6,4},{7,5},{8,10},{9,11},{10,... | collective-permute-start | bytes 1572872 | tf_op jit(solution)/shard_map/ppermute | solution.py:26
  54.0 13.7 %collective-permute-start.14 = (bf16[2,128,1024]{2,1,0:T(8,128)(2,1)S(1)}, bf16[2,128,1024]{2,1,0:T(8,128)(2,1)S(1)}, u32[]{:S(2)}, u32[]{:S(2)}) collective-permute-start(bf16[2,128,1024]{2,1,0:T(8,128)(2,1)S(1)} %get-tuple-element.60), channel_id=1, source_target_pairs={{0,96},{1,97},{2,98},{3,99},{4,100},{5,101},{6,102},{7,103},{8,104... | collective-permute-start | bytes 1572872 | tf_op jit(solution)/shard_map/ppermute | solution.py:26
  54.1 13.6 %collective-permute-start.15 = (bf16[2,128,1024]{2,1,0:T(8,128)(2,1)S(1)}, bf16[2,128,1024]{2,1,0:T(8,128)(2,1)S(1)}, u32[]{:S(2)}, u32[]{:S(2)}) collective-permute-start(bf16[2,128,1024]{2,1,0:T(8,128)(2,1)S(1)} %get-tuple-element.61), channel_id=1, source_target_pairs={{0,32},{1,33},{2,34},{3,35},{4,36},{5,37},{6,38},{7,39},{8,40},{9,... | collective-permute-start | bytes 1572872 | tf_op jit(solution)/shard_map/ppermute | solution.py:26
  57.9 11.7 %collective-permute-start.17 = (bf16[2,128,1024]{2,1,0:T(8,128)(2,1)S(1)}, bf16[2,128,1024]{2,1,0:T(8,128)(2,1)S(1)}, u32[]{:S(2)}, u32[]{:S(2)}) collective-permute-start(bf16[2,128,1024]{2,1,0:T(8,128)(2,1)S(1)} %get-tuple-element.62), channel_id=1, source_target_pairs={{0,24},{1,25},{2,26},{3,27},{4,28},{5,29},{6,30},{7,31},{8,0},{9,1... | collective-permute-start | bytes 1572872 | tf_op jit(solution)/shard_map/ppermute | solution.py:26
  59.9 11.7 %collective-permute-start.18 = (bf16[2,128,1024]{2,1,0:T(8,128)(2,1)S(1)}, bf16[2,128,1024]{2,1,0:T(8,128)(2,1)S(1)}, u32[]{:S(2)}, u32[]{:S(2)}) collective-permute-start(bf16[2,128,1024]{2,1,0:T(8,128)(2,1)S(1)} %get-tuple-element.63), channel_id=1, source_target_pairs={{0,8},{1,9},{2,10},{3,11},{4,12},{5,13},{6,14},{7,15},{8,16},{9,17... | collective-permute-start | bytes 1572872 | tf_op jit(solution)/shard_map/ppermute | solution.py:26
  69.4 6.4 %collective-permute-start.16 = (f32[8,512,128]{2,1,0:T(8,128)S(1)}, f32[8,512,128]{2,1,0:T(8,128)S(1)}, u32[]{:S(2)}, u32[]{:S(2)}) collective-permute-start(f32[8,512,128]{2,1,0:T(8,128)S(1)} %bitcast.8), channel_id=1, source_target_pairs={{0,1},{1,0},{2,3},{3,2},{4,5},{5,4},{6,7},{7,6},{8,9},{9,8},{10,11... | collective-permute-start | bytes 6291464 | tf_op jit(solution)/shard_map/ppermute | solution.py:26
  73.8 2.0 %collective-permute-start.19 = (f32[2,512,128]{2,1,0:T(8,128)S(1)}, f32[2,512,128]{2,1,0:T(8,128)S(1)}, u32[]{:S(2)}, u32[]{:S(2)}) collective-permute-start(f32[2,512,128]{2,1,0:T(8,128)S(1)} %get-tuple-element.65), channel_id=1, source_target_pairs={{0,1},{1,0},{2,3},{3,2},{4,5},{5,4},{6,7},{7,6},{8,9},{9,8},{10,11... | collective-permute-start | bytes 1572872 | tf_op jit(solution)/shard_map/ppermute | solution.py:26
  102.1 19.9 %collective-permute-start.20 = (f32[8,512,128]{2,1,0:T(8,128)S(1)}, f32[8,512,128]{2,1,0:T(8,128)S(1)}, u32[]{:S(2)}, u32[]{:S(2)}) collective-permute-start(f32[8,512,128]{2,1,0:T(8,128)S(1)} %get-tuple-element.71.plan), channel_id=1, source_target_pairs={{0,1},{1,0},{2,3},{3,2},{4,5},{5,4},{6,7},{7,6},{8,9},{9,8},{10,11... | collective-permute-start | bytes 6291464 | tf_op jit(solution)/shard_map/ppermute | solution.py:26
  124.8 10.3 %collective-permute-start.22 = (bf16[144,1024]{1,0:T(8,128)(2,1)S(1)}, bf16[144,1024]{1,0:T(8,128)(2,1)S(1)}, u32[]{:S(2)}, u32[]{:S(2)}) collective-permute-start(bf16[144,1024]{1,0:T(8,128)(2,1)S(1)} %get-tuple-element.80), channel_id=1, source_target_pairs={{0,6},{1,7},{2,4},{3,5},{4,2},{5,3},{6,0},{7,1},{8,14},{9,15},{10,... | collective-permute-start | bytes 884744 | tf_op jit(solution)/shard_map/ppermute | solution.py:26
  126.0 9.9 %collective-permute-start.24 = (bf16[144,1024]{1,0:T(8,128)(2,1)S(1)}, bf16[144,1024]{1,0:T(8,128)(2,1)S(1)}, u32[]{:S(2)}, u32[]{:S(2)}) collective-permute-start(bf16[144,1024]{1,0:T(8,128)(2,1)S(1)} %get-tuple-element.83), channel_id=1, source_target_pairs={{0,4},{1,5},{2,6},{3,7},{4,0},{5,1},{6,2},{7,3},{8,12},{9,13},{10,... | collective-permute-start | bytes 884744 | tf_op jit(solution)/shard_map/ppermute | solution.py:26
  128.1 13.4 %collective-permute-start.21 = (bf16[128,1024]{1,0:T(8,128)(2,1)S(1)}, bf16[128,1024]{1,0:T(8,128)(2,1)S(1)}, u32[]{:S(2)}, u32[]{:S(2)}) collective-permute-start(bf16[128,1024]{1,0:T(8,128)(2,1)S(1)} %get-tuple-element.77), channel_id=1, source_target_pairs={{0,4},{1,5},{2,6},{3,7},{4,0},{5,1},{6,2},{7,3},{8,12},{9,13},{10,... | collective-permute-start | bytes 786440 | tf_op jit(solution)/shard_map/ppermute | solution.py:26
  132.3 10.2 %collective-permute-start.26 = (bf16[128,1024]{1,0:T(8,128)(2,1)S(1)}, bf16[128,1024]{1,0:T(8,128)(2,1)S(1)}, u32[]{:S(2)}, u32[]{:S(2)}) collective-permute-start(bf16[128,1024]{1,0:T(8,128)(2,1)S(1)} %get-tuple-element.84), channel_id=1, source_target_pairs={{0,6},{1,7},{2,4},{3,5},{4,2},{5,3},{6,0},{7,1},{8,14},{9,15},{10,... | collective-permute-start | bytes 786440 | tf_op jit(solution)/shard_map/ppermute | solution.py:26
  135.7 11.0 %collective-permute-start.23 = (bf16[144,1024]{1,0:T(8,128)(2,1)S(1)}, bf16[144,1024]{1,0:T(8,128)(2,1)S(1)}, u32[]{:S(2)}, u32[]{:S(2)}) collective-permute-start(bf16[144,1024]{1,0:T(8,128)(2,1)S(1)} %shard_map.43), channel_id=1, source_target_pairs={{0,4},{1,5},{2,6},{3,7},{4,0},{5,1},{6,2},{7,3},{8,12},{9,13},{10,... | collective-permute-start | bytes 884744 | tf_op jit(solution)/shard_map/ppermute | solution.py:26
  136.6 10.8 %collective-permute-start.25 = (bf16[144,1024]{1,0:T(8,128)(2,1)S(1)}, bf16[144,1024]{1,0:T(8,128)(2,1)S(1)}, u32[]{:S(2)}, u32[]{:S(2)}) collective-permute-start(bf16[144,1024]{1,0:T(8,128)(2,1)S(1)} %shard_map.45), channel_id=1, source_target_pairs={{0,6},{1,7},{2,4},{3,5},{4,2},{5,3},{6,0},{7,1},{8,14},{9,15},{10,... | collective-permute-start | bytes 884744 | tf_op jit(solution)/shard_map/ppermute | solution.py:26

commit v9 on v7

--- a/solution.py
+++ b/solution.py
@@ -407,11 +407,10 @@
     far = flip(lax.dynamic_slice_in_dim(noise_rows, (1 - h) * mid, mid), "h")
     near_1, near_3 = from_y(near, 1), from_y(near, 3)
     far, data_rows = wave((far, data_rows))
-    data_l = flip(data_rows, "l")
+    data_l, data_lh = flip(data_rows, "l"), flip(data_rows, "lh")
     near_2 = from_y(near_1, 1)
-    near_3, far_1, far_3, data_rows = wave((near_3, from_z(far, 1), from_z(far, 3), data_rows))
-    data_lh = flip(data_rows, "lh")
-    far_2, data_l, data_rows = wave((from_z(far_1, 1), data_l, data_rows))
+    near_3, far_1, far_3 = wave((near_3, from_z(far, 1), from_z(far, 3)))
+    far_2, data_l, data_lh, data_rows = wave((from_z(far_1, 1), data_l, data_lh, data_rows))
     sems = pltpu.SemaphoreType.DMA((4,))
 
     def stacked(*blocks):
@@ -429,7 +428,6 @@
     near, far = stacked(near, near_1, near_2, near_3), stacked(far, far_1, far_2, far_3)
     near_next, near_last = from_z(near, 1), from_z(near, 3)
     far_next, far_last = from_y(far, 1), from_y(far, 3)
-    data_lh, data_rows = wave((data_lh, data_rows))
     data_h = flip(data_rows, "h")
     far_next, far_last, data_h = wave((far_next, far_last, data_h))
     nears, fars = (near, near_next, near_last), (far, far_next, far_last)

time: 148 us -> 147 us (level)
  starting transfers between devices: 37.9 us -> 41.5 us
  waiting for transfers between devices: 35.3 us -> 32.2 us
    ppermute x27, starting transfers between devices: 37.9 us -> 41.5 us  [move(): return lax.ppermute(value, AXES, pairs)]
    ppermute x27, waiting for transfers between devices: 35.3 us -> 32.2 us  [move(): return lax.ppermute(value, AXES, pairs)]
  transfers between devices with their start and end apart: 27 -> 27, of which waited for: 16 -> 15; matrix products, arithmetic and copies ran while one was open for 0% -> 0% of each run, Pallas kernels for 16% -> 16%
where the time goes in v9:
time: 147 us
  starting transfers between devices  41.5 us (28%)
  blocking collectives  39.5 us (27%)
  waiting for transfers between devices  32.2 us (22%)
  Pallas kernels  32.2 us (22%)
    ppermute x27, starting transfers between devices, move(): return lax.ppermute(value, AXES, pairs)  41.5 us
    all_to_all x4, blocking collectives, exchange(): return lax.all_to_all(sent, axes, 0, 0, tiled=True)  39.5 us
    ppermute x27, waiting for transfers between devices, move(): return lax.ppermute(value, AXES, pairs)  32.2 us
    pallas_call x19, Pallas kernels, call(): pl.pallas_call(kernel, out_shape=outs, in_specs=[pl.BlockSpec(memory_spac...  32.2 us
  transfers between devices with their start and end apart: 27, of which 15 were waited for; matrix products, arithmetic and copies ran while one was open for 0% of the time, Pallas kernels for 16%

profile of v9, /device:TPU:0, one launch (start us, length us, event | category | flops | bytes accessed | tf_op | source)
XLA Modules:
  0.0 146.7 jit_solution(8214155185417952924)
XLA Ops:
  0.0 1.1 constant_dynamic-slice_fusion
  1.1 3.2 %collective-permute-start.1 = (bf16[128,1024]{1,0:T(8,128)(2,1)S(1)}, bf16[128,1024]{1,0:T(8,128)(2,1)S(1)}, u32[]{:S(2)}, u32[]{:S(2)}) collective-permute-start(bf16[128,1024]{1,0:T(8,128)(2,1)S(1)} %get-tuple-element.83), channel_id=1, source_target_pairs={{0,2},{1,3},{2,0},{3,1},{4,6},{5,7},{6,4},{7,5},{8,10},{9,11},{10,... | collective-permute-start | bytes 786440 | tf_op jit(solution)/shard_map/ppermute | solution.py:26
  4.3 1.6 %collective-permute-start = (bf16[128,1024]{1,0:T(8,128)(2,1)S(1)}, bf16[128,1024]{1,0:T(8,128)(2,1)S(1)}, u32[]{:S(2)}, u32[]{:S(2)}) collective-permute-start(bf16[128,1024]{1,0:T(8,128)(2,1)S(1)} %get-tuple-element.84.refs_0_), channel_id=1, source_target_pairs={{0,8},{1,9},{2,10},{3,11},{4,12},{5,13},{6,14},{7,15},{8,16},{9,17... | collective-permute-start | bytes 786440 | tf_op jit(solution)/shard_map/ppermute | solution.py:26
  5.8 1.7 %collective-permute-start.10 = (bf16[128,1024]{1,0:T(8,128)(2,1)S(1)}, bf16[128,1024]{1,0:T(8,128)(2,1)S(1)}, u32[]{:S(2)}, u32[]{:S(2)}) collective-permute-start(bf16[128,1024]{1,0:T(8,128)(2,1)S(1)} %get-tuple-element.84.refs_0_), channel_id=1, source_target_pairs={{0,24},{1,25},{2,26},{3,27},{4,28},{5,29},{6,30},{7,31},{8,0},{9,1... | collective-permute-start | bytes 786440 | tf_op jit(solution)/shard_map/ppermute | solution.py:26
  7.5 3.1 %collective-permute-done.1.refs_0_ = bf16[128,1024]{1,0:T(8,128)(2,1)S(1)} collective-permute-done((bf16[128,1024]{1,0:T(8,128)(2,1)S(1)}, bf16[128,1024]{1,0:T(8,128)(2,1)S(1)}, u32[]{:S(2)}, u32[]{:S(2)}) %collective-permute-start.1) | collective-permute-done | bytes 262176 | tf_op jit(solution)/shard_map/ppermute | solution.py:26
  10.6 4.3 %collective-permute-start.2 = (bf16[128,1024]{1,0:T(8,128)(2,1)S(1)}, bf16[128,1024]{1,0:T(8,128)(2,1)S(1)}, u32[]{:S(2)}, u32[]{:S(2)}) collective-permute-start(bf16[128,1024]{1,0:T(8,128)(2,1)S(1)} %collective-permute-done.1.refs_0_), channel_id=1, source_target_pairs={{0,96},{1,97},{2,98},{3,99},{4,100},{5,101},{6,102},{7,103},{8,104... | collective-permute-start | bytes 786440 | tf_op jit(solution)/shard_map/ppermute | solution.py:26
  14.8 0.0 collective-permute-start.3
  14.8 1.5 %collective-permute-start.5 = (bf16[256,1024]{1,0:T(8,128)(2,1)}, bf16[256,1024]{1,0:T(8,128)(2,1)S(1)}, u32[]{:S(2)}, u32[]{:S(2)}) collective-permute-start(bf16[256,1024]{1,0:T(8,128)(2,1)} %refs_0_), channel_id=1, source_target_pairs={{0,4},{1,5},{2,6},{3,7},{4,0},{5,1},{6,2},{7,3},{8,12},{9,13},{10,... | collective-permute-start | bytes 1572872 | tf_op jit(solution)/shard_map/ppermute | solution.py:26
  16.3 2.1 %collective-permute-start.6 = (bf16[256,1024]{1,0:T(8,128)(2,1)}, bf16[256,1024]{1,0:T(8,128)(2,1)S(1)}, u32[]{:S(2)}, u32[]{:S(2)}) collective-permute-start(bf16[256,1024]{1,0:T(8,128)(2,1)} %refs_0_), channel_id=1, source_target_pairs={{0,6},{1,7},{2,4},{3,5},{4,2},{5,3},{6,0},{7,1},{8,14},{9,15},{10,... | collective-permute-start | bytes 1572872 | tf_op jit(solution)/shard_map/ppermute | solution.py:26
  18.4 3.0 %collective-permute-start.11 = (bf16[128,1024]{1,0:T(8,128)(2,1)S(1)}, bf16[128,1024]{1,0:T(8,128)(2,1)S(1)}, u32[]{:S(2)}, u32[]{:S(2)}) collective-permute-start(bf16[128,1024]{1,0:T(8,128)(2,1)S(1)} %collective-permute-done.10.refs_1_), channel_id=1, source_target_pairs={{0,24},{1,25},{2,26},{3,27},{4,28},{5,29},{6,30},{7,31},{8,0},{9,1... | collective-permute-start | bytes 786440 | tf_op jit(solution)/shard_map/ppermute | solution.py:26
  21.4 1.5 %collective-permute-done.3.refs_3_ = bf16[128,1024]{1,0:T(8,128)(2,1)S(1)} collective-permute-done((bf16[128,1024]{1,0:T(8,128)(2,1)S(1)}, bf16[128,1024]{1,0:T(8,128)(2,1)S(1)}, u32[]{:S(2)}, u32[]{:S(2)}) %collective-permute-start.3) | collective-permute-done | bytes 262176 | tf_op jit(solution)/shard_map/ppermute | solution.py:26
  22.9 1.7 %collective-permute-start.4 = (bf16[128,1024]{1,0:T(8,128)(2,1)S(1)}, bf16[128,1024]{1,0:T(8,128)(2,1)S(1)}, u32[]{:S(2)}, u32[]{:S(2)}) collective-permute-start(bf16[128,1024]{1,0:T(8,128)(2,1)S(1)} %collective-permute-done.2.refs_1_), channel_id=1, source_target_pairs={{0,96},{1,97},{2,98},{3,99},{4,100},{5,101},{6,102},{7,103},{8,104... | collective-permute-start | bytes 786440 | tf_op jit(solution)/shard_map/ppermute | solution.py:26
  24.7 0.1 stack.23.at
  24.8 0.6 collective-permute-done.11.refs_2_
  25.3 0.7 shard_map.29.refs_4_.p0
  26.0 3.3 %collective-permute-start.12 = (bf16[4,128,1024]{2,1,0:T(8,128)(2,1)S(1)}, bf16[4,128,1024]{2,1,0:T(8,128)(2,1)S(1)}, u32[]{:S(2)}, u32[]{:S(2)}) collective-permute-start(bf16[4,128,1024]{2,1,0:T(8,128)(2,1)S(1)} %shard_map.29.refs_4_.p0), channel_id=1, source_target_pairs={{0,96},{1,97},{2,98},{3,99},{4,100},{5,101},{6,102},{7,103},{8,104... | collective-permute-start | bytes 3145736 | tf_op jit(solution)/shard_map/ppermute | solution.py:26
  29.3 0.0 collective-permute-start.13
  29.3 2.9 %collective-permute-done.4.refs_2_ = bf16[128,1024]{1,0:T(8,128)(2,1)S(1)} collective-permute-done((bf16[128,1024]{1,0:T(8,128)(2,1)S(1)}, bf16[128,1024]{1,0:T(8,128)(2,1)S(1)}, u32[]{:S(2)}, u32[]{:S(2)}) %collective-permute-start.4) | collective-permute-done | bytes 262176 | tf_op jit(solution)/shard_map/ppermute | solution.py:26
  32.2 0.7 shard_map.28.refs_7_.p0
  32.8 2.9 %collective-permute-start.7 = (bf16[4,128,1024]{2,1,0:T(8,128)(2,1)S(1)}, bf16[4,128,1024]{2,1,0:T(8,128)(2,1)S(1)}, u32[]{:S(2)}, u32[]{:S(2)}) collective-permute-start(bf16[4,128,1024]{2,1,0:T(8,128)(2,1)S(1)} %shard_map.28.refs_7_.p0), channel_id=1, source_target_pairs={{0,24},{1,25},{2,26},{3,27},{4,28},{5,29},{6,30},{7,31},{8,0},{9,1... | collective-permute-start | bytes 3145736 | tf_op jit(solution)/shard_map/ppermute | solution.py:26
  35.8 3.2 %collective-permute-start.9 = (bf16[256,1024]{1,0:T(8,128)(2,1)S(1)}, bf16[256,1024]{1,0:T(8,128)(2,1)S(1)}, u32[]{:S(2)}, u32[]{:S(2)}) collective-permute-start(bf16[256,1024]{1,0:T(8,128)(2,1)S(1)} %copy-done), channel_id=1, source_target_pairs={{0,2},{1,3},{2,0},{3,1},{4,6},{5,7},{6,4},{7,5},{8,10},{9,11},{10,... | collective-permute-start | bytes 1572872 | tf_op jit(solution)/shard_map/ppermute | solution.py:26
  39.0 12.4 %collective-permute-done.12.refs_5_.next_.p1 = bf16[4,128,1024]{2,1,0:T(8,128)(2,1)S(1)} collective-permute-done((bf16[4,128,1024]{2,1,0:T(8,128)(2,1)S(1)}, bf16[4,128,1024]{2,1,0:T(8,128)(2,1)S(1)}, u32[]{:S(2)}, u32[]{:S(2)}) %collective-permute-start.12) | collective-permute-done | bytes 1048608 | tf_op jit(solution)/shard_map/ppermute | solution.py:26
  51.4 0.9 collective-permute-done.13.refs_6_.last.p3
  52.3 0.7 shard_map.31
  52.9 2.5 %collective-permute-start.14 = (bf16[2,128,1024]{2,1,0:T(8,128)(2,1)S(1)}, bf16[2,128,1024]{2,1,0:T(8,128)(2,1)S(1)}, u32[]{:S(2)}, u32[]{:S(2)}) collective-permute-start(bf16[2,128,1024]{2,1,0:T(8,128)(2,1)S(1)} %get-tuple-element.58), channel_id=1, source_target_pairs={{0,96},{1,97},{2,98},{3,99},{4,100},{5,101},{6,102},{7,103},{8,104... | collective-permute-start | bytes 1572872 | tf_op jit(solution)/shard_map/ppermute | solution.py:26
  55.5 1.7 %collective-permute-done.8.refs_9_.last.p3 = bf16[4,128,1024]{2,1,0:T(8,128)(2,1)S(1)} collective-permute-done((bf16[4,128,1024]{2,1,0:T(8,128)(2,1)S(1)}, bf16[4,128,1024]{2,1,0:T(8,128)(2,1)S(1)}, u32[]{:S(2)}, u32[]{:S(2)}) %collective-permute-start.8) | collective-permute-done | bytes 1048608 | tf_op jit(solution)/shard_map/ppermute | solution.py:26
  57.2 0.7 shard_map.34
  57.9 1.6 %collective-permute-start.17 = (bf16[2,128,1024]{2,1,0:T(8,128)(2,1)S(1)}, bf16[2,128,1024]{2,1,0:T(8,128)(2,1)S(1)}, u32[]{:S(2)}, u32[]{:S(2)}) collective-permute-start(bf16[2,128,1024]{2,1,0:T(8,128)(2,1)S(1)} %get-tuple-element.60), channel_id=1, source_target_pairs={{0,24},{1,25},{2,26},{3,27},{4,28},{5,29},{6,30},{7,31},{8,0},{9,1... | collective-permute-start | bytes 1572872 | tf_op jit(solution)/shard_map/ppermute | solution.py:26
  59.5 0.5 collective-permute-start.18
  60.0 7.7 %shard_map.30 = (f32[4,4,512,128]{3,2,1,0:T(8,128)S(1)}, bf16[2,512,1024]{2,1,0:T(8,128)(2,1)S(1)}) custom-call(s32[5]{0:T(128)S(1)} %stack.23.at, bf16[256,1024]{1,0:T(8,128)(2,1)S(1)} %copy-done, bf16[256,1024]{1,0:T(8,128)(2,1)S(1)} %collective-permute-done.5.refs_1_, bf16[256,1024]{1,0:T(8,128)(2,1)S(1)} %collective-permute-done.9.refs_2_, ...), custom_call_target="tpu_custom_call" | custom-call | flops 3221225472 | bytes 14680084 | tf_op jit(solution)/shard_map/pallas_call | solution.py:76
  67.6 0.5 collective-permute-done.15.n_b.p2_b
  68.1 1.8 %shard_map.33 = f32[2,4,512,128]{3,2,1,0:T(8,128)S(1)} custom-call(s32[5]{0:T(128)S(1)} %stack.23.at, bf16[2,512,1024]{2,1,0:T(8,128)(2,1)S(1)} %get-tuple-element.56.x, f32[4,4,512,128]{3,2,1,0:T(8,128)S(1)} %get-tuple-element.57.acc, bf16[2,128,1024]{2,1,0:T(8,128)(2,1)S(1)} %collective-permute-done.14.n_a.p2_a, ...), custom_call_target="tpu_custom_call" | custom-call | flops 26843545600 | bytes 9437204 | tf_op jit(solution)/shard_map/pallas_call | solution.py:76
  69.9 0.1 collective-permute-start.16
  70.0 2.2 %shard_map.35 = (f32[2,512,128]{2,1,0:T(8,128)S(1)}, f32[2,512,128]{2,1,0:T(8,128)S(1)}) custom-call(s32[5]{0:T(128)S(1)} %stack.23.at, bf16[2,512,1024]{2,1,0:T(8,128)(2,1)S(1)} %get-tuple-element.56.x, bf16[2,128,1024]{2,1,0:T(8,128)(2,1)S(1)} %collective-permute-done.17.f_a.p2_a, bf16[2,128,1024]{2,1,0:T(8,128)(2,1)S(1)} %collective-permute-done.18.f_b.p2_b), custom_call_target="tpu_custom_call" | custom-call | flops 536870912 | bytes 4194324 | tf_op jit(solution)/shard_map/pallas_call | solution.py:76
  72.2 0.6 collective-permute-start.19
  72.8 0.8 shard_map.32
  73.6 1.3 collective-permute-done.19.far_got
  74.9 1.8 %shard_map.36 = (f32[8,512,128]{2,1,0:T(8,128)S(1)}, f32[8,1,512]{2,1,0:T(1,128)S(1)}) custom-call(s32[5]{0:T(128)S(1)} %stack.23.at, f32[8,512,128]{2,1,0:T(8,128)S(1)} %bitcast.7, f32[8,512,128]{2,1,0:T(8,128)S(1)} %collective-permute-done.16.got, f32[2,512,128]{2,1,0:T(8,128)S(1)} %get-tuple-element.62.far_keep, ...), custom_call_target="tpu_custom_call" | custom-call | bytes 7356436 | tf_op jit(solution)/shard_map/pallas_call | solution.py:76
  76.7 8.7 %all_to_all.20.came = f32[8,1,512]{2,1,0:T(1,128)S(1)} all-to-all(f32[8,1,512]{2,1,0:T(1,128)S(1)} %get-tuple-element.64), channel_id=1, replica_groups=mesh['z'=4,'y'=4,'l'=2,'h'=2,'c'=2] {'l','h','c'}, dimensions={0} | all-to-all | bytes 32768 | tf_op jit(solution)/shard_map/all_to_all | solution.py:476
  85.4 1.3 shard_map.37
  86.7 11.9 %all_to_all.21.came = f32[16,8,128]{2,1,0:T(8,128)S(1)} all-to-all(f32[16,8,128]{2,1,0:T(8,128)S(1)} %get-tuple-element.66), channel_id=1, replica_groups=mesh['z'=4,'y'=4,'l'=2,'h'=2,'c'=2] {'z','y'}, dimensions={0} | all-to-all | bytes 131072 | tf_op jit(solution)/shard_map/all_to_all | solution.py:476
  98.5 1.3 shard_map.38
  99.8 0.0 collective-permute-start.20
  99.8 7.7 %all_to_all.22.came = f32[8,1,512]{2,1,0:T(1,128)S(1)} all-to-all(f32[8,1,512]{2,1,0:T(1,128)S(1)} %get-tuple-element.68), channel_id=1, replica_groups=mesh['z'=4,'y'=4,'l'=2,'h'=2,'c'=2] {'l','h','c'}, dimensions={0} | all-to-all | bytes 32768 | tf_op jit(solution)/shard_map/all_to_all | solution.py:476
  107.5 0.9 shard_map.39
  108.4 11.2 %all_to_all.23.came = f32[32,8,128]{2,1,0:T(8,128)S(1)} all-to-all(f32[32,8,128]{2,1,0:T(8,128)S(1)} %get-tuple-element.70), channel_id=1, replica_groups=mesh['z'=4,'y'=4,'l'=2,'h'=2,'c'=2] {'z','y','c'}, dimensions={0} | all-to-all | bytes 262144 | tf_op jit(solution)/shard_map/all_to_all | solution.py:476
  119.6 2.8 %shard_map.40 = (bf16[4,4,512,128]{3,2,1,0:T(8,128)(2,1)S(1)}, bf16[144,1024]{1,0:T(8,128)(2,1)S(1)}, bf16[144,1024]{1,0:T(8,128)(2,1)S(1)}) custom-call(s32[5]{0:T(128)S(1)} %stack.23.at, f32[32,8,128]{2,1,0:T(8,128)S(1)} %all_to_all.23.came, f32[8,512,128]{2,1,0:T(8,128)S(1)} %get-tuple-element.69.plan, f32[8,512,128]{2,1,0:T(8,128)S(1)} %collective-permute-done.20.other, ...), custom_call_target="tpu_custom_call" | custom-call | flops 2147483648 | bytes 11468820 | tf_op jit(solution)/shard_map/pallas_call | solution.py:76
  122.5 1.2 collective-permute-start.22
  123.7 2.1 %shard_map.42 = (bf16[128,1024]{1,0:T(8,128)(2,1)S(1)}, f32[128,1024]{1,0:T(8,128)S(1)}, f32[8,256]{1,0:T(8,128)S(1)}) custom-call(s32[5]{0:T(128)S(1)} %stack.23.at, bf16[4,4,512,128]{3,2,1,0:T(8,128)(2,1)S(1)} %get-tuple-element.72.weights, bf16[4,128,1024]{2,1,0:T(8,128)(2,1)S(1)} %shard_map.29.refs_4_.p0, ...), custom_call_target="tpu_custom_call" | custom-call | flops 2147483648 | bytes 7086100 | tf_op jit(solution)/shard_map/pallas_call | solution.py:76
  125.8 2.1 %collective-permute-start.21 = (bf16[128,1024]{1,0:T(8,128)(2,1)S(1)}, bf16[128,1024]{1,0:T(8,128)(2,1)S(1)}, u32[]{:S(2)}, u32[]{:S(2)}) collective-permute-start(bf16[128,1024]{1,0:T(8,128)(2,1)S(1)} %get-tuple-element.75), channel_id=1, source_target_pairs={{0,4},{1,5},{2,6},{3,7},{4,0},{5,1},{6,2},{7,3},{8,12},{9,13},{10,... | collective-permute-start | bytes 786440 | tf_op jit(solution)/shard_map/ppermute | solution.py:26
  127.9 2.1 %shard_map.44 = (bf16[128,1024]{1,0:T(8,128)(2,1)S(1)}, f32[128,1024]{1,0:T(8,128)S(1)}, f32[8,256]{1,0:T(8,128)S(1)}) custom-call(s32[5]{0:T(128)S(1)} %stack.23.at, bf16[4,4,512,128]{3,2,1,0:T(8,128)(2,1)S(1)} %get-tuple-element.72.weights, bf16[4,128,1024]{2,1,0:T(8,128)(2,1)S(1)} %shard_map.28.refs_7_.p0, ...), custom_call_target="tpu_custom_call" | custom-call | flops 2147483648 | bytes 7086100 | tf_op jit(solution)/shard_map/pallas_call | solution.py:76
  130.0 2.1 %collective-permute-start.26 = (bf16[128,1024]{1,0:T(8,128)(2,1)S(1)}, bf16[128,1024]{1,0:T(8,128)(2,1)S(1)}, u32[]{:S(2)}, u32[]{:S(2)}) collective-permute-start(bf16[128,1024]{1,0:T(8,128)(2,1)S(1)} %get-tuple-element.82), channel_id=1, source_target_pairs={{0,6},{1,7},{2,4},{3,5},{4,2},{5,3},{6,0},{7,1},{8,14},{9,15},{10,... | collective-permute-start | bytes 786440 | tf_op jit(solution)/shard_map/ppermute | solution.py:26
  132.1 0.7 collective-permute-done.22.came
  132.8 0.6 shard_map.43
  133.4 0.1 collective-permute-start.23
  133.5 0.1 collective-permute-done.24.came
  133.6 0.6 shard_map.45
  134.2 2.1 %collective-permute-start.25 = (bf16[144,1024]{1,0:T(8,128)(2,1)S(1)}, bf16[144,1024]{1,0:T(8,128)(2,1)S(1)}, u32[]{:S(2)}, u32[]{:S(2)}) collective-permute-start(bf16[144,1024]{1,0:T(8,128)(2,1)S(1)} %shard_map.45), channel_id=1, source_target_pairs={{0,6},{1,7},{2,4},{3,5},{4,2},{5,3},{6,0},{7,1},{8,14},{9,15},{10,... | collective-permute-start | bytes 884744 | tf_op jit(solution)/shard_map/ppermute | solution.py:26
  136.4 2.1 %shard_map.41 = (f32[256,1024]{1,0:T(8,128)S(1)}, f32[8,256]{1,0:T(8,128)S(1)}) custom-call(s32[5]{0:T(128)S(1)} %stack.23.at, bf16[4,4,512,128]{3,2,1,0:T(8,128)(2,1)S(1)} %get-tuple-element.72.weights, bf16[4,128,1024]{2,1,0:T(8,128)(2,1)S(1)} %shard_map.29.refs_4_.p0, bf16[4,128,1024]{2,1,0:T(8,128)(2,1)S(1)} %collective-permute-done.12.refs_5_.next_.p1, ...), custom_call_target="tpu_custom_call" | custom-call | flops 17179869184 | bytes 7348244 | tf_op jit(solution)/shard_map/pallas_call | solution.py:76
  138.4 0.8 collective-permute-done.21.l_low
  139.2 0.9 collective-permute-done.26.lh_high
  140.1 4.2 %collective-permute-done.23.l_high = bf16[144,1024]{1,0:T(8,128)(2,1)S(1)} collective-permute-done((bf16[144,1024]{1,0:T(8,128)(2,1)S(1)}, bf16[144,1024]{1,0:T(8,128)(2,1)S(1)}, u32[]{:S(2)}, u32[]{:S(2)}) %collective-permute-start.23) | collective-permute-done | bytes 294944 | tf_op jit(solution)/shard_map/ppermute | solution.py:26
  144.4 0.7 collective-permute-done.25.lh_low
  145.1 1.7 %shard_map.46 = bf16[256,1024]{1,0:T(8,128)(2,1)} custom-call(s32[5]{0:T(128)S(1)} %stack.23.at, f32[256,1024]{1,0:T(8,128)S(1)} %get-tuple-element.73.own, f32[8,256]{1,0:T(8,128)S(1)} %get-tuple-element.74.own_total, bf16[128,1024]{1,0:T(8,128)(2,1)S(1)} %collective-permute-done.21.l_low, bf16[144,1024]{1,0:T(8,128)(2,1)S(1)} %collective-permute-done.23.l_high, ...), custom_call_target="tpu_custom_call" | custom-call | bytes 2695188 | tf_op jit(solution)/shard_map/pallas_call | solution.py:76
  (17 shorter events, 0.0 us)
Async XLA Ops:
  1.1 9.5 %collective-permute-start.1 = (bf16[128,1024]{1,0:T(8,128)(2,1)S(1)}, bf16[128,1024]{1,0:T(8,128)(2,1)S(1)}, u32[]{:S(2)}, u32[]{:S(2)}) collective-permute-start(bf16[128,1024]{1,0:T(8,128)(2,1)S(1)} %get-tuple-element.83), channel_id=1, source_target_pairs={{0,2},{1,3},{2,0},{3,1},{4,6},{5,7},{6,4},{7,5},{8,10},{9,11},{10,... | collective-permute-start | bytes 786440 | tf_op jit(solution)/shard_map/ppermute | solution.py:26
  4.3 12.1 %collective-permute-start = (bf16[128,1024]{1,0:T(8,128)(2,1)S(1)}, bf16[128,1024]{1,0:T(8,128)(2,1)S(1)}, u32[]{:S(2)}, u32[]{:S(2)}) collective-permute-start(bf16[128,1024]{1,0:T(8,128)(2,1)S(1)} %get-tuple-element.84.refs_0_), channel_id=1, source_target_pairs={{0,8},{1,9},{2,10},{3,11},{4,12},{5,13},{6,14},{7,15},{8,16},{9,17... | collective-permute-start | bytes 786440 | tf_op jit(solution)/shard_map/ppermute | solution.py:26
  5.8 12.6 %collective-permute-start.10 = (bf16[128,1024]{1,0:T(8,128)(2,1)S(1)}, bf16[128,1024]{1,0:T(8,128)(2,1)S(1)}, u32[]{:S(2)}, u32[]{:S(2)}) collective-permute-start(bf16[128,1024]{1,0:T(8,128)(2,1)S(1)} %get-tuple-element.84.refs_0_), channel_id=1, source_target_pairs={{0,24},{1,25},{2,26},{3,27},{4,28},{5,29},{6,30},{7,31},{8,0},{9,1... | collective-permute-start | bytes 786440 | tf_op jit(solution)/shard_map/ppermute | solution.py:26
  10.6 10.9 %collective-permute-start.2 = (bf16[128,1024]{1,0:T(8,128)(2,1)S(1)}, bf16[128,1024]{1,0:T(8,128)(2,1)S(1)}, u32[]{:S(2)}, u32[]{:S(2)}) collective-permute-start(bf16[128,1024]{1,0:T(8,128)(2,1)S(1)} %collective-permute-done.1.refs_0_), channel_id=1, source_target_pairs={{0,96},{1,97},{2,98},{3,99},{4,100},{5,101},{6,102},{7,103},{8,104... | collective-permute-start | bytes 786440 | tf_op jit(solution)/shard_map/ppermute | solution.py:26
  14.8 8.1 %collective-permute-start.3 = (bf16[128,1024]{1,0:T(8,128)(2,1)S(1)}, bf16[128,1024]{1,0:T(8,128)(2,1)S(1)}, u32[]{:S(2)}, u32[]{:S(2)}) collective-permute-start(bf16[128,1024]{1,0:T(8,128)(2,1)S(1)} %collective-permute-done.1.refs_0_), channel_id=1, source_target_pairs={{0,32},{1,33},{2,34},{3,35},{4,36},{5,37},{6,38},{7,39},{8,40},{9,... | collective-permute-start | bytes 786440 | tf_op jit(solution)/shard_map/ppermute | solution.py:26
  14.8 17.3 %collective-permute-start.5 = (bf16[256,1024]{1,0:T(8,128)(2,1)}, bf16[256,1024]{1,0:T(8,128)(2,1)S(1)}, u32[]{:S(2)}, u32[]{:S(2)}) collective-permute-start(bf16[256,1024]{1,0:T(8,128)(2,1)} %refs_0_), channel_id=1, source_target_pairs={{0,4},{1,5},{2,6},{3,7},{4,0},{5,1},{6,2},{7,3},{8,12},{9,13},{10,... | collective-permute-start | bytes 1572872 | tf_op jit(solution)/shard_map/ppermute | solution.py:26
  16.3 15.9 %collective-permute-start.6 = (bf16[256,1024]{1,0:T(8,128)(2,1)}, bf16[256,1024]{1,0:T(8,128)(2,1)S(1)}, u32[]{:S(2)}, u32[]{:S(2)}) collective-permute-start(bf16[256,1024]{1,0:T(8,128)(2,1)} %refs_0_), channel_id=1, source_target_pairs={{0,6},{1,7},{2,4},{3,5},{4,2},{5,3},{6,0},{7,1},{8,14},{9,15},{10,... | collective-permute-start | bytes 1572872 | tf_op jit(solution)/shard_map/ppermute | solution.py:26
  18.4 6.9 %collective-permute-start.11 = (bf16[128,1024]{1,0:T(8,128)(2,1)S(1)}, bf16[128,1024]{1,0:T(8,128)(2,1)S(1)}, u32[]{:S(2)}, u32[]{:S(2)}) collective-permute-start(bf16[128,1024]{1,0:T(8,128)(2,1)S(1)} %collective-permute-done.10.refs_1_), channel_id=1, source_target_pairs={{0,24},{1,25},{2,26},{3,27},{4,28},{5,29},{6,30},{7,31},{8,0},{9,1... | collective-permute-start | bytes 786440 | tf_op jit(solution)/shard_map/ppermute | solution.py:26
  22.9 9.2 %collective-permute-start.4 = (bf16[128,1024]{1,0:T(8,128)(2,1)S(1)}, bf16[128,1024]{1,0:T(8,128)(2,1)S(1)}, u32[]{:S(2)}, u32[]{:S(2)}) collective-permute-start(bf16[128,1024]{1,0:T(8,128)(2,1)S(1)} %collective-permute-done.2.refs_1_), channel_id=1, source_target_pairs={{0,96},{1,97},{2,98},{3,99},{4,100},{5,101},{6,102},{7,103},{8,104... | collective-permute-start | bytes 786440 | tf_op jit(solution)/shard_map/ppermute | solution.py:26
  24.8 11.0 %copy-start = (bf16[256,1024]{1,0:T(8,128)(2,1)S(1)}, bf16[256,1024]{1,0:T(8,128)(2,1)}, u32[]{:S(2)}) copy-start(bf16[256,1024]{1,0:T(8,128)(2,1)} %refs_0_) | copy-start | bytes 1572868
  26.0 25.4 %collective-permute-start.12 = (bf16[4,128,1024]{2,1,0:T(8,128)(2,1)S(1)}, bf16[4,128,1024]{2,1,0:T(8,128)(2,1)S(1)}, u32[]{:S(2)}, u32[]{:S(2)}) collective-permute-start(bf16[4,128,1024]{2,1,0:T(8,128)(2,1)S(1)} %shard_map.29.refs_4_.p0), channel_id=1, source_target_pairs={{0,96},{1,97},{2,98},{3,99},{4,100},{5,101},{6,102},{7,103},{8,104... | collective-permute-start | bytes 3145736 | tf_op jit(solution)/shard_map/ppermute | solution.py:26
  29.3 23.0 %collective-permute-start.13 = (bf16[4,128,1024]{2,1,0:T(8,128)(2,1)S(1)}, bf16[4,128,1024]{2,1,0:T(8,128)(2,1)S(1)}, u32[]{:S(2)}, u32[]{:S(2)}) collective-permute-start(bf16[4,128,1024]{2,1,0:T(8,128)(2,1)S(1)} %shard_map.29.refs_4_.p0), channel_id=1, source_target_pairs={{0,32},{1,33},{2,34},{3,35},{4,36},{5,37},{6,38},{7,39},{8,40},{9,... | collective-permute-start | bytes 3145736 | tf_op jit(solution)/shard_map/ppermute | solution.py:26
  32.8 22.6 %collective-permute-start.7 = (bf16[4,128,1024]{2,1,0:T(8,128)(2,1)S(1)}, bf16[4,128,1024]{2,1,0:T(8,128)(2,1)S(1)}, u32[]{:S(2)}, u32[]{:S(2)}) collective-permute-start(bf16[4,128,1024]{2,1,0:T(8,128)(2,1)S(1)} %shard_map.28.refs_7_.p0), channel_id=1, source_target_pairs={{0,24},{1,25},{2,26},{3,27},{4,28},{5,29},{6,30},{7,31},{8,0},{9,1... | collective-permute-start | bytes 3145736 | tf_op jit(solution)/shard_map/ppermute | solution.py:26
  35.8 21.4 %collective-permute-start.8 = (bf16[4,128,1024]{2,1,0:T(8,128)(2,1)S(1)}, bf16[4,128,1024]{2,1,0:T(8,128)(2,1)S(1)}, u32[]{:S(2)}, u32[]{:S(2)}) collective-permute-start(bf16[4,128,1024]{2,1,0:T(8,128)(2,1)S(1)} %shard_map.28.refs_7_.p0), channel_id=1, source_target_pairs={{0,8},{1,9},{2,10},{3,11},{4,12},{5,13},{6,14},{7,15},{8,16},{9,17... | collective-permute-start | bytes 3145736 | tf_op jit(solution)/shard_map/ppermute | solution.py:26
  35.8 19.7 %collective-permute-start.9 = (bf16[256,1024]{1,0:T(8,128)(2,1)S(1)}, bf16[256,1024]{1,0:T(8,128)(2,1)S(1)}, u32[]{:S(2)}, u32[]{:S(2)}) collective-permute-start(bf16[256,1024]{1,0:T(8,128)(2,1)S(1)} %copy-done), channel_id=1, source_target_pairs={{0,2},{1,3},{2,0},{3,1},{4,6},{5,7},{6,4},{7,5},{8,10},{9,11},{10,... | collective-permute-start | bytes 1572872 | tf_op jit(solution)/shard_map/ppermute | solution.py:26
  52.9 14.7 %collective-permute-start.14 = (bf16[2,128,1024]{2,1,0:T(8,128)(2,1)S(1)}, bf16[2,128,1024]{2,1,0:T(8,128)(2,1)S(1)}, u32[]{:S(2)}, u32[]{:S(2)}) collective-permute-start(bf16[2,128,1024]{2,1,0:T(8,128)(2,1)S(1)} %get-tuple-element.58), channel_id=1, source_target_pairs={{0,96},{1,97},{2,98},{3,99},{4,100},{5,101},{6,102},{7,103},{8,104... | collective-permute-start | bytes 1572872 | tf_op jit(solution)/shard_map/ppermute | solution.py:26
  55.5 12.6 %collective-permute-start.15 = (bf16[2,128,1024]{2,1,0:T(8,128)(2,1)S(1)}, bf16[2,128,1024]{2,1,0:T(8,128)(2,1)S(1)}, u32[]{:S(2)}, u32[]{:S(2)}) collective-permute-start(bf16[2,128,1024]{2,1,0:T(8,128)(2,1)S(1)} %get-tuple-element.59), channel_id=1, source_target_pairs={{0,32},{1,33},{2,34},{3,35},{4,36},{5,37},{6,38},{7,39},{8,40},{9,... | collective-permute-start | bytes 1572872 | tf_op jit(solution)/shard_map/ppermute | solution.py:26
  57.9 12.1 %collective-permute-start.17 = (bf16[2,128,1024]{2,1,0:T(8,128)(2,1)S(1)}, bf16[2,128,1024]{2,1,0:T(8,128)(2,1)S(1)}, u32[]{:S(2)}, u32[]{:S(2)}) collective-permute-start(bf16[2,128,1024]{2,1,0:T(8,128)(2,1)S(1)} %get-tuple-element.60), channel_id=1, source_target_pairs={{0,24},{1,25},{2,26},{3,27},{4,28},{5,29},{6,30},{7,31},{8,0},{9,1... | collective-permute-start | bytes 1572872 | tf_op jit(solution)/shard_map/ppermute | solution.py:26
  59.5 10.5 %collective-permute-start.18 = (bf16[2,128,1024]{2,1,0:T(8,128)(2,1)S(1)}, bf16[2,128,1024]{2,1,0:T(8,128)(2,1)S(1)}, u32[]{:S(2)}, u32[]{:S(2)}) collective-permute-start(bf16[2,128,1024]{2,1,0:T(8,128)(2,1)S(1)} %get-tuple-element.61), channel_id=1, source_target_pairs={{0,8},{1,9},{2,10},{3,11},{4,12},{5,13},{6,14},{7,15},{8,16},{9,17... | collective-permute-start | bytes 1572872 | tf_op jit(solution)/shard_map/ppermute | solution.py:26
  69.9 5.0 %collective-permute-start.16 = (f32[8,512,128]{2,1,0:T(8,128)S(1)}, f32[8,512,128]{2,1,0:T(8,128)S(1)}, u32[]{:S(2)}, u32[]{:S(2)}) collective-permute-start(f32[8,512,128]{2,1,0:T(8,128)S(1)} %bitcast.8), channel_id=1, source_target_pairs={{0,1},{1,0},{2,3},{3,2},{4,5},{5,4},{6,7},{7,6},{8,9},{9,8},{10,11... | collective-permute-start | bytes 6291464 | tf_op jit(solution)/shard_map/ppermute | solution.py:26
  72.2 2.7 %collective-permute-start.19 = (f32[2,512,128]{2,1,0:T(8,128)S(1)}, f32[2,512,128]{2,1,0:T(8,128)S(1)}, u32[]{:S(2)}, u32[]{:S(2)}) collective-permute-start(f32[2,512,128]{2,1,0:T(8,128)S(1)} %get-tuple-element.63), channel_id=1, source_target_pairs={{0,1},{1,0},{2,3},{3,2},{4,5},{5,4},{6,7},{7,6},{8,9},{9,8},{10,11... | collective-permute-start | bytes 1572872 | tf_op jit(solution)/shard_map/ppermute | solution.py:26
  99.8 19.9 %collective-permute-start.20 = (f32[8,512,128]{2,1,0:T(8,128)S(1)}, f32[8,512,128]{2,1,0:T(8,128)S(1)}, u32[]{:S(2)}, u32[]{:S(2)}) collective-permute-start(f32[8,512,128]{2,1,0:T(8,128)S(1)} %get-tuple-element.69.plan), channel_id=1, source_target_pairs={{0,1},{1,0},{2,3},{3,2},{4,5},{5,4},{6,7},{7,6},{8,9},{9,8},{10,11... | collective-permute-start | bytes 6291464 | tf_op jit(solution)/shard_map/ppermute | solution.py:26
  122.5 10.3 %collective-permute-start.22 = (bf16[144,1024]{1,0:T(8,128)(2,1)S(1)}, bf16[144,1024]{1,0:T(8,128)(2,1)S(1)}, u32[]{:S(2)}, u32[]{:S(2)}) collective-permute-start(bf16[144,1024]{1,0:T(8,128)(2,1)S(1)} %get-tuple-element.78), channel_id=1, source_target_pairs={{0,6},{1,7},{2,4},{3,5},{4,2},{5,3},{6,0},{7,1},{8,14},{9,15},{10,... | collective-permute-start | bytes 884744 | tf_op jit(solution)/shard_map/ppermute | solution.py:26
  123.7 9.9 %collective-permute-start.24 = (bf16[144,1024]{1,0:T(8,128)(2,1)S(1)}, bf16[144,1024]{1,0:T(8,128)(2,1)S(1)}, u32[]{:S(2)}, u32[]{:S(2)}) collective-permute-start(bf16[144,1024]{1,0:T(8,128)(2,1)S(1)} %get-tuple-element.81), channel_id=1, source_target_pairs={{0,4},{1,5},{2,6},{3,7},{4,0},{5,1},{6,2},{7,3},{8,12},{9,13},{10,... | collective-permute-start | bytes 884744 | tf_op jit(solution)/shard_map/ppermute | solution.py:26
  125.8 13.4 %collective-permute-start.21 = (bf16[128,1024]{1,0:T(8,128)(2,1)S(1)}, bf16[128,1024]{1,0:T(8,128)(2,1)S(1)}, u32[]{:S(2)}, u32[]{:S(2)}) collective-permute-start(bf16[128,1024]{1,0:T(8,128)(2,1)S(1)} %get-tuple-element.75), channel_id=1, source_target_pairs={{0,4},{1,5},{2,6},{3,7},{4,0},{5,1},{6,2},{7,3},{8,12},{9,13},{10,... | collective-permute-start | bytes 786440 | tf_op jit(solution)/shard_map/ppermute | solution.py:26
  130.0 10.2 %collective-permute-start.26 = (bf16[128,1024]{1,0:T(8,128)(2,1)S(1)}, bf16[128,1024]{1,0:T(8,128)(2,1)S(1)}, u32[]{:S(2)}, u32[]{:S(2)}) collective-permute-start(bf16[128,1024]{1,0:T(8,128)(2,1)S(1)} %get-tuple-element.82), channel_id=1, source_target_pairs={{0,6},{1,7},{2,4},{3,5},{4,2},{5,3},{6,0},{7,1},{8,14},{9,15},{10,... | collective-permute-start | bytes 786440 | tf_op jit(solution)/shard_map/ppermute | solution.py:26
  133.4 11.0 %collective-permute-start.23 = (bf16[144,1024]{1,0:T(8,128)(2,1)S(1)}, bf16[144,1024]{1,0:T(8,128)(2,1)S(1)}, u32[]{:S(2)}, u32[]{:S(2)}) collective-permute-start(bf16[144,1024]{1,0:T(8,128)(2,1)S(1)} %shard_map.43), channel_id=1, source_target_pairs={{0,4},{1,5},{2,6},{3,7},{4,0},{5,1},{6,2},{7,3},{8,12},{9,13},{10,... | collective-permute-start | bytes 884744 | tf_op jit(solution)/shard_map/ppermute | solution.py:26
  134.2 10.8 %collective-permute-start.25 = (bf16[144,1024]{1,0:T(8,128)(2,1)S(1)}, bf16[144,1024]{1,0:T(8,128)(2,1)S(1)}, u32[]{:S(2)}, u32[]{:S(2)}) collective-permute-start(bf16[144,1024]{1,0:T(8,128)(2,1)S(1)} %shard_map.45), channel_id=1, source_target_pairs={{0,6},{1,7},{2,4},{3,5},{4,2},{5,3},{6,0},{7,1},{8,14},{9,15},{10,... | collective-permute-start | bytes 884744 | tf_op jit(solution)/shard_map/ppermute | solution.py:26

commit v10 on v9

--- a/solution.py
+++ b/solution.py
@@ -294,17 +294,21 @@
     out[mid:, : 2 * mid] = terms_in_rows(jnp.concatenate(total, axis=1))
 
 
-def last_kernel(at, own, own_total, l_low, l_high, lh_low, lh_high, out):
-    mid = own.shape[0] // 2
-    terms = [m[mid:, : 2 * mid] for m in (l_high, lh_low)]
+def early_kernel(at, own, low, high, out):
+    mid = low.shape[0]
+    out[:mid, :] = own[:mid] + low[...].astype(jnp.float32)
+    out[mid:, :] = own[mid:] + high[...].astype(jnp.float32)
+
+
+def last_kernel(at, sums, own_total, low, high, out):
+    mid = sums.shape[0] // 2
+    terms = [m[mid:, : 2 * mid] for m in (low, high)]
     total = 1.0 / to_rows(jnp.concatenate([terms_in_rows(own_total[:1])] + terms, axis=0))
-    for n, messages in enumerate(((l_low, lh_low), (l_high, lh_high))):
+    for n, message in enumerate((low, high)):
         here = slice(n * mid, n * mid + mid)
-        for column in range(0, own.shape[1], 128):
+        for column in range(0, sums.shape[1], 128):
             span = slice(column, column + 128)
-            value = own[here, span]
-            for m in messages:
-                value = value + m[:mid, span].astype(jnp.float32)
+            value = sums[here, span] + message[:mid, span].astype(jnp.float32)
             out[here, span] = (value * total[here]).astype(out.dtype)
 
 
@@ -521,14 +525,14 @@
 
     lh_high, lh_low = other_rows(far_place, 0, low, "lh")
     l_low, l_high = other_rows(near_place, 1, high, "l")
-    own = call(
+    own, own_total = call(
         target_3_kernel,
         [float32(rows, part), float32(8, rows)],
         64 * one,
         *(at, weights, *near_noise),
     )
-    messages = l_low, l_high, lh_low, lh_high
-    return call(last_kernel, [bfloat16(rows, part)], 0, at, *own, *messages)[0]
+    (sums,) = call(early_kernel, [float32(rows, part)], 0, at, own, l_low, lh_high)
+    return call(last_kernel, [bfloat16(rows, part)], 0, at, sums, own_total, lh_low, l_high)[0]
 
 
 def solution(mesh):

time: 147 us -> 147 us (level)
  starting transfers between devices: 41.5 us -> 40 us
    ppermute x27, starting transfers between devices: 41.5 us -> 40 us  [move(): return lax.ppermute(value, AXES, pairs)]
    pallas_call x19 -> x20, Pallas kernels: 32.2 us -> 32.9 us  [call(): pl.pallas_call(kernel, out_shape=outs, in_specs=[pl.BlockSpec(memory_spac...]
  transfers between devices with their start and end apart: 27 -> 27, of which waited for: 15 -> 13; matrix products, arithmetic and copies ran while one was open for 0% -> 0% of each run, Pallas kernels for 16% -> 16%
where the time goes in v10:
time: 147 us
  starting transfers between devices  40 us (27%)
  blocking collectives  39.5 us (27%)
  waiting for transfers between devices  32.9 us (22%)
  Pallas kernels  32.9 us (22%)
    ppermute x27, starting transfers between devices, move(): return lax.ppermute(value, AXES, pairs)  40 us
    all_to_all x4, blocking collectives, exchange(): return lax.all_to_all(sent, axes, 0, 0, tiled=True)  39.5 us
    ppermute x27, waiting for transfers between devices, move(): return lax.ppermute(value, AXES, pairs)  32.9 us
    pallas_call x20, Pallas kernels, call(): pl.pallas_call(kernel, out_shape=outs, in_specs=[pl.BlockSpec(memory_spac...  32.9 us
  transfers between devices with their start and end apart: 27, of which 13 were waited for; matrix products, arithmetic and copies ran while one was open for 0% of the time, Pallas kernels for 16%

profile of v10, /device:TPU:0, one launch (start us, length us, event | category | flops | bytes accessed | tf_op | source)
XLA Modules:
  0.0 146.7 jit_solution(1805563634378185860)
XLA Ops:
  0.0 1.1 constant_dynamic-slice_fusion
  1.1 3.2 %collective-permute-start.1 = (bf16[128,1024]{1,0:T(8,128)(2,1)S(1)}, bf16[128,1024]{1,0:T(8,128)(2,1)S(1)}, u32[]{:S(2)}, u32[]{:S(2)}) collective-permute-start(bf16[128,1024]{1,0:T(8,128)(2,1)S(1)} %get-tuple-element.83), channel_id=1, source_target_pairs={{0,2},{1,3},{2,0},{3,1},{4,6},{5,7},{6,4},{7,5},{8,10},{9,11},{10,... | collective-permute-start | bytes 786440 | tf_op jit(solution)/shard_map/ppermute | solution.py:26
  4.3 1.6 %collective-permute-start = (bf16[128,1024]{1,0:T(8,128)(2,1)S(1)}, bf16[128,1024]{1,0:T(8,128)(2,1)S(1)}, u32[]{:S(2)}, u32[]{:S(2)}) collective-permute-start(bf16[128,1024]{1,0:T(8,128)(2,1)S(1)} %get-tuple-element.84.refs_0_), channel_id=1, source_target_pairs={{0,8},{1,9},{2,10},{3,11},{4,12},{5,13},{6,14},{7,15},{8,16},{9,17... | collective-permute-start | bytes 786440 | tf_op jit(solution)/shard_map/ppermute | solution.py:26
  5.8 1.7 %collective-permute-start.10 = (bf16[128,1024]{1,0:T(8,128)(2,1)S(1)}, bf16[128,1024]{1,0:T(8,128)(2,1)S(1)}, u32[]{:S(2)}, u32[]{:S(2)}) collective-permute-start(bf16[128,1024]{1,0:T(8,128)(2,1)S(1)} %get-tuple-element.84.refs_0_), channel_id=1, source_target_pairs={{0,24},{1,25},{2,26},{3,27},{4,28},{5,29},{6,30},{7,31},{8,0},{9,1... | collective-permute-start | bytes 786440 | tf_op jit(solution)/shard_map/ppermute | solution.py:26
  7.5 3.1 %collective-permute-done.1.refs_0_ = bf16[128,1024]{1,0:T(8,128)(2,1)S(1)} collective-permute-done((bf16[128,1024]{1,0:T(8,128)(2,1)S(1)}, bf16[128,1024]{1,0:T(8,128)(2,1)S(1)}, u32[]{:S(2)}, u32[]{:S(2)}) %collective-permute-start.1) | collective-permute-done | bytes 262176 | tf_op jit(solution)/shard_map/ppermute | solution.py:26
  10.6 4.3 %collective-permute-start.2 = (bf16[128,1024]{1,0:T(8,128)(2,1)S(1)}, bf16[128,1024]{1,0:T(8,128)(2,1)S(1)}, u32[]{:S(2)}, u32[]{:S(2)}) collective-permute-start(bf16[128,1024]{1,0:T(8,128)(2,1)S(1)} %collective-permute-done.1.refs_0_), channel_id=1, source_target_pairs={{0,96},{1,97},{2,98},{3,99},{4,100},{5,101},{6,102},{7,103},{8,104... | collective-permute-start | bytes 786440 | tf_op jit(solution)/shard_map/ppermute | solution.py:26
  14.8 1.5 %collective-permute-start.5 = (bf16[256,1024]{1,0:T(8,128)(2,1)}, bf16[256,1024]{1,0:T(8,128)(2,1)S(1)}, u32[]{:S(2)}, u32[]{:S(2)}) collective-permute-start(bf16[256,1024]{1,0:T(8,128)(2,1)} %refs_0_), channel_id=1, source_target_pairs={{0,4},{1,5},{2,6},{3,7},{4,0},{5,1},{6,2},{7,3},{8,12},{9,13},{10,... | collective-permute-start | bytes 1572872 | tf_op jit(solution)/shard_map/ppermute | solution.py:26
  16.3 0.0 collective-permute-done.refs_3_
  16.3 2.1 %collective-permute-start.6 = (bf16[256,1024]{1,0:T(8,128)(2,1)}, bf16[256,1024]{1,0:T(8,128)(2,1)S(1)}, u32[]{:S(2)}, u32[]{:S(2)}) collective-permute-start(bf16[256,1024]{1,0:T(8,128)(2,1)} %refs_0_), channel_id=1, source_target_pairs={{0,6},{1,7},{2,4},{3,5},{4,2},{5,3},{6,0},{7,1},{8,14},{9,15},{10,... | collective-permute-start | bytes 1572872 | tf_op jit(solution)/shard_map/ppermute | solution.py:26
  18.4 0.0 collective-permute-done.10.refs_1_
  18.4 3.0 %collective-permute-start.11 = (bf16[128,1024]{1,0:T(8,128)(2,1)S(1)}, bf16[128,1024]{1,0:T(8,128)(2,1)S(1)}, u32[]{:S(2)}, u32[]{:S(2)}) collective-permute-start(bf16[128,1024]{1,0:T(8,128)(2,1)S(1)} %collective-permute-done.10.refs_1_), channel_id=1, source_target_pairs={{0,24},{1,25},{2,26},{3,27},{4,28},{5,29},{6,30},{7,31},{8,0},{9,1... | collective-permute-start | bytes 786440 | tf_op jit(solution)/shard_map/ppermute | solution.py:26
  21.4 1.5 %collective-permute-done.3.refs_3_ = bf16[128,1024]{1,0:T(8,128)(2,1)S(1)} collective-permute-done((bf16[128,1024]{1,0:T(8,128)(2,1)S(1)}, bf16[128,1024]{1,0:T(8,128)(2,1)S(1)}, u32[]{:S(2)}, u32[]{:S(2)}) %collective-permute-start.3) | collective-permute-done | bytes 262176 | tf_op jit(solution)/shard_map/ppermute | solution.py:26
  22.9 1.7 %collective-permute-start.4 = (bf16[128,1024]{1,0:T(8,128)(2,1)S(1)}, bf16[128,1024]{1,0:T(8,128)(2,1)S(1)}, u32[]{:S(2)}, u32[]{:S(2)}) collective-permute-start(bf16[128,1024]{1,0:T(8,128)(2,1)S(1)} %collective-permute-done.2.refs_1_), channel_id=1, source_target_pairs={{0,96},{1,97},{2,98},{3,99},{4,100},{5,101},{6,102},{7,103},{8,104... | collective-permute-start | bytes 786440 | tf_op jit(solution)/shard_map/ppermute | solution.py:26
  24.7 0.1 stack.23.at
  24.8 0.6 collective-permute-done.11.refs_2_
  25.3 0.7 shard_map.29.refs_4_.p0
  26.0 3.3 %collective-permute-start.12 = (bf16[4,128,1024]{2,1,0:T(8,128)(2,1)S(1)}, bf16[4,128,1024]{2,1,0:T(8,128)(2,1)S(1)}, u32[]{:S(2)}, u32[]{:S(2)}) collective-permute-start(bf16[4,128,1024]{2,1,0:T(8,128)(2,1)S(1)} %shard_map.29.refs_4_.p0), channel_id=1, source_target_pairs={{0,96},{1,97},{2,98},{3,99},{4,100},{5,101},{6,102},{7,103},{8,104... | collective-permute-start | bytes 3145736 | tf_op jit(solution)/shard_map/ppermute | solution.py:26
  29.3 2.9 %collective-permute-done.4.refs_2_ = bf16[128,1024]{1,0:T(8,128)(2,1)S(1)} collective-permute-done((bf16[128,1024]{1,0:T(8,128)(2,1)S(1)}, bf16[128,1024]{1,0:T(8,128)(2,1)S(1)}, u32[]{:S(2)}, u32[]{:S(2)}) %collective-permute-start.4) | collective-permute-done | bytes 262176 | tf_op jit(solution)/shard_map/ppermute | solution.py:26
  32.2 0.7 shard_map.28.refs_7_.p0
  32.8 2.9 %collective-permute-start.7 = (bf16[4,128,1024]{2,1,0:T(8,128)(2,1)S(1)}, bf16[4,128,1024]{2,1,0:T(8,128)(2,1)S(1)}, u32[]{:S(2)}, u32[]{:S(2)}) collective-permute-start(bf16[4,128,1024]{2,1,0:T(8,128)(2,1)S(1)} %shard_map.28.refs_7_.p0), channel_id=1, source_target_pairs={{0,24},{1,25},{2,26},{3,27},{4,28},{5,29},{6,30},{7,31},{8,0},{9,1... | collective-permute-start | bytes 3145736 | tf_op jit(solution)/shard_map/ppermute | solution.py:26
  35.8 3.2 %collective-permute-start.9 = (bf16[256,1024]{1,0:T(8,128)(2,1)S(1)}, bf16[256,1024]{1,0:T(8,128)(2,1)S(1)}, u32[]{:S(2)}, u32[]{:S(2)}) collective-permute-start(bf16[256,1024]{1,0:T(8,128)(2,1)S(1)} %copy-done), channel_id=1, source_target_pairs={{0,2},{1,3},{2,0},{3,1},{4,6},{5,7},{6,4},{7,5},{8,10},{9,11},{10,... | collective-permute-start | bytes 1572872 | tf_op jit(solution)/shard_map/ppermute | solution.py:26
  39.0 12.4 %collective-permute-done.12.refs_5_.next_.p1 = bf16[4,128,1024]{2,1,0:T(8,128)(2,1)S(1)} collective-permute-done((bf16[4,128,1024]{2,1,0:T(8,128)(2,1)S(1)}, bf16[4,128,1024]{2,1,0:T(8,128)(2,1)S(1)}, u32[]{:S(2)}, u32[]{:S(2)}) %collective-permute-start.12) | collective-permute-done | bytes 1048608 | tf_op jit(solution)/shard_map/ppermute | solution.py:26
  51.4 0.9 collective-permute-done.13.refs_6_.last.p3
  52.3 0.7 shard_map.31
  52.9 2.5 %collective-permute-start.14 = (bf16[2,128,1024]{2,1,0:T(8,128)(2,1)S(1)}, bf16[2,128,1024]{2,1,0:T(8,128)(2,1)S(1)}, u32[]{:S(2)}, u32[]{:S(2)}) collective-permute-start(bf16[2,128,1024]{2,1,0:T(8,128)(2,1)S(1)} %get-tuple-element.58), channel_id=1, source_target_pairs={{0,96},{1,97},{2,98},{3,99},{4,100},{5,101},{6,102},{7,103},{8,104... | collective-permute-start | bytes 1572872 | tf_op jit(solution)/shard_map/ppermute | solution.py:26
  55.5 1.7 %collective-permute-done.8.refs_9_.last.p3 = bf16[4,128,1024]{2,1,0:T(8,128)(2,1)S(1)} collective-permute-done((bf16[4,128,1024]{2,1,0:T(8,128)(2,1)S(1)}, bf16[4,128,1024]{2,1,0:T(8,128)(2,1)S(1)}, u32[]{:S(2)}, u32[]{:S(2)}) %collective-permute-start.8) | collective-permute-done | bytes 1048608 | tf_op jit(solution)/shard_map/ppermute | solution.py:26
  57.2 0.7 shard_map.34
  57.9 1.6 %collective-permute-start.17 = (bf16[2,128,1024]{2,1,0:T(8,128)(2,1)S(1)}, bf16[2,128,1024]{2,1,0:T(8,128)(2,1)S(1)}, u32[]{:S(2)}, u32[]{:S(2)}) collective-permute-start(bf16[2,128,1024]{2,1,0:T(8,128)(2,1)S(1)} %get-tuple-element.60), channel_id=1, source_target_pairs={{0,24},{1,25},{2,26},{3,27},{4,28},{5,29},{6,30},{7,31},{8,0},{9,1... | collective-permute-start | bytes 1572872 | tf_op jit(solution)/shard_map/ppermute | solution.py:26
  59.5 0.5 collective-permute-start.18
  60.0 7.7 %shard_map.30 = (f32[4,4,512,128]{3,2,1,0:T(8,128)S(1)}, bf16[2,512,1024]{2,1,0:T(8,128)(2,1)S(1)}) custom-call(s32[5]{0:T(128)S(1)} %stack.23.at, bf16[256,1024]{1,0:T(8,128)(2,1)S(1)} %copy-done, bf16[256,1024]{1,0:T(8,128)(2,1)S(1)} %collective-permute-done.5.refs_1_, bf16[256,1024]{1,0:T(8,128)(2,1)S(1)} %collective-permute-done.9.refs_2_, ...), custom_call_target="tpu_custom_call" | custom-call | flops 3221225472 | bytes 14680084 | tf_op jit(solution)/shard_map/pallas_call | solution.py:76
  67.6 0.5 collective-permute-done.15.n_b.p2_b
  68.1 1.8 %shard_map.33 = f32[2,4,512,128]{3,2,1,0:T(8,128)S(1)} custom-call(s32[5]{0:T(128)S(1)} %stack.23.at, bf16[2,512,1024]{2,1,0:T(8,128)(2,1)S(1)} %get-tuple-element.56.x, f32[4,4,512,128]{3,2,1,0:T(8,128)S(1)} %get-tuple-element.57.acc, bf16[2,128,1024]{2,1,0:T(8,128)(2,1)S(1)} %collective-permute-done.14.n_a.p2_a, ...), custom_call_target="tpu_custom_call" | custom-call | flops 26843545600 | bytes 9437204 | tf_op jit(solution)/shard_map/pallas_call | solution.py:76
  69.9 0.1 collective-permute-start.16
  70.0 2.2 %shard_map.35 = (f32[2,512,128]{2,1,0:T(8,128)S(1)}, f32[2,512,128]{2,1,0:T(8,128)S(1)}) custom-call(s32[5]{0:T(128)S(1)} %stack.23.at, bf16[2,512,1024]{2,1,0:T(8,128)(2,1)S(1)} %get-tuple-element.56.x, bf16[2,128,1024]{2,1,0:T(8,128)(2,1)S(1)} %collective-permute-done.17.f_a.p2_a, bf16[2,128,1024]{2,1,0:T(8,128)(2,1)S(1)} %collective-permute-done.18.f_b.p2_b), custom_call_target="tpu_custom_call" | custom-call | flops 536870912 | bytes 4194324 | tf_op jit(solution)/shard_map/pallas_call | solution.py:76
  72.2 0.6 collective-permute-start.19
  72.8 0.8 shard_map.32
  73.6 1.3 collective-permute-done.19.far_got
  74.9 1.8 %shard_map.36 = (f32[8,512,128]{2,1,0:T(8,128)S(1)}, f32[8,1,512]{2,1,0:T(1,128)S(1)}) custom-call(s32[5]{0:T(128)S(1)} %stack.23.at, f32[8,512,128]{2,1,0:T(8,128)S(1)} %bitcast.7, f32[8,512,128]{2,1,0:T(8,128)S(1)} %collective-permute-done.16.got, f32[2,512,128]{2,1,0:T(8,128)S(1)} %get-tuple-element.62.far_keep, ...), custom_call_target="tpu_custom_call" | custom-call | bytes 7356436 | tf_op jit(solution)/shard_map/pallas_call | solution.py:76
  76.7 8.7 %all_to_all.20.came = f32[8,1,512]{2,1,0:T(1,128)S(1)} all-to-all(f32[8,1,512]{2,1,0:T(1,128)S(1)} %get-tuple-element.64), channel_id=1, replica_groups=mesh['z'=4,'y'=4,'l'=2,'h'=2,'c'=2] {'l','h','c'}, dimensions={0} | all-to-all | bytes 32768 | tf_op jit(solution)/shard_map/all_to_all | solution.py:480
  85.4 1.3 shard_map.37
  86.7 11.9 %all_to_all.21.came = f32[16,8,128]{2,1,0:T(8,128)S(1)} all-to-all(f32[16,8,128]{2,1,0:T(8,128)S(1)} %get-tuple-element.66), channel_id=1, replica_groups=mesh['z'=4,'y'=4,'l'=2,'h'=2,'c'=2] {'z','y'}, dimensions={0} | all-to-all | bytes 131072 | tf_op jit(solution)/shard_map/all_to_all | solution.py:480
  98.5 1.3 shard_map.38
  99.8 0.0 collective-permute-start.20
  99.8 7.7 %all_to_all.22.came = f32[8,1,512]{2,1,0:T(1,128)S(1)} all-to-all(f32[8,1,512]{2,1,0:T(1,128)S(1)} %get-tuple-element.68), channel_id=1, replica_groups=mesh['z'=4,'y'=4,'l'=2,'h'=2,'c'=2] {'l','h','c'}, dimensions={0} | all-to-all | bytes 32768 | tf_op jit(solution)/shard_map/all_to_all | solution.py:480
  107.5 0.9 shard_map.39
  108.4 11.2 %all_to_all.23.came = f32[32,8,128]{2,1,0:T(8,128)S(1)} all-to-all(f32[32,8,128]{2,1,0:T(8,128)S(1)} %get-tuple-element.70), channel_id=1, replica_groups=mesh['z'=4,'y'=4,'l'=2,'h'=2,'c'=2] {'z','y','c'}, dimensions={0} | all-to-all | bytes 262144 | tf_op jit(solution)/shard_map/all_to_all | solution.py:480
  119.6 2.8 %shard_map.40 = (bf16[4,4,512,128]{3,2,1,0:T(8,128)(2,1)S(1)}, bf16[144,1024]{1,0:T(8,128)(2,1)S(1)}, bf16[144,1024]{1,0:T(8,128)(2,1)S(1)}) custom-call(s32[5]{0:T(128)S(1)} %stack.23.at, f32[32,8,128]{2,1,0:T(8,128)S(1)} %all_to_all.23.came, f32[8,512,128]{2,1,0:T(8,128)S(1)} %get-tuple-element.69.plan, f32[8,512,128]{2,1,0:T(8,128)S(1)} %collective-permute-done.20.other, ...), custom_call_target="tpu_custom_call" | custom-call | flops 2147483648 | bytes 11468820 | tf_op jit(solution)/shard_map/pallas_call | solution.py:76
  122.5 0.6 collective-permute-start.23
  123.1 1.2 collective-permute-start.25
  124.3 2.1 %shard_map.42 = (bf16[128,1024]{1,0:T(8,128)(2,1)S(1)}, f32[128,1024]{1,0:T(8,128)S(1)}, f32[8,256]{1,0:T(8,128)S(1)}) custom-call(s32[5]{0:T(128)S(1)} %stack.23.at, bf16[4,4,512,128]{3,2,1,0:T(8,128)(2,1)S(1)} %get-tuple-element.72.weights, bf16[4,128,1024]{2,1,0:T(8,128)(2,1)S(1)} %shard_map.29.refs_4_.p0, ...), custom_call_target="tpu_custom_call" | custom-call | flops 2147483648 | bytes 7086100 | tf_op jit(solution)/shard_map/pallas_call | solution.py:76
  126.4 0.9 collective-permute-start.21
  127.3 2.1 %shard_map.43 = (bf16[128,1024]{1,0:T(8,128)(2,1)S(1)}, f32[128,1024]{1,0:T(8,128)S(1)}, f32[8,256]{1,0:T(8,128)S(1)}) custom-call(s32[5]{0:T(128)S(1)} %stack.23.at, bf16[4,4,512,128]{3,2,1,0:T(8,128)(2,1)S(1)} %get-tuple-element.72.weights, bf16[4,128,1024]{2,1,0:T(8,128)(2,1)S(1)} %shard_map.28.refs_7_.p0, ...), custom_call_target="tpu_custom_call" | custom-call | flops 2147483648 | bytes 7086100 | tf_op jit(solution)/shard_map/pallas_call | solution.py:76
  129.4 2.2 %collective-permute-start.22 = (bf16[128,1024]{1,0:T(8,128)(2,1)S(1)}, bf16[128,1024]{1,0:T(8,128)(2,1)S(1)}, u32[]{:S(2)}, u32[]{:S(2)}) collective-permute-start(bf16[128,1024]{1,0:T(8,128)(2,1)S(1)} %get-tuple-element.75), channel_id=1, source_target_pairs={{0,6},{1,7},{2,4},{3,5},{4,2},{5,3},{6,0},{7,1},{8,14},{9,15},{10,... | collective-permute-start | bytes 786440 | tf_op jit(solution)/shard_map/ppermute | solution.py:26
  131.6 0.8 collective-permute-done.23.came
  132.4 0.6 shard_map.45
  133.0 1.3 collective-permute-start.24
  134.3 0.6 shard_map.46
  134.9 0.1 collective-permute-start.26
  135.0 2.1 %shard_map.41 = (f32[256,1024]{1,0:T(8,128)S(1)}, f32[8,256]{1,0:T(8,128)S(1)}) custom-call(s32[5]{0:T(128)S(1)} %stack.23.at, bf16[4,4,512,128]{3,2,1,0:T(8,128)(2,1)S(1)} %get-tuple-element.72.weights, bf16[4,128,1024]{2,1,0:T(8,128)(2,1)S(1)} %shard_map.29.refs_4_.p0, bf16[4,128,1024]{2,1,0:T(8,128)(2,1)S(1)} %collective-permute-done.12.refs_5_.next_.p1, ...), custom_call_target="tpu_custom_call" | custom-call | flops 17179869184 | bytes 7348244 | tf_op jit(solution)/shard_map/pallas_call | solution.py:76
  137.1 0.9 collective-permute-done.21.low
  138.0 1.9 %collective-permute-done.22.high = bf16[128,1024]{1,0:T(8,128)(2,1)S(1)} collective-permute-done((bf16[128,1024]{1,0:T(8,128)(2,1)S(1)}, bf16[128,1024]{1,0:T(8,128)(2,1)S(1)}, u32[]{:S(2)}, u32[]{:S(2)}) %collective-permute-start.22) | collective-permute-done | bytes 262176 | tf_op jit(solution)/shard_map/ppermute | solution.py:26
  140.0 0.6 shard_map.44.sums
  140.6 4.4 %collective-permute-done.24.low = bf16[144,1024]{1,0:T(8,128)(2,1)S(1)} collective-permute-done((bf16[144,1024]{1,0:T(8,128)(2,1)S(1)}, bf16[144,1024]{1,0:T(8,128)(2,1)S(1)}, u32[]{:S(2)}, u32[]{:S(2)}) %collective-permute-start.24) | collective-permute-done | bytes 294944 | tf_op jit(solution)/shard_map/ppermute | solution.py:26
  145.0 1.6 %shard_map.47 = bf16[256,1024]{1,0:T(8,128)(2,1)} custom-call(s32[5]{0:T(128)S(1)} %stack.23.at, f32[256,1024]{1,0:T(8,128)S(1)} %shard_map.44.sums, f32[8,256]{1,0:T(8,128)S(1)} %get-tuple-element.76.own_total, bf16[144,1024]{1,0:T(8,128)(2,1)S(1)} %collective-permute-done.24.low, bf16[144,1024]{1,0:T(8,128)(2,1)S(1)} %collective-permute-done.26.high), custom_call_target="tpu_custom_call" | custom-call | bytes 2170900 | tf_op jit(solution)/shard_map/pallas_call | solution.py:76
  (18 shorter events, 0.0 us)
Async XLA Ops:
  1.1 9.5 %collective-permute-start.1 = (bf16[128,1024]{1,0:T(8,128)(2,1)S(1)}, bf16[128,1024]{1,0:T(8,128)(2,1)S(1)}, u32[]{:S(2)}, u32[]{:S(2)}) collective-permute-start(bf16[128,1024]{1,0:T(8,128)(2,1)S(1)} %get-tuple-element.83), channel_id=1, source_target_pairs={{0,2},{1,3},{2,0},{3,1},{4,6},{5,7},{6,4},{7,5},{8,10},{9,11},{10,... | collective-permute-start | bytes 786440 | tf_op jit(solution)/shard_map/ppermute | solution.py:26
  4.3 12.1 %collective-permute-start = (bf16[128,1024]{1,0:T(8,128)(2,1)S(1)}, bf16[128,1024]{1,0:T(8,128)(2,1)S(1)}, u32[]{:S(2)}, u32[]{:S(2)}) collective-permute-start(bf16[128,1024]{1,0:T(8,128)(2,1)S(1)} %get-tuple-element.84.refs_0_), channel_id=1, source_target_pairs={{0,8},{1,9},{2,10},{3,11},{4,12},{5,13},{6,14},{7,15},{8,16},{9,17... | collective-permute-start | bytes 786440 | tf_op jit(solution)/shard_map/ppermute | solution.py:26
  5.8 12.6 %collective-permute-start.10 = (bf16[128,1024]{1,0:T(8,128)(2,1)S(1)}, bf16[128,1024]{1,0:T(8,128)(2,1)S(1)}, u32[]{:S(2)}, u32[]{:S(2)}) collective-permute-start(bf16[128,1024]{1,0:T(8,128)(2,1)S(1)} %get-tuple-element.84.refs_0_), channel_id=1, source_target_pairs={{0,24},{1,25},{2,26},{3,27},{4,28},{5,29},{6,30},{7,31},{8,0},{9,1... | collective-permute-start | bytes 786440 | tf_op jit(solution)/shard_map/ppermute | solution.py:26
  10.6 10.9 %collective-permute-start.2 = (bf16[128,1024]{1,0:T(8,128)(2,1)S(1)}, bf16[128,1024]{1,0:T(8,128)(2,1)S(1)}, u32[]{:S(2)}, u32[]{:S(2)}) collective-permute-start(bf16[128,1024]{1,0:T(8,128)(2,1)S(1)} %collective-permute-done.1.refs_0_), channel_id=1, source_target_pairs={{0,96},{1,97},{2,98},{3,99},{4,100},{5,101},{6,102},{7,103},{8,104... | collective-permute-start | bytes 786440 | tf_op jit(solution)/shard_map/ppermute | solution.py:26
  14.8 8.1 %collective-permute-start.3 = (bf16[128,1024]{1,0:T(8,128)(2,1)S(1)}, bf16[128,1024]{1,0:T(8,128)(2,1)S(1)}, u32[]{:S(2)}, u32[]{:S(2)}) collective-permute-start(bf16[128,1024]{1,0:T(8,128)(2,1)S(1)} %collective-permute-done.1.refs_0_), channel_id=1, source_target_pairs={{0,32},{1,33},{2,34},{3,35},{4,36},{5,37},{6,38},{7,39},{8,40},{9,... | collective-permute-start | bytes 786440 | tf_op jit(solution)/shard_map/ppermute | solution.py:26
  14.8 17.3 %collective-permute-start.5 = (bf16[256,1024]{1,0:T(8,128)(2,1)}, bf16[256,1024]{1,0:T(8,128)(2,1)S(1)}, u32[]{:S(2)}, u32[]{:S(2)}) collective-permute-start(bf16[256,1024]{1,0:T(8,128)(2,1)} %refs_0_), channel_id=1, source_target_pairs={{0,4},{1,5},{2,6},{3,7},{4,0},{5,1},{6,2},{7,3},{8,12},{9,13},{10,... | collective-permute-start | bytes 1572872 | tf_op jit(solution)/shard_map/ppermute | solution.py:26
  16.3 15.9 %collective-permute-start.6 = (bf16[256,1024]{1,0:T(8,128)(2,1)}, bf16[256,1024]{1,0:T(8,128)(2,1)S(1)}, u32[]{:S(2)}, u32[]{:S(2)}) collective-permute-start(bf16[256,1024]{1,0:T(8,128)(2,1)} %refs_0_), channel_id=1, source_target_pairs={{0,6},{1,7},{2,4},{3,5},{4,2},{5,3},{6,0},{7,1},{8,14},{9,15},{10,... | collective-permute-start | bytes 1572872 | tf_op jit(solution)/shard_map/ppermute | solution.py:26
  18.4 6.9 %collective-permute-start.11 = (bf16[128,1024]{1,0:T(8,128)(2,1)S(1)}, bf16[128,1024]{1,0:T(8,128)(2,1)S(1)}, u32[]{:S(2)}, u32[]{:S(2)}) collective-permute-start(bf16[128,1024]{1,0:T(8,128)(2,1)S(1)} %collective-permute-done.10.refs_1_), channel_id=1, source_target_pairs={{0,24},{1,25},{2,26},{3,27},{4,28},{5,29},{6,30},{7,31},{8,0},{9,1... | collective-permute-start | bytes 786440 | tf_op jit(solution)/shard_map/ppermute | solution.py:26
  22.9 9.2 %collective-permute-start.4 = (bf16[128,1024]{1,0:T(8,128)(2,1)S(1)}, bf16[128,1024]{1,0:T(8,128)(2,1)S(1)}, u32[]{:S(2)}, u32[]{:S(2)}) collective-permute-start(bf16[128,1024]{1,0:T(8,128)(2,1)S(1)} %collective-permute-done.2.refs_1_), channel_id=1, source_target_pairs={{0,96},{1,97},{2,98},{3,99},{4,100},{5,101},{6,102},{7,103},{8,104... | collective-permute-start | bytes 786440 | tf_op jit(solution)/shard_map/ppermute | solution.py:26
  24.8 11.0 %copy-start = (bf16[256,1024]{1,0:T(8,128)(2,1)S(1)}, bf16[256,1024]{1,0:T(8,128)(2,1)}, u32[]{:S(2)}) copy-start(bf16[256,1024]{1,0:T(8,128)(2,1)} %refs_0_) | copy-start | bytes 1572868
  26.0 25.4 %collective-permute-start.12 = (bf16[4,128,1024]{2,1,0:T(8,128)(2,1)S(1)}, bf16[4,128,1024]{2,1,0:T(8,128)(2,1)S(1)}, u32[]{:S(2)}, u32[]{:S(2)}) collective-permute-start(bf16[4,128,1024]{2,1,0:T(8,128)(2,1)S(1)} %shard_map.29.refs_4_.p0), channel_id=1, source_target_pairs={{0,96},{1,97},{2,98},{3,99},{4,100},{5,101},{6,102},{7,103},{8,104... | collective-permute-start | bytes 3145736 | tf_op jit(solution)/shard_map/ppermute | solution.py:26
  29.3 23.0 %collective-permute-start.13 = (bf16[4,128,1024]{2,1,0:T(8,128)(2,1)S(1)}, bf16[4,128,1024]{2,1,0:T(8,128)(2,1)S(1)}, u32[]{:S(2)}, u32[]{:S(2)}) collective-permute-start(bf16[4,128,1024]{2,1,0:T(8,128)(2,1)S(1)} %shard_map.29.refs_4_.p0), channel_id=1, source_target_pairs={{0,32},{1,33},{2,34},{3,35},{4,36},{5,37},{6,38},{7,39},{8,40},{9,... | collective-permute-start | bytes 3145736 | tf_op jit(solution)/shard_map/ppermute | solution.py:26
  32.8 22.6 %collective-permute-start.7 = (bf16[4,128,1024]{2,1,0:T(8,128)(2,1)S(1)}, bf16[4,128,1024]{2,1,0:T(8,128)(2,1)S(1)}, u32[]{:S(2)}, u32[]{:S(2)}) collective-permute-start(bf16[4,128,1024]{2,1,0:T(8,128)(2,1)S(1)} %shard_map.28.refs_7_.p0), channel_id=1, source_target_pairs={{0,24},{1,25},{2,26},{3,27},{4,28},{5,29},{6,30},{7,31},{8,0},{9,1... | collective-permute-start | bytes 3145736 | tf_op jit(solution)/shard_map/ppermute | solution.py:26
  35.8 21.4 %collective-permute-start.8 = (bf16[4,128,1024]{2,1,0:T(8,128)(2,1)S(1)}, bf16[4,128,1024]{2,1,0:T(8,128)(2,1)S(1)}, u32[]{:S(2)}, u32[]{:S(2)}) collective-permute-start(bf16[4,128,1024]{2,1,0:T(8,128)(2,1)S(1)} %shard_map.28.refs_7_.p0), channel_id=1, source_target_pairs={{0,8},{1,9},{2,10},{3,11},{4,12},{5,13},{6,14},{7,15},{8,16},{9,17... | collective-permute-start | bytes 3145736 | tf_op jit(solution)/shard_map/ppermute | solution.py:26
  35.8 19.7 %collective-permute-start.9 = (bf16[256,1024]{1,0:T(8,128)(2,1)S(1)}, bf16[256,1024]{1,0:T(8,128)(2,1)S(1)}, u32[]{:S(2)}, u32[]{:S(2)}) collective-permute-start(bf16[256,1024]{1,0:T(8,128)(2,1)S(1)} %copy-done), channel_id=1, source_target_pairs={{0,2},{1,3},{2,0},{3,1},{4,6},{5,7},{6,4},{7,5},{8,10},{9,11},{10,... | collective-permute-start | bytes 1572872 | tf_op jit(solution)/shard_map/ppermute | solution.py:26
  52.9 14.7 %collective-permute-start.14 = (bf16[2,128,1024]{2,1,0:T(8,128)(2,1)S(1)}, bf16[2,128,1024]{2,1,0:T(8,128)(2,1)S(1)}, u32[]{:S(2)}, u32[]{:S(2)}) collective-permute-start(bf16[2,128,1024]{2,1,0:T(8,128)(2,1)S(1)} %get-tuple-element.58), channel_id=1, source_target_pairs={{0,96},{1,97},{2,98},{3,99},{4,100},{5,101},{6,102},{7,103},{8,104... | collective-permute-start | bytes 1572872 | tf_op jit(solution)/shard_map/ppermute | solution.py:26
  55.5 12.6 %collective-permute-start.15 = (bf16[2,128,1024]{2,1,0:T(8,128)(2,1)S(1)}, bf16[2,128,1024]{2,1,0:T(8,128)(2,1)S(1)}, u32[]{:S(2)}, u32[]{:S(2)}) collective-permute-start(bf16[2,128,1024]{2,1,0:T(8,128)(2,1)S(1)} %get-tuple-element.59), channel_id=1, source_target_pairs={{0,32},{1,33},{2,34},{3,35},{4,36},{5,37},{6,38},{7,39},{8,40},{9,... | collective-permute-start | bytes 1572872 | tf_op jit(solution)/shard_map/ppermute | solution.py:26
  57.9 12.1 %collective-permute-start.17 = (bf16[2,128,1024]{2,1,0:T(8,128)(2,1)S(1)}, bf16[2,128,1024]{2,1,0:T(8,128)(2,1)S(1)}, u32[]{:S(2)}, u32[]{:S(2)}) collective-permute-start(bf16[2,128,1024]{2,1,0:T(8,128)(2,1)S(1)} %get-tuple-element.60), channel_id=1, source_target_pairs={{0,24},{1,25},{2,26},{3,27},{4,28},{5,29},{6,30},{7,31},{8,0},{9,1... | collective-permute-start | bytes 1572872 | tf_op jit(solution)/shard_map/ppermute | solution.py:26
  59.5 10.5 %collective-permute-start.18 = (bf16[2,128,1024]{2,1,0:T(8,128)(2,1)S(1)}, bf16[2,128,1024]{2,1,0:T(8,128)(2,1)S(1)}, u32[]{:S(2)}, u32[]{:S(2)}) collective-permute-start(bf16[2,128,1024]{2,1,0:T(8,128)(2,1)S(1)} %get-tuple-element.61), channel_id=1, source_target_pairs={{0,8},{1,9},{2,10},{3,11},{4,12},{5,13},{6,14},{7,15},{8,16},{9,17... | collective-permute-start | bytes 1572872 | tf_op jit(solution)/shard_map/ppermute | solution.py:26
  69.9 5.0 %collective-permute-start.16 = (f32[8,512,128]{2,1,0:T(8,128)S(1)}, f32[8,512,128]{2,1,0:T(8,128)S(1)}, u32[]{:S(2)}, u32[]{:S(2)}) collective-permute-start(f32[8,512,128]{2,1,0:T(8,128)S(1)} %bitcast.8), channel_id=1, source_target_pairs={{0,1},{1,0},{2,3},{3,2},{4,5},{5,4},{6,7},{7,6},{8,9},{9,8},{10,11... | collective-permute-start | bytes 6291464 | tf_op jit(solution)/shard_map/ppermute | solution.py:26
  72.2 2.7 %collective-permute-start.19 = (f32[2,512,128]{2,1,0:T(8,128)S(1)}, f32[2,512,128]{2,1,0:T(8,128)S(1)}, u32[]{:S(2)}, u32[]{:S(2)}) collective-permute-start(f32[2,512,128]{2,1,0:T(8,128)S(1)} %get-tuple-element.63), channel_id=1, source_target_pairs={{0,1},{1,0},{2,3},{3,2},{4,5},{5,4},{6,7},{7,6},{8,9},{9,8},{10,11... | collective-permute-start | bytes 1572872 | tf_op jit(solution)/shard_map/ppermute | solution.py:26
  99.8 19.9 %collective-permute-start.20 = (f32[8,512,128]{2,1,0:T(8,128)S(1)}, f32[8,512,128]{2,1,0:T(8,128)S(1)}, u32[]{:S(2)}, u32[]{:S(2)}) collective-permute-start(f32[8,512,128]{2,1,0:T(8,128)S(1)} %get-tuple-element.69.plan), channel_id=1, source_target_pairs={{0,1},{1,0},{2,3},{3,2},{4,5},{5,4},{6,7},{7,6},{8,9},{9,8},{10,11... | collective-permute-start | bytes 6291464 | tf_op jit(solution)/shard_map/ppermute | solution.py:26
  122.5 9.9 %collective-permute-start.23 = (bf16[144,1024]{1,0:T(8,128)(2,1)S(1)}, bf16[144,1024]{1,0:T(8,128)(2,1)S(1)}, u32[]{:S(2)}, u32[]{:S(2)}) collective-permute-start(bf16[144,1024]{1,0:T(8,128)(2,1)S(1)} %get-tuple-element.79), channel_id=1, source_target_pairs={{0,4},{1,5},{2,6},{3,7},{4,0},{5,1},{6,2},{7,3},{8,12},{9,13},{10,... | collective-permute-start | bytes 884744 | tf_op jit(solution)/shard_map/ppermute | solution.py:26
  123.1 11.2 %collective-permute-start.25 = (bf16[144,1024]{1,0:T(8,128)(2,1)S(1)}, bf16[144,1024]{1,0:T(8,128)(2,1)S(1)}, u32[]{:S(2)}, u32[]{:S(2)}) collective-permute-start(bf16[144,1024]{1,0:T(8,128)(2,1)S(1)} %get-tuple-element.82), channel_id=1, source_target_pairs={{0,6},{1,7},{2,4},{3,5},{4,2},{5,3},{6,0},{7,1},{8,14},{9,15},{10,... | collective-permute-start | bytes 884744 | tf_op jit(solution)/shard_map/ppermute | solution.py:26
  126.4 11.6 %collective-permute-start.21 = (bf16[128,1024]{1,0:T(8,128)(2,1)S(1)}, bf16[128,1024]{1,0:T(8,128)(2,1)S(1)}, u32[]{:S(2)}, u32[]{:S(2)}) collective-permute-start(bf16[128,1024]{1,0:T(8,128)(2,1)S(1)} %get-tuple-element.74), channel_id=1, source_target_pairs={{0,4},{1,5},{2,6},{3,7},{4,0},{5,1},{6,2},{7,3},{8,12},{9,13},{10,... | collective-permute-start | bytes 786440 | tf_op jit(solution)/shard_map/ppermute | solution.py:26
  129.4 10.5 %collective-permute-start.22 = (bf16[128,1024]{1,0:T(8,128)(2,1)S(1)}, bf16[128,1024]{1,0:T(8,128)(2,1)S(1)}, u32[]{:S(2)}, u32[]{:S(2)}) collective-permute-start(bf16[128,1024]{1,0:T(8,128)(2,1)S(1)} %get-tuple-element.75), channel_id=1, source_target_pairs={{0,6},{1,7},{2,4},{3,5},{4,2},{5,3},{6,0},{7,1},{8,14},{9,15},{10,... | collective-permute-start | bytes 786440 | tf_op jit(solution)/shard_map/ppermute | solution.py:26
  133.0 12.0 %collective-permute-start.24 = (bf16[144,1024]{1,0:T(8,128)(2,1)S(1)}, bf16[144,1024]{1,0:T(8,128)(2,1)S(1)}, u32[]{:S(2)}, u32[]{:S(2)}) collective-permute-start(bf16[144,1024]{1,0:T(8,128)(2,1)S(1)} %shard_map.45), channel_id=1, source_target_pairs={{0,6},{1,7},{2,4},{3,5},{4,2},{5,3},{6,0},{7,1},{8,14},{9,15},{10,... | collective-permute-start | bytes 884744 | tf_op jit(solution)/shard_map/ppermute | solution.py:26
  134.9 10.1 %collective-permute-start.26 = (bf16[144,1024]{1,0:T(8,128)(2,1)S(1)}, bf16[144,1024]{1,0:T(8,128)(2,1)S(1)}, u32[]{:S(2)}, u32[]{:S(2)}) collective-permute-start(bf16[144,1024]{1,0:T(8,128)(2,1)S(1)} %shard_map.46), channel_id=1, source_target_pairs={{0,4},{1,5},{2,6},{3,7},{4,0},{5,1},{6,2},{7,3},{8,12},{9,13},{10,... | collective-permute-start | bytes 884744 | tf_op jit(solution)/shard_map/ppermute | solution.py:26

commit v11 on v9

--- a/solution.py
+++ b/solution.py
@@ -308,7 +308,7 @@
             out[here, span] = (value * total[here]).astype(out.dtype)
 
 
-TILE = 64
+TILE = 128
 
 
 def rows_1_kernel(scale, at, keep, got, far_keep, far_got, score, sent, tops, sums):

time: 147 us -> 147 us (level)
  no operation moved by 1% of the time
where the time goes in v11:
time: 147 us
  starting transfers between devices  41.5 us (28%)
  blocking collectives  39.5 us (27%)
  waiting for transfers between devices  32.2 us (22%)
  Pallas kernels  32.1 us (22%)
    ppermute x27, starting transfers between devices, move(): return lax.ppermute(value, AXES, pairs)  41.5 us
    all_to_all x4, blocking collectives, exchange(): return lax.all_to_all(sent, axes, 0, 0, tiled=True)  39.5 us
    ppermute x27, waiting for transfers between devices, move(): return lax.ppermute(value, AXES, pairs)  32.2 us
    pallas_call x19, Pallas kernels, call(): pl.pallas_call(kernel, out_shape=outs, in_specs=[pl.BlockSpec(memory_spac...  32.1 us
  transfers between devices with their start and end apart: 27, of which 15 were waited for; matrix products, arithmetic and copies ran while one was open for 0% of the time, Pallas kernels for 16%

profile of v11, /device:TPU:0, one launch (start us, length us, event | category | flops | bytes accessed | tf_op | source)
XLA Modules:
  0.0 146.6 jit_solution(13867532878994369346)
XLA Ops:
  0.0 1.1 constant_dynamic-slice_fusion
  1.1 3.2 %collective-permute-start.1 = (bf16[128,1024]{1,0:T(8,128)(2,1)S(1)}, bf16[128,1024]{1,0:T(8,128)(2,1)S(1)}, u32[]{:S(2)}, u32[]{:S(2)}) collective-permute-start(bf16[128,1024]{1,0:T(8,128)(2,1)S(1)} %get-tuple-element.83), channel_id=1, source_target_pairs={{0,2},{1,3},{2,0},{3,1},{4,6},{5,7},{6,4},{7,5},{8,10},{9,11},{10,... | collective-permute-start | bytes 786440 | tf_op jit(solution)/shard_map/ppermute | solution.py:26
  4.3 1.6 %collective-permute-start = (bf16[128,1024]{1,0:T(8,128)(2,1)S(1)}, bf16[128,1024]{1,0:T(8,128)(2,1)S(1)}, u32[]{:S(2)}, u32[]{:S(2)}) collective-permute-start(bf16[128,1024]{1,0:T(8,128)(2,1)S(1)} %get-tuple-element.84.refs_0_), channel_id=1, source_target_pairs={{0,8},{1,9},{2,10},{3,11},{4,12},{5,13},{6,14},{7,15},{8,16},{9,17... | collective-permute-start | bytes 786440 | tf_op jit(solution)/shard_map/ppermute | solution.py:26
  5.8 1.7 %collective-permute-start.10 = (bf16[128,1024]{1,0:T(8,128)(2,1)S(1)}, bf16[128,1024]{1,0:T(8,128)(2,1)S(1)}, u32[]{:S(2)}, u32[]{:S(2)}) collective-permute-start(bf16[128,1024]{1,0:T(8,128)(2,1)S(1)} %get-tuple-element.84.refs_0_), channel_id=1, source_target_pairs={{0,24},{1,25},{2,26},{3,27},{4,28},{5,29},{6,30},{7,31},{8,0},{9,1... | collective-permute-start | bytes 786440 | tf_op jit(solution)/shard_map/ppermute | solution.py:26
  7.5 3.1 %collective-permute-done.1.refs_0_ = bf16[128,1024]{1,0:T(8,128)(2,1)S(1)} collective-permute-done((bf16[128,1024]{1,0:T(8,128)(2,1)S(1)}, bf16[128,1024]{1,0:T(8,128)(2,1)S(1)}, u32[]{:S(2)}, u32[]{:S(2)}) %collective-permute-start.1) | collective-permute-done | bytes 262176 | tf_op jit(solution)/shard_map/ppermute | solution.py:26
  10.6 4.3 %collective-permute-start.2 = (bf16[128,1024]{1,0:T(8,128)(2,1)S(1)}, bf16[128,1024]{1,0:T(8,128)(2,1)S(1)}, u32[]{:S(2)}, u32[]{:S(2)}) collective-permute-start(bf16[128,1024]{1,0:T(8,128)(2,1)S(1)} %collective-permute-done.1.refs_0_), channel_id=1, source_target_pairs={{0,96},{1,97},{2,98},{3,99},{4,100},{5,101},{6,102},{7,103},{8,104... | collective-permute-start | bytes 786440 | tf_op jit(solution)/shard_map/ppermute | solution.py:26
  14.8 1.5 %collective-permute-start.5 = (bf16[256,1024]{1,0:T(8,128)(2,1)}, bf16[256,1024]{1,0:T(8,128)(2,1)S(1)}, u32[]{:S(2)}, u32[]{:S(2)}) collective-permute-start(bf16[256,1024]{1,0:T(8,128)(2,1)} %refs_0_), channel_id=1, source_target_pairs={{0,4},{1,5},{2,6},{3,7},{4,0},{5,1},{6,2},{7,3},{8,12},{9,13},{10,... | collective-permute-start | bytes 1572872 | tf_op jit(solution)/shard_map/ppermute | solution.py:26
  16.3 2.1 %collective-permute-start.6 = (bf16[256,1024]{1,0:T(8,128)(2,1)}, bf16[256,1024]{1,0:T(8,128)(2,1)S(1)}, u32[]{:S(2)}, u32[]{:S(2)}) collective-permute-start(bf16[256,1024]{1,0:T(8,128)(2,1)} %refs_0_), channel_id=1, source_target_pairs={{0,6},{1,7},{2,4},{3,5},{4,2},{5,3},{6,0},{7,1},{8,14},{9,15},{10,... | collective-permute-start | bytes 1572872 | tf_op jit(solution)/shard_map/ppermute | solution.py:26
  18.4 3.0 %collective-permute-start.11 = (bf16[128,1024]{1,0:T(8,128)(2,1)S(1)}, bf16[128,1024]{1,0:T(8,128)(2,1)S(1)}, u32[]{:S(2)}, u32[]{:S(2)}) collective-permute-start(bf16[128,1024]{1,0:T(8,128)(2,1)S(1)} %collective-permute-done.10.refs_1_), channel_id=1, source_target_pairs={{0,24},{1,25},{2,26},{3,27},{4,28},{5,29},{6,30},{7,31},{8,0},{9,1... | collective-permute-start | bytes 786440 | tf_op jit(solution)/shard_map/ppermute | solution.py:26
  21.4 1.5 %collective-permute-done.3.refs_3_ = bf16[128,1024]{1,0:T(8,128)(2,1)S(1)} collective-permute-done((bf16[128,1024]{1,0:T(8,128)(2,1)S(1)}, bf16[128,1024]{1,0:T(8,128)(2,1)S(1)}, u32[]{:S(2)}, u32[]{:S(2)}) %collective-permute-start.3) | collective-permute-done | bytes 262176 | tf_op jit(solution)/shard_map/ppermute | solution.py:26
  22.9 1.7 %collective-permute-start.4 = (bf16[128,1024]{1,0:T(8,128)(2,1)S(1)}, bf16[128,1024]{1,0:T(8,128)(2,1)S(1)}, u32[]{:S(2)}, u32[]{:S(2)}) collective-permute-start(bf16[128,1024]{1,0:T(8,128)(2,1)S(1)} %collective-permute-done.2.refs_1_), channel_id=1, source_target_pairs={{0,96},{1,97},{2,98},{3,99},{4,100},{5,101},{6,102},{7,103},{8,104... | collective-permute-start | bytes 786440 | tf_op jit(solution)/shard_map/ppermute | solution.py:26
  24.7 0.1 stack.23.at
  24.8 0.6 collective-permute-done.11.refs_2_
  25.3 0.7 shard_map.29.refs_4_.p0
  26.0 3.3 %collective-permute-start.12 = (bf16[4,128,1024]{2,1,0:T(8,128)(2,1)S(1)}, bf16[4,128,1024]{2,1,0:T(8,128)(2,1)S(1)}, u32[]{:S(2)}, u32[]{:S(2)}) collective-permute-start(bf16[4,128,1024]{2,1,0:T(8,128)(2,1)S(1)} %shard_map.29.refs_4_.p0), channel_id=1, source_target_pairs={{0,96},{1,97},{2,98},{3,99},{4,100},{5,101},{6,102},{7,103},{8,104... | collective-permute-start | bytes 3145736 | tf_op jit(solution)/shard_map/ppermute | solution.py:26
  29.3 0.0 collective-permute-start.13
  29.3 2.9 %collective-permute-done.4.refs_2_ = bf16[128,1024]{1,0:T(8,128)(2,1)S(1)} collective-permute-done((bf16[128,1024]{1,0:T(8,128)(2,1)S(1)}, bf16[128,1024]{1,0:T(8,128)(2,1)S(1)}, u32[]{:S(2)}, u32[]{:S(2)}) %collective-permute-start.4) | collective-permute-done | bytes 262176 | tf_op jit(solution)/shard_map/ppermute | solution.py:26
  32.2 0.0 collective-permute-done.5.refs_1_
  32.2 0.7 shard_map.28.refs_7_.p0
  32.8 2.9 %collective-permute-start.7 = (bf16[4,128,1024]{2,1,0:T(8,128)(2,1)S(1)}, bf16[4,128,1024]{2,1,0:T(8,128)(2,1)S(1)}, u32[]{:S(2)}, u32[]{:S(2)}) collective-permute-start(bf16[4,128,1024]{2,1,0:T(8,128)(2,1)S(1)} %shard_map.28.refs_7_.p0), channel_id=1, source_target_pairs={{0,24},{1,25},{2,26},{3,27},{4,28},{5,29},{6,30},{7,31},{8,0},{9,1... | collective-permute-start | bytes 3145736 | tf_op jit(solution)/shard_map/ppermute | solution.py:26
  35.8 3.2 %collective-permute-start.9 = (bf16[256,1024]{1,0:T(8,128)(2,1)S(1)}, bf16[256,1024]{1,0:T(8,128)(2,1)S(1)}, u32[]{:S(2)}, u32[]{:S(2)}) collective-permute-start(bf16[256,1024]{1,0:T(8,128)(2,1)S(1)} %copy-done), channel_id=1, source_target_pairs={{0,2},{1,3},{2,0},{3,1},{4,6},{5,7},{6,4},{7,5},{8,10},{9,11},{10,... | collective-permute-start | bytes 1572872 | tf_op jit(solution)/shard_map/ppermute | solution.py:26
  39.0 12.4 %collective-permute-done.12.refs_5_.next_.p1 = bf16[4,128,1024]{2,1,0:T(8,128)(2,1)S(1)} collective-permute-done((bf16[4,128,1024]{2,1,0:T(8,128)(2,1)S(1)}, bf16[4,128,1024]{2,1,0:T(8,128)(2,1)S(1)}, u32[]{:S(2)}, u32[]{:S(2)}) %collective-permute-start.12) | collective-permute-done | bytes 1048608 | tf_op jit(solution)/shard_map/ppermute | solution.py:26
  51.4 0.9 collective-permute-done.13.refs_6_.last.p3
  52.3 0.7 shard_map.31
  52.9 2.5 %collective-permute-start.14 = (bf16[2,128,1024]{2,1,0:T(8,128)(2,1)S(1)}, bf16[2,128,1024]{2,1,0:T(8,128)(2,1)S(1)}, u32[]{:S(2)}, u32[]{:S(2)}) collective-permute-start(bf16[2,128,1024]{2,1,0:T(8,128)(2,1)S(1)} %get-tuple-element.58), channel_id=1, source_target_pairs={{0,96},{1,97},{2,98},{3,99},{4,100},{5,101},{6,102},{7,103},{8,104... | collective-permute-start | bytes 1572872 | tf_op jit(solution)/shard_map/ppermute | solution.py:26
  55.5 1.7 %collective-permute-done.8.refs_9_.last.p3 = bf16[4,128,1024]{2,1,0:T(8,128)(2,1)S(1)} collective-permute-done((bf16[4,128,1024]{2,1,0:T(8,128)(2,1)S(1)}, bf16[4,128,1024]{2,1,0:T(8,128)(2,1)S(1)}, u32[]{:S(2)}, u32[]{:S(2)}) %collective-permute-start.8) | collective-permute-done | bytes 1048608 | tf_op jit(solution)/shard_map/ppermute | solution.py:26
  57.2 0.7 shard_map.34
  57.9 1.6 %collective-permute-start.17 = (bf16[2,128,1024]{2,1,0:T(8,128)(2,1)S(1)}, bf16[2,128,1024]{2,1,0:T(8,128)(2,1)S(1)}, u32[]{:S(2)}, u32[]{:S(2)}) collective-permute-start(bf16[2,128,1024]{2,1,0:T(8,128)(2,1)S(1)} %get-tuple-element.60), channel_id=1, source_target_pairs={{0,24},{1,25},{2,26},{3,27},{4,28},{5,29},{6,30},{7,31},{8,0},{9,1... | collective-permute-start | bytes 1572872 | tf_op jit(solution)/shard_map/ppermute | solution.py:26
  59.5 0.5 collective-permute-start.18
  60.0 7.7 %shard_map.30 = (f32[4,4,512,128]{3,2,1,0:T(8,128)S(1)}, bf16[2,512,1024]{2,1,0:T(8,128)(2,1)S(1)}) custom-call(s32[5]{0:T(128)S(1)} %stack.23.at, bf16[256,1024]{1,0:T(8,128)(2,1)S(1)} %copy-done, bf16[256,1024]{1,0:T(8,128)(2,1)S(1)} %collective-permute-done.5.refs_1_, bf16[256,1024]{1,0:T(8,128)(2,1)S(1)} %collective-permute-done.9.refs_2_, ...), custom_call_target="tpu_custom_call" | custom-call | flops 3221225472 | bytes 14680084 | tf_op jit(solution)/shard_map/pallas_call | solution.py:76
  67.6 0.5 collective-permute-done.15.n_b.p2_b
  68.1 1.8 %shard_map.33 = f32[2,4,512,128]{3,2,1,0:T(8,128)S(1)} custom-call(s32[5]{0:T(128)S(1)} %stack.23.at, bf16[2,512,1024]{2,1,0:T(8,128)(2,1)S(1)} %get-tuple-element.56.x, f32[4,4,512,128]{3,2,1,0:T(8,128)S(1)} %get-tuple-element.57.acc, bf16[2,128,1024]{2,1,0:T(8,128)(2,1)S(1)} %collective-permute-done.14.n_a.p2_a, ...), custom_call_target="tpu_custom_call" | custom-call | flops 26843545600 | bytes 9437204 | tf_op jit(solution)/shard_map/pallas_call | solution.py:76
  69.9 0.1 collective-permute-start.16
  70.0 2.2 %shard_map.35 = (f32[2,512,128]{2,1,0:T(8,128)S(1)}, f32[2,512,128]{2,1,0:T(8,128)S(1)}) custom-call(s32[5]{0:T(128)S(1)} %stack.23.at, bf16[2,512,1024]{2,1,0:T(8,128)(2,1)S(1)} %get-tuple-element.56.x, bf16[2,128,1024]{2,1,0:T(8,128)(2,1)S(1)} %collective-permute-done.17.f_a.p2_a, bf16[2,128,1024]{2,1,0:T(8,128)(2,1)S(1)} %collective-permute-done.18.f_b.p2_b), custom_call_target="tpu_custom_call" | custom-call | flops 536870912 | bytes 4194324 | tf_op jit(solution)/shard_map/pallas_call | solution.py:76
  72.2 0.6 collective-permute-start.19
  72.8 0.8 shard_map.32
  73.6 1.3 collective-permute-done.19.far_got
  74.9 1.7 %shard_map.36 = (f32[8,512,128]{2,1,0:T(8,128)S(1)}, f32[8,1,512]{2,1,0:T(1,128)S(1)}) custom-call(s32[5]{0:T(128)S(1)} %stack.23.at, f32[8,512,128]{2,1,0:T(8,128)S(1)} %bitcast.7, f32[8,512,128]{2,1,0:T(8,128)S(1)} %collective-permute-done.16.got, f32[2,512,128]{2,1,0:T(8,128)S(1)} %get-tuple-element.62.far_keep, ...), custom_call_target="tpu_custom_call" | custom-call | bytes 7356436 | tf_op jit(solution)/shard_map/pallas_call | solution.py:76
  76.6 8.7 %all_to_all.20.came = f32[8,1,512]{2,1,0:T(1,128)S(1)} all-to-all(f32[8,1,512]{2,1,0:T(1,128)S(1)} %get-tuple-element.64), channel_id=1, replica_groups=mesh['z'=4,'y'=4,'l'=2,'h'=2,'c'=2] {'l','h','c'}, dimensions={0} | all-to-all | bytes 32768 | tf_op jit(solution)/shard_map/all_to_all | solution.py:476
  85.3 1.3 shard_map.37
  86.6 11.9 %all_to_all.21.came = f32[16,8,128]{2,1,0:T(8,128)S(1)} all-to-all(f32[16,8,128]{2,1,0:T(8,128)S(1)} %get-tuple-element.66), channel_id=1, replica_groups=mesh['z'=4,'y'=4,'l'=2,'h'=2,'c'=2] {'z','y'}, dimensions={0} | all-to-all | bytes 131072 | tf_op jit(solution)/shard_map/all_to_all | solution.py:476
  98.5 1.2 shard_map.38
  99.7 0.0 collective-permute-start.20
  99.7 7.7 %all_to_all.22.came = f32[8,1,512]{2,1,0:T(1,128)S(1)} all-to-all(f32[8,1,512]{2,1,0:T(1,128)S(1)} %get-tuple-element.68), channel_id=1, replica_groups=mesh['z'=4,'y'=4,'l'=2,'h'=2,'c'=2] {'l','h','c'}, dimensions={0} | all-to-all | bytes 32768 | tf_op jit(solution)/shard_map/all_to_all | solution.py:476
  107.4 0.9 shard_map.39
  108.3 11.2 %all_to_all.23.came = f32[32,8,128]{2,1,0:T(8,128)S(1)} all-to-all(f32[32,8,128]{2,1,0:T(8,128)S(1)} %get-tuple-element.70), channel_id=1, replica_groups=mesh['z'=4,'y'=4,'l'=2,'h'=2,'c'=2] {'z','y','c'}, dimensions={0} | all-to-all | bytes 262144 | tf_op jit(solution)/shard_map/all_to_all | solution.py:476
  119.6 2.8 %shard_map.40 = (bf16[4,4,512,128]{3,2,1,0:T(8,128)(2,1)S(1)}, bf16[144,1024]{1,0:T(8,128)(2,1)S(1)}, bf16[144,1024]{1,0:T(8,128)(2,1)S(1)}) custom-call(s32[5]{0:T(128)S(1)} %stack.23.at, f32[32,8,128]{2,1,0:T(8,128)S(1)} %all_to_all.23.came, f32[8,512,128]{2,1,0:T(8,128)S(1)} %get-tuple-element.69.plan, f32[8,512,128]{2,1,0:T(8,128)S(1)} %collective-permute-done.20.other, ...), custom_call_target="tpu_custom_call" | custom-call | flops 2147483648 | bytes 11468820 | tf_op jit(solution)/shard_map/pallas_call | solution.py:76
  122.4 1.3 collective-permute-start.22
  123.6 2.1 %shard_map.42 = (bf16[128,1024]{1,0:T(8,128)(2,1)S(1)}, f32[128,1024]{1,0:T(8,128)S(1)}, f32[8,256]{1,0:T(8,128)S(1)}) custom-call(s32[5]{0:T(128)S(1)} %stack.23.at, bf16[4,4,512,128]{3,2,1,0:T(8,128)(2,1)S(1)} %get-tuple-element.72.weights, bf16[4,128,1024]{2,1,0:T(8,128)(2,1)S(1)} %shard_map.29.refs_4_.p0, ...), custom_call_target="tpu_custom_call" | custom-call | flops 2147483648 | bytes 7086100 | tf_op jit(solution)/shard_map/pallas_call | solution.py:76
  125.7 2.1 %collective-permute-start.21 = (bf16[128,1024]{1,0:T(8,128)(2,1)S(1)}, bf16[128,1024]{1,0:T(8,128)(2,1)S(1)}, u32[]{:S(2)}, u32[]{:S(2)}) collective-permute-start(bf16[128,1024]{1,0:T(8,128)(2,1)S(1)} %get-tuple-element.75), channel_id=1, source_target_pairs={{0,4},{1,5},{2,6},{3,7},{4,0},{5,1},{6,2},{7,3},{8,12},{9,13},{10,... | collective-permute-start | bytes 786440 | tf_op jit(solution)/shard_map/ppermute | solution.py:26
  127.8 2.1 %shard_map.44 = (bf16[128,1024]{1,0:T(8,128)(2,1)S(1)}, f32[128,1024]{1,0:T(8,128)S(1)}, f32[8,256]{1,0:T(8,128)S(1)}) custom-call(s32[5]{0:T(128)S(1)} %stack.23.at, bf16[4,4,512,128]{3,2,1,0:T(8,128)(2,1)S(1)} %get-tuple-element.72.weights, bf16[4,128,1024]{2,1,0:T(8,128)(2,1)S(1)} %shard_map.28.refs_7_.p0, ...), custom_call_target="tpu_custom_call" | custom-call | flops 2147483648 | bytes 7086100 | tf_op jit(solution)/shard_map/pallas_call | solution.py:76
  129.9 2.1 %collective-permute-start.26 = (bf16[128,1024]{1,0:T(8,128)(2,1)S(1)}, bf16[128,1024]{1,0:T(8,128)(2,1)S(1)}, u32[]{:S(2)}, u32[]{:S(2)}) collective-permute-start(bf16[128,1024]{1,0:T(8,128)(2,1)S(1)} %get-tuple-element.82), channel_id=1, source_target_pairs={{0,6},{1,7},{2,4},{3,5},{4,2},{5,3},{6,0},{7,1},{8,14},{9,15},{10,... | collective-permute-start | bytes 786440 | tf_op jit(solution)/shard_map/ppermute | solution.py:26
  132.0 0.7 collective-permute-done.22.came
  132.7 0.6 shard_map.43
  133.3 0.1 collective-permute-start.23
  133.4 0.1 collective-permute-done.24.came
  133.5 0.6 shard_map.45
  134.1 2.1 %collective-permute-start.25 = (bf16[144,1024]{1,0:T(8,128)(2,1)S(1)}, bf16[144,1024]{1,0:T(8,128)(2,1)S(1)}, u32[]{:S(2)}, u32[]{:S(2)}) collective-permute-start(bf16[144,1024]{1,0:T(8,128)(2,1)S(1)} %shard_map.45), channel_id=1, source_target_pairs={{0,6},{1,7},{2,4},{3,5},{4,2},{5,3},{6,0},{7,1},{8,14},{9,15},{10,... | collective-permute-start | bytes 884744 | tf_op jit(solution)/shard_map/ppermute | solution.py:26
  136.3 2.1 %shard_map.41 = (f32[256,1024]{1,0:T(8,128)S(1)}, f32[8,256]{1,0:T(8,128)S(1)}) custom-call(s32[5]{0:T(128)S(1)} %stack.23.at, bf16[4,4,512,128]{3,2,1,0:T(8,128)(2,1)S(1)} %get-tuple-element.72.weights, bf16[4,128,1024]{2,1,0:T(8,128)(2,1)S(1)} %shard_map.29.refs_4_.p0, bf16[4,128,1024]{2,1,0:T(8,128)(2,1)S(1)} %collective-permute-done.12.refs_5_.next_.p1, ...), custom_call_target="tpu_custom_call" | custom-call | flops 17179869184 | bytes 7348244 | tf_op jit(solution)/shard_map/pallas_call | solution.py:76
  138.3 0.8 collective-permute-done.21.l_low
  139.1 0.9 collective-permute-done.26.lh_high
  140.1 4.2 %collective-permute-done.23.l_high = bf16[144,1024]{1,0:T(8,128)(2,1)S(1)} collective-permute-done((bf16[144,1024]{1,0:T(8,128)(2,1)S(1)}, bf16[144,1024]{1,0:T(8,128)(2,1)S(1)}, u32[]{:S(2)}, u32[]{:S(2)}) %collective-permute-start.23) | collective-permute-done | bytes 294944 | tf_op jit(solution)/shard_map/ppermute | solution.py:26
  144.3 0.7 collective-permute-done.25.lh_low
  145.0 1.7 %shard_map.46 = bf16[256,1024]{1,0:T(8,128)(2,1)} custom-call(s32[5]{0:T(128)S(1)} %stack.23.at, f32[256,1024]{1,0:T(8,128)S(1)} %get-tuple-element.73.own, f32[8,256]{1,0:T(8,128)S(1)} %get-tuple-element.74.own_total, bf16[128,1024]{1,0:T(8,128)(2,1)S(1)} %collective-permute-done.21.l_low, bf16[144,1024]{1,0:T(8,128)(2,1)S(1)} %collective-permute-done.23.l_high, ...), custom_call_target="tpu_custom_call" | custom-call | bytes 2695188 | tf_op jit(solution)/shard_map/pallas_call | solution.py:76
  (17 shorter events, 0.0 us)
Async XLA Ops:
  1.1 9.5 %collective-permute-start.1 = (bf16[128,1024]{1,0:T(8,128)(2,1)S(1)}, bf16[128,1024]{1,0:T(8,128)(2,1)S(1)}, u32[]{:S(2)}, u32[]{:S(2)}) collective-permute-start(bf16[128,1024]{1,0:T(8,128)(2,1)S(1)} %get-tuple-element.83), channel_id=1, source_target_pairs={{0,2},{1,3},{2,0},{3,1},{4,6},{5,7},{6,4},{7,5},{8,10},{9,11},{10,... | collective-permute-start | bytes 786440 | tf_op jit(solution)/shard_map/ppermute | solution.py:26
  4.3 12.1 %collective-permute-start = (bf16[128,1024]{1,0:T(8,128)(2,1)S(1)}, bf16[128,1024]{1,0:T(8,128)(2,1)S(1)}, u32[]{:S(2)}, u32[]{:S(2)}) collective-permute-start(bf16[128,1024]{1,0:T(8,128)(2,1)S(1)} %get-tuple-element.84.refs_0_), channel_id=1, source_target_pairs={{0,8},{1,9},{2,10},{3,11},{4,12},{5,13},{6,14},{7,15},{8,16},{9,17... | collective-permute-start | bytes 786440 | tf_op jit(solution)/shard_map/ppermute | solution.py:26
  5.8 12.6 %collective-permute-start.10 = (bf16[128,1024]{1,0:T(8,128)(2,1)S(1)}, bf16[128,1024]{1,0:T(8,128)(2,1)S(1)}, u32[]{:S(2)}, u32[]{:S(2)}) collective-permute-start(bf16[128,1024]{1,0:T(8,128)(2,1)S(1)} %get-tuple-element.84.refs_0_), channel_id=1, source_target_pairs={{0,24},{1,25},{2,26},{3,27},{4,28},{5,29},{6,30},{7,31},{8,0},{9,1... | collective-permute-start | bytes 786440 | tf_op jit(solution)/shard_map/ppermute | solution.py:26
  10.6 10.9 %collective-permute-start.2 = (bf16[128,1024]{1,0:T(8,128)(2,1)S(1)}, bf16[128,1024]{1,0:T(8,128)(2,1)S(1)}, u32[]{:S(2)}, u32[]{:S(2)}) collective-permute-start(bf16[128,1024]{1,0:T(8,128)(2,1)S(1)} %collective-permute-done.1.refs_0_), channel_id=1, source_target_pairs={{0,96},{1,97},{2,98},{3,99},{4,100},{5,101},{6,102},{7,103},{8,104... | collective-permute-start | bytes 786440 | tf_op jit(solution)/shard_map/ppermute | solution.py:26
  14.8 8.1 %collective-permute-start.3 = (bf16[128,1024]{1,0:T(8,128)(2,1)S(1)}, bf16[128,1024]{1,0:T(8,128)(2,1)S(1)}, u32[]{:S(2)}, u32[]{:S(2)}) collective-permute-start(bf16[128,1024]{1,0:T(8,128)(2,1)S(1)} %collective-permute-done.1.refs_0_), channel_id=1, source_target_pairs={{0,32},{1,33},{2,34},{3,35},{4,36},{5,37},{6,38},{7,39},{8,40},{9,... | collective-permute-start | bytes 786440 | tf_op jit(solution)/shard_map/ppermute | solution.py:26
  14.8 17.3 %collective-permute-start.5 = (bf16[256,1024]{1,0:T(8,128)(2,1)}, bf16[256,1024]{1,0:T(8,128)(2,1)S(1)}, u32[]{:S(2)}, u32[]{:S(2)}) collective-permute-start(bf16[256,1024]{1,0:T(8,128)(2,1)} %refs_0_), channel_id=1, source_target_pairs={{0,4},{1,5},{2,6},{3,7},{4,0},{5,1},{6,2},{7,3},{8,12},{9,13},{10,... | collective-permute-start | bytes 1572872 | tf_op jit(solution)/shard_map/ppermute | solution.py:26
  16.3 15.9 %collective-permute-start.6 = (bf16[256,1024]{1,0:T(8,128)(2,1)}, bf16[256,1024]{1,0:T(8,128)(2,1)S(1)}, u32[]{:S(2)}, u32[]{:S(2)}) collective-permute-start(bf16[256,1024]{1,0:T(8,128)(2,1)} %refs_0_), channel_id=1, source_target_pairs={{0,6},{1,7},{2,4},{3,5},{4,2},{5,3},{6,0},{7,1},{8,14},{9,15},{10,... | collective-permute-start | bytes 1572872 | tf_op jit(solution)/shard_map/ppermute | solution.py:26
  18.4 6.9 %collective-permute-start.11 = (bf16[128,1024]{1,0:T(8,128)(2,1)S(1)}, bf16[128,1024]{1,0:T(8,128)(2,1)S(1)}, u32[]{:S(2)}, u32[]{:S(2)}) collective-permute-start(bf16[128,1024]{1,0:T(8,128)(2,1)S(1)} %collective-permute-done.10.refs_1_), channel_id=1, source_target_pairs={{0,24},{1,25},{2,26},{3,27},{4,28},{5,29},{6,30},{7,31},{8,0},{9,1... | collective-permute-start | bytes 786440 | tf_op jit(solution)/shard_map/ppermute | solution.py:26
  22.9 9.2 %collective-permute-start.4 = (bf16[128,1024]{1,0:T(8,128)(2,1)S(1)}, bf16[128,1024]{1,0:T(8,128)(2,1)S(1)}, u32[]{:S(2)}, u32[]{:S(2)}) collective-permute-start(bf16[128,1024]{1,0:T(8,128)(2,1)S(1)} %collective-permute-done.2.refs_1_), channel_id=1, source_target_pairs={{0,96},{1,97},{2,98},{3,99},{4,100},{5,101},{6,102},{7,103},{8,104... | collective-permute-start | bytes 786440 | tf_op jit(solution)/shard_map/ppermute | solution.py:26
  24.8 11.0 %copy-start = (bf16[256,1024]{1,0:T(8,128)(2,1)S(1)}, bf16[256,1024]{1,0:T(8,128)(2,1)}, u32[]{:S(2)}) copy-start(bf16[256,1024]{1,0:T(8,128)(2,1)} %refs_0_) | copy-start | bytes 1572868
  26.0 25.4 %collective-permute-start.12 = (bf16[4,128,1024]{2,1,0:T(8,128)(2,1)S(1)}, bf16[4,128,1024]{2,1,0:T(8,128)(2,1)S(1)}, u32[]{:S(2)}, u32[]{:S(2)}) collective-permute-start(bf16[4,128,1024]{2,1,0:T(8,128)(2,1)S(1)} %shard_map.29.refs_4_.p0), channel_id=1, source_target_pairs={{0,96},{1,97},{2,98},{3,99},{4,100},{5,101},{6,102},{7,103},{8,104... | collective-permute-start | bytes 3145736 | tf_op jit(solution)/shard_map/ppermute | solution.py:26
  29.3 23.0 %collective-permute-start.13 = (bf16[4,128,1024]{2,1,0:T(8,128)(2,1)S(1)}, bf16[4,128,1024]{2,1,0:T(8,128)(2,1)S(1)}, u32[]{:S(2)}, u32[]{:S(2)}) collective-permute-start(bf16[4,128,1024]{2,1,0:T(8,128)(2,1)S(1)} %shard_map.29.refs_4_.p0), channel_id=1, source_target_pairs={{0,32},{1,33},{2,34},{3,35},{4,36},{5,37},{6,38},{7,39},{8,40},{9,... | collective-permute-start | bytes 3145736 | tf_op jit(solution)/shard_map/ppermute | solution.py:26
  32.8 22.6 %collective-permute-start.7 = (bf16[4,128,1024]{2,1,0:T(8,128)(2,1)S(1)}, bf16[4,128,1024]{2,1,0:T(8,128)(2,1)S(1)}, u32[]{:S(2)}, u32[]{:S(2)}) collective-permute-start(bf16[4,128,1024]{2,1,0:T(8,128)(2,1)S(1)} %shard_map.28.refs_7_.p0), channel_id=1, source_target_pairs={{0,24},{1,25},{2,26},{3,27},{4,28},{5,29},{6,30},{7,31},{8,0},{9,1... | collective-permute-start | bytes 3145736 | tf_op jit(solution)/shard_map/ppermute | solution.py:26
  35.8 21.4 %collective-permute-start.8 = (bf16[4,128,1024]{2,1,0:T(8,128)(2,1)S(1)}, bf16[4,128,1024]{2,1,0:T(8,128)(2,1)S(1)}, u32[]{:S(2)}, u32[]{:S(2)}) collective-permute-start(bf16[4,128,1024]{2,1,0:T(8,128)(2,1)S(1)} %shard_map.28.refs_7_.p0), channel_id=1, source_target_pairs={{0,8},{1,9},{2,10},{3,11},{4,12},{5,13},{6,14},{7,15},{8,16},{9,17... | collective-permute-start | bytes 3145736 | tf_op jit(solution)/shard_map/ppermute | solution.py:26
  35.8 19.7 %collective-permute-start.9 = (bf16[256,1024]{1,0:T(8,128)(2,1)S(1)}, bf16[256,1024]{1,0:T(8,128)(2,1)S(1)}, u32[]{:S(2)}, u32[]{:S(2)}) collective-permute-start(bf16[256,1024]{1,0:T(8,128)(2,1)S(1)} %copy-done), channel_id=1, source_target_pairs={{0,2},{1,3},{2,0},{3,1},{4,6},{5,7},{6,4},{7,5},{8,10},{9,11},{10,... | collective-permute-start | bytes 1572872 | tf_op jit(solution)/shard_map/ppermute | solution.py:26
  52.9 14.7 %collective-permute-start.14 = (bf16[2,128,1024]{2,1,0:T(8,128)(2,1)S(1)}, bf16[2,128,1024]{2,1,0:T(8,128)(2,1)S(1)}, u32[]{:S(2)}, u32[]{:S(2)}) collective-permute-start(bf16[2,128,1024]{2,1,0:T(8,128)(2,1)S(1)} %get-tuple-element.58), channel_id=1, source_target_pairs={{0,96},{1,97},{2,98},{3,99},{4,100},{5,101},{6,102},{7,103},{8,104... | collective-permute-start | bytes 1572872 | tf_op jit(solution)/shard_map/ppermute | solution.py:26
  55.5 12.6 %collective-permute-start.15 = (bf16[2,128,1024]{2,1,0:T(8,128)(2,1)S(1)}, bf16[2,128,1024]{2,1,0:T(8,128)(2,1)S(1)}, u32[]{:S(2)}, u32[]{:S(2)}) collective-permute-start(bf16[2,128,1024]{2,1,0:T(8,128)(2,1)S(1)} %get-tuple-element.59), channel_id=1, source_target_pairs={{0,32},{1,33},{2,34},{3,35},{4,36},{5,37},{6,38},{7,39},{8,40},{9,... | collective-permute-start | bytes 1572872 | tf_op jit(solution)/shard_map/ppermute | solution.py:26
  57.9 12.1 %collective-permute-start.17 = (bf16[2,128,1024]{2,1,0:T(8,128)(2,1)S(1)}, bf16[2,128,1024]{2,1,0:T(8,128)(2,1)S(1)}, u32[]{:S(2)}, u32[]{:S(2)}) collective-permute-start(bf16[2,128,1024]{2,1,0:T(8,128)(2,1)S(1)} %get-tuple-element.60), channel_id=1, source_target_pairs={{0,24},{1,25},{2,26},{3,27},{4,28},{5,29},{6,30},{7,31},{8,0},{9,1... | collective-permute-start | bytes 1572872 | tf_op jit(solution)/shard_map/ppermute | solution.py:26
  59.5 10.5 %collective-permute-start.18 = (bf16[2,128,1024]{2,1,0:T(8,128)(2,1)S(1)}, bf16[2,128,1024]{2,1,0:T(8,128)(2,1)S(1)}, u32[]{:S(2)}, u32[]{:S(2)}) collective-permute-start(bf16[2,128,1024]{2,1,0:T(8,128)(2,1)S(1)} %get-tuple-element.61), channel_id=1, source_target_pairs={{0,8},{1,9},{2,10},{3,11},{4,12},{5,13},{6,14},{7,15},{8,16},{9,17... | collective-permute-start | bytes 1572872 | tf_op jit(solution)/shard_map/ppermute | solution.py:26
  69.9 5.0 %collective-permute-start.16 = (f32[8,512,128]{2,1,0:T(8,128)S(1)}, f32[8,512,128]{2,1,0:T(8,128)S(1)}, u32[]{:S(2)}, u32[]{:S(2)}) collective-permute-start(f32[8,512,128]{2,1,0:T(8,128)S(1)} %bitcast.8), channel_id=1, source_target_pairs={{0,1},{1,0},{2,3},{3,2},{4,5},{5,4},{6,7},{7,6},{8,9},{9,8},{10,11... | collective-permute-start | bytes 6291464 | tf_op jit(solution)/shard_map/ppermute | solution.py:26
  72.2 2.7 %collective-permute-start.19 = (f32[2,512,128]{2,1,0:T(8,128)S(1)}, f32[2,512,128]{2,1,0:T(8,128)S(1)}, u32[]{:S(2)}, u32[]{:S(2)}) collective-permute-start(f32[2,512,128]{2,1,0:T(8,128)S(1)} %get-tuple-element.63), channel_id=1, source_target_pairs={{0,1},{1,0},{2,3},{3,2},{4,5},{5,4},{6,7},{7,6},{8,9},{9,8},{10,11... | collective-permute-start | bytes 1572872 | tf_op jit(solution)/shard_map/ppermute | solution.py:26
  99.7 19.9 %collective-permute-start.20 = (f32[8,512,128]{2,1,0:T(8,128)S(1)}, f32[8,512,128]{2,1,0:T(8,128)S(1)}, u32[]{:S(2)}, u32[]{:S(2)}) collective-permute-start(f32[8,512,128]{2,1,0:T(8,128)S(1)} %get-tuple-element.69.plan), channel_id=1, source_target_pairs={{0,1},{1,0},{2,3},{3,2},{4,5},{5,4},{6,7},{7,6},{8,9},{9,8},{10,11... | collective-permute-start | bytes 6291464 | tf_op jit(solution)/shard_map/ppermute | solution.py:26
  122.4 10.3 %collective-permute-start.22 = (bf16[144,1024]{1,0:T(8,128)(2,1)S(1)}, bf16[144,1024]{1,0:T(8,128)(2,1)S(1)}, u32[]{:S(2)}, u32[]{:S(2)}) collective-permute-start(bf16[144,1024]{1,0:T(8,128)(2,1)S(1)} %get-tuple-element.78), channel_id=1, source_target_pairs={{0,6},{1,7},{2,4},{3,5},{4,2},{5,3},{6,0},{7,1},{8,14},{9,15},{10,... | collective-permute-start | bytes 884744 | tf_op jit(solution)/shard_map/ppermute | solution.py:26
  123.6 9.9 %collective-permute-start.24 = (bf16[144,1024]{1,0:T(8,128)(2,1)S(1)}, bf16[144,1024]{1,0:T(8,128)(2,1)S(1)}, u32[]{:S(2)}, u32[]{:S(2)}) collective-permute-start(bf16[144,1024]{1,0:T(8,128)(2,1)S(1)} %get-tuple-element.81), channel_id=1, source_target_pairs={{0,4},{1,5},{2,6},{3,7},{4,0},{5,1},{6,2},{7,3},{8,12},{9,13},{10,... | collective-permute-start | bytes 884744 | tf_op jit(solution)/shard_map/ppermute | solution.py:26
  125.7 13.4 %collective-permute-start.21 = (bf16[128,1024]{1,0:T(8,128)(2,1)S(1)}, bf16[128,1024]{1,0:T(8,128)(2,1)S(1)}, u32[]{:S(2)}, u32[]{:S(2)}) collective-permute-start(bf16[128,1024]{1,0:T(8,128)(2,1)S(1)} %get-tuple-element.75), channel_id=1, source_target_pairs={{0,4},{1,5},{2,6},{3,7},{4,0},{5,1},{6,2},{7,3},{8,12},{9,13},{10,... | collective-permute-start | bytes 786440 | tf_op jit(solution)/shard_map/ppermute | solution.py:26
  129.9 10.2 %collective-permute-start.26 = (bf16[128,1024]{1,0:T(8,128)(2,1)S(1)}, bf16[128,1024]{1,0:T(8,128)(2,1)S(1)}, u32[]{:S(2)}, u32[]{:S(2)}) collective-permute-start(bf16[128,1024]{1,0:T(8,128)(2,1)S(1)} %get-tuple-element.82), channel_id=1, source_target_pairs={{0,6},{1,7},{2,4},{3,5},{4,2},{5,3},{6,0},{7,1},{8,14},{9,15},{10,... | collective-permute-start | bytes 786440 | tf_op jit(solution)/shard_map/ppermute | solution.py:26
  133.3 11.0 %collective-permute-start.23 = (bf16[144,1024]{1,0:T(8,128)(2,1)S(1)}, bf16[144,1024]{1,0:T(8,128)(2,1)S(1)}, u32[]{:S(2)}, u32[]{:S(2)}) collective-permute-start(bf16[144,1024]{1,0:T(8,128)(2,1)S(1)} %shard_map.43), channel_id=1, source_target_pairs={{0,4},{1,5},{2,6},{3,7},{4,0},{5,1},{6,2},{7,3},{8,12},{9,13},{10,... | collective-permute-start | bytes 884744 | tf_op jit(solution)/shard_map/ppermute | solution.py:26
  134.1 10.8 %collective-permute-start.25 = (bf16[144,1024]{1,0:T(8,128)(2,1)S(1)}, bf16[144,1024]{1,0:T(8,128)(2,1)S(1)}, u32[]{:S(2)}, u32[]{:S(2)}) collective-permute-start(bf16[144,1024]{1,0:T(8,128)(2,1)S(1)} %shard_map.45), channel_id=1, source_target_pairs={{0,6},{1,7},{2,4},{3,5},{4,2},{5,3},{6,0},{7,1},{8,14},{9,15},{10,... | collective-permute-start | bytes 884744 | tf_op jit(solution)/shard_map/ppermute | solution.py:26
